TPU v7x, 32 devices: a whole 2x2x4 slice. The times are simulated.
32 devices in a mesh: row: 8 (over y, x, core), col: 4 (over z).
Axes of the slice: x: 2, y: 2, z: 4, core: 2. Of those that a mesh axis runs over, the one named last changes fastest.
Arguments:
- tokens: bfloat16 [32, 128, 256], P('row', 'col'), may hold values from -6 to 6
- gain: float32 [256], replicated, may hold values from 0.25 to 1.75
- w_qkv: bfloat16 [256, 768], replicated, may hold values from -0.375 to 0.375
- head_scale: float32 [4], replicated, may hold values from 3 to 12
- w_out: bfloat16 [256, 256], replicated, may hold values from -0.375 to 0.375
- w_merge: bfloat16 [1024, 512], replicated, may hold values from -0.1875 to 0.1875
- d_merged: bfloat16 [16, 64, 512], P('row', 'col'), may hold values from -1 to 1
- d_skip: bfloat16 [32, 128, 256], P('row', 'col'), may hold values from -1 to 1
Outputs:
- skip_out: bfloat16 [32, 128, 256], P('row', 'col')
- merged: bfloat16 [16, 64, 512], P('row', 'col')
- grad_tokens: bfloat16 [32, 128, 256], P('row', 'col')
- grad_qkv: float32 [256, 768], P('row', 'col')
- grad_out: float32 [256, 256], P('row', 'col')
- grad_merge: float32 [1024, 512], P('row', 'col')
- grad_gain: float32 [256], replicated
- grad_scale: float32 [4], replicated
All inputs are finite; a program needn't handle non-finite values.
Results may differ from a plain program's by a relative error of at most 0.012.
The roundings to bfloat16 on the way count: a program that leaves them out, or rounds other values in their place, can miss the bound.
Values may be sent and summed in bfloat16 or wider, within the bound.
No kernel may reach another device: no remote copies, remote signals or barrier semaphores. Data moves between devices by JAX's collectives and lax.ppermute only.
A program may use at most 64 MiB of HBM per device.

v0:
```python
import jax
import jax.numpy as jnp
import numpy as np
from jax import lax
from jax.sharding import PartitionSpec as P

RADIUS = 3
TILE_R = 4
TILE_C = 16
IMG_MAX = 512


EPS = 1e-06


def extended(value, sides, width):
    for axis, dim in sides:
        count, length = (lax.axis_size(axis), value.shape[dim])
        up = [(i, (i + 1) % count) for i in range(count - 1)]
        down = [(j, i) for i, j in up]
        last = lax.slice_in_dim(value, length - width, length, axis=dim)
        initial = lax.slice_in_dim(value, 0, width, axis=dim)
        before = lax.ppermute(last, axis, up)
        after = lax.ppermute(initial, axis, down)
        value = jnp.concatenate([before, value, after], axis=dim)
    return value


def passed_along(value, axis, steps):
    count = lax.axis_size(axis)
    initial, last = (max(0, -steps), min(count, count - steps))
    return lax.ppermute(value, axis, [(source, source + steps) for source in range(initial, last)])


def split_queries(block):
    rows, cols, feats = block.shape
    part = block.reshape(rows // TILE_R, TILE_R, cols // TILE_C, TILE_C, feats).transpose(
        0, 2, 1, 3, 4
    )
    return part.reshape(rows // TILE_R, cols // TILE_C, TILE_R * TILE_C, feats)


def join_queries(tiles, rows, cols):
    feats = tiles.shape[-1]
    part = tiles.reshape(rows // TILE_R, cols // TILE_C, TILE_R, TILE_C, feats).transpose(
        0, 2, 1, 3, 4
    )
    return part.reshape(rows, cols, feats)


def cut_block(padded, cols):
    span_r = TILE_R + 2 * RADIUS
    span_c = TILE_C + 2 * RADIUS
    feats = padded.shape[-1]
    count = cols // TILE_C
    parts = [padded[:, j * TILE_C : j * TILE_C + span_c] for j in range(count)]
    return jnp.stack(parts, axis=0).reshape(1, count, span_r * span_c, feats)


def add_block(tiles, cols):
    span_r = TILE_R + 2 * RADIUS
    span_c = TILE_C + 2 * RADIUS
    feats = tiles.shape[-1]
    count = cols // TILE_C
    pieces = tiles.reshape(count, span_r, span_c, feats)
    total = jnp.zeros((span_r, cols + 2 * RADIUS, feats), tiles.dtype)
    for j in range(count):
        total = total.at[:, j * TILE_C : j * TILE_C + span_c].add(pieces[j])
    return total


def window_mask():
    span_c = TILE_C + 2 * RADIUS
    count = (TILE_R + 2 * RADIUS) * span_c
    query_r = np.arange(TILE_R * TILE_C) // TILE_C
    query_c = np.arange(TILE_R * TILE_C) % TILE_C
    key_r = np.arange(count) // span_c
    key_c = np.arange(count) % span_c
    diff_r = key_r[None, :] - query_r[:, None]
    diff_c = key_c[None, :] - query_c[:, None]
    return jnp.asarray(
        (diff_r >= 0) & (diff_r <= 2 * RADIUS) & (diff_c >= 0) & (diff_c <= 2 * RADIUS)
    )


def attend(q_tiles, kv_tiles, valid_tiles, heads):
    nrow, ncol, nq, width = q_tiles.shape
    nk = kv_tiles.shape[2]
    dim = width // heads
    query = q_tiles.reshape(nrow, ncol, nq, heads, dim)
    keys = kv_tiles[..., :width].reshape(nrow, ncol, nk, heads, dim)
    values = kv_tiles[..., width:].reshape(nrow, ncol, nk, heads, dim)
    scores = jnp.einsum("abqhe,abkhe->abhqk", query, keys, preferred_element_type=jnp.float32)
    allowed = window_mask()[None, None, None] & valid_tiles[:, :, None, None, :]
    expo = jnp.where(allowed, jnp.exp(scores), 0.0)
    prob = expo / jnp.sum(expo, axis=-1, keepdims=True)
    weights = prob.astype(jnp.bfloat16)
    out = jnp.einsum("abhqk,abkhe->abqhe", weights, values, preferred_element_type=jnp.float32)
    return (out.reshape(nrow, ncol, nq, width).astype(jnp.bfloat16), prob)


def attend_back(q_tiles, kv_tiles, prob, grad_tiles, heads):
    nrow, ncol, nq, width = q_tiles.shape
    nk = kv_tiles.shape[2]
    dim = width // heads
    query = q_tiles.reshape(nrow, ncol, nq, heads, dim)
    keys = kv_tiles[..., :width].reshape(nrow, ncol, nk, heads, dim)
    values = kv_tiles[..., width:].reshape(nrow, ncol, nk, heads, dim)
    grads = grad_tiles.reshape(nrow, ncol, nq, heads, dim)
    d_weights = jnp.einsum("abqhe,abkhe->abhqk", grads, values, preferred_element_type=jnp.float32)
    d_scores = prob * (d_weights - jnp.sum(d_weights * prob, axis=-1, keepdims=True))
    score_grad = d_scores.astype(jnp.bfloat16)
    weights = prob.astype(jnp.bfloat16)
    d_query = jnp.einsum("abhqk,abkhe->abqhe", score_grad, keys, preferred_element_type=jnp.float32)
    d_keys = jnp.einsum("abhqk,abqhe->abkhe", score_grad, query, preferred_element_type=jnp.float32)
    d_values = jnp.einsum("abhqk,abqhe->abkhe", weights, grads, preferred_element_type=jnp.float32)
    kv_grad = jnp.concatenate(
        [d_keys.reshape(nrow, ncol, nk, width), d_values.reshape(nrow, ncol, nk, width)], axis=-1
    )
    return (d_query.reshape(nrow, ncol, nq, width), kv_grad)


def on_device(tokens, gain, w_qkv, head_scale, w_out, w_merge, d_merged, d_skip):
    rows, cols, width = tokens.shape
    heads = head_scale.shape[0]
    head_dim = width // heads
    x = tokens.astype(jnp.float32)
    inverse = lax.rsqrt(jnp.mean(x * x, axis=-1, keepdims=True) + EPS)
    normed = (x * inverse * gain).astype(jnp.bfloat16)
    flat_normed = normed.reshape(rows * cols, width)
    qkv = jnp.dot(flat_normed, w_qkv, preferred_element_type=jnp.float32).reshape(
        rows, cols, 3, heads, head_dim
    )
    query, key_raw, value = (qkv[:, :, 0], qkv[:, :, 1], qkv[:, :, 2])
    q_norm = lax.rsqrt(jnp.sum(query * query, axis=-1, keepdims=True) + EPS)
    k_norm = lax.rsqrt(jnp.sum(key_raw * key_raw, axis=-1, keepdims=True) + EPS)
    q_unit = query * q_norm
    k_unit = key_raw * k_norm
    q_hat = (q_unit * head_scale[:, None]).reshape(rows, cols, width).astype(jnp.bfloat16)
    kv = jnp.concatenate(
        [k_unit.reshape(rows, cols, width), value.reshape(rows, cols, width)], axis=-1
    ).astype(jnp.bfloat16)
    kv_pad = extended(kv, (("row", 0), ("col", 1)), RADIUS)
    image_rows = min(IMG_MAX, rows * lax.axis_size("row"))
    row_start = lax.axis_index("row") * rows
    col_start = lax.axis_index("col") * cols
    first = row_start // image_rows * image_rows
    grid_r = jnp.arange(rows + 2 * RADIUS, dtype=jnp.int32) + row_start - RADIUS
    grid_c = jnp.arange(cols + 2 * RADIUS, dtype=jnp.int32) + col_start - RADIUS
    inside_r = (grid_r >= first) & (grid_r < first + image_rows)
    inside_c = (grid_c >= 0) & (grid_c < cols * lax.axis_size("col"))
    inside = inside_r[:, None] & inside_c[None, :]
    starts = jnp.arange(rows // TILE_R, dtype=jnp.int32) * TILE_R

    def pieces(start):
        q_tiles = split_queries(q_hat)
        kv_tiles = cut_block(kv_pad, cols)
        valid_tiles = cut_block(inside[:, :, None], cols)[..., 0]
        return (q_tiles, kv_tiles, valid_tiles)

    def forward_rows(start):
        q_tiles, kv_tiles, valid_tiles = pieces(start)
        out, prob = attend(q_tiles, kv_tiles, valid_tiles, heads)
        return join_queries(out, TILE_R, cols)

    attn = lax.map(forward_rows, starts).reshape(rows, cols, width)
    flat_attn = attn.reshape(rows * cols, width)
    proj = jnp.dot(flat_attn, w_out, preferred_element_type=jnp.float32).reshape(rows, cols, width)
    skip_out = (x + proj).astype(jnp.bfloat16)
    merge_in = skip_out.reshape(rows // 2, 2, cols // 2, 2, width).transpose(0, 2, 1, 3, 4)
    merge_in = merge_in.reshape(rows // 2 * (cols // 2), 4 * width)
    merged = jnp.dot(merge_in, w_merge, preferred_element_type=jnp.float32).astype(jnp.bfloat16)
    merged = merged.reshape(rows // 2, cols // 2, w_merge.shape[1])
    flat_dm = d_merged.reshape(rows // 2 * (cols // 2), d_merged.shape[-1])
    grad_merge = jnp.dot(merge_in.T, flat_dm, preferred_element_type=jnp.float32)
    d_in = jnp.dot(flat_dm, w_merge.T, preferred_element_type=jnp.float32)
    d_in = (
        d_in.reshape(rows // 2, cols // 2, 2, 2, width)
        .transpose(0, 2, 1, 3, 4)
        .reshape(rows, cols, width)
    )
    d_y = d_skip.astype(jnp.float32) + d_in
    dy_b = d_y.astype(jnp.bfloat16).reshape(rows * cols, width)
    grad_out = jnp.dot(flat_attn.T, dy_b, preferred_element_type=jnp.float32)
    d_attn = (
        jnp.dot(dy_b, w_out.T, preferred_element_type=jnp.float32)
        .astype(jnp.bfloat16)
        .reshape(rows, cols, width)
    )

    def backward_rows(start):
        q_tiles, kv_tiles, valid_tiles = pieces(start)
        out, prob = attend(q_tiles, kv_tiles, valid_tiles, heads)
        d_q_tiles, d_kv_tiles = attend_back(q_tiles, kv_tiles, prob, split_queries(d_attn), heads)
        d_kv_block = add_block(d_kv_tiles, cols)
        top = d_kv_block[:RADIUS]
        middle = d_kv_block[RADIUS : RADIUS + TILE_R]
        bottom = d_kv_block[RADIUS + TILE_R :]
        return (join_queries(d_q_tiles, TILE_R, cols), top, middle, bottom)

    d_qrows, top, middle, bottom = lax.map(backward_rows, starts)
    d_qhat = d_qrows.reshape(rows, cols, width)
    top_next = jnp.concatenate([top[1:], jnp.zeros_like(top)], axis=0)
    bottom_prev = jnp.concatenate([jnp.zeros_like(bottom), bottom[:-1]], axis=0)
    full = middle + jnp.pad(top_next, ((0, 0), (TILE_R - RADIUS, 0), (0, 0), (0, 0)))
    full = full + jnp.pad(bottom_prev, ((0, 0), (0, TILE_R - RADIUS), (0, 0), (0, 0)))
    full = full.reshape(rows, cols + 2 * RADIUS, 2 * width)
    d_kv_pad = jnp.concatenate([top[0], full, bottom[-1]], axis=0)
    left_rim = d_kv_pad[:, :RADIUS]
    right_rim = d_kv_pad[:, RADIUS + cols :]
    inner = d_kv_pad[:, RADIUS : RADIUS + cols]
    from_right = passed_along(left_rim.astype(jnp.bfloat16), "col", -1).astype(left_rim.dtype)
    from_left = passed_along(right_rim.astype(jnp.bfloat16), "col", 1).astype(right_rim.dtype)
    inner = inner.at[:, cols - RADIUS :].add(from_right)
    inner = inner.at[:, :RADIUS].add(from_left)
    top_rim = inner[:RADIUS]
    bottom_rim = inner[RADIUS + rows :]
    d_kv = inner[RADIUS : RADIUS + rows]
    from_below = passed_along(top_rim.astype(jnp.bfloat16), "row", -1).astype(top_rim.dtype)
    from_above = passed_along(bottom_rim.astype(jnp.bfloat16), "row", 1).astype(bottom_rim.dtype)
    d_kv = d_kv.at[rows - RADIUS :].add(from_below)
    d_kv = d_kv.at[:RADIUS].add(from_above)
    g_qhat = d_qhat.reshape(rows, cols, heads, head_dim)
    local_scale = jnp.sum(q_unit * g_qhat, axis=(0, 1, 3))
    g_unit = g_qhat * head_scale[:, None]
    d_query = q_norm * (g_unit - q_unit * jnp.sum(q_unit * g_unit, axis=-1, keepdims=True))
    g_key = d_kv[:, :, :width].reshape(rows, cols, heads, head_dim)
    d_key = k_norm * (g_key - k_unit * jnp.sum(k_unit * g_key, axis=-1, keepdims=True))
    d_value = d_kv[:, :, width:].reshape(rows, cols, heads, head_dim)
    d_qkv = (
        jnp.stack([d_query, d_key, d_value], axis=2)
        .reshape(rows * cols, 3 * width)
        .astype(jnp.bfloat16)
    )
    grad_qkv = jnp.dot(flat_normed.T, d_qkv, preferred_element_type=jnp.float32)
    d_normed = jnp.dot(d_qkv, w_qkv.T, preferred_element_type=jnp.float32).reshape(
        rows, cols, width
    )
    local_gain = jnp.sum(x * inverse * d_normed, axis=(0, 1))
    scaled = gain * d_normed
    g_x = inverse * scaled - x * inverse**3 * jnp.mean(x * scaled, axis=-1, keepdims=True)
    grad_tokens = (d_y + g_x).astype(jnp.bfloat16)
    partial_sums = (
        lax.psum_scatter(grad_qkv, "row", scatter_dimension=0, tiled=True),
        lax.psum_scatter(grad_out, "row", scatter_dimension=0, tiled=True),
        lax.psum_scatter(grad_merge, "row", scatter_dimension=0, tiled=True),
    )
    summed = (
        lax.psum_scatter(partial_sums[0], "col", scatter_dimension=1, tiled=True),
        lax.psum_scatter(partial_sums[1], "col", scatter_dimension=1, tiled=True),
        lax.psum_scatter(partial_sums[2], "col", scatter_dimension=1, tiled=True),
    )
    grad_gain, grad_scale = lax.psum((local_gain, local_scale), ("row", "col"))
    return (skip_out, merged, grad_tokens, summed[0], summed[1], summed[2], grad_gain, grad_scale)


def solution(mesh):
    return jax.shard_map(
        on_device,
        mesh=mesh,
        in_specs=(
            P("row", "col", None),
            P(),
            P(),
            P(),
            P(),
            P(),
            P("row", "col", None),
            P("row", "col", None),
        ),
        out_specs=(
            P("row", "col", None),
            P("row", "col", None),
            P("row", "col", None),
            P("row", "col"),
            P("row", "col"),
            P("row", "col"),
            P(),
            P(),
        ),
        check_vma=False,
    )
```

profile of v0, /device:TPU:0, one launch (start us, length us, event | category | flops | bytes accessed | tf_op | source)
XLA Modules:
  0.0 253.7 jit_solution(4932736104597029103)
XLA Ops:
  7.2 1.0 fusion.26
  8.2 0.6 multiply_multiply_fusion
  8.8 1.2 copy.113
  10.0 0.9 fusion.24
  11.0 0.3 fusion.39
  11.3 0.2 fusion.9
  12.2 0.2 mul.217
  12.6 0.2 squeeze.16
  12.9 2.5 collective-permute-start
  15.4 1.3 collective-permute-start.1
  17.3 0.4 convolution_bitcast_fusion.1
  18.2 0.2 mul.224
  19.0 0.7 fusion.38
  19.7 0.9 collective-permute-done.1
  20.7 1.3 collective-permute-start.3
  22.0 4.5 %collective-permute-start.2 = (bf16[10,3,512]{2,1,0:T(4,128)(2,1)S(1)}, bf16[10,3,512]{2,1,0:T(4,128)(2,1)S(1)}, u32[]{:S(2)}, u32[]{:S(2)}) collective-permute-start(bf16[10,3,512]{2,1,0:T(4,128)(2,1)S(1)} %get-tuple-element.165), channel_id=1, source_target_pairs={{0,1},{1,2},{2,3},{4,5},{5,6},{6,7},{8,9},{9,10},{10,11},{12,13},{... | collective-permute-start | bytes 92168 | tf_op jit(solution)/shard_map/ppermute | solution.py:23
  27.0 0.8 copy.133
  27.8 0.4 collective-permute-done.2
  28.9 1.3 fusion.19
  30.2 0.9 fusion.1
  31.1 1.0 multiply_reduce_fusion
  32.0 1.1 fusion.33
  33.2 1.7 copy.123
  34.8 1.7 convert_element_type.115
  36.5 0.8 copy.124
  37.4 0.6 copy-done.9
  38.0 1.8 fusion.53
  39.7 0.9 copy.136
  40.7 0.8 multiply_convert_fusion
  41.5 1.2 fusion.51
  42.7 1.0 copy.135
  43.6 2.1 pad_maximum_fusion.1
  45.8 1.1 reshape.587
  46.8 1.1 add.162
  48.4 1.3 collective-permute-start.4
  49.8 5.0 %collective-permute-start.5 = (bf16[10,3,512]{2,1,0:T(4,128)(2,1)S(1)}, bf16[10,3,512]{2,1,0:T(4,128)(2,1)S(1)}, u32[]{:S(2)}, u32[]{:S(2)}) collective-permute-start(bf16[10,3,512]{2,1,0:T(4,128)(2,1)S(1)} %get-tuple-element.158), channel_id=1, source_target_pairs={{0,1},{1,2},{2,3},{4,5},{5,6},{6,7},{8,9},{9,10},{10,11},{12,13},{... | collective-permute-start | bytes 92168 | tf_op jit(solution)/shard_map/ppermute | solution.py:32
  54.9 0.3 scatter-add.26
  55.2 1.2 collective-permute-done.5
  56.5 0.3 scatter-add.27
  56.8 0.7 fusion.49
  57.5 1.3 collective-permute-start.6
  58.8 0.2 convolution_bitcast_fusion
  59.4 0.8 reshape_reshape.14
  60.5 3.5 %collective-permute-start.7 = (bf16[3,32,512]{2,1,0:T(8,128)(2,1)S(1)}, bf16[3,32,512]{2,1,0:T(8,128)(2,1)S(1)}, u32[]{:S(2)}, u32[]{:S(2)}) collective-permute-start(bf16[3,32,512]{2,1,0:T(8,128)(2,1)S(1)} %get-tuple-element.160), channel_id=1, source_target_pairs={{0,4},{4,8},{8,12},{12,16},{16,20},{20,24},{24,28},{1,5},{5,9},{9,... | collective-permute-start | bytes 294920 | tf_op jit(solution)/shard_map/ppermute | solution.py:32
  64.0 0.9 fusion.21
  65.3 1.4 fusion.11
  66.7 1.0 fusion.17
  68.3 0.3 convert_element_type.130
  68.6 1.2 fusion.52
  70.2 1.8 fusion.54
  72.1 28.4 %reduce-scatter.13.cloned.1.call-done = f32[32,256]{1,0:T(8,128)} async-done(((f32[256,256]{1,0:T(8,128)}), f32[32,256]{1,0:T(8,128)}) %reduce-scatter.13.cloned.1.call-update) | async-done | bytes 32784 | tf_op jit(solution)/shard_map/reduce_scatter | solution.py:245
  100.5 1.5 copy.147
  102.3 36.6 %reduce-scatter.11.cloned.1.call-done = f32[32,768]{1,0:T(8,128)} async-done(((f32[256,768]{1,0:T(8,128)}), f32[32,768]{1,0:T(8,128)}) %reduce-scatter.11.cloned.1.call-update) | async-done | bytes 98320 | tf_op jit(solution)/shard_map/reduce_scatter | solution.py:244
  138.9 1.8 copy.145
  140.8 0.9 convolution_convert_fusion.2
  141.7 0.3 convert_element_type.128
  142.0 41.9 %reduce-scatter.15.cloned.1.call-done = f32[128,512]{1,0:T(8,128)} async-done(((f32[1024,512]{1,0:T(8,128)}), f32[128,512]{1,0:T(8,128)}) %reduce-scatter.15.cloned.1.call-update) | async-done | bytes 262160 | tf_op jit(solution)/shard_map/reduce_scatter | solution.py:246
  183.9 0.4 fusion.25
  184.3 39.4 %all-reduce.3 = (f32[256]{0:T(256)}, f32[4]{0:T(128)}) all-reduce(f32[256]{0:T(256)S(1)} %get-tuple-element.142, f32[4]{0:T(128)S(1)} %reduce_sum.121), channel_id=1, replica_groups=mesh['row'=8,'col'=4] {'row','col'}, use_global_device_ids=true, to_apply=%region_16.17 | all-reduce | flops 260 | bytes 2080 | tf_op jit(solution)/shard_map/psum | solution.py:253
  223.7 0.8 fusion.30
  224.4 1.4 copy.148
  225.9 0.3 reduce-scatter.19.cloned.1.call-done
  226.2 1.6 copy.146
  227.8 19.0 %reduce-scatter.17.cloned.1.call-done = f32[128,128]{1,0:T(8,128)} async-done(((f32[128,512]{1,0:T(8,128)}), f32[128,128]{1,0:T(8,128)}) %reduce-scatter.17.cloned.1.call-update) | async-done | bytes 65552 | tf_op jit(solution)/shard_map/reduce_scatter | solution.py:251
  (146 shorter events, 6.6 us)
Async XLA Ops:
  7.2 10.1 %copy-start = (bf16[1024,512]{1,0:T(8,128)(2,1)S(1)}, bf16[1024,512]{1,0:T(8,128)(2,1)}, u32[]{:S(2)}) copy-start(bf16[1024,512]{1,0:T(8,128)(2,1)} %param.27) | copy-start | bytes 3145732
  7.2 93.3 %reduce-scatter.13.cloned.1.call-start = ((), (), s32[]{:S(2)}) async-start(), calls=%async_computation.7 | async-start | bytes 294912 | tf_op jit(solution)/shard_map/reduce_scatter | solution.py:245
  8.8 2.1 copy-start.20
  11.0 0.6 copy-start.7
  11.6 5.1 %copy-start.25 = (f32[4]{0:T(128)S(1)}, f32[4]{0:T(128)}, u32[]{:S(2)}) copy-start(f32[4]{0:T(128)} %param.25) | copy-start | bytes 52
  11.6 5.6 %copy-start.22 = (pred[64,220]{1,0:T(32,128)(4,1)S(1)}, pred[64,220]{1,0:T(32,128)(4,1)}, u32[]{:S(2)}) copy-start(pred[64,220]{1,0:T(32,128)(4,1)} %constant.244.clone) | copy-start | bytes 42244
  11.6 5.7 %copy-start.18 = (bf16[2,16,512]{2,1,0:T(8,128)(2,1)S(1)}, bf16[2,16,512]{2,1,0:T(8,128)(2,1)}, u32[]{:S(2)}) copy-start(bf16[2,16,512]{2,1,0:T(8,128)(2,1)} %param.28) | copy-start | bytes 98308
  12.8 6.0 %copy-start.16 = (bf16[4,32,256]{2,1,0:T(8,128)(2,1)S(1)}, bf16[4,32,256]{2,1,0:T(8,128)(2,1)}, u32[]{:S(2)}) copy-start(bf16[4,32,256]{2,1,0:T(8,128)(2,1)} %param.29) | copy-start | bytes 196612
  12.8 6.0 %copy-start.13 = (bf16[256,256]{1,0:T(8,128)(2,1)S(1)}, bf16[256,256]{1,0:T(8,128)(2,1)}, u32[]{:S(2)}) copy-start(bf16[256,256]{1,0:T(8,128)(2,1)} %param.26) | copy-start | bytes 393220
  12.9 6.8 %collective-permute-start = (bf16[3,32,512]{2,1,0:T(8,128)(2,1)S(1)}, bf16[3,32,512]{2,1,0:T(8,128)(2,1)S(1)}, u32[]{:S(2)}, u32[]{:S(2)}) collective-permute-start(bf16[3,32,512]{2,1,0:T(8,128)(2,1)S(1)} %get-tuple-element.166), channel_id=1, source_target_pairs={{0,4},{4,8},{8,12},{12,16},{16,20},{20,24},{24,28},{1,5},{5,9},{9,... | collective-permute-start | bytes 294920 | tf_op jit(solution)/shard_map/ppermute | solution.py:23
  15.4 5.3 %collective-permute-start.1 = (bf16[3,32,512]{2,1,0:T(8,128)(2,1)S(1)}, bf16[3,32,512]{2,1,0:T(8,128)(2,1)S(1)}, u32[]{:S(2)}, u32[]{:S(2)}) collective-permute-start(bf16[3,32,512]{2,1,0:T(8,128)(2,1)S(1)} %get-tuple-element.167), channel_id=1, source_target_pairs={{4,0},{8,4},{12,8},{16,12},{20,16},{24,20},{28,24},{5,1},{9,5},{13... | collective-permute-start | bytes 294920 | tf_op jit(solution)/shard_map/ppermute | solution.py:24
  18.8 9.0 %copy-start.11 = (bf16[4,32,256]{2,1,0:T(8,128)(2,1)}, bf16[4,32,256]{2,1,0:T(8,128)(2,1)S(1)}, u32[]{:S(2)}) copy-start(bf16[4,32,256]{2,1,0:T(8,128)(2,1)S(1)} %fusion.37) | copy-start | bytes 196612
  20.7 7.1 %collective-permute-start.3 = (bf16[10,3,512]{2,1,0:T(4,128)(2,1)S(1)}, bf16[10,3,512]{2,1,0:T(4,128)(2,1)S(1)}, u32[]{:S(2)}, u32[]{:S(2)}) collective-permute-start(bf16[10,3,512]{2,1,0:T(4,128)(2,1)S(1)} %get-tuple-element.164), channel_id=1, source_target_pairs={{1,0},{2,1},{3,2},{5,4},{6,5},{7,6},{9,8},{10,9},{11,10},{13,12},{... | collective-permute-start | bytes 92168 | tf_op jit(solution)/shard_map/ppermute | solution.py:24
  22.0 6.2 %collective-permute-start.2 = (bf16[10,3,512]{2,1,0:T(4,128)(2,1)S(1)}, bf16[10,3,512]{2,1,0:T(4,128)(2,1)S(1)}, u32[]{:S(2)}, u32[]{:S(2)}) collective-permute-start(bf16[10,3,512]{2,1,0:T(4,128)(2,1)S(1)} %get-tuple-element.165), channel_id=1, source_target_pairs={{0,1},{1,2},{2,3},{4,5},{5,6},{6,7},{8,9},{9,10},{10,11},{12,13},{... | collective-permute-start | bytes 92168 | tf_op jit(solution)/shard_map/ppermute | solution.py:23
  26.9 4.2 %copy-start.4 = (bf16[2,64,4,64]{1,3,2,0:T(8,128)(2,1)}, bf16[2,64,4,64]{1,3,2,0:T(8,128)(2,1)S(1)}, u32[]{:S(2)}) copy-start(bf16[2,64,4,64]{1,3,2,0:T(8,128)(2,1)S(1)} %copy.134) | copy-start | bytes 196612
  28.8 1.4 copy-start.5
  37.3 0.6 copy-start.9
  41.5 2.1 copy-start.1
  48.4 6.5 %collective-permute-start.4 = (bf16[10,3,512]{2,1,0:T(4,128)(2,1)S(1)}, bf16[10,3,512]{2,1,0:T(4,128)(2,1)S(1)}, u32[]{:S(2)}, u32[]{:S(2)}) collective-permute-start(bf16[10,3,512]{2,1,0:T(4,128)(2,1)S(1)} %get-tuple-element.159), channel_id=1, source_target_pairs={{1,0},{2,1},{3,2},{5,4},{6,5},{7,6},{9,8},{10,9},{11,10},{13,12},{... | collective-permute-start | bytes 92168 | tf_op jit(solution)/shard_map/ppermute | solution.py:32
  49.8 9.0 %copy-start.6 = (bf16[1,2,220,256]{2,3,1,0:T(8,128)(2,1)S(1)}, bf16[1,2,220,256]{2,3,1,0:T(8,128)(2,1)}, u32[]{:S(2)}) copy-start(bf16[1,2,220,256]{2,3,1,0:T(8,128)(2,1)} %copy-done.5) | copy-start | bytes 675844
  49.8 6.7 %collective-permute-start.5 = (bf16[10,3,512]{2,1,0:T(4,128)(2,1)S(1)}, bf16[10,3,512]{2,1,0:T(4,128)(2,1)S(1)}, u32[]{:S(2)}, u32[]{:S(2)}) collective-permute-start(bf16[10,3,512]{2,1,0:T(4,128)(2,1)S(1)} %get-tuple-element.158), channel_id=1, source_target_pairs={{0,1},{1,2},{2,3},{4,5},{5,6},{6,7},{8,9},{9,10},{10,11},{12,13},{... | collective-permute-start | bytes 92168 | tf_op jit(solution)/shard_map/ppermute | solution.py:32
  57.5 6.5 %collective-permute-start.6 = (bf16[3,32,512]{2,1,0:T(8,128)(2,1)}, bf16[3,32,512]{2,1,0:T(8,128)(2,1)}, u32[]{:S(2)}, u32[]{:S(2)}) collective-permute-start(bf16[3,32,512]{2,1,0:T(8,128)(2,1)} %get-tuple-element.161), channel_id=1, source_target_pairs={{4,0},{8,4},{12,8},{16,12},{20,16},{24,20},{28,24},{5,1},{9,5},{13... | collective-permute-start | bytes 294920 | tf_op jit(solution)/shard_map/ppermute | solution.py:32
  60.4 78.5 %reduce-scatter.11.cloned.1.call-start = ((), (), s32[]{:S(2)}) async-start(), calls=%async_computation.6 | async-start | bytes 884736 | tf_op jit(solution)/shard_map/reduce_scatter | solution.py:244
  60.5 4.4 %collective-permute-start.7 = (bf16[3,32,512]{2,1,0:T(8,128)(2,1)S(1)}, bf16[3,32,512]{2,1,0:T(8,128)(2,1)S(1)}, u32[]{:S(2)}, u32[]{:S(2)}) collective-permute-start(bf16[3,32,512]{2,1,0:T(8,128)(2,1)S(1)} %get-tuple-element.160), channel_id=1, source_target_pairs={{0,4},{4,8},{8,12},{12,16},{16,20},{20,24},{24,28},{1,5},{5,9},{9,... | collective-permute-start | bytes 294920 | tf_op jit(solution)/shard_map/ppermute | solution.py:32
  66.7 1.8 copy-start.8
  67.9 1.9 copy-start.2
  67.9 1.9 copy-start.10
  67.9 1.9 copy-start.14
  68.1 2.1 copy-start.19
  69.8 114.1 %reduce-scatter.15.cloned.1.call-start = ((), (), s32[]{:S(2)}) async-start(), calls=%async_computation.8 | async-start | bytes 2359296 | tf_op jit(solution)/shard_map/reduce_scatter | solution.py:246
  70.0 2.0 copy-start.15
  70.2 31.9 %copy-start.12 = (f32[1,4,2,16,256]{4,3,2,1,0:T(8,128)S(1)}, f32[1,4,2,16,256]{4,3,2,1,0:T(8,128)}, u32[]{:S(2)}) copy-start(f32[1,4,2,16,256]{4,3,2,1,0:T(8,128)} %get-tuple-element.147) | copy-start | bytes 393220
  72.0 111.9 %copy-start.3 = (bf16[256,768]{1,0:T(8,128)(2,1)S(1)}, bf16[256,768]{1,0:T(8,128)(2,1)}, u32[]{:S(2)}) copy-start(bf16[256,768]{1,0:T(8,128)(2,1)} %param.24) | copy-start | bytes 1179652
  72.0 111.9 %copy-start.21 = (f32[4,32]{1,0:T(4,128)S(1)}, f32[4,32]{1,0:T(4,128)}, u32[]{:S(2)}) copy-start(f32[4,32]{1,0:T(4,128)} %copy-done.20) | copy-start | bytes 1540
  72.0 111.9 %copy-start.23 = (f32[256]{0:T(256)S(1)}, f32[256]{0:T(256)}, u32[]{:S(2)}) copy-start(f32[256]{0:T(256)} %param.23) | copy-start | bytes 3076
  72.0 151.6 %copy-start.17 = (bf16[4,32,256]{2,1,0:T(8,128)(2,1)S(1)}, bf16[4,32,256]{2,1,0:T(8,128)(2,1)}, u32[]{:S(2)}) copy-start(bf16[4,32,256]{2,1,0:T(8,128)(2,1)} %param.29) | copy-start | bytes 196612
  72.0 151.6 %copy-start.24 = (f32[4,32]{1,0:T(4,128)S(1)}, f32[4,32]{1,0:T(4,128)}, u32[]{:S(2)}) copy-start(f32[4,32]{1,0:T(4,128)} %get-tuple-element.168) | copy-start | bytes 1540
  72.1 152.4 %reduce-scatter.21.cloned.1.call-start = ((), (), s32[]{:S(2)}) async-start(), calls=%async_computation.11 | async-start | bytes 163840
  102.0 124.2 %reduce-scatter.19.cloned.1.call-start = ((), (), s32[]{:S(2)}) async-start(), calls=%async_computation.10 | async-start | bytes 491520
  140.8 106.0 %reduce-scatter.17.cloned.1.call-start = ((), (), s32[]{:S(2)}) async-start(), calls=%async_computation.9 | async-start | bytes 327680 | tf_op jit(solution)/shard_map/reduce_scatter | solution.py:251
Sparse Core Ops, SparseCore 0:
  60.6 39.8 reduce-scatter.12
  103.9 34.9 reduce-scatter.10
  142.6 41.2 reduce-scatter.14
  186.0 19.1 reduce-scatter.20
  207.4 18.7 reduce-scatter.18
  228.9 17.8 reduce-scatter.16
where the time goes:
time: 255 us; the launch traced here: 254 us
  waiting for transfers between devices  129 us (51%)
  blocking collectives  39.4 us (15%)
  local copies, waits for them, and re-layouts  25.2 us (10%)
  starting transfers between devices  20.9 us (8%)
  between operations  15.1 us (6%)
  matrix products  12.7 us (5%)
  other arithmetic  11.5 us (5%)
    reduce_scatter x1, waiting for transfers between devices, on_device(): lax.psum_scatter(grad_merge, 'row', scatter_dimension=0, tiled=True)  41.9 us
    psum x1, blocking collectives, on_device(): grad_gain, grad_scale = lax.psum((local_gain, local_scale), ('row', 'col'))  39.4 us
    reduce_scatter x1, waiting for transfers between devices, on_device(): lax.psum_scatter(grad_qkv, 'row', scatter_dimension=0, tiled=True)  36.6 us
    reduce_scatter x1, waiting for transfers between devices, on_device(): lax.psum_scatter(grad_out, 'row', scatter_dimension=0, tiled=True)  28.4 us
    reduce_scatter x1, waiting for transfers between devices, on_device(): lax.psum_scatter(partial_sums[2], 'col', scatter_dimension=1, tiled=True)  19 us
    ppermute x4, starting transfers between devices, passed_along(): lax.ppermute(value, axis, [(source, source + steps) for source in range(i...  11.1 us
    unnamed x61, local copies, waits for them, and re-layouts  8.56 us
    ppermute x2, starting transfers between devices, extended(): before = lax.ppermute(last, axis, up)  7.04 us
  transfers between devices with their start and end apart: 14, of which 8 were waited for; matrix products, arithmetic and copies ran while one was open for 9% of the time, Pallas kernels for 0%

commit v1 on v0

v1 whole, which is shorter than its diff:
```python
import functools
import jax
import jax.numpy as jnp
from jax import lax
from jax.experimental import pallas as pl
from jax.experimental.pallas import tpu as pltpu
from jax.sharding import PartitionSpec as P

RADIUS = 3
IMG_MAX = 512
EPS = 1e-06
EDGE = 4
SIDE = 8
LANES = 128
BF = jnp.bfloat16
F32 = jnp.float32


def mm(a, b):
    return lax.dot_general(a, b, (((1,), (0,)), ((), ())), preferred_element_type=F32)


def mm_t(a, b):
    return lax.dot_general(a, b, (((1,), (1,)), ((), ())), preferred_element_type=F32)


def split_two(value):
    high = value.astype(BF)
    return (high, (value - high.astype(F32)).astype(BF))


def by_side(axis, near, far):
    even = lax.rem(lax.axis_index(axis), 2) == 0
    return (jnp.where(even, far, near), jnp.where(even, near, far))


def own_edge_kernel(scale_ref, tok_ref, dm_ref, gain_ref, edges_ref, dm_own_ref, rows_ref):
    rows, cols, width = tok_ref.shape
    tok = tok_ref[...].astype(F32)
    left = tok[:, :EDGE].reshape(rows * EDGE, width)
    right = tok[:, cols - EDGE :].reshape(rows * EDGE, width)
    edges_ref[...] = jnp.concatenate([left, right], axis=0).astype(BF)
    dm_own_ref[...] = dm_ref[...].reshape(dm_own_ref.shape)
    lane = lax.broadcasted_iota(jnp.int32, (1, width), 1)
    heads = scale_ref.shape[0]
    scale_row = jnp.zeros((1, width), F32)
    for h in range(heads):
        scale_row = jnp.where(lane // (width // heads) == h, scale_ref[h], scale_row)
    blank = jnp.zeros((6, width), F32)
    rows_ref[...] = jnp.concatenate([gain_ref[...], scale_row, blank], axis=0)


def edge_kernel(edges_ref, near_ref, far_ref, edge_near_ref, edge_far_ref):
    rows, cols, width = near_ref.shape
    up, down = by_side("row", near_ref[...].astype(F32), far_ref[...].astype(F32))
    up = up[rows - RADIUS :]
    down = down[:RADIUS]
    own = edges_ref[...].astype(F32)
    sides = []
    for side, at in enumerate((0, cols - EDGE)):
        parts = [
            up[:, at : at + EDGE].reshape(RADIUS * EDGE, width),
            own[side * rows * EDGE : (side + 1) * rows * EDGE],
            down[:, at : at + EDGE].reshape(RADIUS * EDGE, width),
        ]
        sides.append(jnp.concatenate(parts, axis=0))
    far, near = by_side("col", sides[1], sides[0])
    edge_near_ref[...] = near.astype(BF)
    edge_far_ref[...] = far.astype(BF)


def pair_kernel(dm_ref, dm_near_ref, dm_pair_ref):
    size = dm_pair_ref.shape[0] // 2
    own, near = [ref[...].reshape(size, -1).astype(F32) for ref in (dm_ref, dm_near_ref)]
    dm_pair_ref[...] = jnp.concatenate(in_order("row", own, near), axis=0).astype(BF)


def in_order(axis, own, partner):
    even = lax.rem(lax.axis_index(axis), 2) == 0
    return (jnp.where(even, own, partner), jnp.where(even, partner, own))


def head_sum(value, heads):
    width = value.shape[1]
    head_dim = width // heads
    same_head = lax.broadcasted_iota(jnp.int32, (width, width), 0) // head_dim == (
        lax.broadcasted_iota(jnp.int32, (width, width), 1) // head_dim
    )
    ones_bd = jnp.where(same_head, 1.0, 0.0).astype(BF)
    high, low = split_two(value)
    return mm(high, ones_bd) + mm(low, ones_bd)


def own_kernel(
    heads, tok_ref, dm_ref, dskip_ref, rows_ref, wqkv_ref, wout_ref, wmerge_ref, *refs
):
    *dm_refs, q_norm_ref, q_unit_ref, dy_ref, d_attn_ref, dm_all_ref, dscr = refs
    dm_all_ref[...] = jnp.concatenate([ref[...] for ref in dm_refs], axis=0)
    rows, cols, width = tok_ref.shape
    tokens = rows * cols
    x = tok_ref[...].reshape(tokens, width).astype(F32)
    inverse = lax.rsqrt(jnp.mean(x * x, axis=1, keepdims=True) + EPS)
    normed = (x * inverse * rows_ref[0:1]).astype(BF)
    query = mm(normed, wqkv_ref[:, :width])
    q_norm = lax.rsqrt(head_sum(query * query, heads) + EPS)
    q_norm_ref[...] = q_norm
    q_unit_ref[...] = query * q_norm
    group_wide = cols // 2
    d_in = mm_t(dm_ref[...], wmerge_ref[...])
    for i in range(rows // 2):
        for pr in range(2):
            for pc in range(2):
                for part in range(width // LANES):
                    at = (2 * pr + pc) * width + part * LANES
                    dscr[part, 2 * i + pr, pl.ds(pc, group_wide, stride=2), :] = d_in[
                        i * group_wide : (i + 1) * group_wide, at : at + LANES
                    ]
    d_group = jnp.concatenate(
        [dscr[part].reshape(tokens, LANES) for part in range(width // LANES)], axis=1
    )
    d_y = dskip_ref[...].reshape(tokens, width).astype(F32) + d_group
    dy_ref[...] = d_y
    d_attn_ref[...] = mm_t(d_y.astype(BF), wout_ref[...]).astype(BF)


def layer_kernel(
    sizes,
    tok_ref,
    row_near_ref,
    row_far_ref,
    col_near_ref,
    col_far_ref,
    rows_ref,
    q_norm_ref,
    q_unit_ref,
    dy_ref,
    d_attn_ref,
    wqkv_ref,
    wout_ref,
    wmerge_ref,
    skip_ref,
    merged_ref,
    gx_ref,
    gx_near_ref,
    gx_far_ref,
    *refs,
):
    rows, cols, width, heads, n_row, n_col = sizes
    *sum_refs, yscr = refs
    head_dim = width // heads
    wide = cols + 2 * SIDE
    ext_rows = rows + 2 * RADIUS
    tokens = rows * cols
    image_rows = min(IMG_MAX, rows * n_row)
    row_start = lax.axis_index("row") * rows
    col_index = lax.axis_index("col")
    col_start = col_index * cols
    first = row_start // image_rows * image_rows

    def inner(value, at_row=RADIUS):
        pieces = []
        for i in range(at_row, at_row + rows):
            pieces.append(value[i * wide + SIDE : i * wide + SIDE + cols])
        return jnp.concatenate(pieces, axis=0)

    lane = lax.broadcasted_iota(jnp.int32, (1, width), 1)
    def blocks(value):
        zero = jnp.zeros_like(value)
        kept = [jnp.where(lane // head_dim == h, value, zero) for h in range(heads)]
        return jnp.concatenate(kept, axis=0).astype(BF)

    gain = rows_ref[0:1]
    scale_row = rows_ref[1:2]
    up, down = by_side("row", row_near_ref[...].astype(F32), row_far_ref[...].astype(F32))
    left, right = by_side("col", col_near_ref[...].astype(F32), col_far_ref[...].astype(F32))
    own = tok_ref[...].astype(F32)
    blank = jnp.zeros((SIDE - EDGE, width), F32)
    pieces = []
    for i in range(ext_rows):
        if i < RADIUS:
            row = up[rows - RADIUS + i]
        elif i < RADIUS + rows:
            row = own[i - RADIUS]
        else:
            row = down[i - RADIUS - rows]
        edge = slice(i * EDGE, (i + 1) * EDGE)
        pieces += [blank, left[edge], row, right[edge], blank]
    x = jnp.concatenate(pieces, axis=0)
    inverse = lax.rsqrt(jnp.mean(x * x, axis=1, keepdims=True) + EPS)
    unit = x * inverse
    normed32 = (unit * gain).astype(BF).astype(F32)
    normed = normed32.astype(BF)
    x_own = inner(x)
    normed_own32 = inner(normed32)
    kv = mm(normed, wqkv_ref[:, width:])
    key_raw = kv[:, :width]
    k_norm = lax.rsqrt(head_sum(key_raw * key_raw, heads) + EPS)
    k_unit = key_raw * k_norm
    keys = k_unit.astype(BF)
    values = kv[:, width:].astype(BF)
    q_norm = q_norm_ref[...]
    q_unit = q_unit_ref[...]
    q_hat = (q_unit * scale_row).astype(BF).astype(F32)
    d_y = dy_ref[...]
    dy_b = d_y.astype(BF)
    d_attn = d_attn_ref[...].astype(F32)

    index = lax.broadcasted_iota(jnp.int32, (1, tokens), 1)
    q_row = jnp.zeros_like(index)
    for i in range(1, rows):
        q_row = q_row + (index >= i * cols).astype(jnp.int32)
    q_col = index - q_row * cols
    key_col = lax.broadcasted_iota(jnp.int32, (wide, tokens), 0) - SIDE
    near = (key_col - q_col <= RADIUS) & (key_col - q_col >= -RADIUS)
    near = near & (key_col + col_start >= 0) & (key_col + col_start < cols * n_col)
    near = jnp.where(near, 1.0, 0.0)
    parts = []
    for i in range(-RADIUS, rows + RADIUS):
        ok = (q_row - i <= RADIUS) & (q_row - i >= -RADIUS)
        ok = ok & (row_start + i >= first) & (row_start + i < first + image_rows)
        parts.append(near * jnp.where(ok, 1.0, 0.0))
    allowed = jnp.concatenate([jnp.concatenate(parts, axis=0)] * heads, axis=1)
    q_blocks = blocks(q_hat)
    g_blocks = blocks(d_attn)
    expo = jnp.exp(mm_t(keys, q_blocks)) * allowed
    prob = expo * (1.0 / jnp.sum(expo, axis=0, keepdims=True))
    weights = prob.astype(BF)
    d_w = mm_t(values, g_blocks)
    delta = jnp.sum(d_w * prob, axis=0, keepdims=True)
    d_s = (prob * (d_w - delta)).astype(BF)
    values_t = values.astype(F32).T.astype(BF)
    keys_t = keys.astype(F32).T.astype(BF)
    attn_t = []
    d_qhat_t = []
    for h in range(heads):
        feats = slice(h * head_dim, (h + 1) * head_dim)
        lanes = slice(h * tokens, (h + 1) * tokens)
        attn_t.append(mm(values_t[feats], weights[:, lanes]))
        d_qhat_t.append(mm(keys_t[feats], d_s[:, lanes]))
    attn_t = jnp.concatenate(attn_t, axis=0)
    d_qhat = jnp.concatenate(d_qhat_t, axis=0).T
    d_k = mm(d_s, q_blocks)
    d_v = mm(weights, g_blocks)

    attn = attn_t.T.astype(BF)
    y = (x_own + mm(attn, wout_ref[...])).astype(BF)
    skip_ref[...] = y.reshape(rows, cols, width)
    y32 = y.astype(F32)
    for part in range(width // LANES):
        yscr[part] = y32[:, part * LANES : (part + 1) * LANES].reshape(rows, cols, LANES)
    lines = []
    for i in range(rows // 2):
        pieces = []
        for pr in range(2):
            for pc in range(2):
                for part in range(width // LANES):
                    pieces.append(yscr[part, 2 * i + pr, pl.ds(pc, cols // 2, stride=2), :])
        lines.append(jnp.concatenate(pieces, axis=1))
    group = jnp.concatenate(lines, axis=0).astype(BF)
    merged_ref[...] = mm(group, wmerge_ref[...]).astype(BF).reshape(merged_ref.shape)
    grad_out = mm(attn_t.astype(BF), dy_b)

    scale_part = jnp.sum(q_unit * d_qhat, axis=0, keepdims=True)
    g_unit = d_qhat * scale_row
    d_query = (q_norm * (g_unit - q_unit * head_sum(q_unit * g_unit, heads))).astype(BF)
    d_key = k_norm * (d_k - k_unit * head_sum(k_unit * d_k, heads))
    d_kv = jnp.concatenate([d_key, d_v], axis=1).astype(BF)
    grad_q = mm(normed_own32.T.astype(BF), d_query)
    grad_kv = mm(normed32.T.astype(BF), d_kv)
    sums = jnp.concatenate([grad_q, grad_kv, grad_out], axis=1)
    from_q = mm_t(d_query, wqkv_ref[:, :width])
    d_normed = mm_t(d_kv, wqkv_ref[:, width:])
    pieces = []
    side = jnp.zeros((SIDE, width), F32)
    for i in range(ext_rows):
        if RADIUS <= i < RADIUS + rows:
            at = (i - RADIUS) * cols
            pieces += [side, from_q[at : at + cols], side]
        else:
            pieces.append(jnp.zeros((wide, width), F32))
    d_normed = d_normed + jnp.concatenate(pieces, axis=0)
    gain_part = jnp.sum(unit * d_normed, axis=0, keepdims=True)
    scaled = gain * d_normed
    mean = jnp.mean(x * scaled, axis=1, keepdims=True)
    g_x = inverse * scaled - x * (inverse * inverse * inverse) * mean
    far, near = by_side("row", g_x[(RADIUS + rows) * wide :], g_x[: RADIUS * wide])
    gx_near_ref[...] = near.astype(BF)
    gx_far_ref[...] = far.astype(BF)
    pieces = []
    for i in range(rows):
        at = (RADIUS + i) * wide
        middle = g_x[at + SIDE : at + SIDE + cols] + d_y[i * cols : (i + 1) * cols]
        pieces += [g_x[at : at + SIDE], middle, g_x[at + SIDE + cols : at + wide]]
    gx_ref[...] = jnp.concatenate(pieces, axis=0)
    scale_lane = lax.broadcasted_iota(jnp.int32, (1, LANES), 1)
    scale_sums = jnp.zeros((1, LANES), F32)
    for h in range(heads):
        of_head = jnp.sum(jnp.where(lane // head_dim == h, scale_part, 0.0), axis=1, keepdims=True)
        scale_sums = jnp.where(scale_lane == h, of_head, scale_sums)
    small = [gain_part[:, i * LANES : (i + 1) * LANES] for i in range(width // LANES)] + [scale_sums]
    small = jnp.concatenate(small + [jnp.zeros((8 - len(small), LANES), F32)], axis=0)
    if len(sum_refs) == 3:
        sum_refs[0][...] = sums.astype(BF)
        sum_refs[1][...] = group
        sum_refs[2][...] = small
        return
    send_ref, keep_ref, keep_group_ref, small_ref = sum_refs
    small_ref[...] = small
    per = width // n_row
    feats = 4 * width // n_row
    small = small_rows(small, per)
    group = group.astype(F32)
    even = lax.rem(lax.axis_index("row"), 2) == 0
    for q in range(n_row // 2):
        parts = []
        for value, axis, size in ((sums, 0, per), (group, 1, feats)):
            first = lax.slice_in_dim(value, 2 * q * size, (2 * q + 1) * size, axis=axis)
            second = lax.slice_in_dim(value, (2 * q + 1) * size, (2 * q + 2) * size, axis=axis)
            parts.append((jnp.where(even, first, second), jnp.where(even, second, first)))
        (keep_ref[q], sums_send), (keep_group, group_send) = parts
        keep_group_ref[q] = keep_group.astype(BF)
        sent = jnp.concatenate([sums_send, group_send], axis=1).astype(BF)
        send_ref[q] = jnp.concatenate([sent, small], axis=1)


def small_rows(small, rows):
    high = small.astype(BF).astype(F32)
    blank = jnp.zeros((rows - 16, LANES), F32)
    return jnp.concatenate([high, small - high, blank], axis=0).astype(BF)


def small_value(rows):
    value = rows.astype(F32)
    return value[:8] + value[8:16]


def core_sum_kernel(got_ref, keep_ref, keep_group_ref, small_ref, *refs):
    *out_refs, own_ref, own_group_ref, small_sum_ref, blocks_ref = refs
    chips, per, width = keep_ref.shape
    feats = keep_group_ref.shape[2]
    end = width + feats
    small = small_value(small_rows(small_ref[...], per)) + small_value(got_ref[0, :, end:])
    small_sum_ref[...] = small
    small = small_rows(small, per)
    chip = lax.axis_index("row") // 2
    own_ref[...] = keep_ref[chip] + got_ref[chip, :, :width].astype(F32)
    for q in range(chips):
        sums = keep_ref[q] + got_ref[q, :, :width].astype(F32)
        kept = keep_group_ref[q].astype(F32)
        first, second = in_order("row", kept, got_ref[q, :, width:end].astype(F32))
        block = jnp.concatenate([sums, first, second], axis=1).astype(BF)
        blocks_ref[q] = jnp.concatenate([block, small], axis=1)
    own_group_ref[...] = blocks_ref[chip, :, width : width + 2 * feats]
    for step, out_ref in enumerate(out_refs, 1):
        out_ref[...] = blocks_ref[partner(chip, step)]


def row_sum_kernel(sizes, *refs):
    rows, cols, width, n_col = sizes
    own_ref, own_group_ref, small_ref, *refs = refs
    got_refs, dm_ref, refs = (refs[:3], refs[3], refs[4:])
    gx_ref, near_ref, far_ref, *out_refs, grad_ref, slots_ref = refs
    wide = cols + 2 * SIDE
    per = own_ref.shape[0]
    feats = own_group_ref.shape[1] // 2
    at = 4 * width
    end = at + 2 * feats

    def summed(first, part):
        second, third, fourth = [part(ref) for ref in got_refs]
        return (first + second) + (third + fourth)

    sums = summed(own_ref[...], lambda ref: ref[:, :at].astype(F32))
    small = small_value(small_rows(small_ref[...], per))
    small = summed(small, lambda ref: small_value(ref[:, end:]))
    group = [own_group_ref[...]] + [ref[:, at:end] for ref in got_refs]
    group = [part[:, i * feats : (i + 1) * feats].astype(F32) for part in group for i in range(2)]
    group = jnp.concatenate(group, axis=0)
    merge = mm(group.T.astype(BF), dm_ref[...])
    g_x = gx_ref[...]
    blank = jnp.zeros(((rows - RADIUS) * wide, width), F32)
    above, below = by_side("row", near_ref[...].astype(F32), far_ref[...].astype(F32))
    g_x = g_x + jnp.concatenate([above, blank], axis=0)
    g_x = g_x + jnp.concatenate([blank, below], axis=0)
    grad = []
    left = []
    right = []
    for i in range(rows):
        spot = i * wide + SIDE
        grad.append(g_x[spot : spot + cols])
        left.append(g_x[spot - SIDE : spot][SIDE - RADIUS :])
        right.append(g_x[spot + cols : spot + cols + SIDE][:RADIUS])
    grad_ref[...] = jnp.concatenate(grad, axis=0)
    left, right = [jnp.concatenate(part, axis=0) for part in (left, right)]
    left, right = [jnp.concatenate([v[:, :LANES], v[:, LANES:]], axis=0) for v in (left, right)]
    high = small.astype(BF).astype(F32)
    small = jnp.concatenate([high[:4], (small - high)[:4]], axis=0)
    col = lax.axis_index("col")
    third = 3 * width // n_col
    fourth = width // n_col
    depth = merge.shape[1] // n_col
    for slot in range(n_col):
        parts = [
            sums[:, slot * third : (slot + 1) * third],
            sums[:, 3 * width + slot * fourth : 3 * width + (slot + 1) * fourth],
        ]
        for k in range(feats // per):
            parts.append(merge[k * per : (k + 1) * per, slot * depth : (slot + 1) * depth])
        rim = jnp.where(slot < col, left, right)
        parts.append(jnp.concatenate([rim, small], axis=0))
        slots_ref[slot] = jnp.concatenate(parts, axis=1).astype(BF)
    for step, out_ref in enumerate(out_refs):
        out_ref[...] = slots_ref[partner(col, step)]


def partner(index, step):
    if step == 0:
        return index
    low = lax.rem(index, 2)
    if step == 1:
        return index + 1 - 2 * low
    if step == 2:
        return lax.rem(index + 2, 4)
    return 3 - index


def col_sum_kernel(
    sizes, a_ref, b_ref, c_ref, d_ref, grad_ref, gqkv_ref, gout_ref, gmerge_ref, ggain_ref, gscale_ref, gtok_ref
):
    rows, cols, width = sizes
    per, lanes = a_ref.shape
    third = gqkv_ref.shape[1]
    fourth = gout_ref.shape[1]
    depth = gmerge_ref.shape[1]
    end = lanes - LANES
    reach = per - 8

    def summed(part):
        first, second, third, fourth = [part(ref) for ref in (a_ref, b_ref, c_ref, d_ref)]
        return (first + second) + (third + fourth)

    def tiny(ref):
        value = ref[:, end:].astype(F32)
        return value[reach : reach + 4] + value[reach + 4 :]

    total = summed(lambda ref: ref[:, :end].astype(F32))
    small = summed(tiny)
    gqkv_ref[...] = total[:, :third]
    gout_ref[...] = total[:, third : third + fourth]
    for k in range(gmerge_ref.shape[0] // per):
        at = third + fourth + k * depth
        gmerge_ref[k * per : (k + 1) * per] = total[:, at : at + depth]
    ggain_ref[...] = jnp.concatenate([small[i : i + 1] for i in range(width // LANES)], axis=1)
    for h in range(gscale_ref.shape[0]):
        gscale_ref[h] = small[width // LANES, h]
    col = lax.axis_index("col")

    def rim(ref):
        value = ref[:, end:].astype(F32)
        half = reach // 2
        return jnp.concatenate([value[:half], value[half:reach]], axis=1)

    left, right = by_side("col", rim(b_ref), rim(d_ref))
    left = jnp.where(col > 0, left, 0.0)
    right = jnp.where(col < lax.axis_size("col") - 1, right, 0.0)
    blank = jnp.zeros((cols - 2 * RADIUS, width), F32)
    pieces = []
    for i in range(rows):
        edge = slice(i * RADIUS, (i + 1) * RADIUS)
        pieces += [left[edge], blank, right[edge]]
    grad = grad_ref[...] + jnp.concatenate(pieces, axis=0)
    gtok_ref[...] = grad.astype(BF).reshape(rows, cols, width)


def plain_sums(sizes, sums, group, small, dm, gx, above, below):
    rows, cols, width = sizes
    wide = cols + 2 * SIDE
    sums = sums.astype(F32)
    merge = jnp.dot(group.T, dm, preferred_element_type=F32)
    outs = []
    for part in (sums[:, : 3 * width], sums[:, 3 * width :], merge):
        part = lax.psum_scatter(part, "row", scatter_dimension=0, tiled=True)
        outs.append(lax.psum_scatter(part, "col", scatter_dimension=1, tiled=True))
    small = lax.psum(small, ("row", "col"))
    gx = gx.reshape(rows, wide, width)
    gx = gx.at[:RADIUS].add(above.astype(F32).reshape(RADIUS, wide, width))
    gx = gx.at[rows - RADIUS :].add(below.astype(F32).reshape(RADIUS, wide, width))
    from_right = shifted(gx[:, :SIDE].astype(BF), "col", -1).astype(F32)
    from_left = shifted(gx[:, SIDE + cols :].astype(BF), "col", 1).astype(F32)
    grad = gx[:, SIDE : SIDE + cols].at[:, :SIDE].add(from_left)
    grad = grad.at[:, cols - SIDE :].add(from_right)
    return (grad.astype(BF), *outs, small[: width // LANES].reshape(1, width), small[width // LANES])


def shifted(value, axis, step):
    count = lax.axis_size(axis)
    pairs = [(i, i + step) for i in range(count) if 0 <= i + step < count]
    return lax.ppermute(value, axis, pairs)


def swapped(near, far, axis):
    count = lax.axis_size(axis)
    first = [(i, i + 1) for i in range(0, count - 1, 2)]
    second = [(i, i + 1) for i in range(1, count - 1, 2)]
    first = first + [(j, i) for i, j in first]
    second = second + [(j, i) for i, j in second]
    return (lax.ppermute(near, axis, first), lax.ppermute(far, axis, second))


def swap(value, axis, step):
    count = lax.axis_size(axis)
    return lax.ppermute(value, axis, [(i, i ^ step) for i in range(count)])


def vmem(count):
    return [pl.BlockSpec(memory_space=pltpu.VMEM)] * count


def on_device(tokens, gain, w_qkv, head_scale, w_out, w_merge, d_merged, d_skip):
    rows, cols, width = tokens.shape
    heads = head_scale.shape[0]
    n_row, n_col = (lax.axis_size("row"), lax.axis_size("col"))
    g_rows, g_cols, depth = d_merged.shape
    groups = g_rows * g_cols
    wide = cols + 2 * SIDE
    ext_rows = rows + 2 * RADIUS
    shape = jax.ShapeDtypeStruct
    params = pltpu.CompilerParams(vmem_limit_bytes=24 * 1024 * 1024)
    less = pltpu.CompilerParams(vmem_limit_bytes=8 * 1024 * 1024)
    row_near, row_far = swapped(tokens, tokens, "row")
    edge = shape((ext_rows * EDGE, width), BF)
    dm_pair = pl.pallas_call(
        pair_kernel,
        out_shape=shape((2 * groups, depth), BF),
        in_specs=vmem(2),
        out_specs=vmem(1)[0],
        compiler_params=less,
    )(d_merged, swap(d_merged, "row", 1))
    dm_pairs = [dm_pair] + [swap(dm_pair, "row", 2 * step) for step in range(1, 4)]
    gathered = len(dm_pairs) * 2 * groups
    edges, dm_own, two_rows = pl.pallas_call(
        own_edge_kernel,
        out_shape=(
            shape((2 * rows * EDGE, width), BF),
            shape((groups, depth), BF),
            shape((8, width), F32),
        ),
        in_specs=[pl.BlockSpec(memory_space=pltpu.SMEM)] + vmem(3),
        out_specs=tuple(vmem(3)),
        compiler_params=less,
        cost_estimate=pl.CostEstimate(flops=10**10, bytes_accessed=10**6, transcendentals=0),
    )(head_scale, tokens, d_merged, gain.reshape(1, width))
    tile = shape((rows * cols, width), F32)
    q_norm, q_unit, d_y, d_attn, dm_all = pl.pallas_call(
        functools.partial(own_kernel, heads),
        out_shape=(tile, tile, tile, shape((rows * cols, width), BF), shape((gathered, depth), BF)),
        in_specs=vmem(11),
        out_specs=tuple(vmem(5)),
        scratch_shapes=[pltpu.VMEM((width // LANES, rows, cols, LANES), F32)],
        compiler_params=params,
        cost_estimate=pl.CostEstimate(flops=2 * 10**9, bytes_accessed=10**6, transcendentals=0),
    )(tokens, dm_own, d_skip, two_rows, w_qkv, w_out, w_merge, *dm_pairs)
    edge_near, edge_far = pl.pallas_call(
        edge_kernel,
        out_shape=(edge, edge),
        in_specs=vmem(3),
        out_specs=tuple(vmem(2)),
        compiler_params=less,
    )(edges, row_near, row_far)
    col_near, col_far = swapped(edge_near, edge_far, "col")

    per = width // n_row
    feats = 4 * width // n_row
    packed = per % 16 == 0 and feats % LANES == 0 and groups == per
    packed = packed and 2 * rows * RADIUS + 8 == per and width // LANES < 4 and depth // n_col == LANES and n_col == 4 and n_row == 8
    if packed:
        sum_shapes = (
            shape((n_row // 2, per, 4 * width + feats + LANES), BF),
            shape((n_row // 2, per, 4 * width), F32),
            shape((n_row // 2, per, feats), BF),
            shape((8, LANES), F32),
        )
    else:
        sum_shapes = (
            shape((width, 4 * width), BF),
            shape((groups, 4 * width), BF),
            shape((8, LANES), F32),
        )
    sizes = (rows, cols, width, heads, n_row, n_col)
    reach = RADIUS * wide
    skip_out, merged, gx, gx_near, gx_far, *sums = pl.pallas_call(
        functools.partial(layer_kernel, sizes),
        out_shape=(
            shape((rows, cols, width), BF),
            shape((g_rows, g_cols, depth), BF),
            shape((rows * wide, width), F32),
            shape((reach, width), BF),
            shape((reach, width), BF),
        )
        + sum_shapes,
        in_specs=vmem(13),
        out_specs=tuple(vmem(5 + len(sum_shapes))),
        scratch_shapes=[
            pltpu.VMEM((width // LANES, rows, cols, LANES), F32),
        ],
        compiler_params=params,
        cost_estimate=pl.CostEstimate(flops=4 * 10**9, bytes_accessed=10**6, transcendentals=0),
    )(
        tokens,
        row_near,
        row_far,
        col_near,
        col_far,
        two_rows,
        q_norm,
        q_unit,
        d_y,
        d_attn,
        w_qkv,
        w_out,
        w_merge,
    )
    if not packed:
        above, below = by_side("row", *swapped(gx_near, gx_far, "row"))
        grad_tokens, g_qkv, g_out, g_merge, g_gain, g_scale = plain_sums(
            (rows, cols, width), *sums, d_merged.reshape(groups, depth), gx, above, below
        )
    else:
        near, far = swapped(gx_near, gx_far, "row")
        send, *kept = sums
        block = shape((per, 4 * width + 2 * feats + LANES), BF)
        *blocks, own, own_group, small = pl.pallas_call(
            core_sum_kernel,
            out_shape=(block, block, block)
            + (shape((per, 4 * width), F32), shape((per, 2 * feats), BF), shape((8, LANES), F32)),
            in_specs=vmem(4),
            out_specs=tuple(vmem(6)),
            scratch_shapes=[pltpu.VMEM((n_row // 2,) + block.shape, BF)],
            compiler_params=less,
        )(swap(send, "row", 1), *kept)
        got = [swap(blocks[step - 1], "row", 2 * step) for step in (3, 2, 1)][::-1]
        lanes = 4 * width // n_col + feats // per * (depth // n_col) + LANES
        *slots, grad = pl.pallas_call(
            functools.partial(row_sum_kernel, (rows, cols, width, n_col)),
            out_shape=tuple([shape((per, lanes), BF)] * n_col)
            + (shape((rows * cols, width), F32),),
            in_specs=vmem(10),
            out_specs=tuple(vmem(n_col + 1)),
            scratch_shapes=[pltpu.VMEM((n_col, per, lanes), BF)],
            compiler_params=less,
        )(own, own_group, small, *got, dm_all, gx, near, far)
        got = [slots[0]]
        got += [swap(slots[step], "col", step) for step in (3, 2, 1)][::-1]
        g_qkv, g_out, g_merge, g_gain, g_scale, grad_tokens = pl.pallas_call(
            functools.partial(col_sum_kernel, (rows, cols, width)),
            out_shape=(
                shape((per, 3 * width // n_col), F32),
                shape((per, width // n_col), F32),
                shape((feats, depth // n_col), F32),
                shape((1, width), F32),
                shape((heads,), F32),
                shape((rows, cols, width), BF),
            ),
            in_specs=vmem(5),
            out_specs=tuple(vmem(4)) + (pl.BlockSpec(memory_space=pltpu.SMEM), vmem(1)[0]),
            compiler_params=less,
        )(*got, grad)
    return (
        skip_out,
        merged,
        grad_tokens,
        g_qkv,
        g_out,
        g_merge,
        g_gain.reshape(width),
        g_scale[:heads],
    )


def solution(mesh):
    block = P("row", "col", None)
    return jax.shard_map(
        on_device,
        mesh=mesh,
        in_specs=(block, P(), P(), P(), P(), P(), block, block),
        out_specs=(block, block, block, P("row", "col"), P("row", "col"), P("row", "col"), P(), P()),
        check_vma=False,
    )
```

time: 255 us -> 42.4 us (0.17)
  the two profiles are of different devices: /device:TPU:0 before, /device:TPU:4 now
where the time goes in v1:
time: 42.4 us; the launch traced here: 42.2 us
  starting transfers between devices  24 us (57%)
  waiting for transfers between devices  10.7 us (25%)
  Pallas kernels  5.82 us (14%)
  between operations  0.83 us (2%)
  local copies, waits for them, and re-layouts  0.8 us (2%)
    ppermute x11, starting transfers between devices, swap(): return lax.ppermute(value, axis, [(i, i ^ step) for i in range(count)])  14.7 us
    ppermute x6, starting transfers between devices, swapped(): return (lax.ppermute(near, axis, first), lax.ppermute(far, axis, second))  9.32 us
    ppermute x11, waiting for transfers between devices, swap(): return lax.ppermute(value, axis, [(i, i ^ step) for i in range(count)])  6.43 us
    ppermute x6, waiting for transfers between devices, swapped(): return (lax.ppermute(near, axis, first), lax.ppermute(far, axis, second))  4.29 us
    pallas_call x1, Pallas kernels, on_device(): pl.pallas_call(functools.partial(layer_kernel, sizes), out_shape=(shape((...  3.34 us
  transfers between devices with their start and end apart: 17, of which 6 were waited for; matrix products, arithmetic and copies ran while one was open for 0% of the time, Pallas kernels for 3%

profile of v1, /device:TPU:4, one launch (start us, length us, event | category | flops | bytes accessed | tf_op | source)
XLA Modules:
  0.0 42.2 jit_solution(11682289862390452165)
XLA Ops:
  0.6 0.1 collective-permute-start.4
  0.7 3.4 %collective-permute-start.1 = (bf16[4,32,256]{2,1,0:T(8,128)(2,1)}, bf16[4,32,256]{2,1,0:T(8,128)(2,1)S(1)}, u32[]{:S(2)}, u32[]{:S(2)}) collective-permute-start(bf16[4,32,256]{2,1,0:T(8,128)(2,1)} %tok_ref.5), channel_id=1, source_target_pairs={{4,8},{12,16},{20,24},{8,4},{16,12},{24,20},{5,9},{13,17},{21,25},... | collective-permute-start | bytes 196616 | tf_op jit(solution)/shard_map/ppermute | solution.py:507
  4.2 0.1 collective-permute-start
  4.3 0.0 collective-permute-done.4.dm_near_ref
  4.3 0.0 copy-start
  4.3 0.8 %copy-done = bf16[2,16,512]{2,1,0:T(8,128)(2,1)S(1)} copy-done((bf16[2,16,512]{2,1,0:T(8,128)(2,1)S(1)}, bf16[2,16,512]{2,1,0:T(8,128)(2,1)}, u32[]{:S(2)}) %copy-start) | copy-done | bytes 32792
  5.1 0.0 copy-start.1
  5.1 0.0 copy-start.6
  5.1 0.0 copy-start.7
  5.1 0.0 copy-start.8
  5.1 1.5 %collective-permute-start.7 = (bf16[64,512]{1,0:T(8,128)(2,1)S(1)}, bf16[64,512]{1,0:T(8,128)(2,1)S(1)}, u32[]{:S(2)}, u32[]{:S(2)}) collective-permute-start(bf16[64,512]{1,0:T(8,128)(2,1)S(1)} %shard_map.145.refs_0_), channel_id=1, source_target_pairs={{0,24},{4,28},{8,16},{12,20},{16,8},{20,12},{24,0},{28,4},{1,25},{... | collective-permute-start | bytes 196616 | tf_op jit(solution)/shard_map/ppermute | solution.py:512
  6.6 0.6 %collective-permute-start.6 = (bf16[64,512]{1,0:T(8,128)(2,1)S(1)}, bf16[64,512]{1,0:T(8,128)(2,1)S(1)}, u32[]{:S(2)}, u32[]{:S(2)}) collective-permute-start(bf16[64,512]{1,0:T(8,128)(2,1)S(1)} %shard_map.145.refs_0_), channel_id=1, source_target_pairs={{0,16},{4,20},{8,24},{12,28},{16,0},{20,4},{24,8},{28,12},{1,17},{... | collective-permute-start | bytes 196616 | tf_op jit(solution)/shard_map/ppermute | solution.py:512
  7.2 1.5 %collective-permute-start.5 = (bf16[64,512]{1,0:T(8,128)(2,1)S(1)}, bf16[64,512]{1,0:T(8,128)(2,1)S(1)}, u32[]{:S(2)}, u32[]{:S(2)}) collective-permute-start(bf16[64,512]{1,0:T(8,128)(2,1)S(1)} %shard_map.145.refs_0_), channel_id=1, source_target_pairs={{0,8},{4,12},{8,0},{12,4},{16,24},{20,28},{24,16},{28,20},{1,9},{5... | collective-permute-start | bytes 196616 | tf_op jit(solution)/shard_map/ppermute | solution.py:512
  8.7 0.0 copy-done.1
  8.7 0.0 copy-done.6
  8.7 0.0 copy-done.7
  8.7 0.0 copy-done.8
  8.7 0.0 copy-start.2
  8.7 0.0 copy-start.3
  8.7 0.0 copy-start.5
  8.7 0.6 %shard_map.143 = (bf16[32,256]{1,0:T(8,128)(2,1)S(1)}, bf16[32,512]{1,0:T(8,128)(2,1)S(1)}, f32[8,256]{1,0:T(8,128)S(1)}) custom-call(f32[4]{0:T(128)S(1)} %copy-done.8, bf16[4,32,256]{2,1,0:T(8,128)(2,1)S(1)} %copy-done.6, bf16[2,16,512]{2,1,0:T(8,128)(2,1)S(1)} %copy-done.1, f32[1,256]{1,0:T(1,128)S(1)} %bitcast.2), custom_call_target="tpu_custom_call" | custom-call | flops 10000000000 | bytes 1000000 | tf_op jit(solution)/shard_map/pallas_call | solution.py:541
  9.3 0.0 copy-start.4
  9.3 0.0 collective-permute-done.1.far_ref.row_far_ref
  9.3 0.0 collective-permute-done.near_ref.row_near_ref
  9.4 1.6 %collective-permute-start.2 = (bf16[40,256]{1,0:T(8,128)(2,1)S(1)}, bf16[40,256]{1,0:T(8,128)(2,1)S(1)}, u32[]{:S(2)}, u32[]{:S(2)}) collective-permute-start(bf16[40,256]{1,0:T(8,128)(2,1)S(1)} %get-tuple-element.45), channel_id=1, source_target_pairs={{0,1},{2,3},{1,0},{3,2},{4,5},{6,7},{5,4},{7,6},{8,9},{10,11},{9,8... | collective-permute-start | bytes 61448 | tf_op jit(solution)/shard_map/ppermute | solution.py:507
  11.0 0.7 %collective-permute-start.3 = (bf16[40,256]{1,0:T(8,128)(2,1)S(1)}, bf16[40,256]{1,0:T(8,128)(2,1)S(1)}, u32[]{:S(2)}, u32[]{:S(2)}) collective-permute-start(bf16[40,256]{1,0:T(8,128)(2,1)S(1)} %get-tuple-element.46), channel_id=1, source_target_pairs={{1,2},{2,1},{5,6},{6,5},{9,10},{10,9},{13,14},{14,13},{17,18},{18,... | collective-permute-start | bytes 61448 | tf_op jit(solution)/shard_map/ppermute | solution.py:507
  11.7 0.0 collective-permute-done.7.refs_3_
  11.7 0.1 collective-permute-done.6.refs_2_
  11.8 0.0 collective-permute-done.5.refs_1_
  11.8 0.0 copy-done.2
  11.8 0.0 copy-done.3
  11.8 0.0 copy-done.5
  11.8 0.0 copy-done.4
  11.8 0.8 %shard_map.146 = (f32[128,256]{1,0:T(8,128)S(1)}, f32[128,256]{1,0:T(8,128)S(1)}, f32[128,256]{1,0:T(8,128)S(1)}, bf16[128,256]{1,0:T(8,128)(2,1)S(1)}, bf16[256,512]{1,0:T(8,128)(2,1)S(1)}) custom-call(bf16[4,32,256]{2,1,0:T(8,128)(2,1)S(1)} %copy-done.6, bf16[32,512]{1,0:T(8,128)(2,1)S(1)} %get-tuple-element.48.dm_ref, bf16[4,32,256]{2,1,0:T(8,128)(2,1)S(1)} %copy-done.5, ...), custom_call_target="tpu_custom_call" | custom-call | flops 2000000000 | bytes 1000000 | tf_op jit(solution)/shard_map/pallas_call | solution.py:554
  12.6 0.6 %collective-permute-done.2.col_near_ref = bf16[40,256]{1,0:T(8,128)(2,1)S(1)} collective-permute-done((bf16[40,256]{1,0:T(8,128)(2,1)S(1)}, bf16[40,256]{1,0:T(8,128)(2,1)S(1)}, u32[]{:S(2)}, u32[]{:S(2)}) %collective-permute-start.2) | collective-permute-done | bytes 20512 | tf_op jit(solution)/shard_map/ppermute | solution.py:507
  13.2 0.0 collective-permute-done.3.col_far_ref
  13.2 3.3 %shard_map.147 = (bf16[4,32,256]{2,1,0:T(8,128)(2,1)}, bf16[2,16,512]{2,1,0:T(8,128)(2,1)}, f32[192,256]{1,0:T(8,128)S(1)}, bf16[144,256]{1,0:T(8,128)(2,1)S(1)}...) custom-call(bf16[4,32,256]{2,1,0:T(8,128)(2,1)S(1)} %copy-done.6, ...), custom_call_target="tpu_custom_call" | custom-call | flops 4000000000 | bytes 1000000 | tf_op jit(solution)/shard_map/pallas_call | solution.py:591
  16.5 0.0 collective-permute-start.8
  16.5 1.6 %collective-permute-done.8.got_ref = bf16[4,32,1280]{2,1,0:T(8,128)(2,1)S(1)} collective-permute-done((bf16[4,32,1280]{2,1,0:T(8,128)(2,1)S(1)}, bf16[4,32,1280]{2,1,0:T(8,128)(2,1)S(1)}, u32[]{:S(2)}, u32[]{:S(2)}) %collective-permute-start.8) | collective-permute-done | bytes 327712 | tf_op jit(solution)/shard_map/ppermute | solution.py:512
  18.2 0.1 shard_map.148
  18.3 0.6 %collective-permute-start.9 = (bf16[32,1408]{1,0:T(8,128)(2,1)S(1)}, bf16[32,1408]{1,0:T(8,128)(2,1)S(1)}, u32[]{:S(2)}, u32[]{:S(2)}) collective-permute-start(bf16[32,1408]{1,0:T(8,128)(2,1)S(1)} %get-tuple-element.62), channel_id=1, source_target_pairs={{0,8},{4,12},{8,0},{12,4},{16,24},{20,28},{24,16},{28,20},{1,9},{5... | collective-permute-start | bytes 270344 | tf_op jit(solution)/shard_map/ppermute | solution.py:512
  18.9 1.4 %collective-permute-start.10 = (bf16[32,1408]{1,0:T(8,128)(2,1)S(1)}, bf16[32,1408]{1,0:T(8,128)(2,1)S(1)}, u32[]{:S(2)}, u32[]{:S(2)}) collective-permute-start(bf16[32,1408]{1,0:T(8,128)(2,1)S(1)} %get-tuple-element.63), channel_id=1, source_target_pairs={{0,16},{4,20},{8,24},{12,28},{16,0},{20,4},{24,8},{28,12},{1,17},{... | collective-permute-start | bytes 270344 | tf_op jit(solution)/shard_map/ppermute | solution.py:512
  20.3 1.5 %collective-permute-start.11 = (bf16[32,1408]{1,0:T(8,128)(2,1)S(1)}, bf16[32,1408]{1,0:T(8,128)(2,1)S(1)}, u32[]{:S(2)}, u32[]{:S(2)}) collective-permute-start(bf16[32,1408]{1,0:T(8,128)(2,1)S(1)} %get-tuple-element.64), channel_id=1, source_target_pairs={{0,24},{4,28},{8,16},{12,20},{16,8},{20,12},{24,0},{28,4},{1,25},{... | collective-permute-start | bytes 270344 | tf_op jit(solution)/shard_map/ppermute | solution.py:512
  21.8 0.0 collective-permute-start.12
  21.8 3.4 %collective-permute-start.13 = (bf16[144,256]{1,0:T(8,128)(2,1)S(1)}, bf16[144,256]{1,0:T(8,128)(2,1)S(1)}, u32[]{:S(2)}, u32[]{:S(2)}) collective-permute-start(bf16[144,256]{1,0:T(8,128)(2,1)S(1)} %get-tuple-element.68), channel_id=1, source_target_pairs={{4,8},{12,16},{20,24},{8,4},{16,12},{24,20},{5,9},{13,17},{21,25},... | collective-permute-start | bytes 221192 | tf_op jit(solution)/shard_map/ppermute | solution.py:507
  25.3 0.0 collective-permute-done.12.refs_8_
  25.3 3.7 %collective-permute-done.13.refs_9_ = bf16[144,256]{1,0:T(8,128)(2,1)S(1)} collective-permute-done((bf16[144,256]{1,0:T(8,128)(2,1)S(1)}, bf16[144,256]{1,0:T(8,128)(2,1)S(1)}, u32[]{:S(2)}, u32[]{:S(2)}) %collective-permute-start.13) | collective-permute-done | bytes 73760 | tf_op jit(solution)/shard_map/ppermute | solution.py:507
  29.0 0.0 collective-permute-done.9.refs_3_
  29.0 0.0 collective-permute-done.10.refs_4_
  29.0 0.0 collective-permute-done.11.refs_5_
  29.0 0.3 shard_map.149
  29.2 4.6 %collective-permute-start.14 = (bf16[32,896]{1,0:T(8,128)(2,1)S(1)}, bf16[32,896]{1,0:T(8,128)(2,1)S(1)}, u32[]{:S(2)}, u32[]{:S(2)}) collective-permute-start(bf16[32,896]{1,0:T(8,128)(2,1)S(1)} %get-tuple-element.70), channel_id=1, source_target_pairs={{0,1},{1,0},{2,3},{3,2},{4,5},{5,4},{6,7},{7,6},{8,9},{9,8},{10,11... | collective-permute-start | bytes 172040 | tf_op jit(solution)/shard_map/ppermute | solution.py:512
  33.8 1.5 %collective-permute-start.15 = (bf16[32,896]{1,0:T(8,128)(2,1)S(1)}, bf16[32,896]{1,0:T(8,128)(2,1)S(1)}, u32[]{:S(2)}, u32[]{:S(2)}) collective-permute-start(bf16[32,896]{1,0:T(8,128)(2,1)S(1)} %get-tuple-element.71), channel_id=1, source_target_pairs={{0,2},{1,3},{2,0},{3,1},{4,6},{5,7},{6,4},{7,5},{8,10},{9,11},{10,... | collective-permute-start | bytes 172040 | tf_op jit(solution)/shard_map/ppermute | solution.py:512
  35.4 1.4 %collective-permute-start.16 = (bf16[32,896]{1,0:T(8,128)(2,1)S(1)}, bf16[32,896]{1,0:T(8,128)(2,1)S(1)}, u32[]{:S(2)}, u32[]{:S(2)}) collective-permute-start(bf16[32,896]{1,0:T(8,128)(2,1)S(1)} %get-tuple-element.72), channel_id=1, source_target_pairs={{0,3},{1,2},{2,1},{3,0},{4,7},{5,6},{6,5},{7,4},{8,11},{9,10},{10,... | collective-permute-start | bytes 172040 | tf_op jit(solution)/shard_map/ppermute | solution.py:512
  36.8 0.0 collective-permute-done.14.b_ref
  36.8 3.9 %collective-permute-done.15.c_ref = bf16[32,896]{1,0:T(8,128)(2,1)S(1)} collective-permute-done((bf16[32,896]{1,0:T(8,128)(2,1)S(1)}, bf16[32,896]{1,0:T(8,128)(2,1)S(1)}, u32[]{:S(2)}, u32[]{:S(2)}) %collective-permute-start.15) | collective-permute-done | bytes 57376 | tf_op jit(solution)/shard_map/ppermute | solution.py:512
  40.6 0.8 %collective-permute-done.16.d_ref = bf16[32,896]{1,0:T(8,128)(2,1)S(1)} collective-permute-done((bf16[32,896]{1,0:T(8,128)(2,1)S(1)}, bf16[32,896]{1,0:T(8,128)(2,1)S(1)}, u32[]{:S(2)}, u32[]{:S(2)}) %collective-permute-start.16) | collective-permute-done | bytes 57376 | tf_op jit(solution)/shard_map/ppermute | solution.py:512
  41.5 0.7 %shard_map.150 = (f32[32,192]{1,0:T(8,128)}, f32[32,64]{1,0:T(8,128)}, f32[128,128]{1,0:T(8,128)}, f32[1,256]{1,0:T(1,128)}, f32[4]{0:T(128)}, /*index=5*/bf16[4,32,256]{2,1,0:T(8,128)(2,1)}) custom-call(bf16[32,896]{1,0:T(8,128)(2,1)S(1)} %get-tuple-element.69.a_ref, bf16[32,896]{1,0:T(8,128)(2,1)S(1)} %collective-permute-done.14.b_ref, ...), custom_call_target="tpu_custom_call" | custom-call | tf_op jit(solution)/shard_map/pallas_call | solution.py:654
  (2 shorter events, 0.0 us)
Async XLA Ops:
  0.6 3.7 %collective-permute-start.4 = (bf16[2,16,512]{2,1,0:T(8,128)(2,1)}, bf16[2,16,512]{2,1,0:T(8,128)(2,1)S(1)}, u32[]{:S(2)}, u32[]{:S(2)}) collective-permute-start(bf16[2,16,512]{2,1,0:T(8,128)(2,1)} %dm_ref.3), channel_id=1, source_target_pairs={{0,4},{4,0},{8,12},{12,8},{16,20},{20,16},{24,28},{28,24},{1,5},{5... | collective-permute-start | bytes 98312 | tf_op jit(solution)/shard_map/ppermute | solution.py:512
  0.7 8.6 %collective-permute-start.1 = (bf16[4,32,256]{2,1,0:T(8,128)(2,1)}, bf16[4,32,256]{2,1,0:T(8,128)(2,1)S(1)}, u32[]{:S(2)}, u32[]{:S(2)}) collective-permute-start(bf16[4,32,256]{2,1,0:T(8,128)(2,1)} %tok_ref.5), channel_id=1, source_target_pairs={{4,8},{12,16},{20,24},{8,4},{16,12},{24,20},{5,9},{13,17},{21,25},... | collective-permute-start | bytes 196616 | tf_op jit(solution)/shard_map/ppermute | solution.py:507
  4.2 5.2 %collective-permute-start = (bf16[4,32,256]{2,1,0:T(8,128)(2,1)}, bf16[4,32,256]{2,1,0:T(8,128)(2,1)S(1)}, u32[]{:S(2)}, u32[]{:S(2)}) collective-permute-start(bf16[4,32,256]{2,1,0:T(8,128)(2,1)} %tok_ref.5), channel_id=1, source_target_pairs={{0,4},{8,12},{16,20},{24,28},{4,0},{12,8},{20,16},{28,24},{1,5},{9... | collective-permute-start | bytes 196616 | tf_op jit(solution)/shard_map/ppermute | solution.py:507
  4.3 0.8 %copy-start = (bf16[2,16,512]{2,1,0:T(8,128)(2,1)S(1)}, bf16[2,16,512]{2,1,0:T(8,128)(2,1)}, u32[]{:S(2)}) copy-start(bf16[2,16,512]{2,1,0:T(8,128)(2,1)} %dm_ref.3) | copy-start | bytes 98308
  5.1 3.6 %copy-start.1 = (bf16[2,16,512]{2,1,0:T(8,128)(2,1)S(1)}, bf16[2,16,512]{2,1,0:T(8,128)(2,1)}, u32[]{:S(2)}) copy-start(bf16[2,16,512]{2,1,0:T(8,128)(2,1)} %dm_ref.3) | copy-start | bytes 98308
  5.1 3.6 %copy-start.6 = (bf16[4,32,256]{2,1,0:T(8,128)(2,1)S(1)}, bf16[4,32,256]{2,1,0:T(8,128)(2,1)}, u32[]{:S(2)}) copy-start(bf16[4,32,256]{2,1,0:T(8,128)(2,1)} %tok_ref.5) | copy-start | bytes 196612
  5.1 3.6 %copy-start.7 = (f32[256]{0:T(256)S(1)}, f32[256]{0:T(256)}, u32[]{:S(2)}) copy-start(f32[256]{0:T(256)} %param.9) | copy-start | bytes 3076
  5.1 3.6 %copy-start.8 = (f32[4]{0:T(128)S(1)}, f32[4]{0:T(128)}, u32[]{:S(2)}) copy-start(f32[4]{0:T(128)} %scale_ref.1) | copy-start | bytes 52
  5.1 6.5 %collective-permute-start.7 = (bf16[64,512]{1,0:T(8,128)(2,1)S(1)}, bf16[64,512]{1,0:T(8,128)(2,1)S(1)}, u32[]{:S(2)}, u32[]{:S(2)}) collective-permute-start(bf16[64,512]{1,0:T(8,128)(2,1)S(1)} %shard_map.145.refs_0_), channel_id=1, source_target_pairs={{0,24},{4,28},{8,16},{12,20},{16,8},{20,12},{24,0},{28,4},{1,25},{... | collective-permute-start | bytes 196616 | tf_op jit(solution)/shard_map/ppermute | solution.py:512
  6.6 5.1 %collective-permute-start.6 = (bf16[64,512]{1,0:T(8,128)(2,1)S(1)}, bf16[64,512]{1,0:T(8,128)(2,1)S(1)}, u32[]{:S(2)}, u32[]{:S(2)}) collective-permute-start(bf16[64,512]{1,0:T(8,128)(2,1)S(1)} %shard_map.145.refs_0_), channel_id=1, source_target_pairs={{0,16},{4,20},{8,24},{12,28},{16,0},{20,4},{24,8},{28,12},{1,17},{... | collective-permute-start | bytes 196616 | tf_op jit(solution)/shard_map/ppermute | solution.py:512
  7.2 4.6 %collective-permute-start.5 = (bf16[64,512]{1,0:T(8,128)(2,1)S(1)}, bf16[64,512]{1,0:T(8,128)(2,1)S(1)}, u32[]{:S(2)}, u32[]{:S(2)}) collective-permute-start(bf16[64,512]{1,0:T(8,128)(2,1)S(1)} %shard_map.145.refs_0_), channel_id=1, source_target_pairs={{0,8},{4,12},{8,0},{12,4},{16,24},{20,28},{24,16},{28,20},{1,9},{5... | collective-permute-start | bytes 196616 | tf_op jit(solution)/shard_map/ppermute | solution.py:512
  8.7 3.1 %copy-start.2 = (bf16[1024,512]{1,0:T(8,128)(2,1)S(1)}, bf16[1024,512]{1,0:T(8,128)(2,1)}, u32[]{:S(2)}) copy-start(bf16[1024,512]{1,0:T(8,128)(2,1)} %wmerge_ref.3) | copy-start | bytes 3145732
  8.7 3.1 %copy-start.3 = (bf16[256,768]{1,0:T(8,128)(2,1)S(1)}, bf16[256,768]{1,0:T(8,128)(2,1)}, u32[]{:S(2)}) copy-start(bf16[256,768]{1,0:T(8,128)(2,1)} %wqkv_ref.3) | copy-start | bytes 1179652
  8.7 3.1 %copy-start.5 = (bf16[4,32,256]{2,1,0:T(8,128)(2,1)S(1)}, bf16[4,32,256]{2,1,0:T(8,128)(2,1)}, u32[]{:S(2)}) copy-start(bf16[4,32,256]{2,1,0:T(8,128)(2,1)} %dskip_ref.1) | copy-start | bytes 196612
  9.3 2.5 %copy-start.4 = (bf16[256,256]{1,0:T(8,128)(2,1)S(1)}, bf16[256,256]{1,0:T(8,128)(2,1)}, u32[]{:S(2)}) copy-start(bf16[256,256]{1,0:T(8,128)(2,1)} %wout_ref.3) | copy-start | bytes 393220
  9.4 3.8 %collective-permute-start.2 = (bf16[40,256]{1,0:T(8,128)(2,1)S(1)}, bf16[40,256]{1,0:T(8,128)(2,1)S(1)}, u32[]{:S(2)}, u32[]{:S(2)}) collective-permute-start(bf16[40,256]{1,0:T(8,128)(2,1)S(1)} %get-tuple-element.45), channel_id=1, source_target_pairs={{0,1},{2,3},{1,0},{3,2},{4,5},{6,7},{5,4},{7,6},{8,9},{10,11},{9,8... | collective-permute-start | bytes 61448 | tf_op jit(solution)/shard_map/ppermute | solution.py:507
  11.0 2.2 %collective-permute-start.3 = (bf16[40,256]{1,0:T(8,128)(2,1)S(1)}, bf16[40,256]{1,0:T(8,128)(2,1)S(1)}, u32[]{:S(2)}, u32[]{:S(2)}) collective-permute-start(bf16[40,256]{1,0:T(8,128)(2,1)S(1)} %get-tuple-element.46), channel_id=1, source_target_pairs={{1,2},{2,1},{5,6},{6,5},{9,10},{10,9},{13,14},{14,13},{17,18},{18,... | collective-permute-start | bytes 61448 | tf_op jit(solution)/shard_map/ppermute | solution.py:507
  16.5 1.6 %collective-permute-start.8 = (bf16[4,32,1280]{2,1,0:T(8,128)(2,1)S(1)}, bf16[4,32,1280]{2,1,0:T(8,128)(2,1)S(1)}, u32[]{:S(2)}, u32[]{:S(2)}) collective-permute-start(bf16[4,32,1280]{2,1,0:T(8,128)(2,1)S(1)} %get-tuple-element.55), channel_id=1, source_target_pairs={{0,4},{4,0},{8,12},{12,8},{16,20},{20,16},{24,28},{28,24},{1,5},{5... | collective-permute-start | bytes 983048 | tf_op jit(solution)/shard_map/ppermute | solution.py:512
  18.3 10.7 %collective-permute-start.9 = (bf16[32,1408]{1,0:T(8,128)(2,1)S(1)}, bf16[32,1408]{1,0:T(8,128)(2,1)S(1)}, u32[]{:S(2)}, u32[]{:S(2)}) collective-permute-start(bf16[32,1408]{1,0:T(8,128)(2,1)S(1)} %get-tuple-element.62), channel_id=1, source_target_pairs={{0,8},{4,12},{8,0},{12,4},{16,24},{20,28},{24,16},{28,20},{1,9},{5... | collective-permute-start | bytes 270344 | tf_op jit(solution)/shard_map/ppermute | solution.py:512
  18.9 10.0 %collective-permute-start.10 = (bf16[32,1408]{1,0:T(8,128)(2,1)S(1)}, bf16[32,1408]{1,0:T(8,128)(2,1)S(1)}, u32[]{:S(2)}, u32[]{:S(2)}) collective-permute-start(bf16[32,1408]{1,0:T(8,128)(2,1)S(1)} %get-tuple-element.63), channel_id=1, source_target_pairs={{0,16},{4,20},{8,24},{12,28},{16,0},{20,4},{24,8},{28,12},{1,17},{... | collective-permute-start | bytes 270344 | tf_op jit(solution)/shard_map/ppermute | solution.py:512
  20.3 8.6 %collective-permute-start.11 = (bf16[32,1408]{1,0:T(8,128)(2,1)S(1)}, bf16[32,1408]{1,0:T(8,128)(2,1)S(1)}, u32[]{:S(2)}, u32[]{:S(2)}) collective-permute-start(bf16[32,1408]{1,0:T(8,128)(2,1)S(1)} %get-tuple-element.64), channel_id=1, source_target_pairs={{0,24},{4,28},{8,16},{12,20},{16,8},{20,12},{24,0},{28,4},{1,25},{... | collective-permute-start | bytes 270344 | tf_op jit(solution)/shard_map/ppermute | solution.py:512
  21.8 3.5 %collective-permute-start.12 = (bf16[144,256]{1,0:T(8,128)(2,1)S(1)}, bf16[144,256]{1,0:T(8,128)(2,1)S(1)}, u32[]{:S(2)}, u32[]{:S(2)}) collective-permute-start(bf16[144,256]{1,0:T(8,128)(2,1)S(1)} %get-tuple-element.67), channel_id=1, source_target_pairs={{0,4},{8,12},{16,20},{24,28},{4,0},{12,8},{20,16},{28,24},{1,5},{9... | collective-permute-start | bytes 221192 | tf_op jit(solution)/shard_map/ppermute | solution.py:507
  21.8 7.1 %collective-permute-start.13 = (bf16[144,256]{1,0:T(8,128)(2,1)S(1)}, bf16[144,256]{1,0:T(8,128)(2,1)S(1)}, u32[]{:S(2)}, u32[]{:S(2)}) collective-permute-start(bf16[144,256]{1,0:T(8,128)(2,1)S(1)} %get-tuple-element.68), channel_id=1, source_target_pairs={{4,8},{12,16},{20,24},{8,4},{16,12},{24,20},{5,9},{13,17},{21,25},... | collective-permute-start | bytes 221192 | tf_op jit(solution)/shard_map/ppermute | solution.py:507
  29.2 7.5 %collective-permute-start.14 = (bf16[32,896]{1,0:T(8,128)(2,1)S(1)}, bf16[32,896]{1,0:T(8,128)(2,1)S(1)}, u32[]{:S(2)}, u32[]{:S(2)}) collective-permute-start(bf16[32,896]{1,0:T(8,128)(2,1)S(1)} %get-tuple-element.70), channel_id=1, source_target_pairs={{0,1},{1,0},{2,3},{3,2},{4,5},{5,4},{6,7},{7,6},{8,9},{9,8},{10,11... | collective-permute-start | bytes 172040 | tf_op jit(solution)/shard_map/ppermute | solution.py:512
  33.8 6.8 %collective-permute-start.15 = (bf16[32,896]{1,0:T(8,128)(2,1)S(1)}, bf16[32,896]{1,0:T(8,128)(2,1)S(1)}, u32[]{:S(2)}, u32[]{:S(2)}) collective-permute-start(bf16[32,896]{1,0:T(8,128)(2,1)S(1)} %get-tuple-element.71), channel_id=1, source_target_pairs={{0,2},{1,3},{2,0},{3,1},{4,6},{5,7},{6,4},{7,5},{8,10},{9,11},{10,... | collective-permute-start | bytes 172040 | tf_op jit(solution)/shard_map/ppermute | solution.py:512
  35.4 6.1 %collective-permute-start.16 = (bf16[32,896]{1,0:T(8,128)(2,1)S(1)}, bf16[32,896]{1,0:T(8,128)(2,1)S(1)}, u32[]{:S(2)}, u32[]{:S(2)}) collective-permute-start(bf16[32,896]{1,0:T(8,128)(2,1)S(1)} %get-tuple-element.72), channel_id=1, source_target_pairs={{0,3},{1,2},{2,1},{3,0},{4,7},{5,6},{6,5},{7,4},{8,11},{9,10},{10,... | collective-permute-start | bytes 172040 | tf_op jit(solution)/shard_map/ppermute | solution.py:512

commit v2 on v1

--- a/solution.py
+++ b/solution.py
@@ -34,20 +34,19 @@
     return (jnp.where(even, far, near), jnp.where(even, near, far))
 
 
-def own_edge_kernel(scale_ref, tok_ref, dm_ref, gain_ref, edges_ref, dm_own_ref, rows_ref):
-    rows, cols, width = tok_ref.shape
-    tok = tok_ref[...].astype(F32)
-    left = tok[:, :EDGE].reshape(rows * EDGE, width)
-    right = tok[:, cols - EDGE :].reshape(rows * EDGE, width)
-    edges_ref[...] = jnp.concatenate([left, right], axis=0).astype(BF)
-    dm_own_ref[...] = dm_ref[...].reshape(dm_own_ref.shape)
-    lane = lax.broadcasted_iota(jnp.int32, (1, width), 1)
-    heads = scale_ref.shape[0]
-    scale_row = jnp.zeros((1, width), F32)
-    for h in range(heads):
-        scale_row = jnp.where(lane // (width // heads) == h, scale_ref[h], scale_row)
-    blank = jnp.zeros((6, width), F32)
-    rows_ref[...] = jnp.concatenate([gain_ref[...], scale_row, blank], axis=0)
+def first_kernel(ones_ref, parity_ref):
+    width = ones_ref.shape[0]
+    head_dim = width // (parity_ref.shape[0] // 2)
+    same_head = lax.broadcasted_iota(jnp.int32, (width, width), 0) // head_dim == (
+        lax.broadcasted_iota(jnp.int32, (width, width), 1) // head_dim
+    )
+    ones_ref[...] = jnp.where(same_head, 1.0, 0.0).astype(BF)
+    half = (parity_ref.shape[0] // 2, parity_ref.shape[1])
+    parts = [
+        jnp.where(lax.rem(lax.axis_index(axis), 2) == 0, jnp.ones(half, F32), jnp.zeros(half, F32))
+        for axis in ("row", "col")
+    ]
+    parity_ref[...] = jnp.concatenate(parts, axis=0)
 
 
 def edge_kernel(edges_ref, near_ref, far_ref, edge_near_ref, edge_far_ref):
@@ -55,24 +54,23 @@
     up, down = by_side("row", near_ref[...].astype(F32), far_ref[...].astype(F32))
     up = up[rows - RADIUS :]
     down = down[:RADIUS]
-    own = edges_ref[...].astype(F32)
-    sides = []
-    for side, at in enumerate((0, cols - EDGE)):
-        parts = [
-            up[:, at : at + EDGE].reshape(RADIUS * EDGE, width),
-            own[side * rows * EDGE : (side + 1) * rows * EDGE],
-            down[:, at : at + EDGE].reshape(RADIUS * EDGE, width),
-        ]
-        sides.append(jnp.concatenate(parts, axis=0))
-    far, near = by_side("col", sides[1], sides[0])
-    edge_near_ref[...] = near.astype(BF)
-    edge_far_ref[...] = far.astype(BF)
-
-
-def pair_kernel(dm_ref, dm_near_ref, dm_pair_ref):
+    halo = []
+    for at in (0, cols - EDGE):
+        parts = [part[:, at : at + EDGE].reshape(RADIUS * EDGE, width) for part in (up, down)]
+        halo.append(jnp.concatenate(parts, axis=0))
+    far, near = by_side("col", halo[1], halo[0])
+    for out_ref, own_at, part in ((edge_near_ref, 0, near), (edge_far_ref, rows * EDGE, far)):
+        own = edges_ref[own_at : own_at + rows * EDGE].astype(F32)
+        size = RADIUS * EDGE
+        out_ref[...] = jnp.concatenate([part[:size], own, part[size:]], axis=0).astype(BF)
+
+
+def pair_kernel(parity_ref, dm_ref, dm_near_ref, dm_pair_ref):
     size = dm_pair_ref.shape[0] // 2
     own, near = [ref[...].reshape(size, -1).astype(F32) for ref in (dm_ref, dm_near_ref)]
-    dm_pair_ref[...] = jnp.concatenate(in_order("row", own, near), axis=0).astype(BF)
+    even = parity_ref[0:1, 0:1] > 0.5
+    pair = [jnp.where(even, own, near), jnp.where(even, near, own)]
+    dm_pair_ref[...] = jnp.concatenate(pair, axis=0).astype(BF)
 
 
 def in_order(axis, own, partner):
@@ -80,33 +78,54 @@
     return (jnp.where(even, own, partner), jnp.where(even, partner, own))
 
 
-def head_sum(value, heads):
-    width = value.shape[1]
-    head_dim = width // heads
-    same_head = lax.broadcasted_iota(jnp.int32, (width, width), 0) // head_dim == (
-        lax.broadcasted_iota(jnp.int32, (width, width), 1) // head_dim
-    )
-    ones_bd = jnp.where(same_head, 1.0, 0.0).astype(BF)
+def head_sum(value, ones_ref):
     high, low = split_two(value)
-    return mm(high, ones_bd) + mm(low, ones_bd)
+    return mm(high, ones_ref[...]) + mm(low, ones_ref[...])
 
 
 def own_kernel(
-    heads, tok_ref, dm_ref, dskip_ref, rows_ref, wqkv_ref, wout_ref, wmerge_ref, *refs
+    ones_ref,
+    parity_ref,
+    scale_ref,
+    tok_ref,
+    dm_ref,
+    dskip_ref,
+    gain_ref,
+    wqkv_ref,
+    wout_ref,
+    wmerge_ref,
+    edges_ref,
+    rows_ref,
+    q_norm_ref,
+    q_unit_ref,
+    dy_ref,
+    d_attn_ref,
+    dscr,
 ):
-    *dm_refs, q_norm_ref, q_unit_ref, dy_ref, d_attn_ref, dm_all_ref, dscr = refs
-    dm_all_ref[...] = jnp.concatenate([ref[...] for ref in dm_refs], axis=0)
     rows, cols, width = tok_ref.shape
     tokens = rows * cols
-    x = tok_ref[...].reshape(tokens, width).astype(F32)
+    tok = tok_ref[...].astype(F32)
+    left = tok[:, :EDGE].reshape(rows * EDGE, width)
+    right = tok[:, cols - EDGE :].reshape(rows * EDGE, width)
+    heads = scale_ref.shape[1]
+    even = parity_ref[heads : heads + 1, 0:1] > 0.5
+    near, far = (jnp.where(even, right, left), jnp.where(even, left, right))
+    edges_ref[...] = jnp.concatenate([near, far], axis=0).astype(BF)
+    lane = lax.broadcasted_iota(jnp.int32, (1, width), 1)
+    scale_row = jnp.zeros((1, width), F32)
+    for h in range(heads):
+        scale_row = jnp.where(lane // (width // heads) == h, scale_ref[:, h : h + 1], scale_row)
+    blank = jnp.zeros((6, width), F32)
+    rows_ref[...] = jnp.concatenate([gain_ref[...], scale_row, blank], axis=0)
+    x = tok.reshape(tokens, width)
     inverse = lax.rsqrt(jnp.mean(x * x, axis=1, keepdims=True) + EPS)
-    normed = (x * inverse * rows_ref[0:1]).astype(BF)
+    normed = (x * inverse * gain_ref[...]).astype(BF)
     query = mm(normed, wqkv_ref[:, :width])
-    q_norm = lax.rsqrt(head_sum(query * query, heads) + EPS)
+    q_norm = lax.rsqrt(head_sum(query * query, ones_ref) + EPS)
     q_norm_ref[...] = q_norm
     q_unit_ref[...] = query * q_norm
     group_wide = cols // 2
-    d_in = mm_t(dm_ref[...], wmerge_ref[...])
+    d_in = mm_t(dm_ref[...].reshape(-1, dm_ref.shape[2]), wmerge_ref[...])
     for i in range(rows // 2):
         for pr in range(2):
             for pc in range(2):
@@ -125,6 +144,7 @@
 
 def layer_kernel(
     sizes,
+    ones_ref,
     tok_ref,
     row_near_ref,
     row_far_ref,
@@ -137,16 +157,16 @@
     d_attn_ref,
     wqkv_ref,
     wout_ref,
-    wmerge_ref,
-    skip_ref,
-    merged_ref,
-    gx_ref,
-    gx_near_ref,
-    gx_far_ref,
-    *refs,
+    x_ref,
+    y_ref,
+    d_query_ref,
+    d_kv_ref,
+    grad_out_ref,
+    group_ref,
+    scale_part_ref,
+    yscr,
 ):
     rows, cols, width, heads, n_row, n_col = sizes
-    *sum_refs, yscr = refs
     head_dim = width // heads
     wide = cols + 2 * SIDE
     ext_rows = rows + 2 * RADIUS
@@ -156,12 +176,6 @@
     col_index = lax.axis_index("col")
     col_start = col_index * cols
     first = row_start // image_rows * image_rows
-
-    def inner(value, at_row=RADIUS):
-        pieces = []
-        for i in range(at_row, at_row + rows):
-            pieces.append(value[i * wide + SIDE : i * wide + SIDE + cols])
-        return jnp.concatenate(pieces, axis=0)
 
     lane = lax.broadcasted_iota(jnp.int32, (1, width), 1)
     def blocks(value):
@@ -186,15 +200,15 @@
         edge = slice(i * EDGE, (i + 1) * EDGE)
         pieces += [blank, left[edge], row, right[edge], blank]
     x = jnp.concatenate(pieces, axis=0)
+    x_ref[...] = x
     inverse = lax.rsqrt(jnp.mean(x * x, axis=1, keepdims=True) + EPS)
     unit = x * inverse
     normed32 = (unit * gain).astype(BF).astype(F32)
     normed = normed32.astype(BF)
-    x_own = inner(x)
-    normed_own32 = inner(normed32)
+    x_own = inner_tokens(x, rows, cols)
     kv = mm(normed, wqkv_ref[:, width:])
     key_raw = kv[:, :width]
-    k_norm = lax.rsqrt(head_sum(key_raw * key_raw, heads) + EPS)
+    k_norm = lax.rsqrt(head_sum(key_raw * key_raw, ones_ref) + EPS)
     k_unit = key_raw * k_norm
     keys = k_unit.astype(BF)
     values = kv[:, width:].astype(BF)
@@ -244,7 +258,7 @@
 
     attn = attn_t.T.astype(BF)
     y = (x_own + mm(attn, wout_ref[...])).astype(BF)
-    skip_ref[...] = y.reshape(rows, cols, width)
+    y_ref[...] = y
     y32 = y.astype(F32)
     for part in range(width // LANES):
         yscr[part] = y32[:, part * LANES : (part + 1) * LANES].reshape(rows, cols, LANES)
@@ -257,19 +271,81 @@
                     pieces.append(yscr[part, 2 * i + pr, pl.ds(pc, cols // 2, stride=2), :])
         lines.append(jnp.concatenate(pieces, axis=1))
     group = jnp.concatenate(lines, axis=0).astype(BF)
-    merged_ref[...] = mm(group, wmerge_ref[...]).astype(BF).reshape(merged_ref.shape)
-    grad_out = mm(attn_t.astype(BF), dy_b)
-
-    scale_part = jnp.sum(q_unit * d_qhat, axis=0, keepdims=True)
+    group_ref[...] = group
+    grad_out_ref[...] = mm(attn_t.astype(BF), dy_b)
+
+    scale_part_ref[...] = jnp.broadcast_to(
+        jnp.sum(q_unit * d_qhat, axis=0, keepdims=True), scale_part_ref.shape
+    )
     g_unit = d_qhat * scale_row
-    d_query = (q_norm * (g_unit - q_unit * head_sum(q_unit * g_unit, heads))).astype(BF)
-    d_key = k_norm * (d_k - k_unit * head_sum(k_unit * d_k, heads))
-    d_kv = jnp.concatenate([d_key, d_v], axis=1).astype(BF)
-    grad_q = mm(normed_own32.T.astype(BF), d_query)
-    grad_kv = mm(normed32.T.astype(BF), d_kv)
-    sums = jnp.concatenate([grad_q, grad_kv, grad_out], axis=1)
-    from_q = mm_t(d_query, wqkv_ref[:, :width])
-    d_normed = mm_t(d_kv, wqkv_ref[:, width:])
+    d_query_ref[...] = (q_norm * (g_unit - q_unit * head_sum(q_unit * g_unit, ones_ref))).astype(BF)
+    d_key = k_norm * (d_k - k_unit * head_sum(k_unit * d_k, ones_ref))
+    d_kv_ref[...] = jnp.concatenate([d_key, d_v], axis=1).astype(BF)
+
+
+def inner_tokens(value, rows, cols):
+    wide = cols + 2 * SIDE
+    pieces = []
+    for i in range(RADIUS, RADIUS + rows):
+        pieces.append(value[i * wide + SIDE : i * wide + SIDE + cols])
+    return jnp.concatenate(pieces, axis=0)
+
+
+def output_kernel(y_ref, group_ref, wmerge_ref, skip_ref, merged_ref):
+    skip_ref[...] = y_ref[...].reshape(skip_ref.shape)
+    merged = mm(group_ref[...], wmerge_ref[...])
+    merged_ref[...] = merged.astype(BF).reshape(merged_ref.shape)
+
+
+def weights_kernel(
+    sizes, x_ref, d_query_ref, d_kv_ref, grad_out_ref, group_ref, rows_ref, *refs
+):
+    rows, cols, width, n_row, n_dm = sizes
+    dm_refs, dm_all_ref, sum_refs = (refs[:n_dm], refs[n_dm], refs[n_dm + 1 :])
+    dm_all_ref[...] = jnp.concatenate([ref[...] for ref in dm_refs], axis=0)
+    x = x_ref[...]
+    inverse = lax.rsqrt(jnp.mean(x * x, axis=1, keepdims=True) + EPS)
+    normed32 = (x * inverse * rows_ref[0:1]).astype(BF).astype(F32)
+    grad_q = mm(inner_tokens(normed32, rows, cols).T.astype(BF), d_query_ref[...])
+    grad_kv = mm(normed32.T.astype(BF), d_kv_ref[...])
+    sums = jnp.concatenate([grad_q, grad_kv, grad_out_ref[...]], axis=1)
+    group = group_ref[...]
+    if len(sum_refs) == 2:
+        sum_refs[0][...] = sums.astype(BF)
+        sum_refs[1][...] = group
+        return
+    send_ref, keep_ref, keep_group_ref = sum_refs
+    per = width // n_row
+    feats = 4 * width // n_row
+    group = group.astype(F32)
+    even = lax.rem(lax.axis_index("row"), 2) == 0
+    for q in range(n_row // 2):
+        parts = []
+        for value, axis, size in ((sums, 0, per), (group, 1, feats)):
+            first = lax.slice_in_dim(value, 2 * q * size, (2 * q + 1) * size, axis=axis)
+            second = lax.slice_in_dim(value, (2 * q + 1) * size, (2 * q + 2) * size, axis=axis)
+            parts.append((jnp.where(even, first, second), jnp.where(even, second, first)))
+        (keep_ref[q], sums_send), (keep_group, group_send) = parts
+        keep_group_ref[q] = keep_group.astype(BF)
+        send_ref[q] = jnp.concatenate([sums_send, group_send], axis=1).astype(BF)
+
+
+def norm_kernel(
+    sizes, x_ref, d_query_ref, d_kv_ref, scale_part_ref, rows_ref, dy_ref, wqkv_ref, *refs
+):
+    rows, cols, width, heads = sizes
+    gx_ref, gx_near_ref, gx_far_ref, small_ref = refs
+    head_dim = width // heads
+    wide = cols + 2 * SIDE
+    ext_rows = rows + 2 * RADIUS
+    gain = rows_ref[0:1]
+    lane = lax.broadcasted_iota(jnp.int32, (1, width), 1)
+    x = x_ref[...]
+    inverse = lax.rsqrt(jnp.mean(x * x, axis=1, keepdims=True) + EPS)
+    unit = x * inverse
+    d_y = dy_ref[...]
+    from_q = mm_t(d_query_ref[...], wqkv_ref[:, :width])
+    d_normed = mm_t(d_kv_ref[...], wqkv_ref[:, width:])
     pieces = []
     side = jnp.zeros((SIDE, width), F32)
     for i in range(ext_rows):
@@ -283,15 +359,21 @@
     scaled = gain * d_normed
     mean = jnp.mean(x * scaled, axis=1, keepdims=True)
     g_x = inverse * scaled - x * (inverse * inverse * inverse) * mean
-    far, near = by_side("row", g_x[(RADIUS + rows) * wide :], g_x[: RADIUS * wide])
-    gx_near_ref[...] = near.astype(BF)
-    gx_far_ref[...] = far.astype(BF)
+
+    def rim(first_row):
+        parts = []
+        for i in range(first_row, first_row + RADIUS):
+            parts.append(g_x[i * wide : (i + 1) * wide][SIDE - EDGE : wide - SIDE + EDGE])
+        return jnp.concatenate(parts, axis=0)
+
+    far, near = by_side("row", rim(RADIUS + rows), rim(0))
     pieces = []
     for i in range(rows):
         at = (RADIUS + i) * wide
         middle = g_x[at + SIDE : at + SIDE + cols] + d_y[i * cols : (i + 1) * cols]
         pieces += [g_x[at : at + SIDE], middle, g_x[at + SIDE + cols : at + wide]]
     gx_ref[...] = jnp.concatenate(pieces, axis=0)
+    scale_part = scale_part_ref[0:1]
     scale_lane = lax.broadcasted_iota(jnp.int32, (1, LANES), 1)
     scale_sums = jnp.zeros((1, LANES), F32)
     for h in range(heads):
@@ -299,28 +381,11 @@
         scale_sums = jnp.where(scale_lane == h, of_head, scale_sums)
     small = [gain_part[:, i * LANES : (i + 1) * LANES] for i in range(width // LANES)] + [scale_sums]
     small = jnp.concatenate(small + [jnp.zeros((8 - len(small), LANES), F32)], axis=0)
-    if len(sum_refs) == 3:
-        sum_refs[0][...] = sums.astype(BF)
-        sum_refs[1][...] = group
-        sum_refs[2][...] = small
-        return
-    send_ref, keep_ref, keep_group_ref, small_ref = sum_refs
     small_ref[...] = small
-    per = width // n_row
-    feats = 4 * width // n_row
-    small = small_rows(small, per)
-    group = group.astype(F32)
-    even = lax.rem(lax.axis_index("row"), 2) == 0
-    for q in range(n_row // 2):
-        parts = []
-        for value, axis, size in ((sums, 0, per), (group, 1, feats)):
-            first = lax.slice_in_dim(value, 2 * q * size, (2 * q + 1) * size, axis=axis)
-            second = lax.slice_in_dim(value, (2 * q + 1) * size, (2 * q + 2) * size, axis=axis)
-            parts.append((jnp.where(even, first, second), jnp.where(even, second, first)))
-        (keep_ref[q], sums_send), (keep_group, group_send) = parts
-        keep_group_ref[q] = keep_group.astype(BF)
-        sent = jnp.concatenate([sums_send, group_send], axis=1).astype(BF)
-        send_ref[q] = jnp.concatenate([sent, small], axis=1)
+    high = small.astype(BF).astype(F32)
+    small = jnp.concatenate([high, small - high], axis=1)
+    gx_near_ref[...] = jnp.concatenate([near, small], axis=0).astype(BF)
+    gx_far_ref[...] = far.astype(BF)
 
 
 def small_rows(small, rows):
@@ -329,17 +394,28 @@
     return jnp.concatenate([high, small - high, blank], axis=0).astype(BF)
 
 
+def wide_rim(ref, cols):
+    size = cols + 2 * EDGE
+    blank = jnp.zeros((SIDE - EDGE, ref.shape[1]), F32)
+    pieces = []
+    for i in range(RADIUS):
+        pieces += [blank, ref[...][i * size : (i + 1) * size].astype(F32), blank]
+    return jnp.concatenate(pieces, axis=0)
+
+
 def small_value(rows):
     value = rows.astype(F32)
     return value[:8] + value[8:16]
 
 
-def core_sum_kernel(got_ref, keep_ref, keep_group_ref, small_ref, *refs):
+def core_sum_kernel(got_ref, keep_ref, keep_group_ref, small_ref, near_ref, *refs):
     *out_refs, own_ref, own_group_ref, small_sum_ref, blocks_ref = refs
     chips, per, width = keep_ref.shape
     feats = keep_group_ref.shape[2]
     end = width + feats
-    small = small_value(small_rows(small_ref[...], per)) + small_value(got_ref[0, :, end:])
+    got_small = near_ref[...].astype(F32)[near_ref.shape[0] - 8 :]
+    got_small = got_small[:, :LANES] + got_small[:, LANES:]
+    small = small_value(small_rows(small_ref[...], per)) + got_small
     small_sum_ref[...] = small
     small = small_rows(small, per)
     chip = lax.axis_index("row") // 2
@@ -367,19 +443,19 @@
     end = at + 2 * feats
 
     def summed(first, part):
-        second, third, fourth = [part(ref) for ref in got_refs]
+        fourth, third, second = [part(ref) for ref in got_refs]
         return (first + second) + (third + fourth)
 
     sums = summed(own_ref[...], lambda ref: ref[:, :at].astype(F32))
     small = small_value(small_rows(small_ref[...], per))
     small = summed(small, lambda ref: small_value(ref[:, end:]))
-    group = [own_group_ref[...]] + [ref[:, at:end] for ref in got_refs]
+    group = [own_group_ref[...]] + [ref[:, at:end] for ref in got_refs[::-1]]
     group = [part[:, i * feats : (i + 1) * feats].astype(F32) for part in group for i in range(2)]
     group = jnp.concatenate(group, axis=0)
     merge = mm(group.T.astype(BF), dm_ref[...])
     g_x = gx_ref[...]
     blank = jnp.zeros(((rows - RADIUS) * wide, width), F32)
-    above, below = by_side("row", near_ref[...].astype(F32), far_ref[...].astype(F32))
+    above, below = by_side("row", wide_rim(near_ref, cols), wide_rim(far_ref, cols))
     g_x = g_x + jnp.concatenate([above, blank], axis=0)
     g_x = g_x + jnp.concatenate([blank, below], axis=0)
     grad = []
@@ -425,7 +501,7 @@
 
 
 def col_sum_kernel(
-    sizes, a_ref, b_ref, c_ref, d_ref, grad_ref, gqkv_ref, gout_ref, gmerge_ref, ggain_ref, gscale_ref, gtok_ref
+    sizes, a_ref, d_ref, c_ref, b_ref, grad_ref, gqkv_ref, gout_ref, gmerge_ref, ggain_ref, gscale_ref, gtok_ref
 ):
     rows, cols, width = sizes
     per, lanes = a_ref.shape
@@ -483,8 +559,9 @@
         outs.append(lax.psum_scatter(part, "col", scatter_dimension=1, tiled=True))
     small = lax.psum(small, ("row", "col"))
     gx = gx.reshape(rows, wide, width)
-    gx = gx.at[:RADIUS].add(above.astype(F32).reshape(RADIUS, wide, width))
-    gx = gx.at[rows - RADIUS :].add(below.astype(F32).reshape(RADIUS, wide, width))
+    trim = slice(SIDE - EDGE, wide - SIDE + EDGE)
+    gx = gx.at[:RADIUS, trim].add(above.astype(F32).reshape(RADIUS, -1, width))
+    gx = gx.at[rows - RADIUS :, trim].add(below.astype(F32).reshape(RADIUS, -1, width))
     from_right = shifted(gx[:, :SIDE].astype(BF), "col", -1).astype(F32)
     from_left = shifted(gx[:, SIDE + cols :].astype(BF), "col", 1).astype(F32)
     grad = gx[:, SIDE : SIDE + cols].at[:, :SIDE].add(from_left)
@@ -500,8 +577,8 @@
 
 def swapped(near, far, axis):
     count = lax.axis_size(axis)
-    first = [(i, i + 1) for i in range(0, count - 1, 2)]
-    second = [(i, i + 1) for i in range(1, count - 1, 2)]
+    first = [(i, i + 1) for i in range(0, count, 2)]
+    second = [(i, (i + 1) % count) for i in range(1, count, 2)]
     first = first + [(j, i) for i, j in first]
     second = second + [(j, i) for i, j in second]
     return (lax.ppermute(near, axis, first), lax.ppermute(far, axis, second))
@@ -529,37 +606,44 @@
     less = pltpu.CompilerParams(vmem_limit_bytes=8 * 1024 * 1024)
     row_near, row_far = swapped(tokens, tokens, "row")
     edge = shape((ext_rows * EDGE, width), BF)
+    ones, parity = pl.pallas_call(
+        first_kernel,
+        out_shape=(shape((width, width), BF), shape((2 * heads, LANES), F32)),
+        out_specs=tuple(vmem(2)),
+        compiler_params=less,
+        cost_estimate=pl.CostEstimate(flops=10**10, bytes_accessed=10**5, transcendentals=0),
+    )()
     dm_pair = pl.pallas_call(
         pair_kernel,
         out_shape=shape((2 * groups, depth), BF),
-        in_specs=vmem(2),
+        in_specs=vmem(3),
         out_specs=vmem(1)[0],
         compiler_params=less,
-    )(d_merged, swap(d_merged, "row", 1))
+    )(parity, d_merged, swap(d_merged, "row", 1))
     dm_pairs = [dm_pair] + [swap(dm_pair, "row", 2 * step) for step in range(1, 4)]
     gathered = len(dm_pairs) * 2 * groups
-    edges, dm_own, two_rows = pl.pallas_call(
-        own_edge_kernel,
-        out_shape=(
-            shape((2 * rows * EDGE, width), BF),
-            shape((groups, depth), BF),
-            shape((8, width), F32),
-        ),
-        in_specs=[pl.BlockSpec(memory_space=pltpu.SMEM)] + vmem(3),
-        out_specs=tuple(vmem(3)),
-        compiler_params=less,
-        cost_estimate=pl.CostEstimate(flops=10**10, bytes_accessed=10**6, transcendentals=0),
-    )(head_scale, tokens, d_merged, gain.reshape(1, width))
     tile = shape((rows * cols, width), F32)
-    q_norm, q_unit, d_y, d_attn, dm_all = pl.pallas_call(
-        functools.partial(own_kernel, heads),
-        out_shape=(tile, tile, tile, shape((rows * cols, width), BF), shape((gathered, depth), BF)),
-        in_specs=vmem(11),
-        out_specs=tuple(vmem(5)),
+    half = shape((rows * cols, width), BF)
+    edges, two_rows, q_norm, q_unit, d_y, d_attn = pl.pallas_call(
+        own_kernel,
+        out_shape=(shape((2 * rows * EDGE, width), BF), shape((8, width), F32), tile, tile, tile, half),
+        in_specs=vmem(10),
+        out_specs=tuple(vmem(6)),
         scratch_shapes=[pltpu.VMEM((width // LANES, rows, cols, LANES), F32)],
         compiler_params=params,
-        cost_estimate=pl.CostEstimate(flops=2 * 10**9, bytes_accessed=10**6, transcendentals=0),
-    )(tokens, dm_own, d_skip, two_rows, w_qkv, w_out, w_merge, *dm_pairs)
+        cost_estimate=pl.CostEstimate(flops=10**9, bytes_accessed=10**6, transcendentals=0),
+    )(
+        ones,
+        parity,
+        head_scale.reshape(1, heads),
+        tokens,
+        d_merged,
+        d_skip,
+        gain.reshape(1, width),
+        w_qkv,
+        w_out,
+        w_merge,
+    )
     edge_near, edge_far = pl.pallas_call(
         edge_kernel,
         out_shape=(edge, edge),
@@ -575,37 +659,36 @@
     packed = packed and 2 * rows * RADIUS + 8 == per and width // LANES < 4 and depth // n_col == LANES and n_col == 4 and n_row == 8
     if packed:
         sum_shapes = (
-            shape((n_row // 2, per, 4 * width + feats + LANES), BF),
+            shape((n_row // 2, per, 4 * width + feats), BF),
             shape((n_row // 2, per, 4 * width), F32),
             shape((n_row // 2, per, feats), BF),
-            shape((8, LANES), F32),
         )
     else:
         sum_shapes = (
             shape((width, 4 * width), BF),
             shape((groups, 4 * width), BF),
-            shape((8, LANES), F32),
         )
     sizes = (rows, cols, width, heads, n_row, n_col)
-    reach = RADIUS * wide
-    skip_out, merged, gx, gx_near, gx_far, *sums = pl.pallas_call(
+    reach = RADIUS * (cols + 2 * EDGE)
+    tall = ext_rows * wide
+    x, y, d_query, d_kv, grad_out, group, scale_part = pl.pallas_call(
         functools.partial(layer_kernel, sizes),
         out_shape=(
-            shape((rows, cols, width), BF),
-            shape((g_rows, g_cols, depth), BF),
-            shape((rows * wide, width), F32),
-            shape((reach, width), BF),
-            shape((reach, width), BF),
-        )
-        + sum_shapes,
+            shape((tall, width), F32),
+            half,
+            half,
+            shape((tall, 2 * width), BF),
+            shape((width, width), F32),
+            shape((groups, 4 * width), BF),
+            shape((8, width), F32),
+        ),
         in_specs=vmem(13),
-        out_specs=tuple(vmem(5 + len(sum_shapes))),
-        scratch_shapes=[
-            pltpu.VMEM((width // LANES, rows, cols, LANES), F32),
-        ],
+        out_specs=tuple(vmem(7)),
+        scratch_shapes=[pltpu.VMEM((width // LANES, rows, cols, LANES), F32)],
         compiler_params=params,
         cost_estimate=pl.CostEstimate(flops=4 * 10**9, bytes_accessed=10**6, transcendentals=0),
     )(
+        ones,
         tokens,
         row_near,
         row_far,
@@ -618,12 +701,40 @@
         d_attn,
         w_qkv,
         w_out,
-        w_merge,
     )
+    dm_all, *sums = pl.pallas_call(
+        functools.partial(weights_kernel, (rows, cols, width, n_row, len(dm_pairs))),
+        out_shape=(shape((gathered, depth), BF),) + sum_shapes,
+        in_specs=vmem(6 + len(dm_pairs)),
+        out_specs=tuple(vmem(1 + len(sum_shapes))),
+        compiler_params=params,
+        cost_estimate=pl.CostEstimate(flops=10**9, bytes_accessed=10**6, transcendentals=0),
+    )(x, d_query, d_kv, grad_out, group, two_rows, *dm_pairs)
+    gx, gx_near, gx_far, small = pl.pallas_call(
+        functools.partial(norm_kernel, (rows, cols, width, heads)),
+        out_shape=(
+            shape((rows * wide, width), F32),
+            shape((reach + 8, width), BF),
+            shape((reach, width), BF),
+            shape((8, LANES), F32),
+        ),
+        in_specs=vmem(7),
+        out_specs=tuple(vmem(4)),
+        compiler_params=params,
+        cost_estimate=pl.CostEstimate(flops=5 * 10**8, bytes_accessed=10**6, transcendentals=0),
+    )(x, d_query, d_kv, scale_part, two_rows, d_y, w_qkv)
+    skip_out, merged = pl.pallas_call(
+        output_kernel,
+        out_shape=(shape((rows, cols, width), BF), shape((g_rows, g_cols, depth), BF)),
+        in_specs=vmem(3),
+        out_specs=tuple(vmem(2)),
+        compiler_params=less,
+        cost_estimate=pl.CostEstimate(flops=10**9, bytes_accessed=10**6, transcendentals=0),
+    )(y, group, w_merge)
     if not packed:
-        above, below = by_side("row", *swapped(gx_near, gx_far, "row"))
+        above, below = by_side("row", *swapped(gx_near[:reach], gx_far, "row"))
         grad_tokens, g_qkv, g_out, g_merge, g_gain, g_scale = plain_sums(
-            (rows, cols, width), *sums, d_merged.reshape(groups, depth), gx, above, below
+            (rows, cols, width), *sums, small, d_merged.reshape(groups, depth), gx, above, below
         )
     else:
         near, far = swapped(gx_near, gx_far, "row")
@@ -633,12 +744,13 @@
             core_sum_kernel,
             out_shape=(block, block, block)
             + (shape((per, 4 * width), F32), shape((per, 2 * feats), BF), shape((8, LANES), F32)),
-            in_specs=vmem(4),
+            in_specs=vmem(5),
             out_specs=tuple(vmem(6)),
             scratch_shapes=[pltpu.VMEM((n_row // 2,) + block.shape, BF)],
             compiler_params=less,
-        )(swap(send, "row", 1), *kept)
-        got = [swap(blocks[step - 1], "row", 2 * step) for step in (3, 2, 1)][::-1]
+            cost_estimate=pl.CostEstimate(flops=5 * 10**9, bytes_accessed=10**6, transcendentals=0),
+        )(swap(send, "row", 1), *kept, small, near)
+        got = [swap(blocks[step - 1], "row", 2 * step) for step in (3, 2, 1)]
         lanes = 4 * width // n_col + feats // per * (depth // n_col) + LANES
         *slots, grad = pl.pallas_call(
             functools.partial(row_sum_kernel, (rows, cols, width, n_col)),
@@ -650,7 +762,7 @@
             compiler_params=less,
         )(own, own_group, small, *got, dm_all, gx, near, far)
         got = [slots[0]]
-        got += [swap(slots[step], "col", step) for step in (3, 2, 1)][::-1]
+        got += [swap(slots[step], "col", step) for step in (3, 2, 1)]
         g_qkv, g_out, g_merge, g_gain, g_scale, grad_tokens = pl.pallas_call(
             functools.partial(col_sum_kernel, (rows, cols, width)),
             out_shape=(

time: 42.4 us -> 39.8 us (0.939)
  the two profiles are of different devices: /device:TPU:4 before, /device:TPU:0 now
where the time goes in v2:
time: 39.8 us; the launch traced here: 39.7 us
  starting transfers between devices  21 us (53%)
  waiting for transfers between devices  11.2 us (28%)
  Pallas kernels  5.98 us (15%)
  between operations  0.85 us (2%)
  local copies, waits for them, and re-layouts  0.63 us (2%)
    ppermute x11, starting transfers between devices, swap(): return lax.ppermute(value, axis, [(i, i ^ step) for i in range(count)])  11.6 us
    ppermute x6, starting transfers between devices, swapped(): return (lax.ppermute(near, axis, first), lax.ppermute(far, axis, second))  9.35 us
    ppermute x6, waiting for transfers between devices, swapped(): return (lax.ppermute(near, axis, first), lax.ppermute(far, axis, second))  6.44 us
    ppermute x11, waiting for transfers between devices, swap(): return lax.ppermute(value, axis, [(i, i ^ step) for i in range(count)])  4.81 us
    pallas_call x1, Pallas kernels, on_device(): pl.pallas_call(functools.partial(layer_kernel, sizes), out_shape=(shape((...  1.96 us
    pallas_call x1, Pallas kernels, on_device(): pl.pallas_call(output_kernel, out_shape=(shape((rows, cols, width), BF),...  0.9 us
  transfers between devices with their start and end apart: 17, of which 6 were waited for; matrix products, arithmetic and copies ran while one was open for 0% of the time, Pallas kernels for 11%

profile of v2, /device:TPU:0, one launch (start us, length us, event | category | flops | bytes accessed | tf_op | source)
XLA Modules:
  0.0 39.7 jit_solution(17373563231873907379)
XLA Ops:
  0.6 0.0 copy-start.5
  0.6 0.0 copy-start
  0.7 0.0 copy-start.4
  0.7 0.0 copy-start.2
  0.7 0.0 copy-start.3
  0.7 0.0 copy-start.1
  0.7 0.5 %collective-permute-start = (bf16[4,32,256]{2,1,0:T(8,128)(2,1)}, bf16[4,32,256]{2,1,0:T(8,128)(2,1)S(1)}, u32[]{:S(2)}, u32[]{:S(2)}) collective-permute-start(bf16[4,32,256]{2,1,0:T(8,128)(2,1)} %tok_ref.3), channel_id=1, source_target_pairs={{0,4},{8,12},{16,20},{24,28},{4,0},{12,8},{20,16},{28,24},{1,5},{9... | collective-permute-start | bytes 196616 | tf_op jit(solution)/shard_map/ppermute | solution.py:584
  1.2 3.6 %collective-permute-start.1 = (bf16[4,32,256]{2,1,0:T(8,128)(2,1)}, bf16[4,32,256]{2,1,0:T(8,128)(2,1)S(1)}, u32[]{:S(2)}, u32[]{:S(2)}) collective-permute-start(bf16[4,32,256]{2,1,0:T(8,128)(2,1)} %tok_ref.3), channel_id=1, source_target_pairs={{4,8},{12,16},{20,24},{28,0},{8,4},{16,12},{24,20},{0,28},{5,9},{1... | collective-permute-start | bytes 196616 | tf_op jit(solution)/shard_map/ppermute | solution.py:584
  4.8 0.0 collective-permute-start.4
  4.8 0.0 copy-start.6
  4.8 0.0 copy-start.7
  4.8 0.0 copy-done.5
  4.8 0.0 copy-done
  4.9 0.0 copy-done.4
  4.9 0.0 copy-done.2
  4.9 0.0 copy-done.3
  4.9 0.0 copy-done.1
  4.9 0.6 %copy-done.6 = f32[256]{0:T(256)S(1)} copy-done((f32[256]{0:T(256)S(1)}, f32[256]{0:T(256)}, u32[]{:S(2)}) %copy-start.6) | copy-done | bytes 1048
  5.5 0.0 copy-done.7
  5.5 0.8 %shard_map.144 = (bf16[32,256]{1,0:T(8,128)(2,1)S(1)}, f32[8,256]{1,0:T(8,128)S(1)}, f32[128,256]{1,0:T(8,128)S(1)}, f32[128,256]{1,0:T(8,128)S(1)}, f32[128,256...) custom-call(bf16[256,256]{1,0:T(8,128)(2,1)S(1)} %get-tuple-element.52.ones_ref, f32[8,128]{1,0:T(8,128)S(1)} %get-tuple-element.53.parity_ref, ...), custom_call_target="tpu_custom_call" | custom-call | flops 1000000000 | bytes 1000000 | tf_op jit(solution)/shard_map/pallas_call | solution.py:627
  6.3 0.0 collective-permute-done.near_ref.row_near_ref
  6.3 0.7 %collective-permute-done.1.far_ref.row_far_ref = bf16[4,32,256]{2,1,0:T(8,128)(2,1)S(1)} collective-permute-done((bf16[4,32,256]{2,1,0:T(8,128)(2,1)}, bf16[4,32,256]{2,1,0:T(8,128)(2,1)S(1)}, u32[]{:S(2)}, u32[]{:S(2)}) %collective-permute-start.1) | collective-permute-done | bytes 65568 | tf_op jit(solution)/shard_map/ppermute | solution.py:584
  7.0 1.8 %collective-permute-start.2 = (bf16[40,256]{1,0:T(8,128)(2,1)S(1)}, bf16[40,256]{1,0:T(8,128)(2,1)S(1)}, u32[]{:S(2)}, u32[]{:S(2)}) collective-permute-start(bf16[40,256]{1,0:T(8,128)(2,1)S(1)} %get-tuple-element.55), channel_id=1, source_target_pairs={{0,1},{2,3},{1,0},{3,2},{4,5},{6,7},{5,4},{7,6},{8,9},{10,11},{9,8... | collective-permute-start | bytes 61448 | tf_op jit(solution)/shard_map/ppermute | solution.py:584
  8.8 2.5 %collective-permute-start.3 = (bf16[40,256]{1,0:T(8,128)(2,1)S(1)}, bf16[40,256]{1,0:T(8,128)(2,1)S(1)}, u32[]{:S(2)}, u32[]{:S(2)}) collective-permute-start(bf16[40,256]{1,0:T(8,128)(2,1)S(1)} %get-tuple-element.56), channel_id=1, source_target_pairs={{1,2},{3,0},{2,1},{0,3},{5,6},{7,4},{6,5},{4,7},{9,10},{11,8},{10,... | collective-permute-start | bytes 61448 | tf_op jit(solution)/shard_map/ppermute | solution.py:584
  11.3 0.0 collective-permute-done.4.dm_near_ref
  11.4 0.6 %collective-permute-start.5 = (bf16[64,512]{1,0:T(8,128)(2,1)S(1)}, bf16[64,512]{1,0:T(8,128)(2,1)S(1)}, u32[]{:S(2)}, u32[]{:S(2)}) collective-permute-start(bf16[64,512]{1,0:T(8,128)(2,1)S(1)} %shard_map.148.refs_0_), channel_id=1, source_target_pairs={{0,8},{4,12},{8,0},{12,4},{16,24},{20,28},{24,16},{28,20},{1,9},{5... | collective-permute-start | bytes 196616 | tf_op jit(solution)/shard_map/ppermute | solution.py:589
  12.0 1.7 %collective-permute-start.6 = (bf16[64,512]{1,0:T(8,128)(2,1)S(1)}, bf16[64,512]{1,0:T(8,128)(2,1)S(1)}, u32[]{:S(2)}, u32[]{:S(2)}) collective-permute-start(bf16[64,512]{1,0:T(8,128)(2,1)S(1)} %shard_map.148.refs_0_), channel_id=1, source_target_pairs={{0,16},{4,20},{8,24},{12,28},{16,0},{20,4},{24,8},{28,12},{1,17},{... | collective-permute-start | bytes 196616 | tf_op jit(solution)/shard_map/ppermute | solution.py:589
  13.7 1.2 %collective-permute-start.7 = (bf16[64,512]{1,0:T(8,128)(2,1)S(1)}, bf16[64,512]{1,0:T(8,128)(2,1)S(1)}, u32[]{:S(2)}, u32[]{:S(2)}) collective-permute-start(bf16[64,512]{1,0:T(8,128)(2,1)S(1)} %shard_map.148.refs_0_), channel_id=1, source_target_pairs={{0,24},{4,28},{8,16},{12,20},{16,8},{20,12},{24,0},{28,4},{1,25},{... | collective-permute-start | bytes 196616 | tf_op jit(solution)/shard_map/ppermute | solution.py:589
  14.9 0.0 collective-permute-done.2.col_near_ref
  14.9 0.0 collective-permute-done.3.col_far_ref
  14.9 2.0 %shard_map.146 = (f32[480,256]{1,0:T(8,128)S(1)}, bf16[128,256]{1,0:T(8,128)(2,1)S(1)}, bf16[128,256]{1,0:T(8,128)(2,1)S(1)}, bf16[480,512]{1,0:T(8,128)(2,1)S(1...) custom-call(bf16[256,256]{1,0:T(8,128)(2,1)S(1)} %get-tuple-element.52.ones_ref, ...), custom_call_target="tpu_custom_call" | custom-call | flops 4000000000 | bytes 1000000 | tf_op jit(solution)/shard_map/pallas_call | solution.py:674
  16.9 0.0 collective-permute-done.5.refs_1_
  16.9 0.0 collective-permute-done.6.refs_2_
  16.9 1.9 %collective-permute-done.7.refs_3_ = bf16[64,512]{1,0:T(8,128)(2,1)S(1)} collective-permute-done((bf16[64,512]{1,0:T(8,128)(2,1)S(1)}, bf16[64,512]{1,0:T(8,128)(2,1)S(1)}, u32[]{:S(2)}, u32[]{:S(2)}) %collective-permute-start.7) | collective-permute-done | bytes 65568 | tf_op jit(solution)/shard_map/ppermute | solution.py:589
  18.8 0.6 %shard_map.149 = (bf16[256,512]{1,0:T(8,128)(2,1)S(1)}, bf16[4,32,1152]{2,1,0:T(8,128)(2,1)S(1)}, f32[4,32,1024]{2,1,0:T(8,128)S(1)}, bf16[4,32,128]{2,1,0:T(8,128)(2,1)S(1)}) custom-call(f32[480,256]{1,0:T(8,128)S(1)} %get-tuple-element.66.x_ref, bf16[128,256]{1,0:T(8,128)(2,1)S(1)} %get-tuple-element.67.d_query_ref, ...), custom_call_target="tpu_custom_call" | custom-call | flops 1000000000 | bytes 1000000 | tf_op jit(solution)/shard_map/pallas_call | solution.py:705
  19.4 0.1 collective-permute-start.8
  19.5 0.5 %shard_map.150 = (f32[192,256]{1,0:T(8,128)S(1)}, bf16[128,256]{1,0:T(8,128)(2,1)S(1)}, bf16[120,256]{1,0:T(8,128)(2,1)S(1)}, f32[8,128]{1,0:T(8,128)S(1)}) custom-call(f32[480,256]{1,0:T(8,128)S(1)} %get-tuple-element.66.x_ref, bf16[128,256]{1,0:T(8,128)(2,1)S(1)} %get-tuple-element.67.d_query_ref, bf16[480,512]{1,0:T(8,128)(2,1)S(1)} %get-tuple-element.68.d_kv_ref, ...), custom_call_target="tpu_custom_call" | custom-call | flops 500000000 | bytes 1000000 | tf_op jit(solution)/shard_map/pallas_call | solution.py:713
  20.1 0.6 %collective-permute-start.9 = (bf16[128,256]{1,0:T(8,128)(2,1)S(1)}, bf16[128,256]{1,0:T(8,128)(2,1)S(1)}, u32[]{:S(2)}, u32[]{:S(2)}) collective-permute-start(bf16[128,256]{1,0:T(8,128)(2,1)S(1)} %get-tuple-element.75), channel_id=1, source_target_pairs={{0,4},{8,12},{16,20},{24,28},{4,0},{12,8},{20,16},{28,24},{1,5},{9... | collective-permute-start | bytes 196616 | tf_op jit(solution)/shard_map/ppermute | solution.py:584
  20.6 0.9 %collective-permute-done.9.near_ref.refs_8_ = bf16[128,256]{1,0:T(8,128)(2,1)S(1)} collective-permute-done((bf16[128,256]{1,0:T(8,128)(2,1)S(1)}, bf16[128,256]{1,0:T(8,128)(2,1)S(1)}, u32[]{:S(2)}, u32[]{:S(2)}) %collective-permute-start.9) | collective-permute-done | bytes 65568 | tf_op jit(solution)/shard_map/ppermute | solution.py:584
  21.5 0.0 collective-permute-done.8.got_ref
  21.5 0.1 shard_map.151
  21.6 1.3 %collective-permute-start.10 = (bf16[32,1408]{1,0:T(8,128)(2,1)S(1)}, bf16[32,1408]{1,0:T(8,128)(2,1)S(1)}, u32[]{:S(2)}, u32[]{:S(2)}) collective-permute-start(bf16[32,1408]{1,0:T(8,128)(2,1)S(1)} %get-tuple-element.79), channel_id=1, source_target_pairs={{0,24},{4,28},{8,16},{12,20},{16,8},{20,12},{24,0},{28,4},{1,25},{... | collective-permute-start | bytes 270344 | tf_op jit(solution)/shard_map/ppermute | solution.py:589
  23.0 1.8 %collective-permute-start.11 = (bf16[32,1408]{1,0:T(8,128)(2,1)S(1)}, bf16[32,1408]{1,0:T(8,128)(2,1)S(1)}, u32[]{:S(2)}, u32[]{:S(2)}) collective-permute-start(bf16[32,1408]{1,0:T(8,128)(2,1)S(1)} %get-tuple-element.80), channel_id=1, source_target_pairs={{0,16},{4,20},{8,24},{12,28},{16,0},{20,4},{24,8},{28,12},{1,17},{... | collective-permute-start | bytes 270344 | tf_op jit(solution)/shard_map/ppermute | solution.py:589
  24.7 0.4 %collective-permute-start.12 = (bf16[32,1408]{1,0:T(8,128)(2,1)S(1)}, bf16[32,1408]{1,0:T(8,128)(2,1)S(1)}, u32[]{:S(2)}, u32[]{:S(2)}) collective-permute-start(bf16[32,1408]{1,0:T(8,128)(2,1)S(1)} %get-tuple-element.81), channel_id=1, source_target_pairs={{0,8},{4,12},{8,0},{12,4},{16,24},{20,28},{24,16},{28,20},{1,9},{5... | collective-permute-start | bytes 270344 | tf_op jit(solution)/shard_map/ppermute | solution.py:589
  25.2 0.4 %collective-permute-start.13 = (bf16[120,256]{1,0:T(8,128)(2,1)S(1)}, bf16[120,256]{1,0:T(8,128)(2,1)S(1)}, u32[]{:S(2)}, u32[]{:S(2)}) collective-permute-start(bf16[120,256]{1,0:T(8,128)(2,1)S(1)} %get-tuple-element.84), channel_id=1, source_target_pairs={{4,8},{12,16},{20,24},{28,0},{8,4},{16,12},{24,20},{0,28},{5,9},{1... | collective-permute-start | bytes 184328 | tf_op jit(solution)/shard_map/ppermute | solution.py:584
  25.6 4.8 %collective-permute-done.13.refs_9_ = bf16[120,256]{1,0:T(8,128)(2,1)S(1)} collective-permute-done((bf16[120,256]{1,0:T(8,128)(2,1)S(1)}, bf16[120,256]{1,0:T(8,128)(2,1)S(1)}, u32[]{:S(2)}, u32[]{:S(2)}) %collective-permute-start.13) | collective-permute-done | bytes 61472 | tf_op jit(solution)/shard_map/ppermute | solution.py:584
  30.5 0.0 collective-permute-done.10.refs_3_
  30.5 0.0 collective-permute-done.11.refs_4_
  30.5 0.0 collective-permute-done.12.refs_5_
  30.5 0.3 shard_map.152
  30.7 1.4 %collective-permute-start.14 = (bf16[32,896]{1,0:T(8,128)(2,1)S(1)}, bf16[32,896]{1,0:T(8,128)(2,1)S(1)}, u32[]{:S(2)}, u32[]{:S(2)}) collective-permute-start(bf16[32,896]{1,0:T(8,128)(2,1)S(1)} %get-tuple-element.86), channel_id=1, source_target_pairs={{0,3},{1,2},{2,1},{3,0},{4,7},{5,6},{6,5},{7,4},{8,11},{9,10},{10,... | collective-permute-start | bytes 172040 | tf_op jit(solution)/shard_map/ppermute | solution.py:589
  32.1 0.8 %collective-permute-start.15 = (bf16[32,896]{1,0:T(8,128)(2,1)S(1)}, bf16[32,896]{1,0:T(8,128)(2,1)S(1)}, u32[]{:S(2)}, u32[]{:S(2)}) collective-permute-start(bf16[32,896]{1,0:T(8,128)(2,1)S(1)} %get-tuple-element.87), channel_id=1, source_target_pairs={{0,2},{1,3},{2,0},{3,1},{4,6},{5,7},{6,4},{7,5},{8,10},{9,11},{10,... | collective-permute-start | bytes 172040 | tf_op jit(solution)/shard_map/ppermute | solution.py:589
  32.9 2.2 %collective-permute-start.16 = (bf16[32,896]{1,0:T(8,128)(2,1)S(1)}, bf16[32,896]{1,0:T(8,128)(2,1)S(1)}, u32[]{:S(2)}, u32[]{:S(2)}) collective-permute-start(bf16[32,896]{1,0:T(8,128)(2,1)S(1)} %get-tuple-element.88), channel_id=1, source_target_pairs={{0,1},{1,0},{2,3},{3,2},{4,5},{5,4},{6,7},{7,6},{8,9},{9,8},{10,11... | collective-permute-start | bytes 172040 | tf_op jit(solution)/shard_map/ppermute | solution.py:589
  35.2 0.9 %shard_map.147 = (bf16[4,32,256]{2,1,0:T(8,128)(2,1)}, bf16[2,16,512]{2,1,0:T(8,128)(2,1)}) custom-call(bf16[128,256]{1,0:T(8,128)(2,1)S(1)} %get-tuple-element.62.y_ref, bf16[32,1024]{1,0:T(8,128)(2,1)S(1)} %get-tuple-element.63.group_ref, bf16[1024,512]{1,0:T(8,128)(2,1)S(1)} %copy-done.1), custom_call_target="tpu_custom_call" | custom-call | flops 1000000000 | bytes 1000000 | tf_op jit(solution)/shard_map/pallas_call | solution.py:726
  36.1 1.3 %collective-permute-done.14.d_ref = bf16[32,896]{1,0:T(8,128)(2,1)S(1)} collective-permute-done((bf16[32,896]{1,0:T(8,128)(2,1)S(1)}, bf16[32,896]{1,0:T(8,128)(2,1)S(1)}, u32[]{:S(2)}, u32[]{:S(2)}) %collective-permute-start.14) | collective-permute-done | bytes 57376 | tf_op jit(solution)/shard_map/ppermute | solution.py:589
  37.4 1.5 %collective-permute-done.15.c_ref = bf16[32,896]{1,0:T(8,128)(2,1)S(1)} collective-permute-done((bf16[32,896]{1,0:T(8,128)(2,1)S(1)}, bf16[32,896]{1,0:T(8,128)(2,1)S(1)}, u32[]{:S(2)}, u32[]{:S(2)}) %collective-permute-start.15) | collective-permute-done | bytes 57376 | tf_op jit(solution)/shard_map/ppermute | solution.py:589
  39.0 0.0 collective-permute-done.16.b_ref
  39.0 0.7 %shard_map.153 = (f32[32,192]{1,0:T(8,128)}, f32[32,64]{1,0:T(8,128)}, f32[128,128]{1,0:T(8,128)}, f32[1,256]{1,0:T(1,128)}, f32[4]{0:T(128)}, /*index=5*/bf16[4,32,256]{2,1,0:T(8,128)(2,1)}) custom-call(bf16[32,896]{1,0:T(8,128)(2,1)S(1)} %get-tuple-element.85.a_ref, bf16[32,896]{1,0:T(8,128)(2,1)S(1)} %collective-permute-done.14.d_ref, ...), custom_call_target="tpu_custom_call" | custom-call | tf_op jit(solution)/shard_map/pallas_call | solution.py:766
  (3 shorter events, 0.1 us)
Async XLA Ops:
  0.6 4.2 %copy-start.5 = (bf16[4,32,256]{2,1,0:T(8,128)(2,1)S(1)}, bf16[4,32,256]{2,1,0:T(8,128)(2,1)}, u32[]{:S(2)}) copy-start(bf16[4,32,256]{2,1,0:T(8,128)(2,1)} %tok_ref.3) | copy-start | bytes 196612
  0.6 4.2 %copy-start = (bf16[2,16,512]{2,1,0:T(8,128)(2,1)S(1)}, bf16[2,16,512]{2,1,0:T(8,128)(2,1)}, u32[]{:S(2)}) copy-start(bf16[2,16,512]{2,1,0:T(8,128)(2,1)} %dm_ref.3) | copy-start | bytes 98308
  0.7 4.2 %copy-start.4 = (bf16[4,32,256]{2,1,0:T(8,128)(2,1)S(1)}, bf16[4,32,256]{2,1,0:T(8,128)(2,1)}, u32[]{:S(2)}) copy-start(bf16[4,32,256]{2,1,0:T(8,128)(2,1)} %dskip_ref.1) | copy-start | bytes 196612
  0.7 4.2 %copy-start.2 = (bf16[256,768]{1,0:T(8,128)(2,1)S(1)}, bf16[256,768]{1,0:T(8,128)(2,1)}, u32[]{:S(2)}) copy-start(bf16[256,768]{1,0:T(8,128)(2,1)} %wqkv_ref.5) | copy-start | bytes 1179652
  0.7 4.2 %copy-start.3 = (bf16[256,256]{1,0:T(8,128)(2,1)S(1)}, bf16[256,256]{1,0:T(8,128)(2,1)}, u32[]{:S(2)}) copy-start(bf16[256,256]{1,0:T(8,128)(2,1)} %wout_ref.3) | copy-start | bytes 393220
  0.7 4.2 %copy-start.1 = (bf16[1024,512]{1,0:T(8,128)(2,1)S(1)}, bf16[1024,512]{1,0:T(8,128)(2,1)}, u32[]{:S(2)}) copy-start(bf16[1024,512]{1,0:T(8,128)(2,1)} %wmerge_ref.3) | copy-start | bytes 3145732
  0.7 5.6 %collective-permute-start = (bf16[4,32,256]{2,1,0:T(8,128)(2,1)}, bf16[4,32,256]{2,1,0:T(8,128)(2,1)S(1)}, u32[]{:S(2)}, u32[]{:S(2)}) collective-permute-start(bf16[4,32,256]{2,1,0:T(8,128)(2,1)} %tok_ref.3), channel_id=1, source_target_pairs={{0,4},{8,12},{16,20},{24,28},{4,0},{12,8},{20,16},{28,24},{1,5},{9... | collective-permute-start | bytes 196616 | tf_op jit(solution)/shard_map/ppermute | solution.py:584
  1.2 5.8 %collective-permute-start.1 = (bf16[4,32,256]{2,1,0:T(8,128)(2,1)}, bf16[4,32,256]{2,1,0:T(8,128)(2,1)S(1)}, u32[]{:S(2)}, u32[]{:S(2)}) collective-permute-start(bf16[4,32,256]{2,1,0:T(8,128)(2,1)} %tok_ref.3), channel_id=1, source_target_pairs={{4,8},{12,16},{20,24},{28,0},{8,4},{16,12},{24,20},{0,28},{5,9},{1... | collective-permute-start | bytes 196616 | tf_op jit(solution)/shard_map/ppermute | solution.py:584
  4.8 6.5 %collective-permute-start.4 = (bf16[2,16,512]{2,1,0:T(8,128)(2,1)}, bf16[2,16,512]{2,1,0:T(8,128)(2,1)S(1)}, u32[]{:S(2)}, u32[]{:S(2)}) collective-permute-start(bf16[2,16,512]{2,1,0:T(8,128)(2,1)} %dm_ref.3), channel_id=1, source_target_pairs={{0,4},{4,0},{8,12},{12,8},{16,20},{20,16},{24,28},{28,24},{1,5},{5... | collective-permute-start | bytes 98312 | tf_op jit(solution)/shard_map/ppermute | solution.py:589
  4.8 0.7 %copy-start.6 = (f32[256]{0:T(256)S(1)}, f32[256]{0:T(256)}, u32[]{:S(2)}) copy-start(f32[256]{0:T(256)} %param.9) | copy-start | bytes 3076
  4.8 0.7 %copy-start.7 = (f32[4]{0:T(128)S(1)}, f32[4]{0:T(128)}, u32[]{:S(2)}) copy-start(f32[4]{0:T(128)} %param.11) | copy-start | bytes 52
  7.0 7.9 %collective-permute-start.2 = (bf16[40,256]{1,0:T(8,128)(2,1)S(1)}, bf16[40,256]{1,0:T(8,128)(2,1)S(1)}, u32[]{:S(2)}, u32[]{:S(2)}) collective-permute-start(bf16[40,256]{1,0:T(8,128)(2,1)S(1)} %get-tuple-element.55), channel_id=1, source_target_pairs={{0,1},{2,3},{1,0},{3,2},{4,5},{6,7},{5,4},{7,6},{8,9},{10,11},{9,8... | collective-permute-start | bytes 61448 | tf_op jit(solution)/shard_map/ppermute | solution.py:584
  8.8 6.1 %collective-permute-start.3 = (bf16[40,256]{1,0:T(8,128)(2,1)S(1)}, bf16[40,256]{1,0:T(8,128)(2,1)S(1)}, u32[]{:S(2)}, u32[]{:S(2)}) collective-permute-start(bf16[40,256]{1,0:T(8,128)(2,1)S(1)} %get-tuple-element.56), channel_id=1, source_target_pairs={{1,2},{3,0},{2,1},{0,3},{5,6},{7,4},{6,5},{4,7},{9,10},{11,8},{10,... | collective-permute-start | bytes 61448 | tf_op jit(solution)/shard_map/ppermute | solution.py:584
  11.4 5.5 %collective-permute-start.5 = (bf16[64,512]{1,0:T(8,128)(2,1)S(1)}, bf16[64,512]{1,0:T(8,128)(2,1)S(1)}, u32[]{:S(2)}, u32[]{:S(2)}) collective-permute-start(bf16[64,512]{1,0:T(8,128)(2,1)S(1)} %shard_map.148.refs_0_), channel_id=1, source_target_pairs={{0,8},{4,12},{8,0},{12,4},{16,24},{20,28},{24,16},{28,20},{1,9},{5... | collective-permute-start | bytes 196616 | tf_op jit(solution)/shard_map/ppermute | solution.py:589
  12.0 5.0 %collective-permute-start.6 = (bf16[64,512]{1,0:T(8,128)(2,1)S(1)}, bf16[64,512]{1,0:T(8,128)(2,1)S(1)}, u32[]{:S(2)}, u32[]{:S(2)}) collective-permute-start(bf16[64,512]{1,0:T(8,128)(2,1)S(1)} %shard_map.148.refs_0_), channel_id=1, source_target_pairs={{0,16},{4,20},{8,24},{12,28},{16,0},{20,4},{24,8},{28,12},{1,17},{... | collective-permute-start | bytes 196616 | tf_op jit(solution)/shard_map/ppermute | solution.py:589
  13.7 5.2 %collective-permute-start.7 = (bf16[64,512]{1,0:T(8,128)(2,1)S(1)}, bf16[64,512]{1,0:T(8,128)(2,1)S(1)}, u32[]{:S(2)}, u32[]{:S(2)}) collective-permute-start(bf16[64,512]{1,0:T(8,128)(2,1)S(1)} %shard_map.148.refs_0_), channel_id=1, source_target_pairs={{0,24},{4,28},{8,16},{12,20},{16,8},{20,12},{24,0},{28,4},{1,25},{... | collective-permute-start | bytes 196616 | tf_op jit(solution)/shard_map/ppermute | solution.py:589
  19.4 2.1 %collective-permute-start.8 = (bf16[4,32,1152]{2,1,0:T(8,128)(2,1)S(1)}, bf16[4,32,1152]{2,1,0:T(8,128)(2,1)S(1)}, u32[]{:S(2)}, u32[]{:S(2)}) collective-permute-start(bf16[4,32,1152]{2,1,0:T(8,128)(2,1)S(1)} %get-tuple-element.70), channel_id=1, source_target_pairs={{0,4},{4,0},{8,12},{12,8},{16,20},{20,16},{24,28},{28,24},{1,5},{5... | collective-permute-start | bytes 884744 | tf_op jit(solution)/shard_map/ppermute | solution.py:589
  20.1 1.5 %collective-permute-start.9 = (bf16[128,256]{1,0:T(8,128)(2,1)S(1)}, bf16[128,256]{1,0:T(8,128)(2,1)S(1)}, u32[]{:S(2)}, u32[]{:S(2)}) collective-permute-start(bf16[128,256]{1,0:T(8,128)(2,1)S(1)} %get-tuple-element.75), channel_id=1, source_target_pairs={{0,4},{8,12},{16,20},{24,28},{4,0},{12,8},{20,16},{28,24},{1,5},{9... | collective-permute-start | bytes 196616 | tf_op jit(solution)/shard_map/ppermute | solution.py:584
  21.6 8.8 %collective-permute-start.10 = (bf16[32,1408]{1,0:T(8,128)(2,1)S(1)}, bf16[32,1408]{1,0:T(8,128)(2,1)S(1)}, u32[]{:S(2)}, u32[]{:S(2)}) collective-permute-start(bf16[32,1408]{1,0:T(8,128)(2,1)S(1)} %get-tuple-element.79), channel_id=1, source_target_pairs={{0,24},{4,28},{8,16},{12,20},{16,8},{20,12},{24,0},{28,4},{1,25},{... | collective-permute-start | bytes 270344 | tf_op jit(solution)/shard_map/ppermute | solution.py:589
  23.0 7.5 %collective-permute-start.11 = (bf16[32,1408]{1,0:T(8,128)(2,1)S(1)}, bf16[32,1408]{1,0:T(8,128)(2,1)S(1)}, u32[]{:S(2)}, u32[]{:S(2)}) collective-permute-start(bf16[32,1408]{1,0:T(8,128)(2,1)S(1)} %get-tuple-element.80), channel_id=1, source_target_pairs={{0,16},{4,20},{8,24},{12,28},{16,0},{20,4},{24,8},{28,12},{1,17},{... | collective-permute-start | bytes 270344 | tf_op jit(solution)/shard_map/ppermute | solution.py:589
  24.7 5.7 %collective-permute-start.12 = (bf16[32,1408]{1,0:T(8,128)(2,1)S(1)}, bf16[32,1408]{1,0:T(8,128)(2,1)S(1)}, u32[]{:S(2)}, u32[]{:S(2)}) collective-permute-start(bf16[32,1408]{1,0:T(8,128)(2,1)S(1)} %get-tuple-element.81), channel_id=1, source_target_pairs={{0,8},{4,12},{8,0},{12,4},{16,24},{20,28},{24,16},{28,20},{1,9},{5... | collective-permute-start | bytes 270344 | tf_op jit(solution)/shard_map/ppermute | solution.py:589
  25.2 5.3 %collective-permute-start.13 = (bf16[120,256]{1,0:T(8,128)(2,1)S(1)}, bf16[120,256]{1,0:T(8,128)(2,1)S(1)}, u32[]{:S(2)}, u32[]{:S(2)}) collective-permute-start(bf16[120,256]{1,0:T(8,128)(2,1)S(1)} %get-tuple-element.84), channel_id=1, source_target_pairs={{4,8},{12,16},{20,24},{28,0},{8,4},{16,12},{24,20},{0,28},{5,9},{1... | collective-permute-start | bytes 184328 | tf_op jit(solution)/shard_map/ppermute | solution.py:584
  30.7 6.7 %collective-permute-start.14 = (bf16[32,896]{1,0:T(8,128)(2,1)S(1)}, bf16[32,896]{1,0:T(8,128)(2,1)S(1)}, u32[]{:S(2)}, u32[]{:S(2)}) collective-permute-start(bf16[32,896]{1,0:T(8,128)(2,1)S(1)} %get-tuple-element.86), channel_id=1, source_target_pairs={{0,3},{1,2},{2,1},{3,0},{4,7},{5,6},{6,5},{7,4},{8,11},{9,10},{10,... | collective-permute-start | bytes 172040 | tf_op jit(solution)/shard_map/ppermute | solution.py:589
  32.1 6.8 %collective-permute-start.15 = (bf16[32,896]{1,0:T(8,128)(2,1)S(1)}, bf16[32,896]{1,0:T(8,128)(2,1)S(1)}, u32[]{:S(2)}, u32[]{:S(2)}) collective-permute-start(bf16[32,896]{1,0:T(8,128)(2,1)S(1)} %get-tuple-element.87), channel_id=1, source_target_pairs={{0,2},{1,3},{2,0},{3,1},{4,6},{5,7},{6,4},{7,5},{8,10},{9,11},{10,... | collective-permute-start | bytes 172040 | tf_op jit(solution)/shard_map/ppermute | solution.py:589
  32.9 6.0 %collective-permute-start.16 = (bf16[32,896]{1,0:T(8,128)(2,1)S(1)}, bf16[32,896]{1,0:T(8,128)(2,1)S(1)}, u32[]{:S(2)}, u32[]{:S(2)}) collective-permute-start(bf16[32,896]{1,0:T(8,128)(2,1)S(1)} %get-tuple-element.88), channel_id=1, source_target_pairs={{0,1},{1,0},{2,3},{3,2},{4,5},{5,4},{6,7},{7,6},{8,9},{9,8},{10,11... | collective-permute-start | bytes 172040 | tf_op jit(solution)/shard_map/ppermute | solution.py:589

commit v3 on v2

--- a/solution.py
+++ b/solution.py
@@ -302,7 +302,7 @@
 ):
     rows, cols, width, n_row, n_dm = sizes
     dm_refs, dm_all_ref, sum_refs = (refs[:n_dm], refs[n_dm], refs[n_dm + 1 :])
-    dm_all_ref[...] = jnp.concatenate([ref[...] for ref in dm_refs], axis=0)
+    dm_all_ref[...] = jnp.concatenate([ref[...] for ref in dm_refs[::-1]], axis=0)
     x = x_ref[...]
     inverse = lax.rsqrt(jnp.mean(x * x, axis=1, keepdims=True) + EPS)
     normed32 = (x * inverse * rows_ref[0:1]).astype(BF).astype(F32)
@@ -434,9 +434,14 @@
 def row_sum_kernel(sizes, *refs):
     rows, cols, width, n_col = sizes
     own_ref, own_group_ref, small_ref, *refs = refs
-    got_refs, dm_ref, refs = (refs[:3], refs[3], refs[4:])
-    gx_ref, near_ref, far_ref, *out_refs, grad_ref, slots_ref = refs
+    got_refs, dm_ref, gx_ref, near_ref, *refs = (refs[:3], *refs[3:])
+    *out_refs, gx_sum_ref, slots_ref = refs
     wide = cols + 2 * SIDE
+    blank = jnp.zeros(((rows - RADIUS) * wide, width), F32)
+    near = wide_rim(near_ref, cols)
+    above, below = (jnp.concatenate([near, blank], axis=0), jnp.concatenate([blank, near], axis=0))
+    even = lax.rem(lax.axis_index("row"), 2) == 0
+    gx_sum_ref[...] = gx_ref[...] + jnp.where(even, below, above)
     per = own_ref.shape[0]
     feats = own_group_ref.shape[1] // 2
     at = 4 * width
@@ -453,24 +458,8 @@
     group = [part[:, i * feats : (i + 1) * feats].astype(F32) for part in group for i in range(2)]
     group = jnp.concatenate(group, axis=0)
     merge = mm(group.T.astype(BF), dm_ref[...])
-    g_x = gx_ref[...]
-    blank = jnp.zeros(((rows - RADIUS) * wide, width), F32)
-    above, below = by_side("row", wide_rim(near_ref, cols), wide_rim(far_ref, cols))
-    g_x = g_x + jnp.concatenate([above, blank], axis=0)
-    g_x = g_x + jnp.concatenate([blank, below], axis=0)
-    grad = []
-    left = []
-    right = []
-    for i in range(rows):
-        spot = i * wide + SIDE
-        grad.append(g_x[spot : spot + cols])
-        left.append(g_x[spot - SIDE : spot][SIDE - RADIUS :])
-        right.append(g_x[spot + cols : spot + cols + SIDE][:RADIUS])
-    grad_ref[...] = jnp.concatenate(grad, axis=0)
-    left, right = [jnp.concatenate(part, axis=0) for part in (left, right)]
-    left, right = [jnp.concatenate([v[:, :LANES], v[:, LANES:]], axis=0) for v in (left, right)]
     high = small.astype(BF).astype(F32)
-    small = jnp.concatenate([high[:4], (small - high)[:4]], axis=0)
+    small = jnp.concatenate([high[:4], (small - high)[:4], jnp.zeros((per - 8, LANES), F32)], axis=0)
     col = lax.axis_index("col")
     third = 3 * width // n_col
     fourth = width // n_col
@@ -482,8 +471,7 @@
         ]
         for k in range(feats // per):
             parts.append(merge[k * per : (k + 1) * per, slot * depth : (slot + 1) * depth])
-        rim = jnp.where(slot < col, left, right)
-        parts.append(jnp.concatenate([rim, small], axis=0))
+        parts.append(small)
         slots_ref[slot] = jnp.concatenate(parts, axis=1).astype(BF)
     for step, out_ref in enumerate(out_refs):
         out_ref[...] = slots_ref[partner(col, step)]
@@ -500,8 +488,31 @@
     return 3 - index
 
 
+def side_kernel(sizes, gx_ref, far_ref, grad_ref, side_near_ref, side_far_ref):
+    rows, cols, width = sizes
+    wide = cols + 2 * SIDE
+    blank = jnp.zeros(((rows - RADIUS) * wide, width), F32)
+    far = wide_rim(far_ref, cols)
+    above, below = (jnp.concatenate([far, blank], axis=0), jnp.concatenate([blank, far], axis=0))
+    even = lax.rem(lax.axis_index("row"), 2) == 0
+    g_x = gx_ref[...] + jnp.where(even, above, below)
+    grad = []
+    left = []
+    right = []
+    for i in range(rows):
+        spot = i * wide + SIDE
+        grad.append(g_x[spot : spot + cols])
+        left.append(g_x[spot - SIDE : spot][SIDE - EDGE :])
+        right.append(g_x[spot + cols : spot + cols + SIDE][:EDGE])
+    grad_ref[...] = jnp.concatenate(grad, axis=0)
+    left, right = [jnp.concatenate(part, axis=0) for part in (left, right)]
+    far, near = by_side("col", right, left)
+    side_near_ref[...] = near.astype(BF)
+    side_far_ref[...] = far.astype(BF)
+
+
 def col_sum_kernel(
-    sizes, a_ref, d_ref, c_ref, b_ref, grad_ref, gqkv_ref, gout_ref, gmerge_ref, ggain_ref, gscale_ref, gtok_ref
+    sizes, a_ref, d_ref, c_ref, b_ref, grad_ref, near_ref, far_ref, gqkv_ref, gout_ref, gmerge_ref, ggain_ref, gscale_ref, gtok_ref
 ):
     rows, cols, width = sizes
     per, lanes = a_ref.shape
@@ -509,7 +520,6 @@
     fourth = gout_ref.shape[1]
     depth = gmerge_ref.shape[1]
     end = lanes - LANES
-    reach = per - 8
 
     def summed(part):
         first, second, third, fourth = [part(ref) for ref in (a_ref, b_ref, c_ref, d_ref)]
@@ -517,7 +527,7 @@
 
     def tiny(ref):
         value = ref[:, end:].astype(F32)
-        return value[reach : reach + 4] + value[reach + 4 :]
+        return value[:4] + value[4:8]
 
     total = summed(lambda ref: ref[:, :end].astype(F32))
     small = summed(tiny)
@@ -531,18 +541,13 @@
         gscale_ref[h] = small[width // LANES, h]
     col = lax.axis_index("col")
 
-    def rim(ref):
-        value = ref[:, end:].astype(F32)
-        half = reach // 2
-        return jnp.concatenate([value[:half], value[half:reach]], axis=1)
-
-    left, right = by_side("col", rim(b_ref), rim(d_ref))
+    left, right = by_side("col", near_ref[...].astype(F32), far_ref[...].astype(F32))
     left = jnp.where(col > 0, left, 0.0)
     right = jnp.where(col < lax.axis_size("col") - 1, right, 0.0)
-    blank = jnp.zeros((cols - 2 * RADIUS, width), F32)
+    blank = jnp.zeros((cols - 2 * EDGE, width), F32)
     pieces = []
     for i in range(rows):
-        edge = slice(i * RADIUS, (i + 1) * RADIUS)
+        edge = slice(i * EDGE, (i + 1) * EDGE)
         pieces += [left[edge], blank, right[edge]]
     grad = grad_ref[...] + jnp.concatenate(pieces, axis=0)
     gtok_ref[...] = grad.astype(BF).reshape(rows, cols, width)
@@ -620,7 +625,7 @@
         out_specs=vmem(1)[0],
         compiler_params=less,
     )(parity, d_merged, swap(d_merged, "row", 1))
-    dm_pairs = [dm_pair] + [swap(dm_pair, "row", 2 * step) for step in range(1, 4)]
+    dm_pairs = [swap(dm_pair, "row", 2 * step) for step in (3, 2, 1)] + [dm_pair]
     gathered = len(dm_pairs) * 2 * groups
     tile = shape((rows * cols, width), F32)
     half = shape((rows * cols, width), BF)
@@ -656,7 +661,7 @@
     per = width // n_row
     feats = 4 * width // n_row
     packed = per % 16 == 0 and feats % LANES == 0 and groups == per
-    packed = packed and 2 * rows * RADIUS + 8 == per and width // LANES < 4 and depth // n_col == LANES and n_col == 4 and n_row == 8
+    packed = packed and width // LANES < 4 and depth // n_col == LANES and n_col == 4 and n_row == 8
     if packed:
         sum_shapes = (
             shape((n_row // 2, per, 4 * width + feats), BF),
@@ -752,15 +757,23 @@
         )(swap(send, "row", 1), *kept, small, near)
         got = [swap(blocks[step - 1], "row", 2 * step) for step in (3, 2, 1)]
         lanes = 4 * width // n_col + feats // per * (depth // n_col) + LANES
-        *slots, grad = pl.pallas_call(
+        *slots, gx = pl.pallas_call(
             functools.partial(row_sum_kernel, (rows, cols, width, n_col)),
-            out_shape=tuple([shape((per, lanes), BF)] * n_col)
-            + (shape((rows * cols, width), F32),),
-            in_specs=vmem(10),
+            out_shape=tuple([shape((per, lanes), BF)] * n_col) + (shape(gx.shape, F32),),
+            in_specs=vmem(9),
             out_specs=tuple(vmem(n_col + 1)),
             scratch_shapes=[pltpu.VMEM((n_col, per, lanes), BF)],
             compiler_params=less,
-        )(own, own_group, small, *got, dm_all, gx, near, far)
+        )(own, own_group, small, *got, dm_all, gx, near)
+        side = shape((rows * EDGE, width), BF)
+        grad, *sides = pl.pallas_call(
+            functools.partial(side_kernel, (rows, cols, width)),
+            out_shape=(shape((rows * cols, width), F32), side, side),
+            in_specs=vmem(2),
+            out_specs=tuple(vmem(3)),
+            compiler_params=less,
+        )(gx, far)
+        sides = swapped(*sides, "col")
         got = [slots[0]]
         got += [swap(slots[step], "col", step) for step in (3, 2, 1)]
         g_qkv, g_out, g_merge, g_gain, g_scale, grad_tokens = pl.pallas_call(
@@ -773,10 +786,10 @@
                 shape((heads,), F32),
                 shape((rows, cols, width), BF),
             ),
-            in_specs=vmem(5),
+            in_specs=vmem(7),
             out_specs=tuple(vmem(4)) + (pl.BlockSpec(memory_space=pltpu.SMEM), vmem(1)[0]),
             compiler_params=less,
-        )(*got, grad)
+        )(*got, grad, *sides)
     return (
         skip_out,
         merged,

time: 39.8 us -> 40.5 us (1.018)
  starting transfers between devices: 21 us -> 23.3 us
  waiting for transfers between devices: 11.2 us -> 9.53 us
    ppermute x6 -> x8, starting transfers between devices: 9.35 us -> 11.7 us  [swapped(): return (lax.ppermute(near, axis, first), lax.ppermute(far, axis, second))]
    ppermute x6 -> x8, waiting for transfers between devices: 6.44 us -> 4.75 us  [swapped(): return (lax.ppermute(near, axis, first), lax.ppermute(far, axis, second))]
  transfers between devices with their start and end apart: 17 -> 19, of which waited for: 6 -> 8; matrix products, arithmetic and copies ran while one was open for 0% -> 0% of each run, Pallas kernels for 11% -> 11%
where the time goes in v3:
time: 40.5 us; the launch traced here: 40.3 us
  starting transfers between devices  23.3 us (58%)
  waiting for transfers between devices  9.53 us (24%)
  Pallas kernels  6.02 us (15%)
  between operations  0.86 us (2%)
  local copies, waits for them, and re-layouts  0.63 us (2%)
    ppermute x8, starting transfers between devices, swapped(): return (lax.ppermute(near, axis, first), lax.ppermute(far, axis, second))  11.7 us
    ppermute x11, starting transfers between devices, swap(): return lax.ppermute(value, axis, [(i, i ^ step) for i in range(count)])  11.6 us
    ppermute x11, waiting for transfers between devices, swap(): return lax.ppermute(value, axis, [(i, i ^ step) for i in range(count)])  4.77 us
    ppermute x8, waiting for transfers between devices, swapped(): return (lax.ppermute(near, axis, first), lax.ppermute(far, axis, second))  4.75 us
    pallas_call x1, Pallas kernels, on_device(): pl.pallas_call(functools.partial(layer_kernel, sizes), out_shape=(shape((...  1.97 us
    pallas_call x1, Pallas kernels, on_device(): pl.pallas_call(output_kernel, out_shape=(shape((rows, cols, width), BF),...  0.91 us
  transfers between devices with their start and end apart: 19, of which 8 were waited for; matrix products, arithmetic and copies ran while one was open for 0% of the time, Pallas kernels for 11%

profile of v3, /device:TPU:0, one launch (start us, length us, event | category | flops | bytes accessed | tf_op | source)
XLA Modules:
  0.0 40.3 jit_solution(10992400275505658133)
XLA Ops:
  0.6 0.0 copy-start.5
  0.6 0.0 copy-start
  0.7 0.0 copy-start.4
  0.7 0.0 copy-start.2
  0.7 0.0 copy-start.3
  0.7 0.0 copy-start.1
  0.7 0.5 %collective-permute-start = (bf16[4,32,256]{2,1,0:T(8,128)(2,1)}, bf16[4,32,256]{2,1,0:T(8,128)(2,1)S(1)}, u32[]{:S(2)}, u32[]{:S(2)}) collective-permute-start(bf16[4,32,256]{2,1,0:T(8,128)(2,1)} %tok_ref.3), channel_id=1, source_target_pairs={{0,4},{8,12},{16,20},{24,28},{4,0},{12,8},{20,16},{28,24},{1,5},{9... | collective-permute-start | bytes 196616 | tf_op jit(solution)/shard_map/ppermute | solution.py:589
  1.2 3.6 %collective-permute-start.1 = (bf16[4,32,256]{2,1,0:T(8,128)(2,1)}, bf16[4,32,256]{2,1,0:T(8,128)(2,1)S(1)}, u32[]{:S(2)}, u32[]{:S(2)}) collective-permute-start(bf16[4,32,256]{2,1,0:T(8,128)(2,1)} %tok_ref.3), channel_id=1, source_target_pairs={{4,8},{12,16},{20,24},{28,0},{8,4},{16,12},{24,20},{0,28},{5,9},{1... | collective-permute-start | bytes 196616 | tf_op jit(solution)/shard_map/ppermute | solution.py:589
  4.8 0.0 collective-permute-start.4
  4.8 0.0 copy-start.6
  4.8 0.0 copy-start.7
  4.8 0.0 copy-done.5
  4.8 0.0 copy-done
  4.9 0.0 copy-done.4
  4.9 0.0 copy-done.2
  4.9 0.0 copy-done.3
  4.9 0.0 copy-done.1
  4.9 0.6 %copy-done.6 = f32[256]{0:T(256)S(1)} copy-done((f32[256]{0:T(256)S(1)}, f32[256]{0:T(256)}, u32[]{:S(2)}) %copy-start.6) | copy-done | bytes 1048
  5.5 0.0 copy-done.7
  5.5 0.8 %shard_map.144 = (bf16[32,256]{1,0:T(8,128)(2,1)S(1)}, f32[8,256]{1,0:T(8,128)S(1)}, f32[128,256]{1,0:T(8,128)S(1)}, f32[128,256]{1,0:T(8,128)S(1)}, f32[128,256...) custom-call(bf16[256,256]{1,0:T(8,128)(2,1)S(1)} %get-tuple-element.55.ones_ref, f32[8,128]{1,0:T(8,128)S(1)} %get-tuple-element.56.parity_ref, ...), custom_call_target="tpu_custom_call" | custom-call | flops 1000000000 | bytes 1000000 | tf_op jit(solution)/shard_map/pallas_call | solution.py:632
  6.3 0.0 collective-permute-done.near_ref.row_near_ref
  6.3 0.7 %collective-permute-done.1.far_ref.row_far_ref = bf16[4,32,256]{2,1,0:T(8,128)(2,1)S(1)} collective-permute-done((bf16[4,32,256]{2,1,0:T(8,128)(2,1)}, bf16[4,32,256]{2,1,0:T(8,128)(2,1)S(1)}, u32[]{:S(2)}, u32[]{:S(2)}) %collective-permute-start.1) | collective-permute-done | bytes 65568 | tf_op jit(solution)/shard_map/ppermute | solution.py:589
  7.0 1.8 %collective-permute-start.2 = (bf16[40,256]{1,0:T(8,128)(2,1)S(1)}, bf16[40,256]{1,0:T(8,128)(2,1)S(1)}, u32[]{:S(2)}, u32[]{:S(2)}) collective-permute-start(bf16[40,256]{1,0:T(8,128)(2,1)S(1)} %get-tuple-element.58), channel_id=1, source_target_pairs={{0,1},{2,3},{1,0},{3,2},{4,5},{6,7},{5,4},{7,6},{8,9},{10,11},{9,8... | collective-permute-start | bytes 61448 | tf_op jit(solution)/shard_map/ppermute | solution.py:589
  8.8 2.5 %collective-permute-start.3 = (bf16[40,256]{1,0:T(8,128)(2,1)S(1)}, bf16[40,256]{1,0:T(8,128)(2,1)S(1)}, u32[]{:S(2)}, u32[]{:S(2)}) collective-permute-start(bf16[40,256]{1,0:T(8,128)(2,1)S(1)} %get-tuple-element.59), channel_id=1, source_target_pairs={{1,2},{3,0},{2,1},{0,3},{5,6},{7,4},{6,5},{4,7},{9,10},{11,8},{10,... | collective-permute-start | bytes 61448 | tf_op jit(solution)/shard_map/ppermute | solution.py:589
  11.3 0.0 collective-permute-done.4.dm_near_ref
  11.4 1.7 %collective-permute-start.5 = (bf16[64,512]{1,0:T(8,128)(2,1)S(1)}, bf16[64,512]{1,0:T(8,128)(2,1)S(1)}, u32[]{:S(2)}, u32[]{:S(2)}) collective-permute-start(bf16[64,512]{1,0:T(8,128)(2,1)S(1)} %shard_map.148.refs_3_), channel_id=1, source_target_pairs={{0,24},{4,28},{8,16},{12,20},{16,8},{20,12},{24,0},{28,4},{1,25},{... | collective-permute-start | bytes 196616 | tf_op jit(solution)/shard_map/ppermute | solution.py:594
  13.1 0.3 collective-permute-start.6
  13.4 1.5 %collective-permute-start.7 = (bf16[64,512]{1,0:T(8,128)(2,1)S(1)}, bf16[64,512]{1,0:T(8,128)(2,1)S(1)}, u32[]{:S(2)}, u32[]{:S(2)}) collective-permute-start(bf16[64,512]{1,0:T(8,128)(2,1)S(1)} %shard_map.148.refs_3_), channel_id=1, source_target_pairs={{0,8},{4,12},{8,0},{12,4},{16,24},{20,28},{24,16},{28,20},{1,9},{5... | collective-permute-start | bytes 196616 | tf_op jit(solution)/shard_map/ppermute | solution.py:594
  14.9 0.0 collective-permute-done.2.col_near_ref
  14.9 0.0 collective-permute-done.3.col_far_ref
  14.9 2.0 %shard_map.146 = (f32[480,256]{1,0:T(8,128)S(1)}, bf16[128,256]{1,0:T(8,128)(2,1)S(1)}, bf16[128,256]{1,0:T(8,128)(2,1)S(1)}, bf16[480,512]{1,0:T(8,128)(2,1)S(1...) custom-call(bf16[256,256]{1,0:T(8,128)(2,1)S(1)} %get-tuple-element.55.ones_ref, ...), custom_call_target="tpu_custom_call" | custom-call | flops 4000000000 | bytes 1000000 | tf_op jit(solution)/shard_map/pallas_call | solution.py:679
  16.9 0.0 collective-permute-done.5.refs_0_
  16.9 1.1 %collective-permute-done.6.refs_1_ = bf16[64,512]{1,0:T(8,128)(2,1)S(1)} collective-permute-done((bf16[64,512]{1,0:T(8,128)(2,1)S(1)}, bf16[64,512]{1,0:T(8,128)(2,1)S(1)}, u32[]{:S(2)}, u32[]{:S(2)}) %collective-permute-start.6) | collective-permute-done | bytes 65568 | tf_op jit(solution)/shard_map/ppermute | solution.py:594
  18.0 0.3 collective-permute-done.7.refs_2_
  18.3 0.6 %shard_map.149 = (bf16[256,512]{1,0:T(8,128)(2,1)S(1)}, bf16[4,32,1152]{2,1,0:T(8,128)(2,1)S(1)}, f32[4,32,1024]{2,1,0:T(8,128)S(1)}, bf16[4,32,128]{2,1,0:T(8,128)(2,1)S(1)}) custom-call(f32[480,256]{1,0:T(8,128)S(1)} %get-tuple-element.69.x_ref, bf16[128,256]{1,0:T(8,128)(2,1)S(1)} %get-tuple-element.70.d_query_ref, ...), custom_call_target="tpu_custom_call" | custom-call | flops 1000000000 | bytes 1000000 | tf_op jit(solution)/shard_map/pallas_call | solution.py:710
  18.9 0.1 collective-permute-start.8
  19.0 0.5 %shard_map.150 = (f32[192,256]{1,0:T(8,128)S(1)}, bf16[128,256]{1,0:T(8,128)(2,1)S(1)}, bf16[120,256]{1,0:T(8,128)(2,1)S(1)}, f32[8,128]{1,0:T(8,128)S(1)}) custom-call(f32[480,256]{1,0:T(8,128)S(1)} %get-tuple-element.69.x_ref, bf16[128,256]{1,0:T(8,128)(2,1)S(1)} %get-tuple-element.70.d_query_ref, bf16[480,512]{1,0:T(8,128)(2,1)S(1)} %get-tuple-element.71.d_kv_ref, ...), custom_call_target="tpu_custom_call" | custom-call | flops 500000000 | bytes 1000000 | tf_op jit(solution)/shard_map/pallas_call | solution.py:718
  19.6 0.6 %collective-permute-start.9 = (bf16[128,256]{1,0:T(8,128)(2,1)S(1)}, bf16[128,256]{1,0:T(8,128)(2,1)S(1)}, u32[]{:S(2)}, u32[]{:S(2)}) collective-permute-start(bf16[128,256]{1,0:T(8,128)(2,1)S(1)} %get-tuple-element.78), channel_id=1, source_target_pairs={{0,4},{8,12},{16,20},{24,28},{4,0},{12,8},{20,16},{28,24},{1,5},{9... | collective-permute-start | bytes 196616 | tf_op jit(solution)/shard_map/ppermute | solution.py:589
  20.1 0.9 %collective-permute-done.9.near_ref.refs_8_ = bf16[128,256]{1,0:T(8,128)(2,1)S(1)} collective-permute-done((bf16[128,256]{1,0:T(8,128)(2,1)S(1)}, bf16[128,256]{1,0:T(8,128)(2,1)S(1)}, u32[]{:S(2)}, u32[]{:S(2)}) %collective-permute-start.9) | collective-permute-done | bytes 65568 | tf_op jit(solution)/shard_map/ppermute | solution.py:589
  21.0 0.0 collective-permute-done.8.got_ref
  21.0 0.1 shard_map.151
  21.1 2.2 %collective-permute-start.10 = (bf16[32,1408]{1,0:T(8,128)(2,1)S(1)}, bf16[32,1408]{1,0:T(8,128)(2,1)S(1)}, u32[]{:S(2)}, u32[]{:S(2)}) collective-permute-start(bf16[32,1408]{1,0:T(8,128)(2,1)S(1)} %get-tuple-element.82), channel_id=1, source_target_pairs={{0,24},{4,28},{8,16},{12,20},{16,8},{20,12},{24,0},{28,4},{1,25},{... | collective-permute-start | bytes 270344 | tf_op jit(solution)/shard_map/ppermute | solution.py:594
  23.3 0.2 collective-permute-start.11
  23.5 1.2 %collective-permute-start.12 = (bf16[32,1408]{1,0:T(8,128)(2,1)S(1)}, bf16[32,1408]{1,0:T(8,128)(2,1)S(1)}, u32[]{:S(2)}, u32[]{:S(2)}) collective-permute-start(bf16[32,1408]{1,0:T(8,128)(2,1)S(1)} %get-tuple-element.84), channel_id=1, source_target_pairs={{0,8},{4,12},{8,0},{12,4},{16,24},{20,28},{24,16},{28,20},{1,9},{5... | collective-permute-start | bytes 270344 | tf_op jit(solution)/shard_map/ppermute | solution.py:594
  24.7 1.2 %collective-permute-start.16 = (bf16[120,256]{1,0:T(8,128)(2,1)S(1)}, bf16[120,256]{1,0:T(8,128)(2,1)S(1)}, u32[]{:S(2)}, u32[]{:S(2)}) collective-permute-start(bf16[120,256]{1,0:T(8,128)(2,1)S(1)} %get-tuple-element.92), channel_id=1, source_target_pairs={{4,8},{12,16},{20,24},{28,0},{8,4},{16,12},{24,20},{0,28},{5,9},{1... | collective-permute-start | bytes 184328 | tf_op jit(solution)/shard_map/ppermute | solution.py:589
  25.9 1.2 %collective-permute-done.10.refs_3_ = bf16[32,1408]{1,0:T(8,128)(2,1)S(1)} collective-permute-done((bf16[32,1408]{1,0:T(8,128)(2,1)S(1)}, bf16[32,1408]{1,0:T(8,128)(2,1)S(1)}, u32[]{:S(2)}, u32[]{:S(2)}) %collective-permute-start.10) | collective-permute-done | bytes 90144 | tf_op jit(solution)/shard_map/ppermute | solution.py:594
  27.1 2.1 %collective-permute-done.11.refs_4_ = bf16[32,1408]{1,0:T(8,128)(2,1)S(1)} collective-permute-done((bf16[32,1408]{1,0:T(8,128)(2,1)S(1)}, bf16[32,1408]{1,0:T(8,128)(2,1)S(1)}, u32[]{:S(2)}, u32[]{:S(2)}) %collective-permute-start.11) | collective-permute-done | bytes 90144 | tf_op jit(solution)/shard_map/ppermute | solution.py:594
  29.2 0.0 collective-permute-done.12.refs_5_
  29.2 0.3 shard_map.152
  29.5 1.4 %collective-permute-start.13 = (bf16[32,896]{1,0:T(8,128)(2,1)S(1)}, bf16[32,896]{1,0:T(8,128)(2,1)S(1)}, u32[]{:S(2)}, u32[]{:S(2)}) collective-permute-start(bf16[32,896]{1,0:T(8,128)(2,1)S(1)} %get-tuple-element.88), channel_id=1, source_target_pairs={{0,3},{1,2},{2,1},{3,0},{4,7},{5,6},{6,5},{7,4},{8,11},{9,10},{10,... | collective-permute-start | bytes 172040 | tf_op jit(solution)/shard_map/ppermute | solution.py:594
  30.9 0.8 %collective-permute-start.14 = (bf16[32,896]{1,0:T(8,128)(2,1)S(1)}, bf16[32,896]{1,0:T(8,128)(2,1)S(1)}, u32[]{:S(2)}, u32[]{:S(2)}) collective-permute-start(bf16[32,896]{1,0:T(8,128)(2,1)S(1)} %get-tuple-element.89), channel_id=1, source_target_pairs={{0,2},{1,3},{2,0},{3,1},{4,6},{5,7},{6,4},{7,5},{8,10},{9,11},{10,... | collective-permute-start | bytes 172040 | tf_op jit(solution)/shard_map/ppermute | solution.py:594
  31.7 2.2 %collective-permute-start.15 = (bf16[32,896]{1,0:T(8,128)(2,1)S(1)}, bf16[32,896]{1,0:T(8,128)(2,1)S(1)}, u32[]{:S(2)}, u32[]{:S(2)}) collective-permute-start(bf16[32,896]{1,0:T(8,128)(2,1)S(1)} %get-tuple-element.90), channel_id=1, source_target_pairs={{0,1},{1,0},{2,3},{3,2},{4,5},{5,4},{6,7},{7,6},{8,9},{9,8},{10,11... | collective-permute-start | bytes 172040 | tf_op jit(solution)/shard_map/ppermute | solution.py:594
  33.9 0.0 collective-permute-done.16.far_ref
  34.0 0.1 collective-permute-start.17
  34.1 1.5 %collective-permute-start.18 = (bf16[16,256]{1,0:T(8,128)(2,1)S(1)}, bf16[16,256]{1,0:T(8,128)(2,1)S(1)}, u32[]{:S(2)}, u32[]{:S(2)}) collective-permute-start(bf16[16,256]{1,0:T(8,128)(2,1)S(1)} %get-tuple-element.95), channel_id=1, source_target_pairs={{1,2},{3,0},{2,1},{0,3},{5,6},{7,4},{6,5},{4,7},{9,10},{11,8},{10,... | collective-permute-start | bytes 24584 | tf_op jit(solution)/shard_map/ppermute | solution.py:589
  35.5 0.9 %shard_map.147 = (bf16[4,32,256]{2,1,0:T(8,128)(2,1)}, bf16[2,16,512]{2,1,0:T(8,128)(2,1)}) custom-call(bf16[128,256]{1,0:T(8,128)(2,1)S(1)} %get-tuple-element.65.y_ref, bf16[32,1024]{1,0:T(8,128)(2,1)S(1)} %get-tuple-element.66.group_ref, bf16[1024,512]{1,0:T(8,128)(2,1)S(1)} %copy-done.1), custom_call_target="tpu_custom_call" | custom-call | flops 1000000000 | bytes 1000000 | tf_op jit(solution)/shard_map/pallas_call | solution.py:731
  36.4 1.4 %collective-permute-done.17.near_ref = bf16[16,256]{1,0:T(8,128)(2,1)S(1)} collective-permute-done((bf16[16,256]{1,0:T(8,128)(2,1)S(1)}, bf16[16,256]{1,0:T(8,128)(2,1)S(1)}, u32[]{:S(2)}, u32[]{:S(2)}) %collective-permute-start.17) | collective-permute-done | bytes 8224 | tf_op jit(solution)/shard_map/ppermute | solution.py:589
  37.8 1.8 %collective-permute-done.18.far_ref = bf16[16,256]{1,0:T(8,128)(2,1)S(1)} collective-permute-done((bf16[16,256]{1,0:T(8,128)(2,1)S(1)}, bf16[16,256]{1,0:T(8,128)(2,1)S(1)}, u32[]{:S(2)}, u32[]{:S(2)}) %collective-permute-start.18) | collective-permute-done | bytes 8224 | tf_op jit(solution)/shard_map/ppermute | solution.py:589
  39.6 0.0 collective-permute-done.13.d_ref
  39.6 0.0 collective-permute-done.14.c_ref
  39.6 0.0 collective-permute-done.15.b_ref
  39.6 0.7 %shard_map.154 = (f32[32,192]{1,0:T(8,128)}, f32[32,64]{1,0:T(8,128)}, f32[128,128]{1,0:T(8,128)}, f32[1,256]{1,0:T(1,128)}, f32[4]{0:T(128)}, /*index=5*/bf16[4,32,256]{2,1,0:T(8,128)(2,1)}) custom-call(bf16[32,896]{1,0:T(8,128)(2,1)S(1)} %get-tuple-element.87.a_ref, bf16[32,896]{1,0:T(8,128)(2,1)S(1)} %collective-permute-done.13.d_ref, ...), custom_call_target="tpu_custom_call" | custom-call | tf_op jit(solution)/shard_map/pallas_call | solution.py:779
  (4 shorter events, 0.1 us)
Async XLA Ops:
  0.6 4.2 %copy-start.5 = (bf16[4,32,256]{2,1,0:T(8,128)(2,1)S(1)}, bf16[4,32,256]{2,1,0:T(8,128)(2,1)}, u32[]{:S(2)}) copy-start(bf16[4,32,256]{2,1,0:T(8,128)(2,1)} %tok_ref.3) | copy-start | bytes 196612
  0.6 4.2 %copy-start = (bf16[2,16,512]{2,1,0:T(8,128)(2,1)S(1)}, bf16[2,16,512]{2,1,0:T(8,128)(2,1)}, u32[]{:S(2)}) copy-start(bf16[2,16,512]{2,1,0:T(8,128)(2,1)} %dm_ref.3) | copy-start | bytes 98308
  0.7 4.2 %copy-start.4 = (bf16[4,32,256]{2,1,0:T(8,128)(2,1)S(1)}, bf16[4,32,256]{2,1,0:T(8,128)(2,1)}, u32[]{:S(2)}) copy-start(bf16[4,32,256]{2,1,0:T(8,128)(2,1)} %dskip_ref.1) | copy-start | bytes 196612
  0.7 4.2 %copy-start.2 = (bf16[256,768]{1,0:T(8,128)(2,1)S(1)}, bf16[256,768]{1,0:T(8,128)(2,1)}, u32[]{:S(2)}) copy-start(bf16[256,768]{1,0:T(8,128)(2,1)} %wqkv_ref.5) | copy-start | bytes 1179652
  0.7 4.2 %copy-start.3 = (bf16[256,256]{1,0:T(8,128)(2,1)S(1)}, bf16[256,256]{1,0:T(8,128)(2,1)}, u32[]{:S(2)}) copy-start(bf16[256,256]{1,0:T(8,128)(2,1)} %wout_ref.3) | copy-start | bytes 393220
  0.7 4.2 %copy-start.1 = (bf16[1024,512]{1,0:T(8,128)(2,1)S(1)}, bf16[1024,512]{1,0:T(8,128)(2,1)}, u32[]{:S(2)}) copy-start(bf16[1024,512]{1,0:T(8,128)(2,1)} %wmerge_ref.3) | copy-start | bytes 3145732
  0.7 5.6 %collective-permute-start = (bf16[4,32,256]{2,1,0:T(8,128)(2,1)}, bf16[4,32,256]{2,1,0:T(8,128)(2,1)S(1)}, u32[]{:S(2)}, u32[]{:S(2)}) collective-permute-start(bf16[4,32,256]{2,1,0:T(8,128)(2,1)} %tok_ref.3), channel_id=1, source_target_pairs={{0,4},{8,12},{16,20},{24,28},{4,0},{12,8},{20,16},{28,24},{1,5},{9... | collective-permute-start | bytes 196616 | tf_op jit(solution)/shard_map/ppermute | solution.py:589
  1.2 5.8 %collective-permute-start.1 = (bf16[4,32,256]{2,1,0:T(8,128)(2,1)}, bf16[4,32,256]{2,1,0:T(8,128)(2,1)S(1)}, u32[]{:S(2)}, u32[]{:S(2)}) collective-permute-start(bf16[4,32,256]{2,1,0:T(8,128)(2,1)} %tok_ref.3), channel_id=1, source_target_pairs={{4,8},{12,16},{20,24},{28,0},{8,4},{16,12},{24,20},{0,28},{5,9},{1... | collective-permute-start | bytes 196616 | tf_op jit(solution)/shard_map/ppermute | solution.py:589
  4.8 6.5 %collective-permute-start.4 = (bf16[2,16,512]{2,1,0:T(8,128)(2,1)}, bf16[2,16,512]{2,1,0:T(8,128)(2,1)S(1)}, u32[]{:S(2)}, u32[]{:S(2)}) collective-permute-start(bf16[2,16,512]{2,1,0:T(8,128)(2,1)} %dm_ref.3), channel_id=1, source_target_pairs={{0,4},{4,0},{8,12},{12,8},{16,20},{20,16},{24,28},{28,24},{1,5},{5... | collective-permute-start | bytes 98312 | tf_op jit(solution)/shard_map/ppermute | solution.py:594
  4.8 0.7 %copy-start.6 = (f32[256]{0:T(256)S(1)}, f32[256]{0:T(256)}, u32[]{:S(2)}) copy-start(f32[256]{0:T(256)} %param.9) | copy-start | bytes 3076
  4.8 0.7 %copy-start.7 = (f32[4]{0:T(128)S(1)}, f32[4]{0:T(128)}, u32[]{:S(2)}) copy-start(f32[4]{0:T(128)} %param.11) | copy-start | bytes 52
  7.0 7.9 %collective-permute-start.2 = (bf16[40,256]{1,0:T(8,128)(2,1)S(1)}, bf16[40,256]{1,0:T(8,128)(2,1)S(1)}, u32[]{:S(2)}, u32[]{:S(2)}) collective-permute-start(bf16[40,256]{1,0:T(8,128)(2,1)S(1)} %get-tuple-element.58), channel_id=1, source_target_pairs={{0,1},{2,3},{1,0},{3,2},{4,5},{6,7},{5,4},{7,6},{8,9},{10,11},{9,8... | collective-permute-start | bytes 61448 | tf_op jit(solution)/shard_map/ppermute | solution.py:589
  8.8 6.1 %collective-permute-start.3 = (bf16[40,256]{1,0:T(8,128)(2,1)S(1)}, bf16[40,256]{1,0:T(8,128)(2,1)S(1)}, u32[]{:S(2)}, u32[]{:S(2)}) collective-permute-start(bf16[40,256]{1,0:T(8,128)(2,1)S(1)} %get-tuple-element.59), channel_id=1, source_target_pairs={{1,2},{3,0},{2,1},{0,3},{5,6},{7,4},{6,5},{4,7},{9,10},{11,8},{10,... | collective-permute-start | bytes 61448 | tf_op jit(solution)/shard_map/ppermute | solution.py:589
  11.4 5.5 %collective-permute-start.5 = (bf16[64,512]{1,0:T(8,128)(2,1)S(1)}, bf16[64,512]{1,0:T(8,128)(2,1)S(1)}, u32[]{:S(2)}, u32[]{:S(2)}) collective-permute-start(bf16[64,512]{1,0:T(8,128)(2,1)S(1)} %shard_map.148.refs_3_), channel_id=1, source_target_pairs={{0,24},{4,28},{8,16},{12,20},{16,8},{20,12},{24,0},{28,4},{1,25},{... | collective-permute-start | bytes 196616 | tf_op jit(solution)/shard_map/ppermute | solution.py:594
  13.1 4.9 %collective-permute-start.6 = (bf16[64,512]{1,0:T(8,128)(2,1)S(1)}, bf16[64,512]{1,0:T(8,128)(2,1)S(1)}, u32[]{:S(2)}, u32[]{:S(2)}) collective-permute-start(bf16[64,512]{1,0:T(8,128)(2,1)S(1)} %shard_map.148.refs_3_), channel_id=1, source_target_pairs={{0,16},{4,20},{8,24},{12,28},{16,0},{20,4},{24,8},{28,12},{1,17},{... | collective-permute-start | bytes 196616 | tf_op jit(solution)/shard_map/ppermute | solution.py:594
  13.4 4.9 %collective-permute-start.7 = (bf16[64,512]{1,0:T(8,128)(2,1)S(1)}, bf16[64,512]{1,0:T(8,128)(2,1)S(1)}, u32[]{:S(2)}, u32[]{:S(2)}) collective-permute-start(bf16[64,512]{1,0:T(8,128)(2,1)S(1)} %shard_map.148.refs_3_), channel_id=1, source_target_pairs={{0,8},{4,12},{8,0},{12,4},{16,24},{20,28},{24,16},{28,20},{1,9},{5... | collective-permute-start | bytes 196616 | tf_op jit(solution)/shard_map/ppermute | solution.py:594
  18.9 2.1 %collective-permute-start.8 = (bf16[4,32,1152]{2,1,0:T(8,128)(2,1)S(1)}, bf16[4,32,1152]{2,1,0:T(8,128)(2,1)S(1)}, u32[]{:S(2)}, u32[]{:S(2)}) collective-permute-start(bf16[4,32,1152]{2,1,0:T(8,128)(2,1)S(1)} %get-tuple-element.73), channel_id=1, source_target_pairs={{0,4},{4,0},{8,12},{12,8},{16,20},{20,16},{24,28},{28,24},{1,5},{5... | collective-permute-start | bytes 884744 | tf_op jit(solution)/shard_map/ppermute | solution.py:594
  19.6 1.5 %collective-permute-start.9 = (bf16[128,256]{1,0:T(8,128)(2,1)S(1)}, bf16[128,256]{1,0:T(8,128)(2,1)S(1)}, u32[]{:S(2)}, u32[]{:S(2)}) collective-permute-start(bf16[128,256]{1,0:T(8,128)(2,1)S(1)} %get-tuple-element.78), channel_id=1, source_target_pairs={{0,4},{8,12},{16,20},{24,28},{4,0},{12,8},{20,16},{28,24},{1,5},{9... | collective-permute-start | bytes 196616 | tf_op jit(solution)/shard_map/ppermute | solution.py:589
  21.1 5.9 %collective-permute-start.10 = (bf16[32,1408]{1,0:T(8,128)(2,1)S(1)}, bf16[32,1408]{1,0:T(8,128)(2,1)S(1)}, u32[]{:S(2)}, u32[]{:S(2)}) collective-permute-start(bf16[32,1408]{1,0:T(8,128)(2,1)S(1)} %get-tuple-element.82), channel_id=1, source_target_pairs={{0,24},{4,28},{8,16},{12,20},{16,8},{20,12},{24,0},{28,4},{1,25},{... | collective-permute-start | bytes 270344 | tf_op jit(solution)/shard_map/ppermute | solution.py:594
  23.3 5.9 %collective-permute-start.11 = (bf16[32,1408]{1,0:T(8,128)(2,1)S(1)}, bf16[32,1408]{1,0:T(8,128)(2,1)S(1)}, u32[]{:S(2)}, u32[]{:S(2)}) collective-permute-start(bf16[32,1408]{1,0:T(8,128)(2,1)S(1)} %get-tuple-element.83), channel_id=1, source_target_pairs={{0,16},{4,20},{8,24},{12,28},{16,0},{20,4},{24,8},{28,12},{1,17},{... | collective-permute-start | bytes 270344 | tf_op jit(solution)/shard_map/ppermute | solution.py:594
  23.5 5.7 %collective-permute-start.12 = (bf16[32,1408]{1,0:T(8,128)(2,1)S(1)}, bf16[32,1408]{1,0:T(8,128)(2,1)S(1)}, u32[]{:S(2)}, u32[]{:S(2)}) collective-permute-start(bf16[32,1408]{1,0:T(8,128)(2,1)S(1)} %get-tuple-element.84), channel_id=1, source_target_pairs={{0,8},{4,12},{8,0},{12,4},{16,24},{20,28},{24,16},{28,20},{1,9},{5... | collective-permute-start | bytes 270344 | tf_op jit(solution)/shard_map/ppermute | solution.py:594
  24.7 9.3 %collective-permute-start.16 = (bf16[120,256]{1,0:T(8,128)(2,1)S(1)}, bf16[120,256]{1,0:T(8,128)(2,1)S(1)}, u32[]{:S(2)}, u32[]{:S(2)}) collective-permute-start(bf16[120,256]{1,0:T(8,128)(2,1)S(1)} %get-tuple-element.92), channel_id=1, source_target_pairs={{4,8},{12,16},{20,24},{28,0},{8,4},{16,12},{24,20},{0,28},{5,9},{1... | collective-permute-start | bytes 184328 | tf_op jit(solution)/shard_map/ppermute | solution.py:589
  29.5 10.1 %collective-permute-start.13 = (bf16[32,896]{1,0:T(8,128)(2,1)S(1)}, bf16[32,896]{1,0:T(8,128)(2,1)S(1)}, u32[]{:S(2)}, u32[]{:S(2)}) collective-permute-start(bf16[32,896]{1,0:T(8,128)(2,1)S(1)} %get-tuple-element.88), channel_id=1, source_target_pairs={{0,3},{1,2},{2,1},{3,0},{4,7},{5,6},{6,5},{7,4},{8,11},{9,10},{10,... | collective-permute-start | bytes 172040 | tf_op jit(solution)/shard_map/ppermute | solution.py:594
  30.9 8.7 %collective-permute-start.14 = (bf16[32,896]{1,0:T(8,128)(2,1)S(1)}, bf16[32,896]{1,0:T(8,128)(2,1)S(1)}, u32[]{:S(2)}, u32[]{:S(2)}) collective-permute-start(bf16[32,896]{1,0:T(8,128)(2,1)S(1)} %get-tuple-element.89), channel_id=1, source_target_pairs={{0,2},{1,3},{2,0},{3,1},{4,6},{5,7},{6,4},{7,5},{8,10},{9,11},{10,... | collective-permute-start | bytes 172040 | tf_op jit(solution)/shard_map/ppermute | solution.py:594
  31.7 7.9 %collective-permute-start.15 = (bf16[32,896]{1,0:T(8,128)(2,1)S(1)}, bf16[32,896]{1,0:T(8,128)(2,1)S(1)}, u32[]{:S(2)}, u32[]{:S(2)}) collective-permute-start(bf16[32,896]{1,0:T(8,128)(2,1)S(1)} %get-tuple-element.90), channel_id=1, source_target_pairs={{0,1},{1,0},{2,3},{3,2},{4,5},{5,4},{6,7},{7,6},{8,9},{9,8},{10,11... | collective-permute-start | bytes 172040 | tf_op jit(solution)/shard_map/ppermute | solution.py:594
  34.0 3.8 %collective-permute-start.17 = (bf16[16,256]{1,0:T(8,128)(2,1)S(1)}, bf16[16,256]{1,0:T(8,128)(2,1)S(1)}, u32[]{:S(2)}, u32[]{:S(2)}) collective-permute-start(bf16[16,256]{1,0:T(8,128)(2,1)S(1)} %get-tuple-element.94), channel_id=1, source_target_pairs={{0,1},{2,3},{1,0},{3,2},{4,5},{6,7},{5,4},{7,6},{8,9},{10,11},{9,8... | collective-permute-start | bytes 24584 | tf_op jit(solution)/shard_map/ppermute | solution.py:589
  34.1 5.5 %collective-permute-start.18 = (bf16[16,256]{1,0:T(8,128)(2,1)S(1)}, bf16[16,256]{1,0:T(8,128)(2,1)S(1)}, u32[]{:S(2)}, u32[]{:S(2)}) collective-permute-start(bf16[16,256]{1,0:T(8,128)(2,1)S(1)} %get-tuple-element.95), channel_id=1, source_target_pairs={{1,2},{3,0},{2,1},{0,3},{5,6},{7,4},{6,5},{4,7},{9,10},{11,8},{10,... | collective-permute-start | bytes 24584 | tf_op jit(solution)/shard_map/ppermute | solution.py:589

commit v4 on v2

--- a/solution.py
+++ b/solution.py
@@ -63,14 +63,6 @@
         own = edges_ref[own_at : own_at + rows * EDGE].astype(F32)
         size = RADIUS * EDGE
         out_ref[...] = jnp.concatenate([part[:size], own, part[size:]], axis=0).astype(BF)
-
-
-def pair_kernel(parity_ref, dm_ref, dm_near_ref, dm_pair_ref):
-    size = dm_pair_ref.shape[0] // 2
-    own, near = [ref[...].reshape(size, -1).astype(F32) for ref in (dm_ref, dm_near_ref)]
-    even = parity_ref[0:1, 0:1] > 0.5
-    pair = [jnp.where(even, own, near), jnp.where(even, near, own)]
-    dm_pair_ref[...] = jnp.concatenate(pair, axis=0).astype(BF)
 
 
 def in_order(axis, own, partner):
@@ -302,7 +294,9 @@
 ):
     rows, cols, width, n_row, n_dm = sizes
     dm_refs, dm_all_ref, sum_refs = (refs[:n_dm], refs[n_dm], refs[n_dm + 1 :])
-    dm_all_ref[...] = jnp.concatenate([ref[...] for ref in dm_refs], axis=0)
+    size = dm_all_ref.shape[0] // n_dm
+    dm = [ref[...].reshape(size, dm_all_ref.shape[1]) for ref in dm_refs]
+    dm_all_ref[...] = jnp.concatenate(dm[::-1], axis=0)
     x = x_ref[...]
     inverse = lax.rsqrt(jnp.mean(x * x, axis=1, keepdims=True) + EPS)
     normed32 = (x * inverse * rows_ref[0:1]).astype(BF).astype(F32)
@@ -334,7 +328,7 @@
     sizes, x_ref, d_query_ref, d_kv_ref, scale_part_ref, rows_ref, dy_ref, wqkv_ref, *refs
 ):
     rows, cols, width, heads = sizes
-    gx_ref, gx_near_ref, gx_far_ref, small_ref = refs
+    gx_ref, side_near_ref, side_far_ref, small_ref = refs
     head_dim = width // heads
     wide = cols + 2 * SIDE
     ext_rows = rows + 2 * RADIUS
@@ -360,19 +354,22 @@
     mean = jnp.mean(x * scaled, axis=1, keepdims=True)
     g_x = inverse * scaled - x * (inverse * inverse * inverse) * mean
 
-    def rim(first_row):
-        parts = []
-        for i in range(first_row, first_row + RADIUS):
-            parts.append(g_x[i * wide : (i + 1) * wide][SIDE - EDGE : wide - SIDE + EDGE])
-        return jnp.concatenate(parts, axis=0)
-
-    far, near = by_side("row", rim(RADIUS + rows), rim(0))
     pieces = []
-    for i in range(rows):
-        at = (RADIUS + i) * wide
-        middle = g_x[at + SIDE : at + SIDE + cols] + d_y[i * cols : (i + 1) * cols]
-        pieces += [g_x[at : at + SIDE], middle, g_x[at + SIDE + cols : at + wide]]
+    left = []
+    right = []
+    for i in range(ext_rows):
+        row = g_x[i * wide : (i + 1) * wide]
+        middle = row[SIDE : SIDE + cols]
+        if RADIUS <= i < RADIUS + rows:
+            middle = middle + d_y[(i - RADIUS) * cols : (i - RADIUS + 1) * cols]
+        pieces.append(middle)
+        left.append(row[:SIDE][SIDE - EDGE :])
+        right.append(row[SIDE + cols :][:EDGE])
     gx_ref[...] = jnp.concatenate(pieces, axis=0)
+    left, right = [jnp.concatenate(part, axis=0) for part in (left, right)]
+    far, near = by_side("col", right, left)
+    side_near_ref[...] = near.astype(BF)
+    side_far_ref[...] = far.astype(BF)
     scale_part = scale_part_ref[0:1]
     scale_lane = lax.broadcasted_iota(jnp.int32, (1, LANES), 1)
     scale_sums = jnp.zeros((1, LANES), F32)
@@ -382,51 +379,45 @@
     small = [gain_part[:, i * LANES : (i + 1) * LANES] for i in range(width // LANES)] + [scale_sums]
     small = jnp.concatenate(small + [jnp.zeros((8 - len(small), LANES), F32)], axis=0)
     small_ref[...] = small
+
+
+def small_rows(small):
     high = small.astype(BF).astype(F32)
-    small = jnp.concatenate([high, small - high], axis=1)
-    gx_near_ref[...] = jnp.concatenate([near, small], axis=0).astype(BF)
-    gx_far_ref[...] = far.astype(BF)
-
-
-def small_rows(small, rows):
-    high = small.astype(BF).astype(F32)
-    blank = jnp.zeros((rows - 16, LANES), F32)
-    return jnp.concatenate([high, small - high, blank], axis=0).astype(BF)
-
-
-def wide_rim(ref, cols):
-    size = cols + 2 * EDGE
-    blank = jnp.zeros((SIDE - EDGE, ref.shape[1]), F32)
-    pieces = []
-    for i in range(RADIUS):
-        pieces += [blank, ref[...][i * size : (i + 1) * size].astype(F32), blank]
-    return jnp.concatenate(pieces, axis=0)
+    return jnp.concatenate([high[:4], (small - high)[:4]], axis=0)
 
 
 def small_value(rows):
-    value = rows.astype(F32)
-    return value[:8] + value[8:16]
-
-
-def core_sum_kernel(got_ref, keep_ref, keep_group_ref, small_ref, near_ref, *refs):
+    value = rows.astype(BF).astype(F32)
+    return value[:4] + value[4:]
+
+
+def stacked(value):
+    return jnp.concatenate(
+        [value[:, i : i + LANES] for i in range(0, value.shape[1], LANES)], axis=0
+    )
+
+
+def unstacked(value, rows):
+    return jnp.concatenate([value[i : i + rows] for i in range(0, value.shape[0], rows)], axis=1)
+
+
+def core_sum_kernel(got_ref, keep_ref, keep_group_ref, small_ref, small_near_ref, *refs):
     *out_refs, own_ref, own_group_ref, small_sum_ref, blocks_ref = refs
     chips, per, width = keep_ref.shape
     feats = keep_group_ref.shape[2]
-    end = width + feats
-    got_small = near_ref[...].astype(F32)[near_ref.shape[0] - 8 :]
-    got_small = got_small[:, :LANES] + got_small[:, LANES:]
-    small = small_value(small_rows(small_ref[...], per)) + got_small
+    small = small_ref[...] + small_near_ref[...]
     small_sum_ref[...] = small
-    small = small_rows(small, per)
+    small = small_rows(small)
     chip = lax.axis_index("row") // 2
     own_ref[...] = keep_ref[chip] + got_ref[chip, :, :width].astype(F32)
     for q in range(chips):
         sums = keep_ref[q] + got_ref[q, :, :width].astype(F32)
         kept = keep_group_ref[q].astype(F32)
-        first, second = in_order("row", kept, got_ref[q, :, width:end].astype(F32))
-        block = jnp.concatenate([sums, first, second], axis=1).astype(BF)
-        blocks_ref[q] = jnp.concatenate([block, small], axis=1)
-    own_group_ref[...] = blocks_ref[chip, :, width : width + 2 * feats]
+        first, second = in_order("row", kept, got_ref[q, :, width:].astype(F32))
+        block = [stacked(sums), first, second, small]
+        blocks_ref[q] = jnp.concatenate(block, axis=0).astype(BF)
+    size = width // LANES * per
+    own_group_ref[...] = blocks_ref[chip][size : size + 2 * per]
     for step, out_ref in enumerate(out_refs, 1):
         out_ref[...] = blocks_ref[partner(chip, step)]
 
@@ -434,43 +425,28 @@
 def row_sum_kernel(sizes, *refs):
     rows, cols, width, n_col = sizes
     own_ref, own_group_ref, small_ref, *refs = refs
-    got_refs, dm_ref, refs = (refs[:3], refs[3], refs[4:])
-    gx_ref, near_ref, far_ref, *out_refs, grad_ref, slots_ref = refs
-    wide = cols + 2 * SIDE
+    got_refs, dm_ref, dm_near_ref, gx_ref, *refs = (refs[:3], *refs[3:])
+    *out_refs, gx_sum_ref, slots_ref = refs
+    gx_sum_ref[...] = gx_ref[...]
     per = own_ref.shape[0]
-    feats = own_group_ref.shape[1] // 2
-    at = 4 * width
-    end = at + 2 * feats
+    feats = own_group_ref.shape[1]
+    size = 4 * width // LANES * per
 
     def summed(first, part):
-        fourth, third, second = [part(ref) for ref in got_refs]
+        fourth, third, second = [part(ref[...].astype(F32)) for ref in got_refs]
         return (first + second) + (third + fourth)
 
-    sums = summed(own_ref[...], lambda ref: ref[:, :at].astype(F32))
-    small = small_value(small_rows(small_ref[...], per))
-    small = summed(small, lambda ref: small_value(ref[:, end:]))
-    group = [own_group_ref[...]] + [ref[:, at:end] for ref in got_refs[::-1]]
-    group = [part[:, i * feats : (i + 1) * feats].astype(F32) for part in group for i in range(2)]
+    sums = summed(stacked(own_ref[...]), lambda value: value[:size])
+    sums = unstacked(sums, per)
+    small = summed(small_value(small_rows(small_ref[...])), lambda value: small_value(value[size + 2 * per :]))
+    group = [own_group_ref[...].astype(F32)]
+    group += [ref[...].astype(F32)[size : size + 2 * per] for ref in got_refs[::-1]]
+    group = [part[i * per : (i + 1) * per] for i in range(2) for part in group]
     group = jnp.concatenate(group, axis=0)
-    merge = mm(group.T.astype(BF), dm_ref[...])
-    g_x = gx_ref[...]
-    blank = jnp.zeros(((rows - RADIUS) * wide, width), F32)
-    above, below = by_side("row", wide_rim(near_ref, cols), wide_rim(far_ref, cols))
-    g_x = g_x + jnp.concatenate([above, blank], axis=0)
-    g_x = g_x + jnp.concatenate([blank, below], axis=0)
-    grad = []
-    left = []
-    right = []
-    for i in range(rows):
-        spot = i * wide + SIDE
-        grad.append(g_x[spot : spot + cols])
-        left.append(g_x[spot - SIDE : spot][SIDE - RADIUS :])
-        right.append(g_x[spot + cols : spot + cols + SIDE][:RADIUS])
-    grad_ref[...] = jnp.concatenate(grad, axis=0)
-    left, right = [jnp.concatenate(part, axis=0) for part in (left, right)]
-    left, right = [jnp.concatenate([v[:, :LANES], v[:, LANES:]], axis=0) for v in (left, right)]
-    high = small.astype(BF).astype(F32)
-    small = jnp.concatenate([high[:4], (small - high)[:4]], axis=0)
+    own, near = (dm_ref[...].astype(F32), dm_near_ref[...].astype(F32))
+    dm = jnp.concatenate(in_order("row", own, near), axis=0).astype(BF)
+    merge = mm(group.T.astype(BF), dm)
+    small = small_rows(small)
     col = lax.axis_index("col")
     third = 3 * width // n_col
     fourth = width // n_col
@@ -480,11 +456,9 @@
             sums[:, slot * third : (slot + 1) * third],
             sums[:, 3 * width + slot * fourth : 3 * width + (slot + 1) * fourth],
         ]
-        for k in range(feats // per):
-            parts.append(merge[k * per : (k + 1) * per, slot * depth : (slot + 1) * depth])
-        rim = jnp.where(slot < col, left, right)
-        parts.append(jnp.concatenate([rim, small], axis=0))
-        slots_ref[slot] = jnp.concatenate(parts, axis=1).astype(BF)
+        parts = [stacked(jnp.concatenate(parts, axis=1))]
+        parts += [merge[:, slot * depth : (slot + 1) * depth], small]
+        slots_ref[slot] = jnp.concatenate(parts, axis=0).astype(BF)
     for step, out_ref in enumerate(out_refs):
         out_ref[...] = slots_ref[partner(col, step)]
 
@@ -500,57 +474,69 @@
     return 3 - index
 
 
+def side_kernel(sizes, gx_ref, near_ref, far_ref, grad_ref, row_near_ref, row_far_ref):
+    rows, cols, width = sizes
+    ends = lax.axis_index("col")
+    left, right = by_side("col", near_ref[...].astype(F32), far_ref[...].astype(F32))
+    left = jnp.where(ends > 0, left, 0.0)
+    right = jnp.where(ends < lax.axis_size("col") - 1, right, 0.0)
+    blank = jnp.zeros((cols - 2 * EDGE, width), F32)
+    pieces = []
+    for i in range(rows + 2 * RADIUS):
+        edge = slice(i * EDGE, (i + 1) * EDGE)
+        pieces += [left[edge], blank, right[edge]]
+    g_x = gx_ref[...] + jnp.concatenate(pieces, axis=0)
+    reach = RADIUS * cols
+    far, near = by_side("row", g_x[reach + rows * cols :], g_x[:reach])
+    grad_ref[...] = g_x[reach : reach + rows * cols]
+    row_near_ref[...] = near.astype(BF)
+    row_far_ref[...] = far.astype(BF)
+
+
 def col_sum_kernel(
-    sizes, a_ref, d_ref, c_ref, b_ref, grad_ref, gqkv_ref, gout_ref, gmerge_ref, ggain_ref, gscale_ref, gtok_ref
+    sizes,
+    a_ref,
+    d_ref,
+    c_ref,
+    b_ref,
+    grad_ref,
+    near_ref,
+    far_ref,
+    gqkv_ref,
+    gout_ref,
+    gmerge_ref,
+    ggain_ref,
+    gscale_ref,
+    gtok_ref,
 ):
     rows, cols, width = sizes
-    per, lanes = a_ref.shape
-    third = gqkv_ref.shape[1]
-    fourth = gout_ref.shape[1]
-    depth = gmerge_ref.shape[1]
-    end = lanes - LANES
-    reach = per - 8
+    per, third = gqkv_ref.shape
+    size = a_ref.shape[0] - 8
 
     def summed(part):
-        first, second, third, fourth = [part(ref) for ref in (a_ref, b_ref, c_ref, d_ref)]
+        first, second, third, fourth = [
+            part(ref[...].astype(F32)) for ref in (a_ref, b_ref, c_ref, d_ref)
+        ]
         return (first + second) + (third + fourth)
 
-    def tiny(ref):
-        value = ref[:, end:].astype(F32)
-        return value[reach : reach + 4] + value[reach + 4 :]
-
-    total = summed(lambda ref: ref[:, :end].astype(F32))
-    small = summed(tiny)
-    gqkv_ref[...] = total[:, :third]
-    gout_ref[...] = total[:, third : third + fourth]
-    for k in range(gmerge_ref.shape[0] // per):
-        at = third + fourth + k * depth
-        gmerge_ref[k * per : (k + 1) * per] = total[:, at : at + depth]
+    total = summed(lambda value: value[:size])
+    small = summed(lambda value: small_value(value[size:]))
+    merge_at = size - gmerge_ref.shape[0]
+    sums = unstacked(total[:merge_at], per)
+    gqkv_ref[...] = sums[:, :third]
+    gout_ref[...] = sums[:, third:]
+    gmerge_ref[...] = total[merge_at:]
     ggain_ref[...] = jnp.concatenate([small[i : i + 1] for i in range(width // LANES)], axis=1)
     for h in range(gscale_ref.shape[0]):
         gscale_ref[h] = small[width // LANES, h]
-    col = lax.axis_index("col")
-
-    def rim(ref):
-        value = ref[:, end:].astype(F32)
-        half = reach // 2
-        return jnp.concatenate([value[:half], value[half:reach]], axis=1)
-
-    left, right = by_side("col", rim(b_ref), rim(d_ref))
-    left = jnp.where(col > 0, left, 0.0)
-    right = jnp.where(col < lax.axis_size("col") - 1, right, 0.0)
-    blank = jnp.zeros((cols - 2 * RADIUS, width), F32)
-    pieces = []
-    for i in range(rows):
-        edge = slice(i * RADIUS, (i + 1) * RADIUS)
-        pieces += [left[edge], blank, right[edge]]
-    grad = grad_ref[...] + jnp.concatenate(pieces, axis=0)
+    blank = jnp.zeros(((rows - RADIUS) * cols, width), F32)
+    above, below = by_side("row", near_ref[...].astype(F32), far_ref[...].astype(F32))
+    grad = grad_ref[...] + jnp.concatenate([above, blank], axis=0)
+    grad = grad + jnp.concatenate([blank, below], axis=0)
     gtok_ref[...] = grad.astype(BF).reshape(rows, cols, width)
 
 
-def plain_sums(sizes, sums, group, small, dm, gx, above, below):
-    rows, cols, width = sizes
-    wide = cols + 2 * SIDE
+def plain_sums(width, sums, group, small, dm):
     sums = sums.astype(F32)
     merge = jnp.dot(group.T, dm, preferred_element_type=F32)
     outs = []
@@ -558,21 +544,14 @@
         part = lax.psum_scatter(part, "row", scatter_dimension=0, tiled=True)
         outs.append(lax.psum_scatter(part, "col", scatter_dimension=1, tiled=True))
     small = lax.psum(small, ("row", "col"))
-    gx = gx.reshape(rows, wide, width)
-    trim = slice(SIDE - EDGE, wide - SIDE + EDGE)
-    gx = gx.at[:RADIUS, trim].add(above.astype(F32).reshape(RADIUS, -1, width))
-    gx = gx.at[rows - RADIUS :, trim].add(below.astype(F32).reshape(RADIUS, -1, width))
-    from_right = shifted(gx[:, :SIDE].astype(BF), "col", -1).astype(F32)
-    from_left = shifted(gx[:, SIDE + cols :].astype(BF), "col", 1).astype(F32)
-    grad = gx[:, SIDE : SIDE + cols].at[:, :SIDE].add(from_left)
-    grad = grad.at[:, cols - SIDE :].add(from_right)
-    return (grad.astype(BF), *outs, small[: width // LANES].reshape(1, width), small[width // LANES])
-
-
-def shifted(value, axis, step):
-    count = lax.axis_size(axis)
-    pairs = [(i, i + step) for i in range(count) if 0 <= i + step < count]
-    return lax.ppermute(value, axis, pairs)
+    return (*outs, small[: width // LANES].reshape(1, width), small[width // LANES])
+
+
+def add_rows(grad, near, far, rows, cols):
+    above, below = by_side("row", near.astype(F32), far.astype(F32))
+    size = RADIUS * cols
+    grad = grad.at[:size].add(above).at[rows * cols - size :].add(below)
+    return grad.astype(BF).reshape(rows, cols, -1)
 
 
 def swapped(near, far, axis):
@@ -613,15 +592,8 @@
         compiler_params=less,
         cost_estimate=pl.CostEstimate(flops=10**10, bytes_accessed=10**5, transcendentals=0),
     )()
-    dm_pair = pl.pallas_call(
-        pair_kernel,
-        out_shape=shape((2 * groups, depth), BF),
-        in_specs=vmem(3),
-        out_specs=vmem(1)[0],
-        compiler_params=less,
-    )(parity, d_merged, swap(d_merged, "row", 1))
-    dm_pairs = [dm_pair] + [swap(dm_pair, "row", 2 * step) for step in range(1, 4)]
-    gathered = len(dm_pairs) * 2 * groups
+    dm = d_merged.reshape(groups, depth)
+    dms = [swap(dm, "row", 2 * step) for step in (3, 2, 1)] + [dm]
     tile = shape((rows * cols, width), F32)
     half = shape((rows * cols, width), BF)
     edges, two_rows, q_norm, q_unit, d_y, d_attn = pl.pallas_call(
@@ -656,7 +628,7 @@
     per = width // n_row
     feats = 4 * width // n_row
     packed = per % 16 == 0 and feats % LANES == 0 and groups == per
-    packed = packed and 2 * rows * RADIUS + 8 == per and width // LANES < 4 and depth // n_col == LANES and n_col == 4 and n_row == 8
+    packed = packed and width // LANES < 4 and feats == LANES and depth // n_col == LANES and n_col == 4 and n_row == 8
     if packed:
         sum_shapes = (
             shape((n_row // 2, per, 4 * width + feats), BF),
@@ -669,7 +641,6 @@
             shape((groups, 4 * width), BF),
         )
     sizes = (rows, cols, width, heads, n_row, n_col)
-    reach = RADIUS * (cols + 2 * EDGE)
     tall = ext_rows * wide
     x, y, d_query, d_kv, grad_out, group, scale_part = pl.pallas_call(
         functools.partial(layer_kernel, sizes),
@@ -702,27 +673,24 @@
         w_qkv,
         w_out,
     )
-    dm_all, *sums = pl.pallas_call(
-        functools.partial(weights_kernel, (rows, cols, width, n_row, len(dm_pairs))),
-        out_shape=(shape((gathered, depth), BF),) + sum_shapes,
-        in_specs=vmem(6 + len(dm_pairs)),
+    dm_core, *sums = pl.pallas_call(
+        functools.partial(weights_kernel, (rows, cols, width, n_row, len(dms))),
+        out_shape=(shape((len(dms) * groups, depth), BF),) + sum_shapes,
+        in_specs=vmem(6 + len(dms)),
         out_specs=tuple(vmem(1 + len(sum_shapes))),
         compiler_params=params,
         cost_estimate=pl.CostEstimate(flops=10**9, bytes_accessed=10**6, transcendentals=0),
-    )(x, d_query, d_kv, grad_out, group, two_rows, *dm_pairs)
-    gx, gx_near, gx_far, small = pl.pallas_call(
+    )(x, d_query, d_kv, grad_out, group, two_rows, *dms)
+    gx, *sides = pl.pallas_call(
         functools.partial(norm_kernel, (rows, cols, width, heads)),
-        out_shape=(
-            shape((rows * wide, width), F32),
-            shape((reach + 8, width), BF),
-            shape((reach, width), BF),
-            shape((8, LANES), F32),
-        ),
+        out_shape=(shape((ext_rows * cols, width), F32), edge, edge, shape((8, LANES), F32)),
         in_specs=vmem(7),
         out_specs=tuple(vmem(4)),
         compiler_params=params,
         cost_estimate=pl.CostEstimate(flops=5 * 10**8, bytes_accessed=10**6, transcendentals=0),
     )(x, d_query, d_kv, scale_part, two_rows, d_y, w_qkv)
+    *sides, small = sides
+    sides = swapped(*sides, "col")
     skip_out, merged = pl.pallas_call(
         output_kernel,
         out_shape=(shape((rows, cols, width), BF), shape((g_rows, g_cols, depth), BF)),
@@ -731,38 +699,44 @@
         compiler_params=less,
         cost_estimate=pl.CostEstimate(flops=10**9, bytes_accessed=10**6, transcendentals=0),
     )(y, group, w_merge)
+    reach = shape((RADIUS * cols, width), BF)
+    side_call = pl.pallas_call(
+        functools.partial(side_kernel, (rows, cols, width)),
+        out_shape=(tile, reach, reach),
+        in_specs=vmem(3),
+        out_specs=tuple(vmem(3)),
+        compiler_params=less,
+    )
     if not packed:
-        above, below = by_side("row", *swapped(gx_near[:reach], gx_far, "row"))
-        grad_tokens, g_qkv, g_out, g_merge, g_gain, g_scale = plain_sums(
-            (rows, cols, width), *sums, small, d_merged.reshape(groups, depth), gx, above, below
-        )
+        grad, *rims = side_call(gx, *sides)
+        grad_tokens = add_rows(grad, *swapped(*rims, "row"), rows, cols)
+        g_qkv, g_out, g_merge, g_gain, g_scale = plain_sums(width, *sums, small, dm)
     else:
-        near, far = swapped(gx_near, gx_far, "row")
         send, *kept = sums
-        block = shape((per, 4 * width + 2 * feats + LANES), BF)
+        block = shape((4 * width // LANES * per + 2 * per + 8, LANES), BF)
         *blocks, own, own_group, small = pl.pallas_call(
             core_sum_kernel,
             out_shape=(block, block, block)
-            + (shape((per, 4 * width), F32), shape((per, 2 * feats), BF), shape((8, LANES), F32)),
+            + (shape((per, 4 * width), F32), shape((2 * per, LANES), BF), shape((8, LANES), F32)),
             in_specs=vmem(5),
             out_specs=tuple(vmem(6)),
             scratch_shapes=[pltpu.VMEM((n_row // 2,) + block.shape, BF)],
             compiler_params=less,
             cost_estimate=pl.CostEstimate(flops=5 * 10**9, bytes_accessed=10**6, transcendentals=0),
-        )(swap(send, "row", 1), *kept, small, near)
+        )(swap(send, "row", 1), *kept, small, swap(small, "row", 1))
         got = [swap(blocks[step - 1], "row", 2 * step) for step in (3, 2, 1)]
-        lanes = 4 * width // n_col + feats // per * (depth // n_col) + LANES
-        *slots, grad = pl.pallas_call(
+        slot = shape((4 * width // n_col // LANES * per + feats + 8, LANES), BF)
+        *slots, gx = pl.pallas_call(
             functools.partial(row_sum_kernel, (rows, cols, width, n_col)),
-            out_shape=tuple([shape((per, lanes), BF)] * n_col)
-            + (shape((rows * cols, width), F32),),
-            in_specs=vmem(10),
+            out_shape=(slot,) * n_col + (shape(gx.shape, F32),),
+            in_specs=vmem(9),
             out_specs=tuple(vmem(n_col + 1)),
-            scratch_shapes=[pltpu.VMEM((n_col, per, lanes), BF)],
+            scratch_shapes=[pltpu.VMEM((n_col,) + slot.shape, BF)],
             compiler_params=less,
-        )(own, own_group, small, *got, dm_all, gx, near, far)
-        got = [slots[0]]
-        got += [swap(slots[step], "col", step) for step in (3, 2, 1)]
+        )(own, own_group, small, *got, dm_core, swap(dm_core, "row", 1), gx)
+        got = [slots[0]] + [swap(slots[step], "col", step) for step in (3, 2, 1)]
+        grad, *rims = side_call(gx, *sides)
+        rims = swapped(*rims, "row")
         g_qkv, g_out, g_merge, g_gain, g_scale, grad_tokens = pl.pallas_call(
             functools.partial(col_sum_kernel, (rows, cols, width)),
             out_shape=(
@@ -773,10 +747,10 @@
                 shape((heads,), F32),
                 shape((rows, cols, width), BF),
             ),
-            in_specs=vmem(5),
+            in_specs=vmem(7),
             out_specs=tuple(vmem(4)) + (pl.BlockSpec(memory_space=pltpu.SMEM), vmem(1)[0]),
             compiler_params=less,
-        )(*got, grad)
+        )(*got, grad, *rims)
     return (
         skip_out,
         merged,

time: 39.8 us -> 37.9 us (0.952)
  waiting for transfers between devices: 11.2 us -> 6.19 us
  starting transfers between devices: 21 us -> 24.1 us
    ppermute x6 -> x8, waiting for transfers between devices: 6.44 us -> 2.51 us  [swapped(): return (lax.ppermute(near, axis, first), lax.ppermute(far, axis, second))]
    ppermute x6 -> x8, starting transfers between devices: 9.35 us -> 11.9 us  [swapped(): return (lax.ppermute(near, axis, first), lax.ppermute(far, axis, second))]
    ppermute x11 -> x12, waiting for transfers between devices: 4.81 us -> 3.68 us  [swap(): return lax.ppermute(value, axis, [(i, i ^ step) for i in range(count)])]
    ppermute x11 -> x12, starting transfers between devices: 11.6 us -> 12.2 us  [swap(): return lax.ppermute(value, axis, [(i, i ^ step) for i in range(count)])]
  transfers between devices with their start and end apart: 17 -> 20, of which waited for: 6 -> 8; matrix products, arithmetic and copies ran while one was open for 0% -> 0% of each run, Pallas kernels for 11% -> 12%
where the time goes in v4:
time: 37.9 us; the launch traced here: 37.8 us
  starting transfers between devices  24.1 us (64%)
  waiting for transfers between devices  6.19 us (16%)
  Pallas kernels  6.01 us (16%)
  between operations  0.86 us (2%)
  local copies, waits for them, and re-layouts  0.63 us (2%)
    ppermute x12, starting transfers between devices, swap(): return lax.ppermute(value, axis, [(i, i ^ step) for i in range(count)])  12.2 us
    ppermute x8, starting transfers between devices, swapped(): return (lax.ppermute(near, axis, first), lax.ppermute(far, axis, second))  11.9 us
    ppermute x12, waiting for transfers between devices, swap(): return lax.ppermute(value, axis, [(i, i ^ step) for i in range(count)])  3.68 us
    ppermute x8, waiting for transfers between devices, swapped(): return (lax.ppermute(near, axis, first), lax.ppermute(far, axis, second))  2.51 us
    pallas_call x1, Pallas kernels, on_device(): pl.pallas_call(functools.partial(layer_kernel, sizes), out_shape=(shape((...  1.97 us
    pallas_call x1, Pallas kernels, on_device(): pl.pallas_call(output_kernel, out_shape=(shape((rows, cols, width), BF),...  0.91 us
    pallas_call x1, Pallas kernels, on_device(): pl.pallas_call(own_kernel, out_shape=(shape((2 * rows * EDGE, width), BF)...  0.79 us
  transfers between devices with their start and end apart: 20, of which 8 were waited for; matrix products, arithmetic and copies ran while one was open for 0% of the time, Pallas kernels for 12%

profile of v4, /device:TPU:0, one launch (start us, length us, event | category | flops | bytes accessed | tf_op | source)
XLA Modules:
  0.0 37.8 jit_solution(7413365709187598072)
XLA Ops:
  0.6 0.0 copy-start.4
  0.6 0.0 copy-start.5
  0.7 0.0 copy-start.3
  0.7 0.0 copy-start.1
  0.7 0.0 copy-start.2
  0.7 0.0 copy-start
  0.7 0.5 %collective-permute-start = (bf16[4,32,256]{2,1,0:T(8,128)(2,1)}, bf16[4,32,256]{2,1,0:T(8,128)(2,1)S(1)}, u32[]{:S(2)}, u32[]{:S(2)}) collective-permute-start(bf16[4,32,256]{2,1,0:T(8,128)(2,1)} %tok_ref.3), channel_id=1, source_target_pairs={{0,4},{8,12},{16,20},{24,28},{4,0},{12,8},{20,16},{28,24},{1,5},{9... | collective-permute-start | bytes 196616 | tf_op jit(solution)/shard_map/ppermute | solution.py:563
  1.2 3.6 %collective-permute-start.1 = (bf16[4,32,256]{2,1,0:T(8,128)(2,1)}, bf16[4,32,256]{2,1,0:T(8,128)(2,1)S(1)}, u32[]{:S(2)}, u32[]{:S(2)}) collective-permute-start(bf16[4,32,256]{2,1,0:T(8,128)(2,1)} %tok_ref.3), channel_id=1, source_target_pairs={{4,8},{12,16},{20,24},{28,0},{8,4},{16,12},{24,20},{0,28},{5,9},{1... | collective-permute-start | bytes 196616 | tf_op jit(solution)/shard_map/ppermute | solution.py:563
  4.8 0.0 copy-start.6
  4.8 0.0 copy-start.7
  4.8 0.0 copy-done.4
  4.8 0.0 copy-done.5
  4.9 0.0 copy-done.3
  4.9 0.0 copy-done.1
  4.9 0.0 copy-done.2
  4.9 0.0 copy-done
  4.9 0.6 %copy-done.6 = f32[256]{0:T(256)S(1)} copy-done((f32[256]{0:T(256)S(1)}, f32[256]{0:T(256)}, u32[]{:S(2)}) %copy-start.6) | copy-done | bytes 1048
  5.5 0.0 copy-done.7
  5.5 0.8 %shard_map.144 = (bf16[32,256]{1,0:T(8,128)(2,1)S(1)}, f32[8,256]{1,0:T(8,128)S(1)}, f32[128,256]{1,0:T(8,128)S(1)}, f32[128,256]{1,0:T(8,128)S(1)}, f32[128,256...) custom-call(bf16[256,256]{1,0:T(8,128)(2,1)S(1)} %get-tuple-element.55.ones_ref, f32[8,128]{1,0:T(8,128)S(1)} %get-tuple-element.56.parity_ref, ...), custom_call_target="tpu_custom_call" | custom-call | flops 1000000000 | bytes 1000000 | tf_op jit(solution)/shard_map/pallas_call | solution.py:599
  6.3 0.0 collective-permute-done.near_ref.row_near_ref
  6.3 0.7 %collective-permute-done.1.far_ref.row_far_ref = bf16[4,32,256]{2,1,0:T(8,128)(2,1)S(1)} collective-permute-done((bf16[4,32,256]{2,1,0:T(8,128)(2,1)}, bf16[4,32,256]{2,1,0:T(8,128)(2,1)S(1)}, u32[]{:S(2)}, u32[]{:S(2)}) %collective-permute-start.1) | collective-permute-done | bytes 65568 | tf_op jit(solution)/shard_map/ppermute | solution.py:563
  7.0 1.8 %collective-permute-start.2 = (bf16[40,256]{1,0:T(8,128)(2,1)S(1)}, bf16[40,256]{1,0:T(8,128)(2,1)S(1)}, u32[]{:S(2)}, u32[]{:S(2)}) collective-permute-start(bf16[40,256]{1,0:T(8,128)(2,1)S(1)} %get-tuple-element.58), channel_id=1, source_target_pairs={{0,1},{2,3},{1,0},{3,2},{4,5},{6,7},{5,4},{7,6},{8,9},{10,11},{9,8... | collective-permute-start | bytes 61448 | tf_op jit(solution)/shard_map/ppermute | solution.py:563
  8.8 2.5 %collective-permute-start.3 = (bf16[40,256]{1,0:T(8,128)(2,1)S(1)}, bf16[40,256]{1,0:T(8,128)(2,1)S(1)}, u32[]{:S(2)}, u32[]{:S(2)}) collective-permute-start(bf16[40,256]{1,0:T(8,128)(2,1)S(1)} %get-tuple-element.59), channel_id=1, source_target_pairs={{1,2},{3,0},{2,1},{0,3},{5,6},{7,4},{6,5},{4,7},{9,10},{11,8},{10,... | collective-permute-start | bytes 61448 | tf_op jit(solution)/shard_map/ppermute | solution.py:563
  11.3 1.7 %collective-permute-start.4 = (bf16[32,512]{1,0:T(8,128)(2,1)S(1)}, bf16[32,512]{1,0:T(8,128)(2,1)S(1)}, u32[]{:S(2)}, u32[]{:S(2)}) collective-permute-start(bf16[32,512]{1,0:T(8,128)(2,1)S(1)} %bitcast.4), channel_id=1, source_target_pairs={{0,24},{4,28},{8,16},{12,20},{16,8},{20,12},{24,0},{28,4},{1,25},{... | collective-permute-start | bytes 98312 | tf_op jit(solution)/shard_map/ppermute | solution.py:568
  13.0 0.3 collective-permute-start.5
  13.3 1.5 %collective-permute-start.6 = (bf16[32,512]{1,0:T(8,128)(2,1)S(1)}, bf16[32,512]{1,0:T(8,128)(2,1)S(1)}, u32[]{:S(2)}, u32[]{:S(2)}) collective-permute-start(bf16[32,512]{1,0:T(8,128)(2,1)S(1)} %bitcast.6), channel_id=1, source_target_pairs={{0,8},{4,12},{8,0},{12,4},{16,24},{20,28},{24,16},{28,20},{1,9},{5... | collective-permute-start | bytes 98312 | tf_op jit(solution)/shard_map/ppermute | solution.py:568
  14.8 0.0 collective-permute-done.2.col_near_ref
  14.8 0.0 collective-permute-done.3.col_far_ref
  14.8 2.0 %shard_map.146 = (f32[480,256]{1,0:T(8,128)S(1)}, bf16[128,256]{1,0:T(8,128)(2,1)S(1)}, bf16[128,256]{1,0:T(8,128)(2,1)S(1)}, bf16[480,512]{1,0:T(8,128)(2,1)S(1...) custom-call(bf16[256,256]{1,0:T(8,128)(2,1)S(1)} %get-tuple-element.55.ones_ref, ...), custom_call_target="tpu_custom_call" | custom-call | flops 4000000000 | bytes 1000000 | tf_op jit(solution)/shard_map/pallas_call | solution.py:645
  16.8 0.0 collective-permute-done.4.refs_0_
  16.8 0.1 collective-permute-done.5.refs_1_
  16.9 0.3 collective-permute-done.6.refs_2_
  17.2 0.6 %shard_map.148 = (bf16[128,512]{1,0:T(8,128)(2,1)S(1)}, bf16[4,32,1152]{2,1,0:T(8,128)(2,1)S(1)}, f32[4,32,1024]{2,1,0:T(8,128)S(1)}, bf16[4,32,128]{2,1,0:T(8,128)(2,1)S(1)}) custom-call(f32[480,256]{1,0:T(8,128)S(1)} %get-tuple-element.69.x_ref, bf16[128,256]{1,0:T(8,128)(2,1)S(1)} %get-tuple-element.70.d_query_ref, ...), custom_call_target="tpu_custom_call" | custom-call | flops 1000000000 | bytes 1000000 | tf_op jit(solution)/shard_map/pallas_call | solution.py:676
  17.8 0.1 collective-permute-start.7
  17.9 0.5 %shard_map.149 = (f32[320,256]{1,0:T(8,128)S(1)}, bf16[40,256]{1,0:T(8,128)(2,1)S(1)}, bf16[40,256]{1,0:T(8,128)(2,1)S(1)}, f32[8,128]{1,0:T(8,128)S(1)}) custom-call(f32[480,256]{1,0:T(8,128)S(1)} %get-tuple-element.69.x_ref, bf16[128,256]{1,0:T(8,128)(2,1)S(1)} %get-tuple-element.70.d_query_ref, bf16[480,512]{1,0:T(8,128)(2,1)S(1)} %get-tuple-element.71.d_kv_ref, ...), custom_call_target="tpu_custom_call" | custom-call | flops 500000000 | bytes 1000000 | tf_op jit(solution)/shard_map/pallas_call | solution.py:684
  18.4 0.6 %collective-permute-start.8 = (f32[8,128]{1,0:T(8,128)S(1)}, f32[8,128]{1,0:T(8,128)S(1)}, u32[]{:S(2)}, u32[]{:S(2)}) collective-permute-start(f32[8,128]{1,0:T(8,128)S(1)} %get-tuple-element.77.small_ref), channel_id=1, source_target_pairs={{0,4},{4,0},{8,12},{12,8},{16,20},{20,16},{24,28},{28,24},{1,5},{5... | collective-permute-start | bytes 12296 | tf_op jit(solution)/shard_map/ppermute | solution.py:568
  19.0 0.1 collective-permute-start.12
  19.1 0.7 %collective-permute-done.8.small_near_ref = f32[8,128]{1,0:T(8,128)S(1)} collective-permute-done((f32[8,128]{1,0:T(8,128)S(1)}, f32[8,128]{1,0:T(8,128)S(1)}, u32[]{:S(2)}, u32[]{:S(2)}) %collective-permute-start.8) | collective-permute-done | bytes 4128 | tf_op jit(solution)/shard_map/ppermute | solution.py:568
  19.8 0.0 collective-permute-done.7.got_ref
  19.8 0.1 shard_map.150
  19.9 2.8 %collective-permute-start.9 = (bf16[328,128]{1,0:T(8,128)(2,1)S(1)}, bf16[328,128]{1,0:T(8,128)(2,1)S(1)}, u32[]{:S(2)}, u32[]{:S(2)}) collective-permute-start(bf16[328,128]{1,0:T(8,128)(2,1)S(1)} %get-tuple-element.81), channel_id=1, source_target_pairs={{0,24},{4,28},{8,16},{12,20},{16,8},{20,12},{24,0},{28,4},{1,25},{... | collective-permute-start | bytes 251912 | tf_op jit(solution)/shard_map/ppermute | solution.py:568
  22.7 0.2 collective-permute-start.10
  22.9 0.5 %collective-permute-start.11 = (bf16[328,128]{1,0:T(8,128)(2,1)S(1)}, bf16[328,128]{1,0:T(8,128)(2,1)S(1)}, u32[]{:S(2)}, u32[]{:S(2)}) collective-permute-start(bf16[328,128]{1,0:T(8,128)(2,1)S(1)} %get-tuple-element.83), channel_id=1, source_target_pairs={{0,8},{4,12},{8,0},{12,4},{16,24},{20,28},{24,16},{28,20},{1,9},{5... | collective-permute-start | bytes 251912 | tf_op jit(solution)/shard_map/ppermute | solution.py:568
  23.5 0.7 %collective-permute-start.16 = (bf16[40,256]{1,0:T(8,128)(2,1)S(1)}, bf16[40,256]{1,0:T(8,128)(2,1)S(1)}, u32[]{:S(2)}, u32[]{:S(2)}) collective-permute-start(bf16[40,256]{1,0:T(8,128)(2,1)S(1)} %get-tuple-element.91), channel_id=1, source_target_pairs={{0,1},{2,3},{1,0},{3,2},{4,5},{6,7},{5,4},{7,6},{8,9},{10,11},{9,8... | collective-permute-start | bytes 61448 | tf_op jit(solution)/shard_map/ppermute | solution.py:563
  24.1 0.0 collective-permute-done.12.refs_7_
  24.1 1.0 %collective-permute-start.17 = (bf16[40,256]{1,0:T(8,128)(2,1)S(1)}, bf16[40,256]{1,0:T(8,128)(2,1)S(1)}, u32[]{:S(2)}, u32[]{:S(2)}) collective-permute-start(bf16[40,256]{1,0:T(8,128)(2,1)S(1)} %get-tuple-element.92), channel_id=1, source_target_pairs={{1,2},{3,0},{2,1},{0,3},{5,6},{7,4},{6,5},{4,7},{9,10},{11,8},{10,... | collective-permute-start | bytes 61448 | tf_op jit(solution)/shard_map/ppermute | solution.py:563
  25.2 0.6 %collective-permute-done.9.refs_3_ = bf16[328,128]{1,0:T(8,128)(2,1)S(1)} collective-permute-done((bf16[328,128]{1,0:T(8,128)(2,1)S(1)}, bf16[328,128]{1,0:T(8,128)(2,1)S(1)}, u32[]{:S(2)}, u32[]{:S(2)}) %collective-permute-start.9) | collective-permute-done | bytes 84000 | tf_op jit(solution)/shard_map/ppermute | solution.py:568
  25.7 1.8 %collective-permute-done.10.refs_4_ = bf16[328,128]{1,0:T(8,128)(2,1)S(1)} collective-permute-done((bf16[328,128]{1,0:T(8,128)(2,1)S(1)}, bf16[328,128]{1,0:T(8,128)(2,1)S(1)}, u32[]{:S(2)}, u32[]{:S(2)}) %collective-permute-start.10) | collective-permute-done | bytes 84000 | tf_op jit(solution)/shard_map/ppermute | solution.py:568
  27.5 0.2 collective-permute-done.11.refs_5_
  27.7 0.3 shard_map.151
  28.0 1.9 %collective-permute-start.13 = (bf16[200,128]{1,0:T(8,128)(2,1)S(1)}, bf16[200,128]{1,0:T(8,128)(2,1)S(1)}, u32[]{:S(2)}, u32[]{:S(2)}) collective-permute-start(bf16[200,128]{1,0:T(8,128)(2,1)S(1)} %get-tuple-element.87), channel_id=1, source_target_pairs={{0,3},{1,2},{2,1},{3,0},{4,7},{5,6},{6,5},{7,4},{8,11},{9,10},{10,... | collective-permute-start | bytes 153608 | tf_op jit(solution)/shard_map/ppermute | solution.py:568
  29.8 0.3 collective-permute-start.14
  30.2 2.3 %collective-permute-start.15 = (bf16[200,128]{1,0:T(8,128)(2,1)S(1)}, bf16[200,128]{1,0:T(8,128)(2,1)S(1)}, u32[]{:S(2)}, u32[]{:S(2)}) collective-permute-start(bf16[200,128]{1,0:T(8,128)(2,1)S(1)} %get-tuple-element.89), channel_id=1, source_target_pairs={{0,1},{1,0},{2,3},{3,2},{4,5},{5,4},{6,7},{7,6},{8,9},{9,8},{10,11... | collective-permute-start | bytes 153608 | tf_op jit(solution)/shard_map/ppermute | solution.py:568
  32.4 0.0 collective-permute-done.16.near_ref
  32.4 0.0 collective-permute-done.17.far_ref
  32.5 0.1 collective-permute-start.18
  32.6 1.8 %collective-permute-start.19 = (bf16[96,256]{1,0:T(8,128)(2,1)S(1)}, bf16[96,256]{1,0:T(8,128)(2,1)S(1)}, u32[]{:S(2)}, u32[]{:S(2)}) collective-permute-start(bf16[96,256]{1,0:T(8,128)(2,1)S(1)} %get-tuple-element.95), channel_id=1, source_target_pairs={{4,8},{12,16},{20,24},{28,0},{8,4},{16,12},{24,20},{0,28},{5,9},{1... | collective-permute-start | bytes 147464 | tf_op jit(solution)/shard_map/ppermute | solution.py:563
  34.3 0.9 %shard_map.147 = (bf16[4,32,256]{2,1,0:T(8,128)(2,1)}, bf16[2,16,512]{2,1,0:T(8,128)(2,1)}) custom-call(bf16[128,256]{1,0:T(8,128)(2,1)S(1)} %get-tuple-element.65.y_ref, bf16[32,1024]{1,0:T(8,128)(2,1)S(1)} %get-tuple-element.66.group_ref, bf16[1024,512]{1,0:T(8,128)(2,1)S(1)} %copy-done), custom_call_target="tpu_custom_call" | custom-call | flops 1000000000 | bytes 1000000 | tf_op jit(solution)/shard_map/pallas_call | solution.py:694
  35.2 0.0 collective-permute-done.18.near_ref
  35.2 1.8 %collective-permute-done.19.far_ref = bf16[96,256]{1,0:T(8,128)(2,1)S(1)} collective-permute-done((bf16[96,256]{1,0:T(8,128)(2,1)S(1)}, bf16[96,256]{1,0:T(8,128)(2,1)S(1)}, u32[]{:S(2)}, u32[]{:S(2)}) %collective-permute-start.19) | collective-permute-done | bytes 49184 | tf_op jit(solution)/shard_map/ppermute | solution.py:563
  37.0 0.0 collective-permute-done.13.d_ref
  37.0 0.0 collective-permute-done.14.c_ref
  37.0 0.0 collective-permute-done.15.b_ref
  37.0 0.7 %shard_map.153 = (f32[32,192]{1,0:T(8,128)}, f32[32,64]{1,0:T(8,128)}, f32[128,128]{1,0:T(8,128)}, f32[1,256]{1,0:T(1,128)}, f32[4]{0:T(128)}, /*index=5*/bf16[4,32,256]{2,1,0:T(8,128)(2,1)}) custom-call(bf16[200,128]{1,0:T(8,128)(2,1)S(1)} %get-tuple-element.86.a_ref, bf16[200,128]{1,0:T(8,128)(2,1)S(1)} %collective-permute-done.13.d_ref, ...), custom_call_target="tpu_custom_call" | custom-call | tf_op jit(solution)/shard_map/pallas_call | solution.py:740
  (3 shorter events, 0.1 us)
Async XLA Ops:
  0.6 4.2 %copy-start.4 = (bf16[4,32,256]{2,1,0:T(8,128)(2,1)S(1)}, bf16[4,32,256]{2,1,0:T(8,128)(2,1)}, u32[]{:S(2)}) copy-start(bf16[4,32,256]{2,1,0:T(8,128)(2,1)} %tok_ref.3) | copy-start | bytes 196612
  0.6 4.2 %copy-start.5 = (bf16[2,16,512]{2,1,0:T(8,128)(2,1)S(1)}, bf16[2,16,512]{2,1,0:T(8,128)(2,1)}, u32[]{:S(2)}) copy-start(bf16[2,16,512]{2,1,0:T(8,128)(2,1)} %dm_ref.1) | copy-start | bytes 98308
  0.7 4.2 %copy-start.3 = (bf16[4,32,256]{2,1,0:T(8,128)(2,1)S(1)}, bf16[4,32,256]{2,1,0:T(8,128)(2,1)}, u32[]{:S(2)}) copy-start(bf16[4,32,256]{2,1,0:T(8,128)(2,1)} %dskip_ref.1) | copy-start | bytes 196612
  0.7 4.2 %copy-start.1 = (bf16[256,768]{1,0:T(8,128)(2,1)S(1)}, bf16[256,768]{1,0:T(8,128)(2,1)}, u32[]{:S(2)}) copy-start(bf16[256,768]{1,0:T(8,128)(2,1)} %wqkv_ref.5) | copy-start | bytes 1179652
  0.7 4.2 %copy-start.2 = (bf16[256,256]{1,0:T(8,128)(2,1)S(1)}, bf16[256,256]{1,0:T(8,128)(2,1)}, u32[]{:S(2)}) copy-start(bf16[256,256]{1,0:T(8,128)(2,1)} %wout_ref.3) | copy-start | bytes 393220
  0.7 4.2 %copy-start = (bf16[1024,512]{1,0:T(8,128)(2,1)S(1)}, bf16[1024,512]{1,0:T(8,128)(2,1)}, u32[]{:S(2)}) copy-start(bf16[1024,512]{1,0:T(8,128)(2,1)} %wmerge_ref.3) | copy-start | bytes 3145732
  0.7 5.6 %collective-permute-start = (bf16[4,32,256]{2,1,0:T(8,128)(2,1)}, bf16[4,32,256]{2,1,0:T(8,128)(2,1)S(1)}, u32[]{:S(2)}, u32[]{:S(2)}) collective-permute-start(bf16[4,32,256]{2,1,0:T(8,128)(2,1)} %tok_ref.3), channel_id=1, source_target_pairs={{0,4},{8,12},{16,20},{24,28},{4,0},{12,8},{20,16},{28,24},{1,5},{9... | collective-permute-start | bytes 196616 | tf_op jit(solution)/shard_map/ppermute | solution.py:563
  1.2 5.8 %collective-permute-start.1 = (bf16[4,32,256]{2,1,0:T(8,128)(2,1)}, bf16[4,32,256]{2,1,0:T(8,128)(2,1)S(1)}, u32[]{:S(2)}, u32[]{:S(2)}) collective-permute-start(bf16[4,32,256]{2,1,0:T(8,128)(2,1)} %tok_ref.3), channel_id=1, source_target_pairs={{4,8},{12,16},{20,24},{28,0},{8,4},{16,12},{24,20},{0,28},{5,9},{1... | collective-permute-start | bytes 196616 | tf_op jit(solution)/shard_map/ppermute | solution.py:563
  4.8 0.7 %copy-start.6 = (f32[256]{0:T(256)S(1)}, f32[256]{0:T(256)}, u32[]{:S(2)}) copy-start(f32[256]{0:T(256)} %param.9) | copy-start | bytes 3076
  4.8 0.7 %copy-start.7 = (f32[4]{0:T(128)S(1)}, f32[4]{0:T(128)}, u32[]{:S(2)}) copy-start(f32[4]{0:T(128)} %param.11) | copy-start | bytes 52
  7.0 7.8 %collective-permute-start.2 = (bf16[40,256]{1,0:T(8,128)(2,1)S(1)}, bf16[40,256]{1,0:T(8,128)(2,1)S(1)}, u32[]{:S(2)}, u32[]{:S(2)}) collective-permute-start(bf16[40,256]{1,0:T(8,128)(2,1)S(1)} %get-tuple-element.58), channel_id=1, source_target_pairs={{0,1},{2,3},{1,0},{3,2},{4,5},{6,7},{5,4},{7,6},{8,9},{10,11},{9,8... | collective-permute-start | bytes 61448 | tf_op jit(solution)/shard_map/ppermute | solution.py:563
  8.8 6.0 %collective-permute-start.3 = (bf16[40,256]{1,0:T(8,128)(2,1)S(1)}, bf16[40,256]{1,0:T(8,128)(2,1)S(1)}, u32[]{:S(2)}, u32[]{:S(2)}) collective-permute-start(bf16[40,256]{1,0:T(8,128)(2,1)S(1)} %get-tuple-element.59), channel_id=1, source_target_pairs={{1,2},{3,0},{2,1},{0,3},{5,6},{7,4},{6,5},{4,7},{9,10},{11,8},{10,... | collective-permute-start | bytes 61448 | tf_op jit(solution)/shard_map/ppermute | solution.py:563
  11.3 5.5 %collective-permute-start.4 = (bf16[32,512]{1,0:T(8,128)(2,1)S(1)}, bf16[32,512]{1,0:T(8,128)(2,1)S(1)}, u32[]{:S(2)}, u32[]{:S(2)}) collective-permute-start(bf16[32,512]{1,0:T(8,128)(2,1)S(1)} %bitcast.4), channel_id=1, source_target_pairs={{0,24},{4,28},{8,16},{12,20},{16,8},{20,12},{24,0},{28,4},{1,25},{... | collective-permute-start | bytes 98312 | tf_op jit(solution)/shard_map/ppermute | solution.py:568
  13.0 3.9 %collective-permute-start.5 = (bf16[32,512]{1,0:T(8,128)(2,1)S(1)}, bf16[32,512]{1,0:T(8,128)(2,1)S(1)}, u32[]{:S(2)}, u32[]{:S(2)}) collective-permute-start(bf16[32,512]{1,0:T(8,128)(2,1)S(1)} %bitcast.5), channel_id=1, source_target_pairs={{0,16},{4,20},{8,24},{12,28},{16,0},{20,4},{24,8},{28,12},{1,17},{... | collective-permute-start | bytes 98312 | tf_op jit(solution)/shard_map/ppermute | solution.py:568
  13.3 3.9 %collective-permute-start.6 = (bf16[32,512]{1,0:T(8,128)(2,1)S(1)}, bf16[32,512]{1,0:T(8,128)(2,1)S(1)}, u32[]{:S(2)}, u32[]{:S(2)}) collective-permute-start(bf16[32,512]{1,0:T(8,128)(2,1)S(1)} %bitcast.6), channel_id=1, source_target_pairs={{0,8},{4,12},{8,0},{12,4},{16,24},{20,28},{24,16},{28,20},{1,9},{5... | collective-permute-start | bytes 98312 | tf_op jit(solution)/shard_map/ppermute | solution.py:568
  17.8 2.0 %collective-permute-start.7 = (bf16[4,32,1152]{2,1,0:T(8,128)(2,1)S(1)}, bf16[4,32,1152]{2,1,0:T(8,128)(2,1)S(1)}, u32[]{:S(2)}, u32[]{:S(2)}) collective-permute-start(bf16[4,32,1152]{2,1,0:T(8,128)(2,1)S(1)} %get-tuple-element.73), channel_id=1, source_target_pairs={{0,4},{4,0},{8,12},{12,8},{16,20},{20,16},{24,28},{28,24},{1,5},{5... | collective-permute-start | bytes 884744 | tf_op jit(solution)/shard_map/ppermute | solution.py:568
  18.4 1.4 %collective-permute-start.8 = (f32[8,128]{1,0:T(8,128)S(1)}, f32[8,128]{1,0:T(8,128)S(1)}, u32[]{:S(2)}, u32[]{:S(2)}) collective-permute-start(f32[8,128]{1,0:T(8,128)S(1)} %get-tuple-element.77.small_ref), channel_id=1, source_target_pairs={{0,4},{4,0},{8,12},{12,8},{16,20},{20,16},{24,28},{28,24},{1,5},{5... | collective-permute-start | bytes 12296 | tf_op jit(solution)/shard_map/ppermute | solution.py:568
  19.0 5.2 %collective-permute-start.12 = (bf16[128,512]{1,0:T(8,128)(2,1)S(1)}, bf16[128,512]{1,0:T(8,128)(2,1)S(1)}, u32[]{:S(2)}, u32[]{:S(2)}) collective-permute-start(bf16[128,512]{1,0:T(8,128)(2,1)S(1)} %get-tuple-element.84.refs_6_), channel_id=1, source_target_pairs={{0,4},{4,0},{8,12},{12,8},{16,20},{20,16},{24,28},{28,24},{1,5},{5... | collective-permute-start | bytes 393224 | tf_op jit(solution)/shard_map/ppermute | solution.py:568
  19.9 5.8 %collective-permute-start.9 = (bf16[328,128]{1,0:T(8,128)(2,1)S(1)}, bf16[328,128]{1,0:T(8,128)(2,1)S(1)}, u32[]{:S(2)}, u32[]{:S(2)}) collective-permute-start(bf16[328,128]{1,0:T(8,128)(2,1)S(1)} %get-tuple-element.81), channel_id=1, source_target_pairs={{0,24},{4,28},{8,16},{12,20},{16,8},{20,12},{24,0},{28,4},{1,25},{... | collective-permute-start | bytes 251912 | tf_op jit(solution)/shard_map/ppermute | solution.py:568
  22.7 4.8 %collective-permute-start.10 = (bf16[328,128]{1,0:T(8,128)(2,1)S(1)}, bf16[328,128]{1,0:T(8,128)(2,1)S(1)}, u32[]{:S(2)}, u32[]{:S(2)}) collective-permute-start(bf16[328,128]{1,0:T(8,128)(2,1)S(1)} %get-tuple-element.82), channel_id=1, source_target_pairs={{0,16},{4,20},{8,24},{12,28},{16,0},{20,4},{24,8},{28,12},{1,17},{... | collective-permute-start | bytes 251912 | tf_op jit(solution)/shard_map/ppermute | solution.py:568
  22.9 4.7 %collective-permute-start.11 = (bf16[328,128]{1,0:T(8,128)(2,1)S(1)}, bf16[328,128]{1,0:T(8,128)(2,1)S(1)}, u32[]{:S(2)}, u32[]{:S(2)}) collective-permute-start(bf16[328,128]{1,0:T(8,128)(2,1)S(1)} %get-tuple-element.83), channel_id=1, source_target_pairs={{0,8},{4,12},{8,0},{12,4},{16,24},{20,28},{24,16},{28,20},{1,9},{5... | collective-permute-start | bytes 251912 | tf_op jit(solution)/shard_map/ppermute | solution.py:568
  23.5 9.0 %collective-permute-start.16 = (bf16[40,256]{1,0:T(8,128)(2,1)S(1)}, bf16[40,256]{1,0:T(8,128)(2,1)S(1)}, u32[]{:S(2)}, u32[]{:S(2)}) collective-permute-start(bf16[40,256]{1,0:T(8,128)(2,1)S(1)} %get-tuple-element.91), channel_id=1, source_target_pairs={{0,1},{2,3},{1,0},{3,2},{4,5},{6,7},{5,4},{7,6},{8,9},{10,11},{9,8... | collective-permute-start | bytes 61448 | tf_op jit(solution)/shard_map/ppermute | solution.py:563
  24.1 8.3 %collective-permute-start.17 = (bf16[40,256]{1,0:T(8,128)(2,1)S(1)}, bf16[40,256]{1,0:T(8,128)(2,1)S(1)}, u32[]{:S(2)}, u32[]{:S(2)}) collective-permute-start(bf16[40,256]{1,0:T(8,128)(2,1)S(1)} %get-tuple-element.92), channel_id=1, source_target_pairs={{1,2},{3,0},{2,1},{0,3},{5,6},{7,4},{6,5},{4,7},{9,10},{11,8},{10,... | collective-permute-start | bytes 61448 | tf_op jit(solution)/shard_map/ppermute | solution.py:563
  28.0 9.1 %collective-permute-start.13 = (bf16[200,128]{1,0:T(8,128)(2,1)S(1)}, bf16[200,128]{1,0:T(8,128)(2,1)S(1)}, u32[]{:S(2)}, u32[]{:S(2)}) collective-permute-start(bf16[200,128]{1,0:T(8,128)(2,1)S(1)} %get-tuple-element.87), channel_id=1, source_target_pairs={{0,3},{1,2},{2,1},{3,0},{4,7},{5,6},{6,5},{7,4},{8,11},{9,10},{10,... | collective-permute-start | bytes 153608 | tf_op jit(solution)/shard_map/ppermute | solution.py:568
  29.8 7.2 %collective-permute-start.14 = (bf16[200,128]{1,0:T(8,128)(2,1)S(1)}, bf16[200,128]{1,0:T(8,128)(2,1)S(1)}, u32[]{:S(2)}, u32[]{:S(2)}) collective-permute-start(bf16[200,128]{1,0:T(8,128)(2,1)S(1)} %get-tuple-element.88), channel_id=1, source_target_pairs={{0,2},{1,3},{2,0},{3,1},{4,6},{5,7},{6,4},{7,5},{8,10},{9,11},{10,... | collective-permute-start | bytes 153608 | tf_op jit(solution)/shard_map/ppermute | solution.py:568
  30.2 6.9 %collective-permute-start.15 = (bf16[200,128]{1,0:T(8,128)(2,1)S(1)}, bf16[200,128]{1,0:T(8,128)(2,1)S(1)}, u32[]{:S(2)}, u32[]{:S(2)}) collective-permute-start(bf16[200,128]{1,0:T(8,128)(2,1)S(1)} %get-tuple-element.89), channel_id=1, source_target_pairs={{0,1},{1,0},{2,3},{3,2},{4,5},{5,4},{6,7},{7,6},{8,9},{9,8},{10,11... | collective-permute-start | bytes 153608 | tf_op jit(solution)/shard_map/ppermute | solution.py:568
  32.5 2.8 %collective-permute-start.18 = (bf16[96,256]{1,0:T(8,128)(2,1)S(1)}, bf16[96,256]{1,0:T(8,128)(2,1)S(1)}, u32[]{:S(2)}, u32[]{:S(2)}) collective-permute-start(bf16[96,256]{1,0:T(8,128)(2,1)S(1)} %get-tuple-element.94), channel_id=1, source_target_pairs={{0,4},{8,12},{16,20},{24,28},{4,0},{12,8},{20,16},{28,24},{1,5},{9... | collective-permute-start | bytes 147464 | tf_op jit(solution)/shard_map/ppermute | solution.py:563
  32.6 4.5 %collective-permute-start.19 = (bf16[96,256]{1,0:T(8,128)(2,1)S(1)}, bf16[96,256]{1,0:T(8,128)(2,1)S(1)}, u32[]{:S(2)}, u32[]{:S(2)}) collective-permute-start(bf16[96,256]{1,0:T(8,128)(2,1)S(1)} %get-tuple-element.95), channel_id=1, source_target_pairs={{4,8},{12,16},{20,24},{28,0},{8,4},{16,12},{24,20},{0,28},{5,9},{1... | collective-permute-start | bytes 147464 | tf_op jit(solution)/shard_map/ppermute | solution.py:563

commit v5 on v4

--- a/solution.py
+++ b/solution.py
@@ -49,8 +49,9 @@
     parity_ref[...] = jnp.concatenate(parts, axis=0)
 
 
-def edge_kernel(edges_ref, near_ref, far_ref, edge_near_ref, edge_far_ref):
+def edge_kernel(edges_ref, far_ref, near_ref, dm_ref, edge_near_ref, edge_far_ref, dm_out_ref):
     rows, cols, width = near_ref.shape
+    dm_out_ref[...] = dm_ref[...]
     up, down = by_side("row", near_ref[...].astype(F32), far_ref[...].astype(F32))
     up = up[rows - RADIUS :]
     down = down[:RADIUS]
@@ -138,10 +139,10 @@
     sizes,
     ones_ref,
     tok_ref,
+    row_far_ref,
     row_near_ref,
-    row_far_ref,
+    col_far_ref,
     col_near_ref,
-    col_far_ref,
     rows_ref,
     q_norm_ref,
     q_unit_ref,
@@ -474,7 +475,7 @@
     return 3 - index
 
 
-def side_kernel(sizes, gx_ref, near_ref, far_ref, grad_ref, row_near_ref, row_far_ref):
+def side_kernel(sizes, gx_ref, far_ref, near_ref, grad_ref, row_near_ref, row_far_ref):
     rows, cols, width = sizes
     ends = lax.axis_index("col")
     left, right = by_side("col", near_ref[...].astype(F32), far_ref[...].astype(F32))
@@ -500,8 +501,8 @@
     c_ref,
     b_ref,
     grad_ref,
+    far_ref,
     near_ref,
-    far_ref,
     gqkv_ref,
     gout_ref,
     gmerge_ref,
@@ -557,9 +558,9 @@
 def swapped(near, far, axis):
     count = lax.axis_size(axis)
     first = [(i, i + 1) for i in range(0, count, 2)]
-    second = [(i, (i + 1) % count) for i in range(1, count, 2)]
+    second = [(i, i + 1) for i in range(1, count - 1, 2)]
     first = first + [(j, i) for i, j in first]
-    second = second + [(j, i) for i, j in second]
+    second = second + [(j, i) for i, j in second] + [(0, 0), (count - 1, count - 1)]
     return (lax.ppermute(near, axis, first), lax.ppermute(far, axis, second))
 
 
@@ -616,13 +617,13 @@
         w_out,
         w_merge,
     )
-    edge_near, edge_far = pl.pallas_call(
+    edge_near, edge_far, dms[0] = pl.pallas_call(
         edge_kernel,
-        out_shape=(edge, edge),
-        in_specs=vmem(3),
-        out_specs=tuple(vmem(2)),
+        out_shape=(edge, edge, shape(dm.shape, BF)),
+        in_specs=vmem(4),
+        out_specs=tuple(vmem(3)),
         compiler_params=less,
-    )(edges, row_near, row_far)
+    )(edges, row_far, row_near, dms[0])
     col_near, col_far = swapped(edge_near, edge_far, "col")
 
     per = width // n_row
@@ -661,10 +662,10 @@
     )(
         ones,
         tokens,
+        row_far,
         row_near,
-        row_far,
+        col_far,
         col_near,
-        col_far,
         two_rows,
         q_norm,
         q_unit,
@@ -708,7 +709,7 @@
         compiler_params=less,
     )
     if not packed:
-        grad, *rims = side_call(gx, *sides)
+        grad, *rims = side_call(gx, *sides[::-1])
         grad_tokens = add_rows(grad, *swapped(*rims, "row"), rows, cols)
         g_qkv, g_out, g_merge, g_gain, g_scale = plain_sums(width, *sums, small, dm)
     else:
@@ -735,7 +736,7 @@
             compiler_params=less,
         )(own, own_group, small, *got, dm_core, swap(dm_core, "row", 1), gx)
         got = [slots[0]] + [swap(slots[step], "col", step) for step in (3, 2, 1)]
-        grad, *rims = side_call(gx, *sides)
+        grad, *rims = side_call(gx, *sides[::-1])
         rims = swapped(*rims, "row")
         g_qkv, g_out, g_merge, g_gain, g_scale, grad_tokens = pl.pallas_call(
             functools.partial(col_sum_kernel, (rows, cols, width)),
@@ -750,7 +751,7 @@
             in_specs=vmem(7),
             out_specs=tuple(vmem(4)) + (pl.BlockSpec(memory_space=pltpu.SMEM), vmem(1)[0]),
             compiler_params=less,
-        )(*got, grad, *rims)
+        )(*got, grad, *rims[::-1])
     return (
         skip_out,
         merged,

time: 37.9 us -> 41.6 us (1.098)
  the two profiles are of different devices: /device:TPU:0 before, /device:TPU:1 now
where the time goes in v5:
time: 41.6 us; the launch traced here: 41.3 us
  starting transfers between devices  27.8 us (67%)
  Pallas kernels  6.01 us (14%)
  waiting for transfers between devices  5.93 us (14%)
  between operations  0.86 us (2%)
  local copies, waits for them, and re-layouts  0.72 us (2%)
    ppermute x8, starting transfers between devices, swapped(): return (lax.ppermute(near, axis, first), lax.ppermute(far, axis, second))  14.8 us
    ppermute x12, starting transfers between devices, swap(): return lax.ppermute(value, axis, [(i, i ^ step) for i in range(count)])  13 us
    ppermute x12, waiting for transfers between devices, swap(): return lax.ppermute(value, axis, [(i, i ^ step) for i in range(count)])  4.87 us
    pallas_call x1, Pallas kernels, on_device(): pl.pallas_call(functools.partial(layer_kernel, sizes), out_shape=(shape((...  1.97 us
    ppermute x8, waiting for transfers between devices, swapped(): return (lax.ppermute(near, axis, first), lax.ppermute(far, axis, second))  1.06 us
    pallas_call x1, Pallas kernels, on_device(): pl.pallas_call(output_kernel, out_shape=(shape((rows, cols, width), BF),...  0.91 us
  transfers between devices with their start and end apart: 20, of which 5 were waited for; matrix products, arithmetic and copies ran while one was open for 0% of the time, Pallas kernels for 11%

profile of v5, /device:TPU:1, one launch (start us, length us, event | category | flops | bytes accessed | tf_op | source)
XLA Modules:
  0.0 41.3 jit_solution(9012138636461446817)
XLA Ops:
  0.6 4.5 %collective-permute-start = (bf16[4,32,256]{2,1,0:T(8,128)(2,1)}, bf16[4,32,256]{2,1,0:T(8,128)(2,1)S(1)}, u32[]{:S(2)}, u32[]{:S(2)}) collective-permute-start(bf16[4,32,256]{2,1,0:T(8,128)(2,1)} %tok_ref.3), channel_id=1, source_target_pairs={{4,8},{12,16},{20,24},{8,4},{16,12},{24,20},{0,0},{28,28},{5,9},{1... | collective-permute-start | bytes 196616 | tf_op jit(solution)/shard_map/ppermute | solution.py:564
  5.2 0.1 collective-permute-start.1
  5.2 0.0 copy-start
  5.2 0.0 copy-start.1
  5.2 0.0 copy-start.2
  5.3 0.0 copy-start.3
  5.3 0.0 copy-start.4
  5.3 0.0 copy-start.5
  5.3 1.1 %collective-permute-start.2 = (bf16[32,512]{1,0:T(8,128)(2,1)}, bf16[32,512]{1,0:T(8,128)(2,1)S(1)}, u32[]{:S(2)}, u32[]{:S(2)}) collective-permute-start(bf16[32,512]{1,0:T(8,128)(2,1)} %bitcast.4), channel_id=1, source_target_pairs={{0,24},{4,28},{8,16},{12,20},{16,8},{20,12},{24,0},{28,4},{1,25},{... | collective-permute-start | bytes 98312 | tf_op jit(solution)/shard_map/ppermute | solution.py:569
  6.4 0.0 copy-start.6
  6.4 0.0 copy-start.7
  6.5 0.0 copy-done
  6.5 0.1 copy-done.1
  6.5 0.0 copy-done.2
  6.6 0.0 copy-done.3
  6.6 0.0 copy-done.4
  6.6 0.0 copy-done.5
  6.6 0.5 %copy-done.6 = f32[256]{0:T(256)S(1)} copy-done((f32[256]{0:T(256)S(1)}, f32[256]{0:T(256)}, u32[]{:S(2)}) %copy-start.6) | copy-done | bytes 1048
  7.2 0.0 copy-done.7
  7.2 0.8 %shard_map.144 = (bf16[32,256]{1,0:T(8,128)(2,1)S(1)}, f32[8,256]{1,0:T(8,128)S(1)}, f32[128,256]{1,0:T(8,128)S(1)}, f32[128,256]{1,0:T(8,128)S(1)}, f32[128,256...) custom-call(bf16[256,256]{1,0:T(8,128)(2,1)S(1)} %get-tuple-element.56.ones_ref, f32[8,128]{1,0:T(8,128)S(1)} %get-tuple-element.57.parity_ref, ...), custom_call_target="tpu_custom_call" | custom-call | flops 1000000000 | bytes 1000000 | tf_op jit(solution)/shard_map/pallas_call | solution.py:600
  8.0 1.3 %collective-permute-done.2.dm_ref = bf16[32,512]{1,0:T(8,128)(2,1)S(1)} collective-permute-done((bf16[32,512]{1,0:T(8,128)(2,1)}, bf16[32,512]{1,0:T(8,128)(2,1)S(1)}, u32[]{:S(2)}, u32[]{:S(2)}) %collective-permute-start.2) | collective-permute-done | bytes 32800 | tf_op jit(solution)/shard_map/ppermute | solution.py:569
  9.2 0.0 collective-permute-done.far_ref.row_far_ref
  9.2 0.0 collective-permute-done.1.near_ref.row_near_ref
  9.3 0.7 %collective-permute-start.3 = (bf16[40,256]{1,0:T(8,128)(2,1)S(1)}, bf16[40,256]{1,0:T(8,128)(2,1)S(1)}, u32[]{:S(2)}, u32[]{:S(2)}) collective-permute-start(bf16[40,256]{1,0:T(8,128)(2,1)S(1)} %get-tuple-element.59), channel_id=1, source_target_pairs={{1,2},{2,1},{0,0},{3,3},{5,6},{6,5},{4,4},{7,7},{9,10},{10,9},{8,8... | collective-permute-start | bytes 61448 | tf_op jit(solution)/shard_map/ppermute | solution.py:564
  9.9 3.9 %collective-permute-start.4 = (bf16[40,256]{1,0:T(8,128)(2,1)S(1)}, bf16[40,256]{1,0:T(8,128)(2,1)S(1)}, u32[]{:S(2)}, u32[]{:S(2)}) collective-permute-start(bf16[40,256]{1,0:T(8,128)(2,1)S(1)} %get-tuple-element.60), channel_id=1, source_target_pairs={{0,1},{2,3},{1,0},{3,2},{4,5},{6,7},{5,4},{7,6},{8,9},{10,11},{9,8... | collective-permute-start | bytes 61448 | tf_op jit(solution)/shard_map/ppermute | solution.py:564
  13.8 1.2 %collective-permute-start.5 = (bf16[32,512]{1,0:T(8,128)(2,1)S(1)}, bf16[32,512]{1,0:T(8,128)(2,1)S(1)}, u32[]{:S(2)}, u32[]{:S(2)}) collective-permute-start(bf16[32,512]{1,0:T(8,128)(2,1)S(1)} %bitcast.5), channel_id=1, source_target_pairs={{0,16},{4,20},{8,24},{12,28},{16,0},{20,4},{24,8},{28,12},{1,17},{... | collective-permute-start | bytes 98312 | tf_op jit(solution)/shard_map/ppermute | solution.py:569
  15.1 0.1 collective-permute-start.6
  15.2 0.0 collective-permute-done.3.col_far_ref
  15.2 0.0 collective-permute-done.4.col_near_ref
  15.2 2.0 %shard_map.146 = (f32[480,256]{1,0:T(8,128)S(1)}, bf16[128,256]{1,0:T(8,128)(2,1)S(1)}, bf16[128,256]{1,0:T(8,128)(2,1)S(1)}, bf16[480,512]{1,0:T(8,128)(2,1)S(1...) custom-call(bf16[256,256]{1,0:T(8,128)(2,1)S(1)} %get-tuple-element.56.ones_ref, ...), custom_call_target="tpu_custom_call" | custom-call | flops 4000000000 | bytes 1000000 | tf_op jit(solution)/shard_map/pallas_call | solution.py:646
  17.2 0.0 collective-permute-done.5.refs_1_
  17.2 0.7 %collective-permute-done.6.refs_2_ = bf16[32,512]{1,0:T(8,128)(2,1)S(1)} collective-permute-done((bf16[32,512]{1,0:T(8,128)(2,1)S(1)}, bf16[32,512]{1,0:T(8,128)(2,1)S(1)}, u32[]{:S(2)}, u32[]{:S(2)}) %collective-permute-start.6) | collective-permute-done | bytes 32800 | tf_op jit(solution)/shard_map/ppermute | solution.py:569
  17.8 0.6 %shard_map.148 = (bf16[128,512]{1,0:T(8,128)(2,1)S(1)}, bf16[4,32,1152]{2,1,0:T(8,128)(2,1)S(1)}, f32[4,32,1024]{2,1,0:T(8,128)S(1)}, bf16[4,32,128]{2,1,0:T(8,128)(2,1)S(1)}) custom-call(f32[480,256]{1,0:T(8,128)S(1)} %get-tuple-element.70.x_ref, bf16[128,256]{1,0:T(8,128)(2,1)S(1)} %get-tuple-element.71.d_query_ref, ...), custom_call_target="tpu_custom_call" | custom-call | flops 1000000000 | bytes 1000000 | tf_op jit(solution)/shard_map/pallas_call | solution.py:677
  18.4 3.7 %collective-permute-start.7 = (bf16[4,32,1152]{2,1,0:T(8,128)(2,1)S(1)}, bf16[4,32,1152]{2,1,0:T(8,128)(2,1)S(1)}, u32[]{:S(2)}, u32[]{:S(2)}) collective-permute-start(bf16[4,32,1152]{2,1,0:T(8,128)(2,1)S(1)} %get-tuple-element.75), channel_id=1, source_target_pairs={{0,4},{4,0},{8,12},{12,8},{16,20},{20,16},{24,28},{28,24},{1,5},{5... | collective-permute-start | bytes 884744 | tf_op jit(solution)/shard_map/ppermute | solution.py:569
  22.1 0.5 %shard_map.149 = (f32[320,256]{1,0:T(8,128)S(1)}, bf16[40,256]{1,0:T(8,128)(2,1)S(1)}, bf16[40,256]{1,0:T(8,128)(2,1)S(1)}, f32[8,128]{1,0:T(8,128)S(1)}) custom-call(f32[480,256]{1,0:T(8,128)S(1)} %get-tuple-element.70.x_ref, bf16[128,256]{1,0:T(8,128)(2,1)S(1)} %get-tuple-element.71.d_query_ref, bf16[480,512]{1,0:T(8,128)(2,1)S(1)} %get-tuple-element.72.d_kv_ref, ...), custom_call_target="tpu_custom_call" | custom-call | flops 500000000 | bytes 1000000 | tf_op jit(solution)/shard_map/pallas_call | solution.py:685
  22.6 0.1 collective-permute-start.8
  22.7 0.5 %collective-permute-start.12 = (bf16[128,512]{1,0:T(8,128)(2,1)S(1)}, bf16[128,512]{1,0:T(8,128)(2,1)S(1)}, u32[]{:S(2)}, u32[]{:S(2)}) collective-permute-start(bf16[128,512]{1,0:T(8,128)(2,1)S(1)} %get-tuple-element.86.refs_6_), channel_id=1, source_target_pairs={{0,4},{4,0},{8,12},{12,8},{16,20},{20,16},{24,28},{28,24},{1,5},{5... | collective-permute-start | bytes 393224 | tf_op jit(solution)/shard_map/ppermute | solution.py:569
  23.2 0.7 %collective-permute-done.8.small_near_ref = f32[8,128]{1,0:T(8,128)S(1)} collective-permute-done((f32[8,128]{1,0:T(8,128)S(1)}, f32[8,128]{1,0:T(8,128)S(1)}, u32[]{:S(2)}, u32[]{:S(2)}) %collective-permute-start.8) | collective-permute-done | bytes 4128 | tf_op jit(solution)/shard_map/ppermute | solution.py:569
  23.9 0.0 collective-permute-done.7.got_ref
  23.9 0.1 shard_map.150
  24.0 1.2 %collective-permute-start.9 = (bf16[328,128]{1,0:T(8,128)(2,1)S(1)}, bf16[328,128]{1,0:T(8,128)(2,1)S(1)}, u32[]{:S(2)}, u32[]{:S(2)}) collective-permute-start(bf16[328,128]{1,0:T(8,128)(2,1)S(1)} %get-tuple-element.83), channel_id=1, source_target_pairs={{0,24},{4,28},{8,16},{12,20},{16,8},{20,12},{24,0},{28,4},{1,25},{... | collective-permute-start | bytes 251912 | tf_op jit(solution)/shard_map/ppermute | solution.py:569
  25.2 0.0 collective-permute-start.10
  25.2 1.5 %collective-permute-start.11 = (bf16[328,128]{1,0:T(8,128)(2,1)S(1)}, bf16[328,128]{1,0:T(8,128)(2,1)S(1)}, u32[]{:S(2)}, u32[]{:S(2)}) collective-permute-start(bf16[328,128]{1,0:T(8,128)(2,1)S(1)} %get-tuple-element.85), channel_id=1, source_target_pairs={{0,8},{4,12},{8,0},{12,4},{16,24},{20,28},{24,16},{28,20},{1,9},{5... | collective-permute-start | bytes 251912 | tf_op jit(solution)/shard_map/ppermute | solution.py:569
  26.7 0.7 %collective-permute-start.16 = (bf16[40,256]{1,0:T(8,128)(2,1)S(1)}, bf16[40,256]{1,0:T(8,128)(2,1)S(1)}, u32[]{:S(2)}, u32[]{:S(2)}) collective-permute-start(bf16[40,256]{1,0:T(8,128)(2,1)S(1)} %get-tuple-element.93), channel_id=1, source_target_pairs={{1,2},{2,1},{0,0},{3,3},{5,6},{6,5},{4,4},{7,7},{9,10},{10,9},{8,8... | collective-permute-start | bytes 61448 | tf_op jit(solution)/shard_map/ppermute | solution.py:564
  27.4 0.0 collective-permute-done.12.refs_7_
  27.4 1.5 %collective-permute-start.17 = (bf16[40,256]{1,0:T(8,128)(2,1)S(1)}, bf16[40,256]{1,0:T(8,128)(2,1)S(1)}, u32[]{:S(2)}, u32[]{:S(2)}) collective-permute-start(bf16[40,256]{1,0:T(8,128)(2,1)S(1)} %get-tuple-element.94), channel_id=1, source_target_pairs={{0,1},{2,3},{1,0},{3,2},{4,5},{6,7},{5,4},{7,6},{8,9},{10,11},{9,8... | collective-permute-start | bytes 61448 | tf_op jit(solution)/shard_map/ppermute | solution.py:564
  28.9 0.0 collective-permute-done.9.refs_3_
  28.9 2.2 %collective-permute-done.10.refs_4_ = bf16[328,128]{1,0:T(8,128)(2,1)S(1)} collective-permute-done((bf16[328,128]{1,0:T(8,128)(2,1)S(1)}, bf16[328,128]{1,0:T(8,128)(2,1)S(1)}, u32[]{:S(2)}, u32[]{:S(2)}) %collective-permute-start.10) | collective-permute-done | bytes 84000 | tf_op jit(solution)/shard_map/ppermute | solution.py:569
  31.2 0.0 collective-permute-done.11.refs_5_
  31.2 0.3 shard_map.151
  31.5 1.1 %collective-permute-start.13 = (bf16[200,128]{1,0:T(8,128)(2,1)S(1)}, bf16[200,128]{1,0:T(8,128)(2,1)S(1)}, u32[]{:S(2)}, u32[]{:S(2)}) collective-permute-start(bf16[200,128]{1,0:T(8,128)(2,1)S(1)} %get-tuple-element.89), channel_id=1, source_target_pairs={{0,3},{1,2},{2,1},{3,0},{4,7},{5,6},{6,5},{7,4},{8,11},{9,10},{10,... | collective-permute-start | bytes 153608 | tf_op jit(solution)/shard_map/ppermute | solution.py:569
  32.6 0.2 collective-permute-start.14
  32.8 2.3 %collective-permute-start.15 = (bf16[200,128]{1,0:T(8,128)(2,1)S(1)}, bf16[200,128]{1,0:T(8,128)(2,1)S(1)}, u32[]{:S(2)}, u32[]{:S(2)}) collective-permute-start(bf16[200,128]{1,0:T(8,128)(2,1)S(1)} %get-tuple-element.91), channel_id=1, source_target_pairs={{0,1},{1,0},{2,3},{3,2},{4,5},{5,4},{6,7},{7,6},{8,9},{9,8},{10,11... | collective-permute-start | bytes 153608 | tf_op jit(solution)/shard_map/ppermute | solution.py:569
  35.1 0.0 collective-permute-done.16.far_ref
  35.1 0.0 collective-permute-done.17.near_ref
  35.1 3.4 %collective-permute-start.18 = (bf16[96,256]{1,0:T(8,128)(2,1)S(1)}, bf16[96,256]{1,0:T(8,128)(2,1)S(1)}, u32[]{:S(2)}, u32[]{:S(2)}) collective-permute-start(bf16[96,256]{1,0:T(8,128)(2,1)S(1)} %get-tuple-element.96), channel_id=1, source_target_pairs={{4,8},{12,16},{20,24},{8,4},{16,12},{24,20},{0,0},{28,28},{5,9},{1... | collective-permute-start | bytes 147464 | tf_op jit(solution)/shard_map/ppermute | solution.py:564
  38.5 0.1 collective-permute-start.19
  38.6 0.9 %shard_map.147 = (bf16[4,32,256]{2,1,0:T(8,128)(2,1)}, bf16[2,16,512]{2,1,0:T(8,128)(2,1)}) custom-call(bf16[128,256]{1,0:T(8,128)(2,1)S(1)} %get-tuple-element.66.y_ref, bf16[32,1024]{1,0:T(8,128)(2,1)S(1)} %get-tuple-element.67.group_ref, bf16[1024,512]{1,0:T(8,128)(2,1)S(1)} %copy-done), custom_call_target="tpu_custom_call" | custom-call | flops 1000000000 | bytes 1000000 | tf_op jit(solution)/shard_map/pallas_call | solution.py:695
  39.5 1.0 %collective-permute-done.18.far_ref = bf16[96,256]{1,0:T(8,128)(2,1)S(1)} collective-permute-done((bf16[96,256]{1,0:T(8,128)(2,1)S(1)}, bf16[96,256]{1,0:T(8,128)(2,1)S(1)}, u32[]{:S(2)}, u32[]{:S(2)}) %collective-permute-start.18) | collective-permute-done | bytes 49184 | tf_op jit(solution)/shard_map/ppermute | solution.py:564
  40.5 0.0 collective-permute-done.19.near_ref
  40.6 0.0 collective-permute-done.13.d_ref
  40.6 0.0 collective-permute-done.14.c_ref
  40.6 0.0 collective-permute-done.15.b_ref
  40.6 0.7 %shard_map.153 = (f32[32,192]{1,0:T(8,128)}, f32[32,64]{1,0:T(8,128)}, f32[128,128]{1,0:T(8,128)}, f32[1,256]{1,0:T(1,128)}, f32[4]{0:T(128)}, /*index=5*/bf16[4,32,256]{2,1,0:T(8,128)(2,1)}) custom-call(bf16[200,128]{1,0:T(8,128)(2,1)S(1)} %get-tuple-element.88.a_ref, bf16[200,128]{1,0:T(8,128)(2,1)S(1)} %collective-permute-done.13.d_ref, ...), custom_call_target="tpu_custom_call" | custom-call | tf_op jit(solution)/shard_map/pallas_call | solution.py:741
  (3 shorter events, 0.1 us)
Async XLA Ops:
  0.6 8.6 %collective-permute-start = (bf16[4,32,256]{2,1,0:T(8,128)(2,1)}, bf16[4,32,256]{2,1,0:T(8,128)(2,1)S(1)}, u32[]{:S(2)}, u32[]{:S(2)}) collective-permute-start(bf16[4,32,256]{2,1,0:T(8,128)(2,1)} %tok_ref.3), channel_id=1, source_target_pairs={{4,8},{12,16},{20,24},{8,4},{16,12},{24,20},{0,0},{28,28},{5,9},{1... | collective-permute-start | bytes 196616 | tf_op jit(solution)/shard_map/ppermute | solution.py:564
  5.2 4.1 %collective-permute-start.1 = (bf16[4,32,256]{2,1,0:T(8,128)(2,1)}, bf16[4,32,256]{2,1,0:T(8,128)(2,1)S(1)}, u32[]{:S(2)}, u32[]{:S(2)}) collective-permute-start(bf16[4,32,256]{2,1,0:T(8,128)(2,1)} %tok_ref.3), channel_id=1, source_target_pairs={{0,4},{8,12},{16,20},{24,28},{4,0},{12,8},{20,16},{28,24},{1,5},{9... | collective-permute-start | bytes 196616 | tf_op jit(solution)/shard_map/ppermute | solution.py:564
  5.2 1.2 %copy-start = (bf16[1024,512]{1,0:T(8,128)(2,1)S(1)}, bf16[1024,512]{1,0:T(8,128)(2,1)}, u32[]{:S(2)}) copy-start(bf16[1024,512]{1,0:T(8,128)(2,1)} %wmerge_ref.3) | copy-start | bytes 3145732
  5.2 1.3 %copy-start.1 = (bf16[256,768]{1,0:T(8,128)(2,1)S(1)}, bf16[256,768]{1,0:T(8,128)(2,1)}, u32[]{:S(2)}) copy-start(bf16[256,768]{1,0:T(8,128)(2,1)} %wqkv_ref.5) | copy-start | bytes 1179652
  5.2 1.3 %copy-start.2 = (bf16[256,256]{1,0:T(8,128)(2,1)S(1)}, bf16[256,256]{1,0:T(8,128)(2,1)}, u32[]{:S(2)}) copy-start(bf16[256,256]{1,0:T(8,128)(2,1)} %wout_ref.3) | copy-start | bytes 393220
  5.3 1.3 %copy-start.3 = (bf16[4,32,256]{2,1,0:T(8,128)(2,1)S(1)}, bf16[4,32,256]{2,1,0:T(8,128)(2,1)}, u32[]{:S(2)}) copy-start(bf16[4,32,256]{2,1,0:T(8,128)(2,1)} %dskip_ref.1) | copy-start | bytes 196612
  5.3 1.3 %copy-start.4 = (bf16[4,32,256]{2,1,0:T(8,128)(2,1)S(1)}, bf16[4,32,256]{2,1,0:T(8,128)(2,1)}, u32[]{:S(2)}) copy-start(bf16[4,32,256]{2,1,0:T(8,128)(2,1)} %tok_ref.3) | copy-start | bytes 196612
  5.3 1.3 %copy-start.5 = (bf16[2,16,512]{2,1,0:T(8,128)(2,1)S(1)}, bf16[2,16,512]{2,1,0:T(8,128)(2,1)}, u32[]{:S(2)}) copy-start(bf16[2,16,512]{2,1,0:T(8,128)(2,1)} %dm_ref.1) | copy-start | bytes 98308
  5.3 3.9 %collective-permute-start.2 = (bf16[32,512]{1,0:T(8,128)(2,1)}, bf16[32,512]{1,0:T(8,128)(2,1)S(1)}, u32[]{:S(2)}, u32[]{:S(2)}) collective-permute-start(bf16[32,512]{1,0:T(8,128)(2,1)} %bitcast.4), channel_id=1, source_target_pairs={{0,24},{4,28},{8,16},{12,20},{16,8},{20,12},{24,0},{28,4},{1,25},{... | collective-permute-start | bytes 98312 | tf_op jit(solution)/shard_map/ppermute | solution.py:569
  6.4 0.7 %copy-start.6 = (f32[256]{0:T(256)S(1)}, f32[256]{0:T(256)}, u32[]{:S(2)}) copy-start(f32[256]{0:T(256)} %param.9) | copy-start | bytes 3076
  6.4 0.7 %copy-start.7 = (f32[4]{0:T(128)S(1)}, f32[4]{0:T(128)}, u32[]{:S(2)}) copy-start(f32[4]{0:T(128)} %param.11) | copy-start | bytes 52
  9.3 5.9 %collective-permute-start.3 = (bf16[40,256]{1,0:T(8,128)(2,1)S(1)}, bf16[40,256]{1,0:T(8,128)(2,1)S(1)}, u32[]{:S(2)}, u32[]{:S(2)}) collective-permute-start(bf16[40,256]{1,0:T(8,128)(2,1)S(1)} %get-tuple-element.59), channel_id=1, source_target_pairs={{1,2},{2,1},{0,0},{3,3},{5,6},{6,5},{4,4},{7,7},{9,10},{10,9},{8,8... | collective-permute-start | bytes 61448 | tf_op jit(solution)/shard_map/ppermute | solution.py:564
  9.9 5.2 %collective-permute-start.4 = (bf16[40,256]{1,0:T(8,128)(2,1)S(1)}, bf16[40,256]{1,0:T(8,128)(2,1)S(1)}, u32[]{:S(2)}, u32[]{:S(2)}) collective-permute-start(bf16[40,256]{1,0:T(8,128)(2,1)S(1)} %get-tuple-element.60), channel_id=1, source_target_pairs={{0,1},{2,3},{1,0},{3,2},{4,5},{6,7},{5,4},{7,6},{8,9},{10,11},{9,8... | collective-permute-start | bytes 61448 | tf_op jit(solution)/shard_map/ppermute | solution.py:564
  13.8 3.3 %collective-permute-start.5 = (bf16[32,512]{1,0:T(8,128)(2,1)S(1)}, bf16[32,512]{1,0:T(8,128)(2,1)S(1)}, u32[]{:S(2)}, u32[]{:S(2)}) collective-permute-start(bf16[32,512]{1,0:T(8,128)(2,1)S(1)} %bitcast.5), channel_id=1, source_target_pairs={{0,16},{4,20},{8,24},{12,28},{16,0},{20,4},{24,8},{28,12},{1,17},{... | collective-permute-start | bytes 98312 | tf_op jit(solution)/shard_map/ppermute | solution.py:569
  15.1 2.8 %collective-permute-start.6 = (bf16[32,512]{1,0:T(8,128)(2,1)S(1)}, bf16[32,512]{1,0:T(8,128)(2,1)S(1)}, u32[]{:S(2)}, u32[]{:S(2)}) collective-permute-start(bf16[32,512]{1,0:T(8,128)(2,1)S(1)} %bitcast.6), channel_id=1, source_target_pairs={{0,8},{4,12},{8,0},{12,4},{16,24},{20,28},{24,16},{28,20},{1,9},{5... | collective-permute-start | bytes 98312 | tf_op jit(solution)/shard_map/ppermute | solution.py:569
  18.4 5.4 %collective-permute-start.7 = (bf16[4,32,1152]{2,1,0:T(8,128)(2,1)S(1)}, bf16[4,32,1152]{2,1,0:T(8,128)(2,1)S(1)}, u32[]{:S(2)}, u32[]{:S(2)}) collective-permute-start(bf16[4,32,1152]{2,1,0:T(8,128)(2,1)S(1)} %get-tuple-element.75), channel_id=1, source_target_pairs={{0,4},{4,0},{8,12},{12,8},{16,20},{20,16},{24,28},{28,24},{1,5},{5... | collective-permute-start | bytes 884744 | tf_op jit(solution)/shard_map/ppermute | solution.py:569
  22.6 1.2 %collective-permute-start.8 = (f32[8,128]{1,0:T(8,128)S(1)}, f32[8,128]{1,0:T(8,128)S(1)}, u32[]{:S(2)}, u32[]{:S(2)}) collective-permute-start(f32[8,128]{1,0:T(8,128)S(1)} %get-tuple-element.79.small_ref), channel_id=1, source_target_pairs={{0,4},{4,0},{8,12},{12,8},{16,20},{20,16},{24,28},{28,24},{1,5},{5... | collective-permute-start | bytes 12296 | tf_op jit(solution)/shard_map/ppermute | solution.py:569
  22.7 4.6 %collective-permute-start.12 = (bf16[128,512]{1,0:T(8,128)(2,1)S(1)}, bf16[128,512]{1,0:T(8,128)(2,1)S(1)}, u32[]{:S(2)}, u32[]{:S(2)}) collective-permute-start(bf16[128,512]{1,0:T(8,128)(2,1)S(1)} %get-tuple-element.86.refs_6_), channel_id=1, source_target_pairs={{0,4},{4,0},{8,12},{12,8},{16,20},{20,16},{24,28},{28,24},{1,5},{5... | collective-permute-start | bytes 393224 | tf_op jit(solution)/shard_map/ppermute | solution.py:569
  24.0 4.9 %collective-permute-start.9 = (bf16[328,128]{1,0:T(8,128)(2,1)S(1)}, bf16[328,128]{1,0:T(8,128)(2,1)S(1)}, u32[]{:S(2)}, u32[]{:S(2)}) collective-permute-start(bf16[328,128]{1,0:T(8,128)(2,1)S(1)} %get-tuple-element.83), channel_id=1, source_target_pairs={{0,24},{4,28},{8,16},{12,20},{16,8},{20,12},{24,0},{28,4},{1,25},{... | collective-permute-start | bytes 251912 | tf_op jit(solution)/shard_map/ppermute | solution.py:569
  25.2 6.0 %collective-permute-start.10 = (bf16[328,128]{1,0:T(8,128)(2,1)S(1)}, bf16[328,128]{1,0:T(8,128)(2,1)S(1)}, u32[]{:S(2)}, u32[]{:S(2)}) collective-permute-start(bf16[328,128]{1,0:T(8,128)(2,1)S(1)} %get-tuple-element.84), channel_id=1, source_target_pairs={{0,16},{4,20},{8,24},{12,28},{16,0},{20,4},{24,8},{28,12},{1,17},{... | collective-permute-start | bytes 251912 | tf_op jit(solution)/shard_map/ppermute | solution.py:569
  25.2 6.0 %collective-permute-start.11 = (bf16[328,128]{1,0:T(8,128)(2,1)S(1)}, bf16[328,128]{1,0:T(8,128)(2,1)S(1)}, u32[]{:S(2)}, u32[]{:S(2)}) collective-permute-start(bf16[328,128]{1,0:T(8,128)(2,1)S(1)} %get-tuple-element.85), channel_id=1, source_target_pairs={{0,8},{4,12},{8,0},{12,4},{16,24},{20,28},{24,16},{28,20},{1,9},{5... | collective-permute-start | bytes 251912 | tf_op jit(solution)/shard_map/ppermute | solution.py:569
  26.7 8.4 %collective-permute-start.16 = (bf16[40,256]{1,0:T(8,128)(2,1)S(1)}, bf16[40,256]{1,0:T(8,128)(2,1)S(1)}, u32[]{:S(2)}, u32[]{:S(2)}) collective-permute-start(bf16[40,256]{1,0:T(8,128)(2,1)S(1)} %get-tuple-element.93), channel_id=1, source_target_pairs={{1,2},{2,1},{0,0},{3,3},{5,6},{6,5},{4,4},{7,7},{9,10},{10,9},{8,8... | collective-permute-start | bytes 61448 | tf_op jit(solution)/shard_map/ppermute | solution.py:564
  27.4 7.7 %collective-permute-start.17 = (bf16[40,256]{1,0:T(8,128)(2,1)S(1)}, bf16[40,256]{1,0:T(8,128)(2,1)S(1)}, u32[]{:S(2)}, u32[]{:S(2)}) collective-permute-start(bf16[40,256]{1,0:T(8,128)(2,1)S(1)} %get-tuple-element.94), channel_id=1, source_target_pairs={{0,1},{2,3},{1,0},{3,2},{4,5},{6,7},{5,4},{7,6},{8,9},{10,11},{9,8... | collective-permute-start | bytes 61448 | tf_op jit(solution)/shard_map/ppermute | solution.py:564
  31.5 9.1 %collective-permute-start.13 = (bf16[200,128]{1,0:T(8,128)(2,1)S(1)}, bf16[200,128]{1,0:T(8,128)(2,1)S(1)}, u32[]{:S(2)}, u32[]{:S(2)}) collective-permute-start(bf16[200,128]{1,0:T(8,128)(2,1)S(1)} %get-tuple-element.89), channel_id=1, source_target_pairs={{0,3},{1,2},{2,1},{3,0},{4,7},{5,6},{6,5},{7,4},{8,11},{9,10},{10,... | collective-permute-start | bytes 153608 | tf_op jit(solution)/shard_map/ppermute | solution.py:569
  32.6 8.0 %collective-permute-start.14 = (bf16[200,128]{1,0:T(8,128)(2,1)S(1)}, bf16[200,128]{1,0:T(8,128)(2,1)S(1)}, u32[]{:S(2)}, u32[]{:S(2)}) collective-permute-start(bf16[200,128]{1,0:T(8,128)(2,1)S(1)} %get-tuple-element.90), channel_id=1, source_target_pairs={{0,2},{1,3},{2,0},{3,1},{4,6},{5,7},{6,4},{7,5},{8,10},{9,11},{10,... | collective-permute-start | bytes 153608 | tf_op jit(solution)/shard_map/ppermute | solution.py:569
  32.8 7.8 %collective-permute-start.15 = (bf16[200,128]{1,0:T(8,128)(2,1)S(1)}, bf16[200,128]{1,0:T(8,128)(2,1)S(1)}, u32[]{:S(2)}, u32[]{:S(2)}) collective-permute-start(bf16[200,128]{1,0:T(8,128)(2,1)S(1)} %get-tuple-element.91), channel_id=1, source_target_pairs={{0,1},{1,0},{2,3},{3,2},{4,5},{5,4},{6,7},{7,6},{8,9},{9,8},{10,11... | collective-permute-start | bytes 153608 | tf_op jit(solution)/shard_map/ppermute | solution.py:569
  35.1 5.4 %collective-permute-start.18 = (bf16[96,256]{1,0:T(8,128)(2,1)S(1)}, bf16[96,256]{1,0:T(8,128)(2,1)S(1)}, u32[]{:S(2)}, u32[]{:S(2)}) collective-permute-start(bf16[96,256]{1,0:T(8,128)(2,1)S(1)} %get-tuple-element.96), channel_id=1, source_target_pairs={{4,8},{12,16},{20,24},{8,4},{16,12},{24,20},{0,0},{28,28},{5,9},{1... | collective-permute-start | bytes 147464 | tf_op jit(solution)/shard_map/ppermute | solution.py:564
  38.5 2.0 %collective-permute-start.19 = (bf16[96,256]{1,0:T(8,128)(2,1)S(1)}, bf16[96,256]{1,0:T(8,128)(2,1)S(1)}, u32[]{:S(2)}, u32[]{:S(2)}) collective-permute-start(bf16[96,256]{1,0:T(8,128)(2,1)S(1)} %get-tuple-element.97), channel_id=1, source_target_pairs={{0,4},{8,12},{16,20},{24,28},{4,0},{12,8},{20,16},{28,24},{1,5},{9... | collective-permute-start | bytes 147464 | tf_op jit(solution)/shard_map/ppermute | solution.py:564

commit v6 on v4

--- a/solution.py
+++ b/solution.py
@@ -49,8 +49,12 @@
     parity_ref[...] = jnp.concatenate(parts, axis=0)
 
 
-def edge_kernel(edges_ref, near_ref, far_ref, edge_near_ref, edge_far_ref):
+def edge_kernel(
+    edges_ref, far_ref, near_ref, dm_ref, dm_next_ref, edge_near_ref, edge_far_ref, dm_pair_ref
+):
     rows, cols, width = near_ref.shape
+    size = dm_next_ref.shape[0]
+    dm_pair_ref[...] = jnp.concatenate([dm_ref[...].reshape(size, -1), dm_next_ref[...]], axis=0)
     up, down = by_side("row", near_ref[...].astype(F32), far_ref[...].astype(F32))
     up = up[rows - RADIUS :]
     down = down[:RADIUS]
@@ -138,8 +142,8 @@
     sizes,
     ones_ref,
     tok_ref,
+    row_far_ref,
     row_near_ref,
-    row_far_ref,
     col_near_ref,
     col_far_ref,
     rows_ref,
@@ -500,8 +504,8 @@
     c_ref,
     b_ref,
     grad_ref,
+    far_ref,
     near_ref,
-    far_ref,
     gqkv_ref,
     gout_ref,
     gmerge_ref,
@@ -593,7 +597,6 @@
         cost_estimate=pl.CostEstimate(flops=10**10, bytes_accessed=10**5, transcendentals=0),
     )()
     dm = d_merged.reshape(groups, depth)
-    dms = [swap(dm, "row", 2 * step) for step in (3, 2, 1)] + [dm]
     tile = shape((rows * cols, width), F32)
     half = shape((rows * cols, width), BF)
     edges, two_rows, q_norm, q_unit, d_y, d_attn = pl.pallas_call(
@@ -616,13 +619,14 @@
         w_out,
         w_merge,
     )
-    edge_near, edge_far = pl.pallas_call(
+    edge_near, edge_far, dm_pair = pl.pallas_call(
         edge_kernel,
-        out_shape=(edge, edge),
-        in_specs=vmem(3),
-        out_specs=tuple(vmem(2)),
+        out_shape=(edge, edge, shape((2 * groups, depth), BF)),
+        in_specs=vmem(5),
+        out_specs=tuple(vmem(3)),
         compiler_params=less,
-    )(edges, row_near, row_far)
+    )(edges, row_far, row_near, d_merged, swap(dm, "row", 2))
+    dms = [swap(dm_pair, "row", 4), dm_pair]
     col_near, col_far = swapped(edge_near, edge_far, "col")
 
     per = width // n_row
@@ -661,8 +665,8 @@
     )(
         ones,
         tokens,
+        row_far,
         row_near,
-        row_far,
         col_near,
         col_far,
         two_rows,
@@ -675,7 +679,7 @@
     )
     dm_core, *sums = pl.pallas_call(
         functools.partial(weights_kernel, (rows, cols, width, n_row, len(dms))),
-        out_shape=(shape((len(dms) * groups, depth), BF),) + sum_shapes,
+        out_shape=(shape((2 * len(dms) * groups, depth), BF),) + sum_shapes,
         in_specs=vmem(6 + len(dms)),
         out_specs=tuple(vmem(1 + len(sum_shapes))),
         compiler_params=params,
@@ -750,7 +754,7 @@
             in_specs=vmem(7),
             out_specs=tuple(vmem(4)) + (pl.BlockSpec(memory_space=pltpu.SMEM), vmem(1)[0]),
             compiler_params=less,
-        )(*got, grad, *rims)
+        )(*got, grad, *rims[::-1])
     return (
         skip_out,
         merged,

time: 37.9 us -> 37.9 us (level)
  starting transfers between devices: 24.1 us -> 22.6 us
  waiting for transfers between devices: 6.19 us -> 7.69 us
    ppermute x8, waiting for transfers between devices: 2.51 us -> 4.07 us  [swapped(): return (lax.ppermute(near, axis, first), lax.ppermute(far, axis, second))]
    ppermute x12 -> x11, starting transfers between devices: 12.2 us -> 11.2 us  [swap(): return lax.ppermute(value, axis, [(i, i ^ step) for i in range(count)])]
    ppermute x8, starting transfers between devices: 11.9 us -> 11.4 us  [swapped(): return (lax.ppermute(near, axis, first), lax.ppermute(far, axis, second))]
    ppermute x12 -> x11, waiting for transfers between devices: 3.68 us -> 3.62 us  [swap(): return lax.ppermute(value, axis, [(i, i ^ step) for i in range(count)])]
  transfers between devices with their start and end apart: 20 -> 19, of which waited for: 8 -> 5; matrix products, arithmetic and copies ran while one was open for 0% -> 0% of each run, Pallas kernels for 12% -> 12%
where the time goes in v6:
time: 37.9 us; the launch traced here: 37.8 us
  starting transfers between devices  22.6 us (60%)
  waiting for transfers between devices  7.69 us (20%)
  Pallas kernels  6.02 us (16%)
  between operations  0.83 us (2%)
  local copies, waits for them, and re-layouts  0.64 us (2%)
    ppermute x8, starting transfers between devices, swapped(): return (lax.ppermute(near, axis, first), lax.ppermute(far, axis, second))  11.4 us
    ppermute x11, starting transfers between devices, swap(): return lax.ppermute(value, axis, [(i, i ^ step) for i in range(count)])  11.2 us
    ppermute x8, waiting for transfers between devices, swapped(): return (lax.ppermute(near, axis, first), lax.ppermute(far, axis, second))  4.07 us
    ppermute x11, waiting for transfers between devices, swap(): return lax.ppermute(value, axis, [(i, i ^ step) for i in range(count)])  3.62 us
    pallas_call x1, Pallas kernels, on_device(): pl.pallas_call(functools.partial(layer_kernel, sizes), out_shape=(shape((...  1.96 us
    pallas_call x1, Pallas kernels, on_device(): pl.pallas_call(output_kernel, out_shape=(shape((rows, cols, width), BF),...  0.91 us
    pallas_call x1, Pallas kernels, on_device(): pl.pallas_call(own_kernel, out_shape=(shape((2 * rows * EDGE, width), BF)...  0.79 us
  transfers between devices with their start and end apart: 19, of which 5 were waited for; matrix products, arithmetic and copies ran while one was open for 0% of the time, Pallas kernels for 12%

profile of v6, /device:TPU:0, one launch (start us, length us, event | category | flops | bytes accessed | tf_op | source)
XLA Modules:
  0.0 37.8 jit_solution(17511642549283435482)
XLA Ops:
  0.6 3.4 %collective-permute-start = (bf16[4,32,256]{2,1,0:T(8,128)(2,1)}, bf16[4,32,256]{2,1,0:T(8,128)(2,1)S(1)}, u32[]{:S(2)}, u32[]{:S(2)}) collective-permute-start(bf16[4,32,256]{2,1,0:T(8,128)(2,1)} %tok_ref.3), channel_id=1, source_target_pairs={{4,8},{12,16},{20,24},{28,0},{8,4},{16,12},{24,20},{0,28},{5,9},{1... | collective-permute-start | bytes 196616 | tf_op jit(solution)/shard_map/ppermute | solution.py:567
  4.0 0.0 collective-permute-start.1
  4.0 0.0 copy-start
  4.0 0.0 copy-start.1
  4.0 0.0 copy-start.2
  4.0 0.0 copy-start.3
  4.1 0.0 copy-start.4
  4.1 0.0 copy-start.5
  4.1 1.3 %collective-permute-start.2 = (bf16[32,512]{1,0:T(8,128)(2,1)}, bf16[32,512]{1,0:T(8,128)(2,1)S(1)}, u32[]{:S(2)}, u32[]{:S(2)}) collective-permute-start(bf16[32,512]{1,0:T(8,128)(2,1)} %bitcast.4), channel_id=1, source_target_pairs={{0,8},{4,12},{8,0},{12,4},{16,24},{20,28},{24,16},{28,20},{1,9},{5... | collective-permute-start | bytes 98312 | tf_op jit(solution)/shard_map/ppermute | solution.py:572
  5.4 0.0 copy-start.6
  5.4 0.0 copy-start.7
  5.4 0.0 copy-done
  5.4 0.0 copy-done.1
  5.4 0.0 copy-done.2
  5.4 0.0 copy-done.3
  5.4 0.0 copy-done.4
  5.5 0.0 copy-done.5
  5.5 0.6 %copy-done.6 = f32[256]{0:T(256)S(1)} copy-done((f32[256]{0:T(256)S(1)}, f32[256]{0:T(256)}, u32[]{:S(2)}) %copy-start.6) | copy-done | bytes 1048
  6.1 0.0 copy-done.7
  6.1 0.8 %shard_map.144 = (bf16[32,256]{1,0:T(8,128)(2,1)S(1)}, f32[8,256]{1,0:T(8,128)S(1)}, f32[128,256]{1,0:T(8,128)S(1)}, f32[128,256]{1,0:T(8,128)S(1)}, f32[128,256...) custom-call(bf16[256,256]{1,0:T(8,128)(2,1)S(1)} %get-tuple-element.56.ones_ref, f32[8,128]{1,0:T(8,128)S(1)} %get-tuple-element.57.parity_ref, ...), custom_call_target="tpu_custom_call" | custom-call | flops 1000000000 | bytes 1000000 | tf_op jit(solution)/shard_map/pallas_call | solution.py:602
  6.9 1.4 %collective-permute-done.2.dm_next_ref = bf16[32,512]{1,0:T(8,128)(2,1)S(1)} collective-permute-done((bf16[32,512]{1,0:T(8,128)(2,1)}, bf16[32,512]{1,0:T(8,128)(2,1)S(1)}, u32[]{:S(2)}, u32[]{:S(2)}) %collective-permute-start.2) | collective-permute-done | bytes 32800 | tf_op jit(solution)/shard_map/ppermute | solution.py:572
  8.3 0.0 collective-permute-done.far_ref.row_far_ref
  8.3 0.0 collective-permute-done.1.near_ref.row_near_ref
  8.3 1.6 %collective-permute-start.3 = (bf16[40,256]{1,0:T(8,128)(2,1)S(1)}, bf16[40,256]{1,0:T(8,128)(2,1)S(1)}, u32[]{:S(2)}, u32[]{:S(2)}) collective-permute-start(bf16[40,256]{1,0:T(8,128)(2,1)S(1)} %get-tuple-element.59), channel_id=1, source_target_pairs={{0,1},{2,3},{1,0},{3,2},{4,5},{6,7},{5,4},{7,6},{8,9},{10,11},{9,8... | collective-permute-start | bytes 61448 | tf_op jit(solution)/shard_map/ppermute | solution.py:567
  9.9 2.5 %collective-permute-start.4 = (bf16[40,256]{1,0:T(8,128)(2,1)S(1)}, bf16[40,256]{1,0:T(8,128)(2,1)S(1)}, u32[]{:S(2)}, u32[]{:S(2)}) collective-permute-start(bf16[40,256]{1,0:T(8,128)(2,1)S(1)} %get-tuple-element.60), channel_id=1, source_target_pairs={{1,2},{3,0},{2,1},{0,3},{5,6},{7,4},{6,5},{4,7},{9,10},{11,8},{10,... | collective-permute-start | bytes 61448 | tf_op jit(solution)/shard_map/ppermute | solution.py:567
  12.4 1.2 %collective-permute-start.5 = (bf16[64,512]{1,0:T(8,128)(2,1)S(1)}, bf16[64,512]{1,0:T(8,128)(2,1)S(1)}, u32[]{:S(2)}, u32[]{:S(2)}) collective-permute-start(bf16[64,512]{1,0:T(8,128)(2,1)S(1)} %get-tuple-element.74.refs_1_), channel_id=1, source_target_pairs={{0,16},{4,20},{8,24},{12,28},{16,0},{20,4},{24,8},{28,12},{1,17},{... | collective-permute-start | bytes 196616 | tf_op jit(solution)/shard_map/ppermute | solution.py:572
  13.7 0.0 collective-permute-done.3.col_near_ref
  13.7 1.9 %collective-permute-done.4.col_far_ref = bf16[40,256]{1,0:T(8,128)(2,1)S(1)} collective-permute-done((bf16[40,256]{1,0:T(8,128)(2,1)S(1)}, bf16[40,256]{1,0:T(8,128)(2,1)S(1)}, u32[]{:S(2)}, u32[]{:S(2)}) %collective-permute-start.4) | collective-permute-done | bytes 20512 | tf_op jit(solution)/shard_map/ppermute | solution.py:567
  15.5 2.0 %shard_map.146 = (f32[480,256]{1,0:T(8,128)S(1)}, bf16[128,256]{1,0:T(8,128)(2,1)S(1)}, bf16[128,256]{1,0:T(8,128)(2,1)S(1)}, bf16[480,512]{1,0:T(8,128)(2,1)S(1...) custom-call(bf16[256,256]{1,0:T(8,128)(2,1)S(1)} %get-tuple-element.56.ones_ref, ...), custom_call_target="tpu_custom_call" | custom-call | flops 4000000000 | bytes 1000000 | tf_op jit(solution)/shard_map/pallas_call | solution.py:649
  17.5 0.0 collective-permute-done.5.refs_0_
  17.5 0.6 %shard_map.148 = (bf16[128,512]{1,0:T(8,128)(2,1)S(1)}, bf16[4,32,1152]{2,1,0:T(8,128)(2,1)S(1)}, f32[4,32,1024]{2,1,0:T(8,128)S(1)}, bf16[4,32,128]{2,1,0:T(8,128)(2,1)S(1)}) custom-call(f32[480,256]{1,0:T(8,128)S(1)} %get-tuple-element.70.x_ref, bf16[128,256]{1,0:T(8,128)(2,1)S(1)} %get-tuple-element.71.d_query_ref, ...), custom_call_target="tpu_custom_call" | custom-call | flops 1000000000 | bytes 1000000 | tf_op jit(solution)/shard_map/pallas_call | solution.py:680
  18.1 0.1 collective-permute-start.6
  18.2 0.5 %shard_map.149 = (f32[320,256]{1,0:T(8,128)S(1)}, bf16[40,256]{1,0:T(8,128)(2,1)S(1)}, bf16[40,256]{1,0:T(8,128)(2,1)S(1)}, f32[8,128]{1,0:T(8,128)S(1)}) custom-call(f32[480,256]{1,0:T(8,128)S(1)} %get-tuple-element.70.x_ref, bf16[128,256]{1,0:T(8,128)(2,1)S(1)} %get-tuple-element.71.d_query_ref, bf16[480,512]{1,0:T(8,128)(2,1)S(1)} %get-tuple-element.72.d_kv_ref, ...), custom_call_target="tpu_custom_call" | custom-call | flops 500000000 | bytes 1000000 | tf_op jit(solution)/shard_map/pallas_call | solution.py:688
  18.7 0.6 %collective-permute-start.7 = (f32[8,128]{1,0:T(8,128)S(1)}, f32[8,128]{1,0:T(8,128)S(1)}, u32[]{:S(2)}, u32[]{:S(2)}) collective-permute-start(f32[8,128]{1,0:T(8,128)S(1)} %get-tuple-element.79.small_ref), channel_id=1, source_target_pairs={{0,4},{4,0},{8,12},{12,8},{16,20},{20,16},{24,28},{28,24},{1,5},{5... | collective-permute-start | bytes 12296 | tf_op jit(solution)/shard_map/ppermute | solution.py:572
  19.3 0.1 collective-permute-start.11
  19.4 0.7 %collective-permute-done.7.small_near_ref = f32[8,128]{1,0:T(8,128)S(1)} collective-permute-done((f32[8,128]{1,0:T(8,128)S(1)}, f32[8,128]{1,0:T(8,128)S(1)}, u32[]{:S(2)}, u32[]{:S(2)}) %collective-permute-start.7) | collective-permute-done | bytes 4128 | tf_op jit(solution)/shard_map/ppermute | solution.py:572
  20.1 0.0 collective-permute-done.6.got_ref
  20.1 0.1 shard_map.150
  20.2 1.6 %collective-permute-start.8 = (bf16[328,128]{1,0:T(8,128)(2,1)S(1)}, bf16[328,128]{1,0:T(8,128)(2,1)S(1)}, u32[]{:S(2)}, u32[]{:S(2)}) collective-permute-start(bf16[328,128]{1,0:T(8,128)(2,1)S(1)} %get-tuple-element.83), channel_id=1, source_target_pairs={{0,24},{4,28},{8,16},{12,20},{16,8},{20,12},{24,0},{28,4},{1,25},{... | collective-permute-start | bytes 251912 | tf_op jit(solution)/shard_map/ppermute | solution.py:572
  21.8 1.1 %collective-permute-start.9 = (bf16[328,128]{1,0:T(8,128)(2,1)S(1)}, bf16[328,128]{1,0:T(8,128)(2,1)S(1)}, u32[]{:S(2)}, u32[]{:S(2)}) collective-permute-start(bf16[328,128]{1,0:T(8,128)(2,1)S(1)} %get-tuple-element.84), channel_id=1, source_target_pairs={{0,16},{4,20},{8,24},{12,28},{16,0},{20,4},{24,8},{28,12},{1,17},{... | collective-permute-start | bytes 251912 | tf_op jit(solution)/shard_map/ppermute | solution.py:572
  22.9 0.8 %collective-permute-start.10 = (bf16[328,128]{1,0:T(8,128)(2,1)S(1)}, bf16[328,128]{1,0:T(8,128)(2,1)S(1)}, u32[]{:S(2)}, u32[]{:S(2)}) collective-permute-start(bf16[328,128]{1,0:T(8,128)(2,1)S(1)} %get-tuple-element.85), channel_id=1, source_target_pairs={{0,8},{4,12},{8,0},{12,4},{16,24},{20,28},{24,16},{28,20},{1,9},{5... | collective-permute-start | bytes 251912 | tf_op jit(solution)/shard_map/ppermute | solution.py:572
  23.8 0.0 collective-permute-start.15
  23.8 0.0 collective-permute-done.11.refs_7_
  23.8 2.5 %collective-permute-start.16 = (bf16[40,256]{1,0:T(8,128)(2,1)S(1)}, bf16[40,256]{1,0:T(8,128)(2,1)S(1)}, u32[]{:S(2)}, u32[]{:S(2)}) collective-permute-start(bf16[40,256]{1,0:T(8,128)(2,1)S(1)} %get-tuple-element.94), channel_id=1, source_target_pairs={{1,2},{3,0},{2,1},{0,3},{5,6},{7,4},{6,5},{4,7},{9,10},{11,8},{10,... | collective-permute-start | bytes 61448 | tf_op jit(solution)/shard_map/ppermute | solution.py:567
  26.2 0.0 collective-permute-done.8.refs_3_
  26.2 1.5 %collective-permute-done.9.refs_4_ = bf16[328,128]{1,0:T(8,128)(2,1)S(1)} collective-permute-done((bf16[328,128]{1,0:T(8,128)(2,1)S(1)}, bf16[328,128]{1,0:T(8,128)(2,1)S(1)}, u32[]{:S(2)}, u32[]{:S(2)}) %collective-permute-start.9) | collective-permute-done | bytes 84000 | tf_op jit(solution)/shard_map/ppermute | solution.py:572
  27.7 0.0 collective-permute-done.10.refs_5_
  27.7 0.3 shard_map.151
  28.0 2.5 %collective-permute-start.12 = (bf16[200,128]{1,0:T(8,128)(2,1)S(1)}, bf16[200,128]{1,0:T(8,128)(2,1)S(1)}, u32[]{:S(2)}, u32[]{:S(2)}) collective-permute-start(bf16[200,128]{1,0:T(8,128)(2,1)S(1)} %get-tuple-element.89), channel_id=1, source_target_pairs={{0,3},{1,2},{2,1},{3,0},{4,7},{5,6},{6,5},{7,4},{8,11},{9,10},{10,... | collective-permute-start | bytes 153608 | tf_op jit(solution)/shard_map/ppermute | solution.py:572
  30.5 0.0 collective-permute-start.13
  30.5 1.9 %collective-permute-start.14 = (bf16[200,128]{1,0:T(8,128)(2,1)S(1)}, bf16[200,128]{1,0:T(8,128)(2,1)S(1)}, u32[]{:S(2)}, u32[]{:S(2)}) collective-permute-start(bf16[200,128]{1,0:T(8,128)(2,1)S(1)} %get-tuple-element.91), channel_id=1, source_target_pairs={{0,1},{1,0},{2,3},{3,2},{4,5},{5,4},{6,7},{7,6},{8,9},{9,8},{10,11... | collective-permute-start | bytes 153608 | tf_op jit(solution)/shard_map/ppermute | solution.py:572
  32.5 0.0 collective-permute-done.15.near_ref
  32.5 0.0 collective-permute-done.16.far_ref
  32.5 0.4 %collective-permute-start.17 = (bf16[96,256]{1,0:T(8,128)(2,1)S(1)}, bf16[96,256]{1,0:T(8,128)(2,1)S(1)}, u32[]{:S(2)}, u32[]{:S(2)}) collective-permute-start(bf16[96,256]{1,0:T(8,128)(2,1)S(1)} %get-tuple-element.96), channel_id=1, source_target_pairs={{4,8},{12,16},{20,24},{28,0},{8,4},{16,12},{24,20},{0,28},{5,9},{1... | collective-permute-start | bytes 147464 | tf_op jit(solution)/shard_map/ppermute | solution.py:567
  32.9 1.0 %collective-permute-start.18 = (bf16[96,256]{1,0:T(8,128)(2,1)S(1)}, bf16[96,256]{1,0:T(8,128)(2,1)S(1)}, u32[]{:S(2)}, u32[]{:S(2)}) collective-permute-start(bf16[96,256]{1,0:T(8,128)(2,1)S(1)} %get-tuple-element.97), channel_id=1, source_target_pairs={{0,4},{8,12},{16,20},{24,28},{4,0},{12,8},{20,16},{28,24},{1,5},{9... | collective-permute-start | bytes 147464 | tf_op jit(solution)/shard_map/ppermute | solution.py:567
  33.9 0.9 %shard_map.147 = (bf16[4,32,256]{2,1,0:T(8,128)(2,1)}, bf16[2,16,512]{2,1,0:T(8,128)(2,1)}) custom-call(bf16[128,256]{1,0:T(8,128)(2,1)S(1)} %get-tuple-element.66.y_ref, bf16[32,1024]{1,0:T(8,128)(2,1)S(1)} %get-tuple-element.67.group_ref, bf16[1024,512]{1,0:T(8,128)(2,1)S(1)} %copy-done.1), custom_call_target="tpu_custom_call" | custom-call | flops 1000000000 | bytes 1000000 | tf_op jit(solution)/shard_map/pallas_call | solution.py:698
  34.8 2.2 %collective-permute-done.17.far_ref = bf16[96,256]{1,0:T(8,128)(2,1)S(1)} collective-permute-done((bf16[96,256]{1,0:T(8,128)(2,1)S(1)}, bf16[96,256]{1,0:T(8,128)(2,1)S(1)}, u32[]{:S(2)}, u32[]{:S(2)}) %collective-permute-start.17) | collective-permute-done | bytes 49184 | tf_op jit(solution)/shard_map/ppermute | solution.py:567
  37.0 0.0 collective-permute-done.18.near_ref
  37.0 0.0 collective-permute-done.12.d_ref
  37.0 0.0 collective-permute-done.13.c_ref
  37.0 0.0 collective-permute-done.14.b_ref
  37.0 0.7 %shard_map.153 = (f32[32,192]{1,0:T(8,128)}, f32[32,64]{1,0:T(8,128)}, f32[128,128]{1,0:T(8,128)}, f32[1,256]{1,0:T(1,128)}, f32[4]{0:T(128)}, /*index=5*/bf16[4,32,256]{2,1,0:T(8,128)(2,1)}) custom-call(bf16[200,128]{1,0:T(8,128)(2,1)S(1)} %get-tuple-element.88.a_ref, bf16[200,128]{1,0:T(8,128)(2,1)S(1)} %collective-permute-done.12.d_ref, ...), custom_call_target="tpu_custom_call" | custom-call | tf_op jit(solution)/shard_map/pallas_call | solution.py:744
  (3 shorter events, 0.1 us)
Async XLA Ops:
  0.6 7.6 %collective-permute-start = (bf16[4,32,256]{2,1,0:T(8,128)(2,1)}, bf16[4,32,256]{2,1,0:T(8,128)(2,1)S(1)}, u32[]{:S(2)}, u32[]{:S(2)}) collective-permute-start(bf16[4,32,256]{2,1,0:T(8,128)(2,1)} %tok_ref.3), channel_id=1, source_target_pairs={{4,8},{12,16},{20,24},{28,0},{8,4},{16,12},{24,20},{0,28},{5,9},{1... | collective-permute-start | bytes 196616 | tf_op jit(solution)/shard_map/ppermute | solution.py:567
  4.0 4.2 %collective-permute-start.1 = (bf16[4,32,256]{2,1,0:T(8,128)(2,1)}, bf16[4,32,256]{2,1,0:T(8,128)(2,1)S(1)}, u32[]{:S(2)}, u32[]{:S(2)}) collective-permute-start(bf16[4,32,256]{2,1,0:T(8,128)(2,1)} %tok_ref.3), channel_id=1, source_target_pairs={{0,4},{8,12},{16,20},{24,28},{4,0},{12,8},{20,16},{28,24},{1,5},{9... | collective-permute-start | bytes 196616 | tf_op jit(solution)/shard_map/ppermute | solution.py:567
  4.0 1.4 %copy-start = (bf16[2,16,512]{2,1,0:T(8,128)(2,1)S(1)}, bf16[2,16,512]{2,1,0:T(8,128)(2,1)}, u32[]{:S(2)}) copy-start(bf16[2,16,512]{2,1,0:T(8,128)(2,1)} %dm_ref.3) | copy-start | bytes 98308
  4.0 1.4 %copy-start.1 = (bf16[1024,512]{1,0:T(8,128)(2,1)S(1)}, bf16[1024,512]{1,0:T(8,128)(2,1)}, u32[]{:S(2)}) copy-start(bf16[1024,512]{1,0:T(8,128)(2,1)} %wmerge_ref.3) | copy-start | bytes 3145732
  4.0 1.4 %copy-start.2 = (bf16[256,768]{1,0:T(8,128)(2,1)S(1)}, bf16[256,768]{1,0:T(8,128)(2,1)}, u32[]{:S(2)}) copy-start(bf16[256,768]{1,0:T(8,128)(2,1)} %wqkv_ref.5) | copy-start | bytes 1179652
  4.0 1.4 %copy-start.3 = (bf16[256,256]{1,0:T(8,128)(2,1)S(1)}, bf16[256,256]{1,0:T(8,128)(2,1)}, u32[]{:S(2)}) copy-start(bf16[256,256]{1,0:T(8,128)(2,1)} %wout_ref.3) | copy-start | bytes 393220
  4.1 1.4 %copy-start.4 = (bf16[4,32,256]{2,1,0:T(8,128)(2,1)S(1)}, bf16[4,32,256]{2,1,0:T(8,128)(2,1)}, u32[]{:S(2)}) copy-start(bf16[4,32,256]{2,1,0:T(8,128)(2,1)} %dskip_ref.1) | copy-start | bytes 196612
  4.1 1.4 %copy-start.5 = (bf16[4,32,256]{2,1,0:T(8,128)(2,1)S(1)}, bf16[4,32,256]{2,1,0:T(8,128)(2,1)}, u32[]{:S(2)}) copy-start(bf16[4,32,256]{2,1,0:T(8,128)(2,1)} %tok_ref.3) | copy-start | bytes 196612
  4.1 4.2 %collective-permute-start.2 = (bf16[32,512]{1,0:T(8,128)(2,1)}, bf16[32,512]{1,0:T(8,128)(2,1)S(1)}, u32[]{:S(2)}, u32[]{:S(2)}) collective-permute-start(bf16[32,512]{1,0:T(8,128)(2,1)} %bitcast.4), channel_id=1, source_target_pairs={{0,8},{4,12},{8,0},{12,4},{16,24},{20,28},{24,16},{28,20},{1,9},{5... | collective-permute-start | bytes 98312 | tf_op jit(solution)/shard_map/ppermute | solution.py:572
  5.4 0.7 %copy-start.6 = (f32[256]{0:T(256)S(1)}, f32[256]{0:T(256)}, u32[]{:S(2)}) copy-start(f32[256]{0:T(256)} %param.9) | copy-start | bytes 3076
  5.4 0.7 %copy-start.7 = (f32[4]{0:T(128)S(1)}, f32[4]{0:T(128)}, u32[]{:S(2)}) copy-start(f32[4]{0:T(128)} %param.11) | copy-start | bytes 52
  8.3 5.3 %collective-permute-start.3 = (bf16[40,256]{1,0:T(8,128)(2,1)S(1)}, bf16[40,256]{1,0:T(8,128)(2,1)S(1)}, u32[]{:S(2)}, u32[]{:S(2)}) collective-permute-start(bf16[40,256]{1,0:T(8,128)(2,1)S(1)} %get-tuple-element.59), channel_id=1, source_target_pairs={{0,1},{2,3},{1,0},{3,2},{4,5},{6,7},{5,4},{7,6},{8,9},{10,11},{9,8... | collective-permute-start | bytes 61448 | tf_op jit(solution)/shard_map/ppermute | solution.py:567
  9.9 5.6 %collective-permute-start.4 = (bf16[40,256]{1,0:T(8,128)(2,1)S(1)}, bf16[40,256]{1,0:T(8,128)(2,1)S(1)}, u32[]{:S(2)}, u32[]{:S(2)}) collective-permute-start(bf16[40,256]{1,0:T(8,128)(2,1)S(1)} %get-tuple-element.60), channel_id=1, source_target_pairs={{1,2},{3,0},{2,1},{0,3},{5,6},{7,4},{6,5},{4,7},{9,10},{11,8},{10,... | collective-permute-start | bytes 61448 | tf_op jit(solution)/shard_map/ppermute | solution.py:567
  12.4 5.1 %collective-permute-start.5 = (bf16[64,512]{1,0:T(8,128)(2,1)S(1)}, bf16[64,512]{1,0:T(8,128)(2,1)S(1)}, u32[]{:S(2)}, u32[]{:S(2)}) collective-permute-start(bf16[64,512]{1,0:T(8,128)(2,1)S(1)} %get-tuple-element.74.refs_1_), channel_id=1, source_target_pairs={{0,16},{4,20},{8,24},{12,28},{16,0},{20,4},{24,8},{28,12},{1,17},{... | collective-permute-start | bytes 196616 | tf_op jit(solution)/shard_map/ppermute | solution.py:572
  18.1 2.0 %collective-permute-start.6 = (bf16[4,32,1152]{2,1,0:T(8,128)(2,1)S(1)}, bf16[4,32,1152]{2,1,0:T(8,128)(2,1)S(1)}, u32[]{:S(2)}, u32[]{:S(2)}) collective-permute-start(bf16[4,32,1152]{2,1,0:T(8,128)(2,1)S(1)} %get-tuple-element.75), channel_id=1, source_target_pairs={{0,4},{4,0},{8,12},{12,8},{16,20},{20,16},{24,28},{28,24},{1,5},{5... | collective-permute-start | bytes 884744 | tf_op jit(solution)/shard_map/ppermute | solution.py:572
  18.7 1.4 %collective-permute-start.7 = (f32[8,128]{1,0:T(8,128)S(1)}, f32[8,128]{1,0:T(8,128)S(1)}, u32[]{:S(2)}, u32[]{:S(2)}) collective-permute-start(f32[8,128]{1,0:T(8,128)S(1)} %get-tuple-element.79.small_ref), channel_id=1, source_target_pairs={{0,4},{4,0},{8,12},{12,8},{16,20},{20,16},{24,28},{28,24},{1,5},{5... | collective-permute-start | bytes 12296 | tf_op jit(solution)/shard_map/ppermute | solution.py:572
  19.3 4.5 %collective-permute-start.11 = (bf16[128,512]{1,0:T(8,128)(2,1)S(1)}, bf16[128,512]{1,0:T(8,128)(2,1)S(1)}, u32[]{:S(2)}, u32[]{:S(2)}) collective-permute-start(bf16[128,512]{1,0:T(8,128)(2,1)S(1)} %get-tuple-element.86.refs_6_), channel_id=1, source_target_pairs={{0,4},{4,0},{8,12},{12,8},{16,20},{20,16},{24,28},{28,24},{1,5},{5... | collective-permute-start | bytes 393224 | tf_op jit(solution)/shard_map/ppermute | solution.py:572
  20.2 6.0 %collective-permute-start.8 = (bf16[328,128]{1,0:T(8,128)(2,1)S(1)}, bf16[328,128]{1,0:T(8,128)(2,1)S(1)}, u32[]{:S(2)}, u32[]{:S(2)}) collective-permute-start(bf16[328,128]{1,0:T(8,128)(2,1)S(1)} %get-tuple-element.83), channel_id=1, source_target_pairs={{0,24},{4,28},{8,16},{12,20},{16,8},{20,12},{24,0},{28,4},{1,25},{... | collective-permute-start | bytes 251912 | tf_op jit(solution)/shard_map/ppermute | solution.py:572
  21.8 5.9 %collective-permute-start.9 = (bf16[328,128]{1,0:T(8,128)(2,1)S(1)}, bf16[328,128]{1,0:T(8,128)(2,1)S(1)}, u32[]{:S(2)}, u32[]{:S(2)}) collective-permute-start(bf16[328,128]{1,0:T(8,128)(2,1)S(1)} %get-tuple-element.84), channel_id=1, source_target_pairs={{0,16},{4,20},{8,24},{12,28},{16,0},{20,4},{24,8},{28,12},{1,17},{... | collective-permute-start | bytes 251912 | tf_op jit(solution)/shard_map/ppermute | solution.py:572
  22.9 4.8 %collective-permute-start.10 = (bf16[328,128]{1,0:T(8,128)(2,1)S(1)}, bf16[328,128]{1,0:T(8,128)(2,1)S(1)}, u32[]{:S(2)}, u32[]{:S(2)}) collective-permute-start(bf16[328,128]{1,0:T(8,128)(2,1)S(1)} %get-tuple-element.85), channel_id=1, source_target_pairs={{0,8},{4,12},{8,0},{12,4},{16,24},{20,28},{24,16},{28,20},{1,9},{5... | collective-permute-start | bytes 251912 | tf_op jit(solution)/shard_map/ppermute | solution.py:572
  23.8 8.7 %collective-permute-start.15 = (bf16[40,256]{1,0:T(8,128)(2,1)S(1)}, bf16[40,256]{1,0:T(8,128)(2,1)S(1)}, u32[]{:S(2)}, u32[]{:S(2)}) collective-permute-start(bf16[40,256]{1,0:T(8,128)(2,1)S(1)} %get-tuple-element.93), channel_id=1, source_target_pairs={{0,1},{2,3},{1,0},{3,2},{4,5},{6,7},{5,4},{7,6},{8,9},{10,11},{9,8... | collective-permute-start | bytes 61448 | tf_op jit(solution)/shard_map/ppermute | solution.py:567
  23.8 8.7 %collective-permute-start.16 = (bf16[40,256]{1,0:T(8,128)(2,1)S(1)}, bf16[40,256]{1,0:T(8,128)(2,1)S(1)}, u32[]{:S(2)}, u32[]{:S(2)}) collective-permute-start(bf16[40,256]{1,0:T(8,128)(2,1)S(1)} %get-tuple-element.94), channel_id=1, source_target_pairs={{1,2},{3,0},{2,1},{0,3},{5,6},{7,4},{6,5},{4,7},{9,10},{11,8},{10,... | collective-permute-start | bytes 61448 | tf_op jit(solution)/shard_map/ppermute | solution.py:567
  28.0 9.0 %collective-permute-start.12 = (bf16[200,128]{1,0:T(8,128)(2,1)S(1)}, bf16[200,128]{1,0:T(8,128)(2,1)S(1)}, u32[]{:S(2)}, u32[]{:S(2)}) collective-permute-start(bf16[200,128]{1,0:T(8,128)(2,1)S(1)} %get-tuple-element.89), channel_id=1, source_target_pairs={{0,3},{1,2},{2,1},{3,0},{4,7},{5,6},{6,5},{7,4},{8,11},{9,10},{10,... | collective-permute-start | bytes 153608 | tf_op jit(solution)/shard_map/ppermute | solution.py:572
  30.5 6.5 %collective-permute-start.13 = (bf16[200,128]{1,0:T(8,128)(2,1)S(1)}, bf16[200,128]{1,0:T(8,128)(2,1)S(1)}, u32[]{:S(2)}, u32[]{:S(2)}) collective-permute-start(bf16[200,128]{1,0:T(8,128)(2,1)S(1)} %get-tuple-element.90), channel_id=1, source_target_pairs={{0,2},{1,3},{2,0},{3,1},{4,6},{5,7},{6,4},{7,5},{8,10},{9,11},{10,... | collective-permute-start | bytes 153608 | tf_op jit(solution)/shard_map/ppermute | solution.py:572
  30.5 6.5 %collective-permute-start.14 = (bf16[200,128]{1,0:T(8,128)(2,1)S(1)}, bf16[200,128]{1,0:T(8,128)(2,1)S(1)}, u32[]{:S(2)}, u32[]{:S(2)}) collective-permute-start(bf16[200,128]{1,0:T(8,128)(2,1)S(1)} %get-tuple-element.91), channel_id=1, source_target_pairs={{0,1},{1,0},{2,3},{3,2},{4,5},{5,4},{6,7},{7,6},{8,9},{9,8},{10,11... | collective-permute-start | bytes 153608 | tf_op jit(solution)/shard_map/ppermute | solution.py:572
  32.5 4.5 %collective-permute-start.17 = (bf16[96,256]{1,0:T(8,128)(2,1)S(1)}, bf16[96,256]{1,0:T(8,128)(2,1)S(1)}, u32[]{:S(2)}, u32[]{:S(2)}) collective-permute-start(bf16[96,256]{1,0:T(8,128)(2,1)S(1)} %get-tuple-element.96), channel_id=1, source_target_pairs={{4,8},{12,16},{20,24},{28,0},{8,4},{16,12},{24,20},{0,28},{5,9},{1... | collective-permute-start | bytes 147464 | tf_op jit(solution)/shard_map/ppermute | solution.py:567
  32.9 4.1 %collective-permute-start.18 = (bf16[96,256]{1,0:T(8,128)(2,1)S(1)}, bf16[96,256]{1,0:T(8,128)(2,1)S(1)}, u32[]{:S(2)}, u32[]{:S(2)}) collective-permute-start(bf16[96,256]{1,0:T(8,128)(2,1)S(1)} %get-tuple-element.97), channel_id=1, source_target_pairs={{0,4},{8,12},{16,20},{24,28},{4,0},{12,8},{20,16},{28,24},{1,5},{9... | collective-permute-start | bytes 147464 | tf_op jit(solution)/shard_map/ppermute | solution.py:567

commit v7 on v6

--- a/solution.py
+++ b/solution.py
@@ -559,12 +559,18 @@
 
 
 def swapped(near, far, axis):
-    count = lax.axis_size(axis)
-    first = [(i, i + 1) for i in range(0, count, 2)]
-    second = [(i, (i + 1) % count) for i in range(1, count, 2)]
-    first = first + [(j, i) for i, j in first]
-    second = second + [(j, i) for i, j in second]
-    return (lax.ppermute(near, axis, first), lax.ppermute(far, axis, second))
+    n_row, n_col = (lax.axis_size("row"), lax.axis_size("col"))
+    pairs = []
+    for row in range(n_row):
+        for col in range(n_col):
+            if axis == "row":
+                other = row - 1 if row % 2 == 0 else row + 1
+                target = (other, col) if 0 <= other < n_row else (row, col ^ 1)
+            else:
+                other = col - 1 if col % 2 == 0 else col + 1
+                target = (row, other) if 0 <= other < n_col else (row ^ 1, col)
+            pairs.append((row * n_col + col, target[0] * n_col + target[1]))
+    return (swap(near, axis, 1), lax.ppermute(far, ("row", "col"), pairs))
 
 
 def swap(value, axis, step):

time: 37.9 us -> 35.1 us (0.926)
  waiting for transfers between devices: 7.69 us -> 5.92 us
  starting transfers between devices: 22.6 us -> 21.5 us
    ppermute x8 -> x4, starting transfers between devices: 11.4 us -> 5.14 us  [swapped(): return (swap(near, axis, 1), lax.ppermute(far, ('row', 'col'), pairs))]
    ppermute x11 -> x15, starting transfers between devices: 11.2 us -> 16.4 us  [swap(): return lax.ppermute(value, axis, [(i, i ^ step) for i in range(count)])]
    ppermute x8 -> x4, waiting for transfers between devices: 4.07 us -> 1.95 us  [swapped(): return (swap(near, axis, 1), lax.ppermute(far, ('row', 'col'), pairs))]
    ppermute x11 -> x15, waiting for transfers between devices: 3.62 us -> 3.97 us  [swap(): return lax.ppermute(value, axis, [(i, i ^ step) for i in range(count)])]
  transfers between devices with their start and end apart: 19 -> 19, of which waited for: 5 -> 7; matrix products, arithmetic and copies ran while one was open for 0% -> 0% of each run, Pallas kernels for 12% -> 13%
where the time goes in v7:
time: 35.1 us; the launch traced here: 34.9 us
  starting transfers between devices  21.5 us (61%)
  Pallas kernels  6.02 us (17%)
  waiting for transfers between devices  5.92 us (17%)
  between operations  0.82 us (2%)
  local copies, waits for them, and re-layouts  0.63 us (2%)
    ppermute x15, starting transfers between devices, swap(): return lax.ppermute(value, axis, [(i, i ^ step) for i in range(count)])  16.4 us
    ppermute x4, starting transfers between devices, swapped(): return (swap(near, axis, 1), lax.ppermute(far, ('row', 'col'), pairs))  5.14 us
    ppermute x15, waiting for transfers between devices, swap(): return lax.ppermute(value, axis, [(i, i ^ step) for i in range(count)])  3.97 us
    pallas_call x1, Pallas kernels, on_device(): pl.pallas_call(functools.partial(layer_kernel, sizes), out_shape=(shape((...  1.96 us
    ppermute x4, waiting for transfers between devices, swapped(): return (swap(near, axis, 1), lax.ppermute(far, ('row', 'col'), pairs))  1.95 us
    pallas_call x1, Pallas kernels, on_device(): pl.pallas_call(output_kernel, out_shape=(shape((rows, cols, width), BF),...  0.91 us
    pallas_call x1, Pallas kernels, on_device(): pl.pallas_call(own_kernel, out_shape=(shape((2 * rows * EDGE, width), BF)...  0.79 us
    pallas_call x1, Pallas kernels, on_device(): pl.pallas_call(functools.partial(col_sum_kernel, (rows, cols, width)), ou...  0.75 us
  transfers between devices with their start and end apart: 19, of which 7 were waited for; matrix products, arithmetic and copies ran while one was open for 0% of the time, Pallas kernels for 13%

profile of v7, /device:TPU:0, one launch (start us, length us, event | category | flops | bytes accessed | tf_op | source)
XLA Modules:
  0.0 34.9 jit_solution(7797672608731938827)
XLA Ops:
  0.6 3.1 %collective-permute-start = (bf16[4,32,256]{2,1,0:T(8,128)(2,1)}, bf16[4,32,256]{2,1,0:T(8,128)(2,1)S(1)}, u32[]{:S(2)}, u32[]{:S(2)}) collective-permute-start(bf16[4,32,256]{2,1,0:T(8,128)(2,1)} %tok_ref.3), channel_id=1, source_target_pairs={{0,1},{1,0},{2,3},{3,2},{4,8},{5,9},{6,10},{7,11},{8,4},{9,5},{10,... | collective-permute-start | bytes 196616 | tf_op jit(solution)/shard_map/ppermute | solution.py:573
  3.7 0.0 collective-permute-start.1
  3.8 0.0 copy-start
  3.8 0.0 copy-start.1
  3.8 0.0 copy-start.2
  3.8 0.0 copy-start.3
  3.8 0.0 copy-start.4
  3.8 0.0 copy-start.5
  3.8 1.6 %collective-permute-start.2 = (bf16[32,512]{1,0:T(8,128)(2,1)}, bf16[32,512]{1,0:T(8,128)(2,1)S(1)}, u32[]{:S(2)}, u32[]{:S(2)}) collective-permute-start(bf16[32,512]{1,0:T(8,128)(2,1)} %bitcast.4), channel_id=1, source_target_pairs={{0,8},{4,12},{8,0},{12,4},{16,24},{20,28},{24,16},{28,20},{1,9},{5... | collective-permute-start | bytes 98312 | tf_op jit(solution)/shard_map/ppermute | solution.py:578
  5.4 0.0 copy-start.6
  5.4 0.0 copy-start.7
  5.4 0.0 copy-done
  5.4 0.0 copy-done.1
  5.4 0.0 copy-done.2
  5.4 0.0 copy-done.3
  5.4 0.0 copy-done.4
  5.5 0.0 copy-done.5
  5.5 0.6 %copy-done.6 = f32[256]{0:T(256)S(1)} copy-done((f32[256]{0:T(256)S(1)}, f32[256]{0:T(256)}, u32[]{:S(2)}) %copy-start.6) | copy-done | bytes 1048
  6.1 0.0 copy-done.7
  6.1 0.8 %shard_map.144 = (bf16[32,256]{1,0:T(8,128)(2,1)S(1)}, f32[8,256]{1,0:T(8,128)S(1)}, f32[128,256]{1,0:T(8,128)S(1)}, f32[128,256]{1,0:T(8,128)S(1)}, f32[128,256...) custom-call(bf16[256,256]{1,0:T(8,128)(2,1)S(1)} %get-tuple-element.56.ones_ref, f32[8,128]{1,0:T(8,128)S(1)} %get-tuple-element.57.parity_ref, ...), custom_call_target="tpu_custom_call" | custom-call | flops 1000000000 | bytes 1000000 | tf_op jit(solution)/shard_map/pallas_call | solution.py:608
  6.9 1.1 %collective-permute-done.2.dm_next_ref = bf16[32,512]{1,0:T(8,128)(2,1)S(1)} collective-permute-done((bf16[32,512]{1,0:T(8,128)(2,1)}, bf16[32,512]{1,0:T(8,128)(2,1)S(1)}, u32[]{:S(2)}, u32[]{:S(2)}) %collective-permute-start.2) | collective-permute-done | bytes 32800 | tf_op jit(solution)/shard_map/ppermute | solution.py:578
  8.0 0.0 collective-permute-done.far_ref.row_far_ref
  8.0 0.0 collective-permute-done.1.near_ref.row_near_ref
  8.0 1.6 %collective-permute-start.3 = (bf16[40,256]{1,0:T(8,128)(2,1)S(1)}, bf16[40,256]{1,0:T(8,128)(2,1)S(1)}, u32[]{:S(2)}, u32[]{:S(2)}) collective-permute-start(bf16[40,256]{1,0:T(8,128)(2,1)S(1)} %get-tuple-element.59), channel_id=1, source_target_pairs={{0,1},{1,0},{2,3},{3,2},{4,5},{5,4},{6,7},{7,6},{8,9},{9,8},{10,11... | collective-permute-start | bytes 61448 | tf_op jit(solution)/shard_map/ppermute | solution.py:578
  9.7 0.0 collective-permute-start.4
  9.7 1.5 %collective-permute-start.5 = (bf16[64,512]{1,0:T(8,128)(2,1)S(1)}, bf16[64,512]{1,0:T(8,128)(2,1)S(1)}, u32[]{:S(2)}, u32[]{:S(2)}) collective-permute-start(bf16[64,512]{1,0:T(8,128)(2,1)S(1)} %get-tuple-element.74.refs_1_), channel_id=1, source_target_pairs={{0,16},{4,20},{8,24},{12,28},{16,0},{20,4},{24,8},{28,12},{1,17},{... | collective-permute-start | bytes 196616 | tf_op jit(solution)/shard_map/ppermute | solution.py:578
  11.2 0.7 %collective-permute-done.3.col_near_ref = bf16[40,256]{1,0:T(8,128)(2,1)S(1)} collective-permute-done((bf16[40,256]{1,0:T(8,128)(2,1)S(1)}, bf16[40,256]{1,0:T(8,128)(2,1)S(1)}, u32[]{:S(2)}, u32[]{:S(2)}) %collective-permute-start.3) | collective-permute-done | bytes 20512 | tf_op jit(solution)/shard_map/ppermute | solution.py:578
  11.9 0.0 collective-permute-done.4.col_far_ref
  11.9 2.0 %shard_map.146 = (f32[480,256]{1,0:T(8,128)S(1)}, bf16[128,256]{1,0:T(8,128)(2,1)S(1)}, bf16[128,256]{1,0:T(8,128)(2,1)S(1)}, bf16[480,512]{1,0:T(8,128)(2,1)S(1...) custom-call(bf16[256,256]{1,0:T(8,128)(2,1)S(1)} %get-tuple-element.56.ones_ref, ...), custom_call_target="tpu_custom_call" | custom-call | flops 4000000000 | bytes 1000000 | tf_op jit(solution)/shard_map/pallas_call | solution.py:655
  13.8 0.3 collective-permute-done.5.refs_0_
  14.2 0.6 %shard_map.148 = (bf16[128,512]{1,0:T(8,128)(2,1)S(1)}, bf16[4,32,1152]{2,1,0:T(8,128)(2,1)S(1)}, f32[4,32,1024]{2,1,0:T(8,128)S(1)}, bf16[4,32,128]{2,1,0:T(8,128)(2,1)S(1)}) custom-call(f32[480,256]{1,0:T(8,128)S(1)} %get-tuple-element.70.x_ref, bf16[128,256]{1,0:T(8,128)(2,1)S(1)} %get-tuple-element.71.d_query_ref, ...), custom_call_target="tpu_custom_call" | custom-call | flops 1000000000 | bytes 1000000 | tf_op jit(solution)/shard_map/pallas_call | solution.py:686
  14.8 0.1 collective-permute-start.6
  14.8 0.5 %shard_map.149 = (f32[320,256]{1,0:T(8,128)S(1)}, bf16[40,256]{1,0:T(8,128)(2,1)S(1)}, bf16[40,256]{1,0:T(8,128)(2,1)S(1)}, f32[8,128]{1,0:T(8,128)S(1)}) custom-call(f32[480,256]{1,0:T(8,128)S(1)} %get-tuple-element.70.x_ref, bf16[128,256]{1,0:T(8,128)(2,1)S(1)} %get-tuple-element.71.d_query_ref, bf16[480,512]{1,0:T(8,128)(2,1)S(1)} %get-tuple-element.72.d_kv_ref, ...), custom_call_target="tpu_custom_call" | custom-call | flops 500000000 | bytes 1000000 | tf_op jit(solution)/shard_map/pallas_call | solution.py:694
  15.4 0.6 %collective-permute-start.7 = (f32[8,128]{1,0:T(8,128)S(1)}, f32[8,128]{1,0:T(8,128)S(1)}, u32[]{:S(2)}, u32[]{:S(2)}) collective-permute-start(f32[8,128]{1,0:T(8,128)S(1)} %get-tuple-element.79.small_ref), channel_id=1, source_target_pairs={{0,4},{4,0},{8,12},{12,8},{16,20},{20,16},{24,28},{28,24},{1,5},{5... | collective-permute-start | bytes 12296 | tf_op jit(solution)/shard_map/ppermute | solution.py:578
  15.9 0.1 collective-permute-start.11
  16.0 0.7 %collective-permute-done.7.small_near_ref = f32[8,128]{1,0:T(8,128)S(1)} collective-permute-done((f32[8,128]{1,0:T(8,128)S(1)}, f32[8,128]{1,0:T(8,128)S(1)}, u32[]{:S(2)}, u32[]{:S(2)}) %collective-permute-start.7) | collective-permute-done | bytes 4128 | tf_op jit(solution)/shard_map/ppermute | solution.py:578
  16.8 0.0 collective-permute-done.6.got_ref
  16.8 0.1 shard_map.150
  16.9 1.9 %collective-permute-start.8 = (bf16[328,128]{1,0:T(8,128)(2,1)S(1)}, bf16[328,128]{1,0:T(8,128)(2,1)S(1)}, u32[]{:S(2)}, u32[]{:S(2)}) collective-permute-start(bf16[328,128]{1,0:T(8,128)(2,1)S(1)} %get-tuple-element.83), channel_id=1, source_target_pairs={{0,24},{4,28},{8,16},{12,20},{16,8},{20,12},{24,0},{28,4},{1,25},{... | collective-permute-start | bytes 251912 | tf_op jit(solution)/shard_map/ppermute | solution.py:578
  18.8 1.1 %collective-permute-start.9 = (bf16[328,128]{1,0:T(8,128)(2,1)S(1)}, bf16[328,128]{1,0:T(8,128)(2,1)S(1)}, u32[]{:S(2)}, u32[]{:S(2)}) collective-permute-start(bf16[328,128]{1,0:T(8,128)(2,1)S(1)} %get-tuple-element.84), channel_id=1, source_target_pairs={{0,16},{4,20},{8,24},{12,28},{16,0},{20,4},{24,8},{28,12},{1,17},{... | collective-permute-start | bytes 251912 | tf_op jit(solution)/shard_map/ppermute | solution.py:578
  19.9 0.5 %collective-permute-start.10 = (bf16[328,128]{1,0:T(8,128)(2,1)S(1)}, bf16[328,128]{1,0:T(8,128)(2,1)S(1)}, u32[]{:S(2)}, u32[]{:S(2)}) collective-permute-start(bf16[328,128]{1,0:T(8,128)(2,1)S(1)} %get-tuple-element.85), channel_id=1, source_target_pairs={{0,8},{4,12},{8,0},{12,4},{16,24},{20,28},{24,16},{28,20},{1,9},{5... | collective-permute-start | bytes 251912 | tf_op jit(solution)/shard_map/ppermute | solution.py:578
  20.4 2.9 %collective-permute-start.15 = (bf16[40,256]{1,0:T(8,128)(2,1)S(1)}, bf16[40,256]{1,0:T(8,128)(2,1)S(1)}, u32[]{:S(2)}, u32[]{:S(2)}) collective-permute-start(bf16[40,256]{1,0:T(8,128)(2,1)S(1)} %get-tuple-element.93), channel_id=1, source_target_pairs={{0,1},{1,0},{2,3},{3,2},{4,5},{5,4},{6,7},{7,6},{8,9},{9,8},{10,11... | collective-permute-start | bytes 61448 | tf_op jit(solution)/shard_map/ppermute | solution.py:578
  23.3 0.0 collective-permute-done.11.refs_7_
  23.3 0.0 collective-permute-start.16
  23.3 0.0 collective-permute-done.8.refs_3_
  23.3 1.0 %collective-permute-done.9.refs_4_ = bf16[328,128]{1,0:T(8,128)(2,1)S(1)} collective-permute-done((bf16[328,128]{1,0:T(8,128)(2,1)S(1)}, bf16[328,128]{1,0:T(8,128)(2,1)S(1)}, u32[]{:S(2)}, u32[]{:S(2)}) %collective-permute-start.9) | collective-permute-done | bytes 84000 | tf_op jit(solution)/shard_map/ppermute | solution.py:578
  24.4 0.1 collective-permute-done.10.refs_5_
  24.4 0.3 shard_map.151
  24.7 3.3 %collective-permute-start.12 = (bf16[200,128]{1,0:T(8,128)(2,1)S(1)}, bf16[200,128]{1,0:T(8,128)(2,1)S(1)}, u32[]{:S(2)}, u32[]{:S(2)}) collective-permute-start(bf16[200,128]{1,0:T(8,128)(2,1)S(1)} %get-tuple-element.89), channel_id=1, source_target_pairs={{0,3},{1,2},{2,1},{3,0},{4,7},{5,6},{6,5},{7,4},{8,11},{9,10},{10,... | collective-permute-start | bytes 153608 | tf_op jit(solution)/shard_map/ppermute | solution.py:578
  28.1 1.1 %collective-permute-start.13 = (bf16[200,128]{1,0:T(8,128)(2,1)S(1)}, bf16[200,128]{1,0:T(8,128)(2,1)S(1)}, u32[]{:S(2)}, u32[]{:S(2)}) collective-permute-start(bf16[200,128]{1,0:T(8,128)(2,1)S(1)} %get-tuple-element.90), channel_id=1, source_target_pairs={{0,2},{1,3},{2,0},{3,1},{4,6},{5,7},{6,4},{7,5},{8,10},{9,11},{10,... | collective-permute-start | bytes 153608 | tf_op jit(solution)/shard_map/ppermute | solution.py:578
  29.1 0.0 collective-permute-start.14
  29.2 0.0 collective-permute-done.15.near_ref
  29.2 0.0 collective-permute-done.16.far_ref
  29.3 2.0 %collective-permute-start.17 = (bf16[96,256]{1,0:T(8,128)(2,1)S(1)}, bf16[96,256]{1,0:T(8,128)(2,1)S(1)}, u32[]{:S(2)}, u32[]{:S(2)}) collective-permute-start(bf16[96,256]{1,0:T(8,128)(2,1)S(1)} %get-tuple-element.96), channel_id=1, source_target_pairs={{0,1},{1,0},{2,3},{3,2},{4,8},{5,9},{6,10},{7,11},{8,4},{9,5},{10,... | collective-permute-start | bytes 147464 | tf_op jit(solution)/shard_map/ppermute | solution.py:573
  31.3 0.0 collective-permute-start.18
  31.3 0.9 %shard_map.147 = (bf16[4,32,256]{2,1,0:T(8,128)(2,1)}, bf16[2,16,512]{2,1,0:T(8,128)(2,1)}) custom-call(bf16[128,256]{1,0:T(8,128)(2,1)S(1)} %get-tuple-element.66.y_ref, bf16[32,1024]{1,0:T(8,128)(2,1)S(1)} %get-tuple-element.67.group_ref, bf16[1024,512]{1,0:T(8,128)(2,1)S(1)} %copy-done.1), custom_call_target="tpu_custom_call" | custom-call | flops 1000000000 | bytes 1000000 | tf_op jit(solution)/shard_map/pallas_call | solution.py:704
  32.2 1.9 %collective-permute-done.17.far_ref = bf16[96,256]{1,0:T(8,128)(2,1)S(1)} collective-permute-done((bf16[96,256]{1,0:T(8,128)(2,1)S(1)}, bf16[96,256]{1,0:T(8,128)(2,1)S(1)}, u32[]{:S(2)}, u32[]{:S(2)}) %collective-permute-start.17) | collective-permute-done | bytes 49184 | tf_op jit(solution)/shard_map/ppermute | solution.py:573
  34.1 0.0 collective-permute-done.18.near_ref
  34.2 0.0 collective-permute-done.12.d_ref
  34.2 0.0 collective-permute-done.13.c_ref
  34.2 0.0 collective-permute-done.14.b_ref
  34.2 0.7 %shard_map.153 = (f32[32,192]{1,0:T(8,128)}, f32[32,64]{1,0:T(8,128)}, f32[128,128]{1,0:T(8,128)}, f32[1,256]{1,0:T(1,128)}, f32[4]{0:T(128)}, /*index=5*/bf16[4,32,256]{2,1,0:T(8,128)(2,1)}) custom-call(bf16[200,128]{1,0:T(8,128)(2,1)S(1)} %get-tuple-element.88.a_ref, bf16[200,128]{1,0:T(8,128)(2,1)S(1)} %collective-permute-done.12.d_ref, ...), custom_call_target="tpu_custom_call" | custom-call | tf_op jit(solution)/shard_map/pallas_call | solution.py:750
  (3 shorter events, 0.1 us)
Async XLA Ops:
  0.6 7.3 %collective-permute-start = (bf16[4,32,256]{2,1,0:T(8,128)(2,1)}, bf16[4,32,256]{2,1,0:T(8,128)(2,1)S(1)}, u32[]{:S(2)}, u32[]{:S(2)}) collective-permute-start(bf16[4,32,256]{2,1,0:T(8,128)(2,1)} %tok_ref.3), channel_id=1, source_target_pairs={{0,1},{1,0},{2,3},{3,2},{4,8},{5,9},{6,10},{7,11},{8,4},{9,5},{10,... | collective-permute-start | bytes 196616 | tf_op jit(solution)/shard_map/ppermute | solution.py:573
  3.7 4.3 %collective-permute-start.1 = (bf16[4,32,256]{2,1,0:T(8,128)(2,1)}, bf16[4,32,256]{2,1,0:T(8,128)(2,1)S(1)}, u32[]{:S(2)}, u32[]{:S(2)}) collective-permute-start(bf16[4,32,256]{2,1,0:T(8,128)(2,1)} %tok_ref.3), channel_id=1, source_target_pairs={{0,4},{4,0},{8,12},{12,8},{16,20},{20,16},{24,28},{28,24},{1,5},{5... | collective-permute-start | bytes 196616 | tf_op jit(solution)/shard_map/ppermute | solution.py:578
  3.8 1.7 %copy-start = (bf16[2,16,512]{2,1,0:T(8,128)(2,1)S(1)}, bf16[2,16,512]{2,1,0:T(8,128)(2,1)}, u32[]{:S(2)}) copy-start(bf16[2,16,512]{2,1,0:T(8,128)(2,1)} %dm_ref.3) | copy-start | bytes 98308
  3.8 1.7 %copy-start.1 = (bf16[1024,512]{1,0:T(8,128)(2,1)S(1)}, bf16[1024,512]{1,0:T(8,128)(2,1)}, u32[]{:S(2)}) copy-start(bf16[1024,512]{1,0:T(8,128)(2,1)} %wmerge_ref.3) | copy-start | bytes 3145732
  3.8 1.7 %copy-start.2 = (bf16[256,768]{1,0:T(8,128)(2,1)S(1)}, bf16[256,768]{1,0:T(8,128)(2,1)}, u32[]{:S(2)}) copy-start(bf16[256,768]{1,0:T(8,128)(2,1)} %wqkv_ref.5) | copy-start | bytes 1179652
  3.8 1.7 %copy-start.3 = (bf16[256,256]{1,0:T(8,128)(2,1)S(1)}, bf16[256,256]{1,0:T(8,128)(2,1)}, u32[]{:S(2)}) copy-start(bf16[256,256]{1,0:T(8,128)(2,1)} %wout_ref.3) | copy-start | bytes 393220
  3.8 1.7 %copy-start.4 = (bf16[4,32,256]{2,1,0:T(8,128)(2,1)S(1)}, bf16[4,32,256]{2,1,0:T(8,128)(2,1)}, u32[]{:S(2)}) copy-start(bf16[4,32,256]{2,1,0:T(8,128)(2,1)} %dskip_ref.1) | copy-start | bytes 196612
  3.8 1.7 %copy-start.5 = (bf16[4,32,256]{2,1,0:T(8,128)(2,1)S(1)}, bf16[4,32,256]{2,1,0:T(8,128)(2,1)}, u32[]{:S(2)}) copy-start(bf16[4,32,256]{2,1,0:T(8,128)(2,1)} %tok_ref.3) | copy-start | bytes 196612
  3.8 4.2 %collective-permute-start.2 = (bf16[32,512]{1,0:T(8,128)(2,1)}, bf16[32,512]{1,0:T(8,128)(2,1)S(1)}, u32[]{:S(2)}, u32[]{:S(2)}) collective-permute-start(bf16[32,512]{1,0:T(8,128)(2,1)} %bitcast.4), channel_id=1, source_target_pairs={{0,8},{4,12},{8,0},{12,4},{16,24},{20,28},{24,16},{28,20},{1,9},{5... | collective-permute-start | bytes 98312 | tf_op jit(solution)/shard_map/ppermute | solution.py:578
  5.4 0.7 %copy-start.6 = (f32[256]{0:T(256)S(1)}, f32[256]{0:T(256)}, u32[]{:S(2)}) copy-start(f32[256]{0:T(256)} %param.9) | copy-start | bytes 3076
  5.4 0.7 %copy-start.7 = (f32[4]{0:T(128)S(1)}, f32[4]{0:T(128)}, u32[]{:S(2)}) copy-start(f32[4]{0:T(128)} %param.11) | copy-start | bytes 52
  8.0 3.8 %collective-permute-start.3 = (bf16[40,256]{1,0:T(8,128)(2,1)S(1)}, bf16[40,256]{1,0:T(8,128)(2,1)S(1)}, u32[]{:S(2)}, u32[]{:S(2)}) collective-permute-start(bf16[40,256]{1,0:T(8,128)(2,1)S(1)} %get-tuple-element.59), channel_id=1, source_target_pairs={{0,1},{1,0},{2,3},{3,2},{4,5},{5,4},{6,7},{7,6},{8,9},{9,8},{10,11... | collective-permute-start | bytes 61448 | tf_op jit(solution)/shard_map/ppermute | solution.py:578
  9.7 2.2 %collective-permute-start.4 = (bf16[40,256]{1,0:T(8,128)(2,1)S(1)}, bf16[40,256]{1,0:T(8,128)(2,1)S(1)}, u32[]{:S(2)}, u32[]{:S(2)}) collective-permute-start(bf16[40,256]{1,0:T(8,128)(2,1)S(1)} %get-tuple-element.60), channel_id=1, source_target_pairs={{0,4},{1,2},{2,1},{3,7},{4,0},{5,6},{6,5},{7,3},{8,12},{9,10},{10,... | collective-permute-start | bytes 61448 | tf_op jit(solution)/shard_map/ppermute | solution.py:573
  9.7 4.5 %collective-permute-start.5 = (bf16[64,512]{1,0:T(8,128)(2,1)S(1)}, bf16[64,512]{1,0:T(8,128)(2,1)S(1)}, u32[]{:S(2)}, u32[]{:S(2)}) collective-permute-start(bf16[64,512]{1,0:T(8,128)(2,1)S(1)} %get-tuple-element.74.refs_1_), channel_id=1, source_target_pairs={{0,16},{4,20},{8,24},{12,28},{16,0},{20,4},{24,8},{28,12},{1,17},{... | collective-permute-start | bytes 196616 | tf_op jit(solution)/shard_map/ppermute | solution.py:578
  14.8 2.0 %collective-permute-start.6 = (bf16[4,32,1152]{2,1,0:T(8,128)(2,1)S(1)}, bf16[4,32,1152]{2,1,0:T(8,128)(2,1)S(1)}, u32[]{:S(2)}, u32[]{:S(2)}) collective-permute-start(bf16[4,32,1152]{2,1,0:T(8,128)(2,1)S(1)} %get-tuple-element.75), channel_id=1, source_target_pairs={{0,4},{4,0},{8,12},{12,8},{16,20},{20,16},{24,28},{28,24},{1,5},{5... | collective-permute-start | bytes 884744 | tf_op jit(solution)/shard_map/ppermute | solution.py:578
  15.4 1.4 %collective-permute-start.7 = (f32[8,128]{1,0:T(8,128)S(1)}, f32[8,128]{1,0:T(8,128)S(1)}, u32[]{:S(2)}, u32[]{:S(2)}) collective-permute-start(f32[8,128]{1,0:T(8,128)S(1)} %get-tuple-element.79.small_ref), channel_id=1, source_target_pairs={{0,4},{4,0},{8,12},{12,8},{16,20},{20,16},{24,28},{28,24},{1,5},{5... | collective-permute-start | bytes 12296 | tf_op jit(solution)/shard_map/ppermute | solution.py:578
  15.9 7.4 %collective-permute-start.11 = (bf16[128,512]{1,0:T(8,128)(2,1)S(1)}, bf16[128,512]{1,0:T(8,128)(2,1)S(1)}, u32[]{:S(2)}, u32[]{:S(2)}) collective-permute-start(bf16[128,512]{1,0:T(8,128)(2,1)S(1)} %get-tuple-element.86.refs_6_), channel_id=1, source_target_pairs={{0,4},{4,0},{8,12},{12,8},{16,20},{20,16},{24,28},{28,24},{1,5},{5... | collective-permute-start | bytes 393224 | tf_op jit(solution)/shard_map/ppermute | solution.py:578
  16.9 6.5 %collective-permute-start.8 = (bf16[328,128]{1,0:T(8,128)(2,1)S(1)}, bf16[328,128]{1,0:T(8,128)(2,1)S(1)}, u32[]{:S(2)}, u32[]{:S(2)}) collective-permute-start(bf16[328,128]{1,0:T(8,128)(2,1)S(1)} %get-tuple-element.83), channel_id=1, source_target_pairs={{0,24},{4,28},{8,16},{12,20},{16,8},{20,12},{24,0},{28,4},{1,25},{... | collective-permute-start | bytes 251912 | tf_op jit(solution)/shard_map/ppermute | solution.py:578
  18.8 5.6 %collective-permute-start.9 = (bf16[328,128]{1,0:T(8,128)(2,1)S(1)}, bf16[328,128]{1,0:T(8,128)(2,1)S(1)}, u32[]{:S(2)}, u32[]{:S(2)}) collective-permute-start(bf16[328,128]{1,0:T(8,128)(2,1)S(1)} %get-tuple-element.84), channel_id=1, source_target_pairs={{0,16},{4,20},{8,24},{12,28},{16,0},{20,4},{24,8},{28,12},{1,17},{... | collective-permute-start | bytes 251912 | tf_op jit(solution)/shard_map/ppermute | solution.py:578
  19.9 4.5 %collective-permute-start.10 = (bf16[328,128]{1,0:T(8,128)(2,1)S(1)}, bf16[328,128]{1,0:T(8,128)(2,1)S(1)}, u32[]{:S(2)}, u32[]{:S(2)}) collective-permute-start(bf16[328,128]{1,0:T(8,128)(2,1)S(1)} %get-tuple-element.85), channel_id=1, source_target_pairs={{0,8},{4,12},{8,0},{12,4},{16,24},{20,28},{24,16},{28,20},{1,9},{5... | collective-permute-start | bytes 251912 | tf_op jit(solution)/shard_map/ppermute | solution.py:578
  20.4 8.8 %collective-permute-start.15 = (bf16[40,256]{1,0:T(8,128)(2,1)S(1)}, bf16[40,256]{1,0:T(8,128)(2,1)S(1)}, u32[]{:S(2)}, u32[]{:S(2)}) collective-permute-start(bf16[40,256]{1,0:T(8,128)(2,1)S(1)} %get-tuple-element.93), channel_id=1, source_target_pairs={{0,1},{1,0},{2,3},{3,2},{4,5},{5,4},{6,7},{7,6},{8,9},{9,8},{10,11... | collective-permute-start | bytes 61448 | tf_op jit(solution)/shard_map/ppermute | solution.py:578
  23.3 5.9 %collective-permute-start.16 = (bf16[40,256]{1,0:T(8,128)(2,1)S(1)}, bf16[40,256]{1,0:T(8,128)(2,1)S(1)}, u32[]{:S(2)}, u32[]{:S(2)}) collective-permute-start(bf16[40,256]{1,0:T(8,128)(2,1)S(1)} %get-tuple-element.94), channel_id=1, source_target_pairs={{0,4},{1,2},{2,1},{3,7},{4,0},{5,6},{6,5},{7,3},{8,12},{9,10},{10,... | collective-permute-start | bytes 61448 | tf_op jit(solution)/shard_map/ppermute | solution.py:573
  24.7 9.4 %collective-permute-start.12 = (bf16[200,128]{1,0:T(8,128)(2,1)S(1)}, bf16[200,128]{1,0:T(8,128)(2,1)S(1)}, u32[]{:S(2)}, u32[]{:S(2)}) collective-permute-start(bf16[200,128]{1,0:T(8,128)(2,1)S(1)} %get-tuple-element.89), channel_id=1, source_target_pairs={{0,3},{1,2},{2,1},{3,0},{4,7},{5,6},{6,5},{7,4},{8,11},{9,10},{10,... | collective-permute-start | bytes 153608 | tf_op jit(solution)/shard_map/ppermute | solution.py:578
  28.1 6.1 %collective-permute-start.13 = (bf16[200,128]{1,0:T(8,128)(2,1)S(1)}, bf16[200,128]{1,0:T(8,128)(2,1)S(1)}, u32[]{:S(2)}, u32[]{:S(2)}) collective-permute-start(bf16[200,128]{1,0:T(8,128)(2,1)S(1)} %get-tuple-element.90), channel_id=1, source_target_pairs={{0,2},{1,3},{2,0},{3,1},{4,6},{5,7},{6,4},{7,5},{8,10},{9,11},{10,... | collective-permute-start | bytes 153608 | tf_op jit(solution)/shard_map/ppermute | solution.py:578
  29.1 5.0 %collective-permute-start.14 = (bf16[200,128]{1,0:T(8,128)(2,1)S(1)}, bf16[200,128]{1,0:T(8,128)(2,1)S(1)}, u32[]{:S(2)}, u32[]{:S(2)}) collective-permute-start(bf16[200,128]{1,0:T(8,128)(2,1)S(1)} %get-tuple-element.91), channel_id=1, source_target_pairs={{0,1},{1,0},{2,3},{3,2},{4,5},{5,4},{6,7},{7,6},{8,9},{9,8},{10,11... | collective-permute-start | bytes 153608 | tf_op jit(solution)/shard_map/ppermute | solution.py:578
  29.3 4.9 %collective-permute-start.17 = (bf16[96,256]{1,0:T(8,128)(2,1)S(1)}, bf16[96,256]{1,0:T(8,128)(2,1)S(1)}, u32[]{:S(2)}, u32[]{:S(2)}) collective-permute-start(bf16[96,256]{1,0:T(8,128)(2,1)S(1)} %get-tuple-element.96), channel_id=1, source_target_pairs={{0,1},{1,0},{2,3},{3,2},{4,8},{5,9},{6,10},{7,11},{8,4},{9,5},{10,... | collective-permute-start | bytes 147464 | tf_op jit(solution)/shard_map/ppermute | solution.py:573
  31.3 2.9 %collective-permute-start.18 = (bf16[96,256]{1,0:T(8,128)(2,1)S(1)}, bf16[96,256]{1,0:T(8,128)(2,1)S(1)}, u32[]{:S(2)}, u32[]{:S(2)}) collective-permute-start(bf16[96,256]{1,0:T(8,128)(2,1)S(1)} %get-tuple-element.97), channel_id=1, source_target_pairs={{0,4},{4,0},{8,12},{12,8},{16,20},{20,16},{24,28},{28,24},{1,5},{5... | collective-permute-start | bytes 147464 | tf_op jit(solution)/shard_map/ppermute | solution.py:578

commit v8 on v7

--- a/solution.py
+++ b/solution.py
@@ -49,24 +49,25 @@
     parity_ref[...] = jnp.concatenate(parts, axis=0)
 
 
-def edge_kernel(
-    edges_ref, far_ref, near_ref, dm_ref, dm_next_ref, edge_near_ref, edge_far_ref, dm_pair_ref
-):
+def edge_kernel(edges_ref, near_ref, edge_near_ref, edge_far_ref):
     rows, cols, width = near_ref.shape
+    near_row = near_ref[...].astype(F32)
+    even = lax.rem(lax.axis_index("row"), 2) == 0
+    near_row = jnp.where(even, near_row[:RADIUS], near_row[rows - RADIUS :])
+    left, right = [
+        near_row[:, at : at + EDGE].reshape(RADIUS * EDGE, width) for at in (0, cols - EDGE)
+    ]
+    far, near = by_side("col", right, left)
+    for out_ref, own_at, part in ((edge_near_ref, 0, near), (edge_far_ref, rows * EDGE, far)):
+        own = edges_ref[own_at : own_at + rows * EDGE].astype(F32)
+        after = jnp.concatenate([own, part], axis=0)
+        before = jnp.concatenate([part, own], axis=0)
+        out_ref[...] = jnp.where(even, after, before).astype(BF)
+
+
+def pair_kernel(dm_ref, dm_next_ref, dm_pair_ref):
     size = dm_next_ref.shape[0]
     dm_pair_ref[...] = jnp.concatenate([dm_ref[...].reshape(size, -1), dm_next_ref[...]], axis=0)
-    up, down = by_side("row", near_ref[...].astype(F32), far_ref[...].astype(F32))
-    up = up[rows - RADIUS :]
-    down = down[:RADIUS]
-    halo = []
-    for at in (0, cols - EDGE):
-        parts = [part[:, at : at + EDGE].reshape(RADIUS * EDGE, width) for part in (up, down)]
-        halo.append(jnp.concatenate(parts, axis=0))
-    far, near = by_side("col", halo[1], halo[0])
-    for out_ref, own_at, part in ((edge_near_ref, 0, near), (edge_far_ref, rows * EDGE, far)):
-        own = edges_ref[own_at : own_at + rows * EDGE].astype(F32)
-        size = RADIUS * EDGE
-        out_ref[...] = jnp.concatenate([part[:size], own, part[size:]], axis=0).astype(BF)
 
 
 def in_order(axis, own, partner):
@@ -91,6 +92,8 @@
     wout_ref,
     wmerge_ref,
     edges_ref,
+    corner_near_ref,
+    corner_far_ref,
     rows_ref,
     q_norm_ref,
     q_unit_ref,
@@ -107,6 +110,10 @@
     even = parity_ref[heads : heads + 1, 0:1] > 0.5
     near, far = (jnp.where(even, right, left), jnp.where(even, left, right))
     edges_ref[...] = jnp.concatenate([near, far], axis=0).astype(BF)
+    even_row = parity_ref[0:1, 0:1] > 0.5
+    reach = RADIUS * EDGE
+    for out_ref, part in ((corner_near_ref, near), (corner_far_ref, far)):
+        out_ref[...] = jnp.where(even_row, part[:reach], part[rows * EDGE - reach :]).astype(BF)
     lane = lax.broadcasted_iota(jnp.int32, (1, width), 1)
     scale_row = jnp.zeros((1, width), F32)
     for h in range(heads):
@@ -146,6 +153,8 @@
     row_near_ref,
     col_near_ref,
     col_far_ref,
+    corner_near_ref,
+    corner_far_ref,
     rows_ref,
     q_norm_ref,
     q_unit_ref,
@@ -182,7 +191,14 @@
     gain = rows_ref[0:1]
     scale_row = rows_ref[1:2]
     up, down = by_side("row", row_near_ref[...].astype(F32), row_far_ref[...].astype(F32))
-    left, right = by_side("col", col_near_ref[...].astype(F32), col_far_ref[...].astype(F32))
+    even = lax.rem(lax.axis_index("row"), 2) == 0
+    sides = []
+    for col_ref, corner_ref in ((col_near_ref, corner_near_ref), (col_far_ref, corner_far_ref)):
+        col, corner = (col_ref[...].astype(F32), corner_ref[...].astype(F32))
+        above = jnp.concatenate([corner, col], axis=0)
+        below = jnp.concatenate([col, corner], axis=0)
+        sides.append(jnp.where(even, above, below))
+    left, right = by_side("col", *sides)
     own = tok_ref[...].astype(F32)
     blank = jnp.zeros((SIDE - EDGE, width), F32)
     pieces = []
@@ -573,6 +589,23 @@
     return (swap(near, axis, 1), lax.ppermute(far, ("row", "col"), pairs))
 
 
+def far_place(index, count):
+    other = index - 1 if index % 2 == 0 else index + 1
+    return other if 0 <= other < count else index
+
+
+def corner_swapped(value, far_col):
+    n_row, n_col = (lax.axis_size("row"), lax.axis_size("col"))
+    pairs = []
+    for row in range(n_row):
+        for col in range(n_col):
+            target = (far_place(row, n_row), far_place(col, n_col) if far_col else col ^ 1)
+            if target == (row, col):
+                target = (n_row - 1 - row, col)
+            pairs.append((row * n_col + col, target[0] * n_col + target[1]))
+    return lax.ppermute(value, ("row", "col"), pairs)
+
+
 def swap(value, axis, step):
     count = lax.axis_size(axis)
     return lax.ppermute(value, axis, [(i, i ^ step) for i in range(count)])
@@ -605,11 +638,13 @@
     dm = d_merged.reshape(groups, depth)
     tile = shape((rows * cols, width), F32)
     half = shape((rows * cols, width), BF)
-    edges, two_rows, q_norm, q_unit, d_y, d_attn = pl.pallas_call(
+    corner = shape((RADIUS * EDGE, width), BF)
+    edges, *corners, two_rows, q_norm, q_unit, d_y, d_attn = pl.pallas_call(
         own_kernel,
-        out_shape=(shape((2 * rows * EDGE, width), BF), shape((8, width), F32), tile, tile, tile, half),
+        out_shape=(shape((2 * rows * EDGE, width), BF), corner, corner)
+        + (shape((8, width), F32), tile, tile, tile, half),
         in_specs=vmem(10),
-        out_specs=tuple(vmem(6)),
+        out_specs=tuple(vmem(8)),
         scratch_shapes=[pltpu.VMEM((width // LANES, rows, cols, LANES), F32)],
         compiler_params=params,
         cost_estimate=pl.CostEstimate(flops=10**9, bytes_accessed=10**6, transcendentals=0),
@@ -625,13 +660,22 @@
         w_out,
         w_merge,
     )
-    edge_near, edge_far, dm_pair = pl.pallas_call(
+    half_edge = shape(((rows + RADIUS) * EDGE, width), BF)
+    edge_near, edge_far = pl.pallas_call(
         edge_kernel,
-        out_shape=(edge, edge, shape((2 * groups, depth), BF)),
-        in_specs=vmem(5),
-        out_specs=tuple(vmem(3)),
+        out_shape=(half_edge, half_edge),
+        in_specs=vmem(2),
+        out_specs=tuple(vmem(2)),
         compiler_params=less,
-    )(edges, row_far, row_near, d_merged, swap(dm, "row", 2))
+    )(edges, row_near)
+    corners = [corner_swapped(value, bool(i)) for i, value in enumerate(corners)]
+    dm_pair = pl.pallas_call(
+        pair_kernel,
+        out_shape=shape((2 * groups, depth), BF),
+        in_specs=vmem(2),
+        out_specs=vmem(1)[0],
+        compiler_params=less,
+    )(d_merged, swap(dm, "row", 2))
     dms = [swap(dm_pair, "row", 4), dm_pair]
     col_near, col_far = swapped(edge_near, edge_far, "col")
 
@@ -663,7 +707,7 @@
             shape((groups, 4 * width), BF),
             shape((8, width), F32),
         ),
-        in_specs=vmem(13),
+        in_specs=vmem(15),
         out_specs=tuple(vmem(7)),
         scratch_shapes=[pltpu.VMEM((width // LANES, rows, cols, LANES), F32)],
         compiler_params=params,
@@ -675,6 +719,7 @@
         row_near,
         col_near,
         col_far,
+        *corners,
         two_rows,
         q_norm,
         q_unit,

time: 35.1 us -> 38.4 us (1.094)
  waiting for transfers between devices: 5.92 us -> 8.01 us
  starting transfers between devices: 21.5 us -> 22.8 us
    ppermute x0 -> x2, starting transfers between devices: none -> 3.15 us  [corner_swapped(): return lax.ppermute(value, ('row', 'col'), pairs)]
    ppermute x0 -> x2, waiting for transfers between devices: none -> 2.83 us  [corner_swapped(): return lax.ppermute(value, ('row', 'col'), pairs)]
    ppermute x15, starting transfers between devices: 16.4 us -> 15 us  [swap(): return lax.ppermute(value, axis, [(i, i ^ step) for i in range(count)])]
    ppermute x15, waiting for transfers between devices: 3.97 us -> 2.84 us  [swap(): return lax.ppermute(value, axis, [(i, i ^ step) for i in range(count)])]
    ppermute x4, starting transfers between devices: 5.14 us -> 4.61 us  [swapped(): return (swap(near, axis, 1), lax.ppermute(far, ('row', 'col'), pairs))]
    ppermute x4, waiting for transfers between devices: 1.95 us -> 2.34 us  [swapped(): return (swap(near, axis, 1), lax.ppermute(far, ('row', 'col'), pairs))]
  transfers between devices with their start and end apart: 19 -> 21, of which waited for: 7 -> 7; matrix products, arithmetic and copies ran while one was open for 0% -> 0% of each run, Pallas kernels for 13% -> 12%
where the time goes in v8:
time: 38.4 us; the launch traced here: 38.3 us
  starting transfers between devices  22.8 us (59%)
  waiting for transfers between devices  8.01 us (21%)
  Pallas kernels  6.01 us (16%)
  between operations  0.84 us (2%)
  local copies, waits for them, and re-layouts  0.63 us (2%)
    ppermute x15, starting transfers between devices, swap(): return lax.ppermute(value, axis, [(i, i ^ step) for i in range(count)])  15 us
    ppermute x4, starting transfers between devices, swapped(): return (swap(near, axis, 1), lax.ppermute(far, ('row', 'col'), pairs))  4.61 us
    ppermute x2, starting transfers between devices, corner_swapped(): return lax.ppermute(value, ('row', 'col'), pairs)  3.15 us
    ppermute x15, waiting for transfers between devices, swap(): return lax.ppermute(value, axis, [(i, i ^ step) for i in range(count)])  2.84 us
    ppermute x2, waiting for transfers between devices, corner_swapped(): return lax.ppermute(value, ('row', 'col'), pairs)  2.83 us
    ppermute x4, waiting for transfers between devices, swapped(): return (swap(near, axis, 1), lax.ppermute(far, ('row', 'col'), pairs))  2.34 us
    pallas_call x1, Pallas kernels, on_device(): pl.pallas_call(functools.partial(layer_kernel, sizes), out_shape=(shape((...  1.97 us
    pallas_call x1, Pallas kernels, on_device(): pl.pallas_call(output_kernel, out_shape=(shape((rows, cols, width), BF),...  0.9 us
  transfers between devices with their start and end apart: 21, of which 7 were waited for; matrix products, arithmetic and copies ran while one was open for 0% of the time, Pallas kernels for 12%

profile of v8, /device:TPU:0, one launch (start us, length us, event | category | flops | bytes accessed | tf_op | source)
XLA Modules:
  0.0 38.3 jit_solution(5681574761528480874)
XLA Ops:
  0.6 3.1 %collective-permute-start = (bf16[4,32,256]{2,1,0:T(8,128)(2,1)}, bf16[4,32,256]{2,1,0:T(8,128)(2,1)S(1)}, u32[]{:S(2)}, u32[]{:S(2)}) collective-permute-start(bf16[4,32,256]{2,1,0:T(8,128)(2,1)} %tok_ref.3), channel_id=1, source_target_pairs={{0,1},{1,0},{2,3},{3,2},{4,8},{5,9},{6,10},{7,11},{8,4},{9,5},{10,... | collective-permute-start | bytes 196616 | tf_op jit(solution)/shard_map/ppermute | solution.py:589
  3.7 0.0 collective-permute-start.1
  3.8 0.0 copy-start
  3.8 0.0 copy-start.1
  3.8 0.0 copy-start.4
  3.8 0.0 copy-start.5
  3.8 1.6 %collective-permute-start.6 = (bf16[32,512]{1,0:T(8,128)(2,1)}, bf16[32,512]{1,0:T(8,128)(2,1)S(1)}, u32[]{:S(2)}, u32[]{:S(2)}) collective-permute-start(bf16[32,512]{1,0:T(8,128)(2,1)} %bitcast.4), channel_id=1, source_target_pairs={{0,8},{4,12},{8,0},{12,4},{16,24},{20,28},{24,16},{28,20},{1,9},{5... | collective-permute-start | bytes 98312 | tf_op jit(solution)/shard_map/ppermute | solution.py:611
  5.4 0.0 copy-start.6
  5.4 0.0 copy-start.7
  5.4 0.0 copy-done
  5.4 0.0 copy-done.1
  5.4 0.0 copy-done.2
  5.4 0.0 copy-done.3
  5.4 0.0 copy-done.4
  5.5 0.0 copy-done.5
  5.5 0.6 %copy-done.6 = f32[256]{0:T(256)S(1)} copy-done((f32[256]{0:T(256)S(1)}, f32[256]{0:T(256)}, u32[]{:S(2)}) %copy-start.6) | copy-done | bytes 1048
  6.1 0.0 copy-done.7
  6.1 0.8 %shard_map.144 = (bf16[32,256]{1,0:T(8,128)(2,1)S(1)}, bf16[12,256]{1,0:T(8,128)(2,1)S(1)}, bf16[12,256]{1,0:T(8,128)(2,1)S(1)}, f32[8,256]{1,0:T(8,128)S(1)}, f...) custom-call(bf16[256,256]{1,0:T(8,128)(2,1)S(1)} %get-tuple-element.57.on, ...), custom_call_target="tpu_custom_call" | custom-call | flops 1000000000 | bytes 1000000 | tf_op jit(solution)/shard_map/pallas_call | solution.py:642
  6.9 0.0 collective-permute-done.1.near_ref.row_near_ref
  6.9 1.6 %collective-permute-start.2 = (bf16[28,256]{1,0:T(8,128)(2,1)S(1)}, bf16[28,256]{1,0:T(8,128)(2,1)S(1)}, u32[]{:S(2)}, u32[]{:S(2)}) collective-permute-start(bf16[28,256]{1,0:T(8,128)(2,1)S(1)} %get-tuple-element.60), channel_id=1, source_target_pairs={{0,1},{1,0},{2,3},{3,2},{4,5},{5,4},{6,7},{7,6},{8,9},{9,8},{10,11... | collective-permute-start | bytes 43016 | tf_op jit(solution)/shard_map/ppermute | solution.py:611
  8.6 0.0 collective-permute-start.3
  8.6 3.1 %collective-permute-start.4 = (bf16[12,256]{1,0:T(8,128)(2,1)S(1)}, bf16[12,256]{1,0:T(8,128)(2,1)S(1)}, u32[]{:S(2)}, u32[]{:S(2)}) collective-permute-start(bf16[12,256]{1,0:T(8,128)(2,1)S(1)} %get-tuple-element.62), channel_id=1, source_target_pairs={{0,1},{1,0},{2,3},{3,2},{4,9},{5,8},{6,11},{7,10},{8,5},{9,4},{10,... | collective-permute-start | bytes 18440 | tf_op jit(solution)/shard_map/ppermute | solution.py:606
  11.7 0.0 collective-permute-done.6.dm_next_ref
  11.7 0.0 collective-permute-start.5
  11.7 1.6 %collective-permute-done.4.corner_near_ref = bf16[12,256]{1,0:T(8,128)(2,1)S(1)} collective-permute-done((bf16[12,256]{1,0:T(8,128)(2,1)S(1)}, bf16[12,256]{1,0:T(8,128)(2,1)S(1)}, u32[]{:S(2)}, u32[]{:S(2)}) %collective-permute-start.4) | collective-permute-done | bytes 6176 | tf_op jit(solution)/shard_map/ppermute | solution.py:606
  13.3 1.1 %collective-permute-start.7 = (bf16[64,512]{1,0:T(8,128)(2,1)S(1)}, bf16[64,512]{1,0:T(8,128)(2,1)S(1)}, u32[]{:S(2)}, u32[]{:S(2)}) collective-permute-start(bf16[64,512]{1,0:T(8,128)(2,1)S(1)} %shard_map.148.refs_1_), channel_id=1, source_target_pairs={{0,16},{4,20},{8,24},{12,28},{16,0},{20,4},{24,8},{28,12},{1,17},{... | collective-permute-start | bytes 196616 | tf_op jit(solution)/shard_map/ppermute | solution.py:611
  14.5 1.2 %collective-permute-done.5.corner_far_ref = bf16[12,256]{1,0:T(8,128)(2,1)S(1)} collective-permute-done((bf16[12,256]{1,0:T(8,128)(2,1)S(1)}, bf16[12,256]{1,0:T(8,128)(2,1)S(1)}, u32[]{:S(2)}, u32[]{:S(2)}) %collective-permute-start.5) | collective-permute-done | bytes 6176 | tf_op jit(solution)/shard_map/ppermute | solution.py:606
  15.7 0.0 collective-permute-done.row_far_ref
  15.7 0.0 collective-permute-done.2.col_near_ref
  15.7 0.0 collective-permute-done.3.col_far_ref
  15.7 2.0 %shard_map.146 = (f32[480,256]{1,0:T(8,128)S(1)}, bf16[128,256]{1,0:T(8,128)(2,1)S(1)}, bf16[128,256]{1,0:T(8,128)(2,1)S(1)}, bf16[480,512]{1,0:T(8,128)(2,1)S(1...) custom-call(bf16[256,256]{1,0:T(8,128)(2,1)S(1)} %get-tuple-element.57.ones_ref, ...), custom_call_target="tpu_custom_call" | custom-call | flops 4000000000 | bytes 1000000 | tf_op jit(solution)/shard_map/pallas_call | solution.py:699
  17.7 0.0 collective-permute-done.7.refs_0_
  17.7 0.6 %shard_map.149 = (bf16[128,512]{1,0:T(8,128)(2,1)S(1)}, bf16[4,32,1152]{2,1,0:T(8,128)(2,1)S(1)}, f32[4,32,1024]{2,1,0:T(8,128)S(1)}, bf16[4,32,128]{2,1,0:T(8,128)(2,1)S(1)}) custom-call(f32[480,256]{1,0:T(8,128)S(1)} %get-tuple-element.73.x_ref, bf16[128,256]{1,0:T(8,128)(2,1)S(1)} %get-tuple-element.74.d_query_ref, ...), custom_call_target="tpu_custom_call" | custom-call | flops 1000000000 | bytes 1000000 | tf_op jit(solution)/shard_map/pallas_call | solution.py:731
  18.3 0.1 collective-permute-start.8
  18.4 0.5 %shard_map.150 = (f32[320,256]{1,0:T(8,128)S(1)}, bf16[40,256]{1,0:T(8,128)(2,1)S(1)}, bf16[40,256]{1,0:T(8,128)(2,1)S(1)}, f32[8,128]{1,0:T(8,128)S(1)}) custom-call(f32[480,256]{1,0:T(8,128)S(1)} %get-tuple-element.73.x_ref, bf16[128,256]{1,0:T(8,128)(2,1)S(1)} %get-tuple-element.74.d_query_ref, bf16[480,512]{1,0:T(8,128)(2,1)S(1)} %get-tuple-element.75.d_kv_ref, ...), custom_call_target="tpu_custom_call" | custom-call | flops 500000000 | bytes 1000000 | tf_op jit(solution)/shard_map/pallas_call | solution.py:739
  18.9 0.6 %collective-permute-start.9 = (f32[8,128]{1,0:T(8,128)S(1)}, f32[8,128]{1,0:T(8,128)S(1)}, u32[]{:S(2)}, u32[]{:S(2)}) collective-permute-start(f32[8,128]{1,0:T(8,128)S(1)} %get-tuple-element.81.small_ref), channel_id=1, source_target_pairs={{0,4},{4,0},{8,12},{12,8},{16,20},{20,16},{24,28},{28,24},{1,5},{5... | collective-permute-start | bytes 12296 | tf_op jit(solution)/shard_map/ppermute | solution.py:611
  19.4 0.1 collective-permute-start.13
  19.5 0.7 %collective-permute-done.9.small_near_ref = f32[8,128]{1,0:T(8,128)S(1)} collective-permute-done((f32[8,128]{1,0:T(8,128)S(1)}, f32[8,128]{1,0:T(8,128)S(1)}, u32[]{:S(2)}, u32[]{:S(2)}) %collective-permute-start.9) | collective-permute-done | bytes 4128 | tf_op jit(solution)/shard_map/ppermute | solution.py:611
  20.3 0.0 collective-permute-done.8.got_ref
  20.3 0.1 shard_map.151
  20.4 1.2 %collective-permute-start.10 = (bf16[328,128]{1,0:T(8,128)(2,1)S(1)}, bf16[328,128]{1,0:T(8,128)(2,1)S(1)}, u32[]{:S(2)}, u32[]{:S(2)}) collective-permute-start(bf16[328,128]{1,0:T(8,128)(2,1)S(1)} %get-tuple-element.85), channel_id=1, source_target_pairs={{0,24},{4,28},{8,16},{12,20},{16,8},{20,12},{24,0},{28,4},{1,25},{... | collective-permute-start | bytes 251912 | tf_op jit(solution)/shard_map/ppermute | solution.py:611
  21.6 1.9 %collective-permute-start.11 = (bf16[328,128]{1,0:T(8,128)(2,1)S(1)}, bf16[328,128]{1,0:T(8,128)(2,1)S(1)}, u32[]{:S(2)}, u32[]{:S(2)}) collective-permute-start(bf16[328,128]{1,0:T(8,128)(2,1)S(1)} %get-tuple-element.86), channel_id=1, source_target_pairs={{0,16},{4,20},{8,24},{12,28},{16,0},{20,4},{24,8},{28,12},{1,17},{... | collective-permute-start | bytes 251912 | tf_op jit(solution)/shard_map/ppermute | solution.py:611
  23.5 0.5 %collective-permute-start.12 = (bf16[328,128]{1,0:T(8,128)(2,1)S(1)}, bf16[328,128]{1,0:T(8,128)(2,1)S(1)}, u32[]{:S(2)}, u32[]{:S(2)}) collective-permute-start(bf16[328,128]{1,0:T(8,128)(2,1)S(1)} %get-tuple-element.87), channel_id=1, source_target_pairs={{0,8},{4,12},{8,0},{12,4},{16,24},{20,28},{24,16},{28,20},{1,9},{5... | collective-permute-start | bytes 251912 | tf_op jit(solution)/shard_map/ppermute | solution.py:611
  23.9 1.9 %collective-permute-start.17 = (bf16[40,256]{1,0:T(8,128)(2,1)S(1)}, bf16[40,256]{1,0:T(8,128)(2,1)S(1)}, u32[]{:S(2)}, u32[]{:S(2)}) collective-permute-start(bf16[40,256]{1,0:T(8,128)(2,1)S(1)} %get-tuple-element.95), channel_id=1, source_target_pairs={{0,1},{1,0},{2,3},{3,2},{4,5},{5,4},{6,7},{7,6},{8,9},{9,8},{10,11... | collective-permute-start | bytes 61448 | tf_op jit(solution)/shard_map/ppermute | solution.py:611
  25.9 0.0 collective-permute-done.13.refs_7_
  25.9 0.0 collective-permute-start.18
  25.9 0.8 %collective-permute-done.10.refs_3_ = bf16[328,128]{1,0:T(8,128)(2,1)S(1)} collective-permute-done((bf16[328,128]{1,0:T(8,128)(2,1)S(1)}, bf16[328,128]{1,0:T(8,128)(2,1)S(1)}, u32[]{:S(2)}, u32[]{:S(2)}) %collective-permute-start.10) | collective-permute-done | bytes 84000 | tf_op jit(solution)/shard_map/ppermute | solution.py:611
  26.7 1.1 %collective-permute-done.11.refs_4_ = bf16[328,128]{1,0:T(8,128)(2,1)S(1)} collective-permute-done((bf16[328,128]{1,0:T(8,128)(2,1)S(1)}, bf16[328,128]{1,0:T(8,128)(2,1)S(1)}, u32[]{:S(2)}, u32[]{:S(2)}) %collective-permute-start.11) | collective-permute-done | bytes 84000 | tf_op jit(solution)/shard_map/ppermute | solution.py:611
  27.8 0.1 collective-permute-done.12.refs_5_
  27.9 0.3 shard_map.152
  28.2 2.2 %collective-permute-start.14 = (bf16[200,128]{1,0:T(8,128)(2,1)S(1)}, bf16[200,128]{1,0:T(8,128)(2,1)S(1)}, u32[]{:S(2)}, u32[]{:S(2)}) collective-permute-start(bf16[200,128]{1,0:T(8,128)(2,1)S(1)} %get-tuple-element.91), channel_id=1, source_target_pairs={{0,3},{1,2},{2,1},{3,0},{4,7},{5,6},{6,5},{7,4},{8,11},{9,10},{10,... | collective-permute-start | bytes 153608 | tf_op jit(solution)/shard_map/ppermute | solution.py:611
  30.4 1.7 %collective-permute-start.15 = (bf16[200,128]{1,0:T(8,128)(2,1)S(1)}, bf16[200,128]{1,0:T(8,128)(2,1)S(1)}, u32[]{:S(2)}, u32[]{:S(2)}) collective-permute-start(bf16[200,128]{1,0:T(8,128)(2,1)S(1)} %get-tuple-element.92), channel_id=1, source_target_pairs={{0,2},{1,3},{2,0},{3,1},{4,6},{5,7},{6,4},{7,5},{8,10},{9,11},{10,... | collective-permute-start | bytes 153608 | tf_op jit(solution)/shard_map/ppermute | solution.py:611
  32.1 0.6 %collective-permute-start.16 = (bf16[200,128]{1,0:T(8,128)(2,1)S(1)}, bf16[200,128]{1,0:T(8,128)(2,1)S(1)}, u32[]{:S(2)}, u32[]{:S(2)}) collective-permute-start(bf16[200,128]{1,0:T(8,128)(2,1)S(1)} %get-tuple-element.93), channel_id=1, source_target_pairs={{0,1},{1,0},{2,3},{3,2},{4,5},{5,4},{6,7},{7,6},{8,9},{9,8},{10,11... | collective-permute-start | bytes 153608 | tf_op jit(solution)/shard_map/ppermute | solution.py:611
  32.7 0.0 collective-permute-done.17.near_ref
  32.7 0.0 collective-permute-done.18.far_ref
  32.7 1.5 %collective-permute-start.19 = (bf16[96,256]{1,0:T(8,128)(2,1)S(1)}, bf16[96,256]{1,0:T(8,128)(2,1)S(1)}, u32[]{:S(2)}, u32[]{:S(2)}) collective-permute-start(bf16[96,256]{1,0:T(8,128)(2,1)S(1)} %get-tuple-element.98), channel_id=1, source_target_pairs={{0,1},{1,0},{2,3},{3,2},{4,8},{5,9},{6,10},{7,11},{8,4},{9,5},{10,... | collective-permute-start | bytes 147464 | tf_op jit(solution)/shard_map/ppermute | solution.py:589
  34.3 0.0 collective-permute-start.20
  34.3 0.9 %shard_map.147 = (bf16[4,32,256]{2,1,0:T(8,128)(2,1)}, bf16[2,16,512]{2,1,0:T(8,128)(2,1)}) custom-call(bf16[128,256]{1,0:T(8,128)(2,1)S(1)} %get-tuple-element.69.y_ref, bf16[32,1024]{1,0:T(8,128)(2,1)S(1)} %get-tuple-element.70.group_ref, bf16[1024,512]{1,0:T(8,128)(2,1)S(1)} %copy-done.1), custom_call_target="tpu_custom_call" | custom-call | flops 1000000000 | bytes 1000000 | tf_op jit(solution)/shard_map/pallas_call | solution.py:749
  35.2 2.3 %collective-permute-done.19.far_ref = bf16[96,256]{1,0:T(8,128)(2,1)S(1)} collective-permute-done((bf16[96,256]{1,0:T(8,128)(2,1)S(1)}, bf16[96,256]{1,0:T(8,128)(2,1)S(1)}, u32[]{:S(2)}, u32[]{:S(2)}) %collective-permute-start.19) | collective-permute-done | bytes 49184 | tf_op jit(solution)/shard_map/ppermute | solution.py:589
  37.5 0.0 collective-permute-done.20.near_ref
  37.5 0.0 collective-permute-done.14.d_ref
  37.5 0.0 collective-permute-done.15.c_ref
  37.5 0.0 collective-permute-done.16.b_ref
  37.5 0.7 %shard_map.154 = (f32[32,192]{1,0:T(8,128)}, f32[32,64]{1,0:T(8,128)}, f32[128,128]{1,0:T(8,128)}, f32[1,256]{1,0:T(1,128)}, f32[4]{0:T(128)}, /*index=5*/bf16[4,32,256]{2,1,0:T(8,128)(2,1)}) custom-call(bf16[200,128]{1,0:T(8,128)(2,1)S(1)} %get-tuple-element.90.a_ref, bf16[200,128]{1,0:T(8,128)(2,1)S(1)} %collective-permute-done.14.d_ref, ...), custom_call_target="tpu_custom_call" | custom-call | tf_op jit(solution)/shard_map/pallas_call | solution.py:795
  (6 shorter events, 0.1 us)
Async XLA Ops:
  0.6 15.1 %collective-permute-start = (bf16[4,32,256]{2,1,0:T(8,128)(2,1)}, bf16[4,32,256]{2,1,0:T(8,128)(2,1)S(1)}, u32[]{:S(2)}, u32[]{:S(2)}) collective-permute-start(bf16[4,32,256]{2,1,0:T(8,128)(2,1)} %tok_ref.3), channel_id=1, source_target_pairs={{0,1},{1,0},{2,3},{3,2},{4,8},{5,9},{6,10},{7,11},{8,4},{9,5},{10,... | collective-permute-start | bytes 196616 | tf_op jit(solution)/shard_map/ppermute | solution.py:589
  3.7 3.1 %collective-permute-start.1 = (bf16[4,32,256]{2,1,0:T(8,128)(2,1)}, bf16[4,32,256]{2,1,0:T(8,128)(2,1)S(1)}, u32[]{:S(2)}, u32[]{:S(2)}) collective-permute-start(bf16[4,32,256]{2,1,0:T(8,128)(2,1)} %tok_ref.3), channel_id=1, source_target_pairs={{0,4},{4,0},{8,12},{12,8},{16,20},{20,16},{24,28},{28,24},{1,5},{5... | collective-permute-start | bytes 196616 | tf_op jit(solution)/shard_map/ppermute | solution.py:611
  3.8 1.7 %copy-start = (bf16[2,16,512]{2,1,0:T(8,128)(2,1)S(1)}, bf16[2,16,512]{2,1,0:T(8,128)(2,1)}, u32[]{:S(2)}) copy-start(bf16[2,16,512]{2,1,0:T(8,128)(2,1)} %dm_ref.3) | copy-start | bytes 98308
  3.8 1.7 %copy-start.1 = (bf16[1024,512]{1,0:T(8,128)(2,1)S(1)}, bf16[1024,512]{1,0:T(8,128)(2,1)}, u32[]{:S(2)}) copy-start(bf16[1024,512]{1,0:T(8,128)(2,1)} %wmerge_ref.3) | copy-start | bytes 3145732
  3.8 1.7 %copy-start.2 = (bf16[256,768]{1,0:T(8,128)(2,1)S(1)}, bf16[256,768]{1,0:T(8,128)(2,1)}, u32[]{:S(2)}) copy-start(bf16[256,768]{1,0:T(8,128)(2,1)} %wqkv_ref.5) | copy-start | bytes 1179652
  3.8 1.7 %copy-start.3 = (bf16[256,256]{1,0:T(8,128)(2,1)S(1)}, bf16[256,256]{1,0:T(8,128)(2,1)}, u32[]{:S(2)}) copy-start(bf16[256,256]{1,0:T(8,128)(2,1)} %wout_ref.3) | copy-start | bytes 393220
  3.8 1.7 %copy-start.4 = (bf16[4,32,256]{2,1,0:T(8,128)(2,1)S(1)}, bf16[4,32,256]{2,1,0:T(8,128)(2,1)}, u32[]{:S(2)}) copy-start(bf16[4,32,256]{2,1,0:T(8,128)(2,1)} %dskip_ref.1) | copy-start | bytes 196612
  3.8 1.7 %copy-start.5 = (bf16[4,32,256]{2,1,0:T(8,128)(2,1)S(1)}, bf16[4,32,256]{2,1,0:T(8,128)(2,1)}, u32[]{:S(2)}) copy-start(bf16[4,32,256]{2,1,0:T(8,128)(2,1)} %tok_ref.3) | copy-start | bytes 196612
  3.8 7.9 %collective-permute-start.6 = (bf16[32,512]{1,0:T(8,128)(2,1)}, bf16[32,512]{1,0:T(8,128)(2,1)S(1)}, u32[]{:S(2)}, u32[]{:S(2)}) collective-permute-start(bf16[32,512]{1,0:T(8,128)(2,1)} %bitcast.4), channel_id=1, source_target_pairs={{0,8},{4,12},{8,0},{12,4},{16,24},{20,28},{24,16},{28,20},{1,9},{5... | collective-permute-start | bytes 98312 | tf_op jit(solution)/shard_map/ppermute | solution.py:611
  5.4 0.7 %copy-start.6 = (f32[256]{0:T(256)S(1)}, f32[256]{0:T(256)}, u32[]{:S(2)}) copy-start(f32[256]{0:T(256)} %param.9) | copy-start | bytes 3076
  5.4 0.7 %copy-start.7 = (f32[4]{0:T(128)S(1)}, f32[4]{0:T(128)}, u32[]{:S(2)}) copy-start(f32[4]{0:T(128)} %param.11) | copy-start | bytes 52
  6.9 8.8 %collective-permute-start.2 = (bf16[28,256]{1,0:T(8,128)(2,1)S(1)}, bf16[28,256]{1,0:T(8,128)(2,1)S(1)}, u32[]{:S(2)}, u32[]{:S(2)}) collective-permute-start(bf16[28,256]{1,0:T(8,128)(2,1)S(1)} %get-tuple-element.60), channel_id=1, source_target_pairs={{0,1},{1,0},{2,3},{3,2},{4,5},{5,4},{6,7},{7,6},{8,9},{9,8},{10,11... | collective-permute-start | bytes 43016 | tf_op jit(solution)/shard_map/ppermute | solution.py:611
  8.6 7.1 %collective-permute-start.3 = (bf16[28,256]{1,0:T(8,128)(2,1)S(1)}, bf16[28,256]{1,0:T(8,128)(2,1)S(1)}, u32[]{:S(2)}, u32[]{:S(2)}) collective-permute-start(bf16[28,256]{1,0:T(8,128)(2,1)S(1)} %get-tuple-element.61), channel_id=1, source_target_pairs={{0,4},{1,2},{2,1},{3,7},{4,0},{5,6},{6,5},{7,3},{8,12},{9,10},{10,... | collective-permute-start | bytes 43016 | tf_op jit(solution)/shard_map/ppermute | solution.py:589
  8.6 4.8 %collective-permute-start.4 = (bf16[12,256]{1,0:T(8,128)(2,1)S(1)}, bf16[12,256]{1,0:T(8,128)(2,1)S(1)}, u32[]{:S(2)}, u32[]{:S(2)}) collective-permute-start(bf16[12,256]{1,0:T(8,128)(2,1)S(1)} %get-tuple-element.62), channel_id=1, source_target_pairs={{0,1},{1,0},{2,3},{3,2},{4,9},{5,8},{6,11},{7,10},{8,5},{9,4},{10,... | collective-permute-start | bytes 18440 | tf_op jit(solution)/shard_map/ppermute | solution.py:606
  11.7 4.0 %collective-permute-start.5 = (bf16[12,256]{1,0:T(8,128)(2,1)S(1)}, bf16[12,256]{1,0:T(8,128)(2,1)S(1)}, u32[]{:S(2)}, u32[]{:S(2)}) collective-permute-start(bf16[12,256]{1,0:T(8,128)(2,1)S(1)} %get-tuple-element.63), channel_id=1, source_target_pairs={{0,28},{1,2},{2,1},{3,31},{4,8},{5,10},{6,9},{7,11},{8,4},{9,6},{1... | collective-permute-start | bytes 18440 | tf_op jit(solution)/shard_map/ppermute | solution.py:606
  13.3 4.3 %collective-permute-start.7 = (bf16[64,512]{1,0:T(8,128)(2,1)S(1)}, bf16[64,512]{1,0:T(8,128)(2,1)S(1)}, u32[]{:S(2)}, u32[]{:S(2)}) collective-permute-start(bf16[64,512]{1,0:T(8,128)(2,1)S(1)} %shard_map.148.refs_1_), channel_id=1, source_target_pairs={{0,16},{4,20},{8,24},{12,28},{16,0},{20,4},{24,8},{28,12},{1,17},{... | collective-permute-start | bytes 196616 | tf_op jit(solution)/shard_map/ppermute | solution.py:611
  18.3 2.0 %collective-permute-start.8 = (bf16[4,32,1152]{2,1,0:T(8,128)(2,1)S(1)}, bf16[4,32,1152]{2,1,0:T(8,128)(2,1)S(1)}, u32[]{:S(2)}, u32[]{:S(2)}) collective-permute-start(bf16[4,32,1152]{2,1,0:T(8,128)(2,1)S(1)} %get-tuple-element.77), channel_id=1, source_target_pairs={{0,4},{4,0},{8,12},{12,8},{16,20},{20,16},{24,28},{28,24},{1,5},{5... | collective-permute-start | bytes 884744 | tf_op jit(solution)/shard_map/ppermute | solution.py:611
  18.9 1.4 %collective-permute-start.9 = (f32[8,128]{1,0:T(8,128)S(1)}, f32[8,128]{1,0:T(8,128)S(1)}, u32[]{:S(2)}, u32[]{:S(2)}) collective-permute-start(f32[8,128]{1,0:T(8,128)S(1)} %get-tuple-element.81.small_ref), channel_id=1, source_target_pairs={{0,4},{4,0},{8,12},{12,8},{16,20},{20,16},{24,28},{28,24},{1,5},{5... | collective-permute-start | bytes 12296 | tf_op jit(solution)/shard_map/ppermute | solution.py:611
  19.4 6.4 %collective-permute-start.13 = (bf16[128,512]{1,0:T(8,128)(2,1)S(1)}, bf16[128,512]{1,0:T(8,128)(2,1)S(1)}, u32[]{:S(2)}, u32[]{:S(2)}) collective-permute-start(bf16[128,512]{1,0:T(8,128)(2,1)S(1)} %get-tuple-element.88.refs_6_), channel_id=1, source_target_pairs={{0,4},{4,0},{8,12},{12,8},{16,20},{20,16},{24,28},{28,24},{1,5},{5... | collective-permute-start | bytes 393224 | tf_op jit(solution)/shard_map/ppermute | solution.py:611
  20.4 6.3 %collective-permute-start.10 = (bf16[328,128]{1,0:T(8,128)(2,1)S(1)}, bf16[328,128]{1,0:T(8,128)(2,1)S(1)}, u32[]{:S(2)}, u32[]{:S(2)}) collective-permute-start(bf16[328,128]{1,0:T(8,128)(2,1)S(1)} %get-tuple-element.85), channel_id=1, source_target_pairs={{0,24},{4,28},{8,16},{12,20},{16,8},{20,12},{24,0},{28,4},{1,25},{... | collective-permute-start | bytes 251912 | tf_op jit(solution)/shard_map/ppermute | solution.py:611
  21.6 6.3 %collective-permute-start.11 = (bf16[328,128]{1,0:T(8,128)(2,1)S(1)}, bf16[328,128]{1,0:T(8,128)(2,1)S(1)}, u32[]{:S(2)}, u32[]{:S(2)}) collective-permute-start(bf16[328,128]{1,0:T(8,128)(2,1)S(1)} %get-tuple-element.86), channel_id=1, source_target_pairs={{0,16},{4,20},{8,24},{12,28},{16,0},{20,4},{24,8},{28,12},{1,17},{... | collective-permute-start | bytes 251912 | tf_op jit(solution)/shard_map/ppermute | solution.py:611
  23.5 4.5 %collective-permute-start.12 = (bf16[328,128]{1,0:T(8,128)(2,1)S(1)}, bf16[328,128]{1,0:T(8,128)(2,1)S(1)}, u32[]{:S(2)}, u32[]{:S(2)}) collective-permute-start(bf16[328,128]{1,0:T(8,128)(2,1)S(1)} %get-tuple-element.87), channel_id=1, source_target_pairs={{0,8},{4,12},{8,0},{12,4},{16,24},{20,28},{24,16},{28,20},{1,9},{5... | collective-permute-start | bytes 251912 | tf_op jit(solution)/shard_map/ppermute | solution.py:611
  23.9 8.8 %collective-permute-start.17 = (bf16[40,256]{1,0:T(8,128)(2,1)S(1)}, bf16[40,256]{1,0:T(8,128)(2,1)S(1)}, u32[]{:S(2)}, u32[]{:S(2)}) collective-permute-start(bf16[40,256]{1,0:T(8,128)(2,1)S(1)} %get-tuple-element.95), channel_id=1, source_target_pairs={{0,1},{1,0},{2,3},{3,2},{4,5},{5,4},{6,7},{7,6},{8,9},{9,8},{10,11... | collective-permute-start | bytes 61448 | tf_op jit(solution)/shard_map/ppermute | solution.py:611
  25.9 6.8 %collective-permute-start.18 = (bf16[40,256]{1,0:T(8,128)(2,1)S(1)}, bf16[40,256]{1,0:T(8,128)(2,1)S(1)}, u32[]{:S(2)}, u32[]{:S(2)}) collective-permute-start(bf16[40,256]{1,0:T(8,128)(2,1)S(1)} %get-tuple-element.96), channel_id=1, source_target_pairs={{0,4},{1,2},{2,1},{3,7},{4,0},{5,6},{6,5},{7,3},{8,12},{9,10},{10,... | collective-permute-start | bytes 61448 | tf_op jit(solution)/shard_map/ppermute | solution.py:589
  28.2 9.3 %collective-permute-start.14 = (bf16[200,128]{1,0:T(8,128)(2,1)S(1)}, bf16[200,128]{1,0:T(8,128)(2,1)S(1)}, u32[]{:S(2)}, u32[]{:S(2)}) collective-permute-start(bf16[200,128]{1,0:T(8,128)(2,1)S(1)} %get-tuple-element.91), channel_id=1, source_target_pairs={{0,3},{1,2},{2,1},{3,0},{4,7},{5,6},{6,5},{7,4},{8,11},{9,10},{10,... | collective-permute-start | bytes 153608 | tf_op jit(solution)/shard_map/ppermute | solution.py:611
  30.4 7.1 %collective-permute-start.15 = (bf16[200,128]{1,0:T(8,128)(2,1)S(1)}, bf16[200,128]{1,0:T(8,128)(2,1)S(1)}, u32[]{:S(2)}, u32[]{:S(2)}) collective-permute-start(bf16[200,128]{1,0:T(8,128)(2,1)S(1)} %get-tuple-element.92), channel_id=1, source_target_pairs={{0,2},{1,3},{2,0},{3,1},{4,6},{5,7},{6,4},{7,5},{8,10},{9,11},{10,... | collective-permute-start | bytes 153608 | tf_op jit(solution)/shard_map/ppermute | solution.py:611
  32.1 5.4 %collective-permute-start.16 = (bf16[200,128]{1,0:T(8,128)(2,1)S(1)}, bf16[200,128]{1,0:T(8,128)(2,1)S(1)}, u32[]{:S(2)}, u32[]{:S(2)}) collective-permute-start(bf16[200,128]{1,0:T(8,128)(2,1)S(1)} %get-tuple-element.93), channel_id=1, source_target_pairs={{0,1},{1,0},{2,3},{3,2},{4,5},{5,4},{6,7},{7,6},{8,9},{9,8},{10,11... | collective-permute-start | bytes 153608 | tf_op jit(solution)/shard_map/ppermute | solution.py:611
  32.7 4.8 %collective-permute-start.19 = (bf16[96,256]{1,0:T(8,128)(2,1)S(1)}, bf16[96,256]{1,0:T(8,128)(2,1)S(1)}, u32[]{:S(2)}, u32[]{:S(2)}) collective-permute-start(bf16[96,256]{1,0:T(8,128)(2,1)S(1)} %get-tuple-element.98), channel_id=1, source_target_pairs={{0,1},{1,0},{2,3},{3,2},{4,8},{5,9},{6,10},{7,11},{8,4},{9,5},{10,... | collective-permute-start | bytes 147464 | tf_op jit(solution)/shard_map/ppermute | solution.py:589
  34.3 3.2 %collective-permute-start.20 = (bf16[96,256]{1,0:T(8,128)(2,1)S(1)}, bf16[96,256]{1,0:T(8,128)(2,1)S(1)}, u32[]{:S(2)}, u32[]{:S(2)}) collective-permute-start(bf16[96,256]{1,0:T(8,128)(2,1)S(1)} %get-tuple-element.99), channel_id=1, source_target_pairs={{0,4},{4,0},{8,12},{12,8},{16,20},{20,16},{24,28},{28,24},{1,5},{5... | collective-permute-start | bytes 147464 | tf_op jit(solution)/shard_map/ppermute | solution.py:611

commit v9 on v7

--- a/solution.py
+++ b/solution.py
@@ -312,7 +312,7 @@
         sum_refs[0][...] = sums.astype(BF)
         sum_refs[1][...] = group
         return
-    send_ref, keep_ref, keep_group_ref = sum_refs
+    send_ref, send_own_ref, keep_ref, keep_group_ref, sends, keeps, keep_groups = sum_refs
     per = width // n_row
     feats = 4 * width // n_row
     group = group.astype(F32)
@@ -323,25 +323,37 @@
             first = lax.slice_in_dim(value, 2 * q * size, (2 * q + 1) * size, axis=axis)
             second = lax.slice_in_dim(value, (2 * q + 1) * size, (2 * q + 2) * size, axis=axis)
             parts.append((jnp.where(even, first, second), jnp.where(even, second, first)))
-        (keep_ref[q], sums_send), (keep_group, group_send) = parts
-        keep_group_ref[q] = keep_group.astype(BF)
-        send_ref[q] = jnp.concatenate([sums_send, group_send], axis=1).astype(BF)
-
-
-def norm_kernel(
-    sizes, x_ref, d_query_ref, d_kv_ref, scale_part_ref, rows_ref, dy_ref, wqkv_ref, *refs
+        (keeps[q], sums_send), (keep_group, group_send) = parts
+        keep_groups[q] = keep_group.astype(BF)
+        sends[q] = jnp.concatenate([sums_send, group_send], axis=1).astype(BF)
+    chip = lax.axis_index("row") // 2
+    for step in range(n_row // 2):
+        at = partner(chip, step)
+        keep_ref[step] = keeps[at]
+        keep_group_ref[step] = keep_groups[at]
+        if step == 0:
+            send_own_ref[...] = sends[at]
+        else:
+            send_ref[step - 1] = sends[at]
+
+
+def gain_kernel(
+    sizes,
+    x_ref,
+    d_query_ref,
+    d_kv_ref,
+    scale_part_ref,
+    wqkv_ref,
+    d_normed_ref,
+    small_ref,
 ):
     rows, cols, width, heads = sizes
-    gx_ref, side_near_ref, side_far_ref, small_ref = refs
     head_dim = width // heads
     wide = cols + 2 * SIDE
     ext_rows = rows + 2 * RADIUS
-    gain = rows_ref[0:1]
     lane = lax.broadcasted_iota(jnp.int32, (1, width), 1)
     x = x_ref[...]
-    inverse = lax.rsqrt(jnp.mean(x * x, axis=1, keepdims=True) + EPS)
-    unit = x * inverse
-    d_y = dy_ref[...]
+    unit = x * lax.rsqrt(jnp.mean(x * x, axis=1, keepdims=True) + EPS)
     from_q = mm_t(d_query_ref[...], wqkv_ref[:, :width])
     d_normed = mm_t(d_kv_ref[...], wqkv_ref[:, width:])
     pieces = []
@@ -354,7 +366,27 @@
             pieces.append(jnp.zeros((wide, width), F32))
     d_normed = d_normed + jnp.concatenate(pieces, axis=0)
     gain_part = jnp.sum(unit * d_normed, axis=0, keepdims=True)
-    scaled = gain * d_normed
+    d_normed_ref[...] = d_normed
+    scale_part = scale_part_ref[0:1]
+    scale_lane = lax.broadcasted_iota(jnp.int32, (1, LANES), 1)
+    scale_sums = jnp.zeros((1, LANES), F32)
+    for h in range(heads):
+        of_head = jnp.sum(jnp.where(lane // head_dim == h, scale_part, 0.0), axis=1, keepdims=True)
+        scale_sums = jnp.where(scale_lane == h, of_head, scale_sums)
+    small = [gain_part[:, i * LANES : (i + 1) * LANES] for i in range(width // LANES)] + [scale_sums]
+    small = jnp.concatenate(small + [jnp.zeros((8 - len(small), LANES), F32)], axis=0)
+    small_ref[...] = small
+
+
+def norm_kernel(sizes, x_ref, d_normed_ref, rows_ref, dy_ref, *refs):
+    rows, cols, width = sizes
+    gx_ref, side_near_ref, side_far_ref = refs
+    wide = cols + 2 * SIDE
+    ext_rows = rows + 2 * RADIUS
+    x = x_ref[...]
+    inverse = lax.rsqrt(jnp.mean(x * x, axis=1, keepdims=True) + EPS)
+    d_y = dy_ref[...]
+    scaled = rows_ref[0:1] * d_normed_ref[...]
     mean = jnp.mean(x * scaled, axis=1, keepdims=True)
     g_x = inverse * scaled - x * (inverse * inverse * inverse) * mean
 
@@ -374,15 +406,6 @@
     far, near = by_side("col", right, left)
     side_near_ref[...] = near.astype(BF)
     side_far_ref[...] = far.astype(BF)
-    scale_part = scale_part_ref[0:1]
-    scale_lane = lax.broadcasted_iota(jnp.int32, (1, LANES), 1)
-    scale_sums = jnp.zeros((1, LANES), F32)
-    for h in range(heads):
-        of_head = jnp.sum(jnp.where(lane // head_dim == h, scale_part, 0.0), axis=1, keepdims=True)
-        scale_sums = jnp.where(scale_lane == h, of_head, scale_sums)
-    small = [gain_part[:, i * LANES : (i + 1) * LANES] for i in range(width // LANES)] + [scale_sums]
-    small = jnp.concatenate(small + [jnp.zeros((8 - len(small), LANES), F32)], axis=0)
-    small_ref[...] = small
 
 
 def small_rows(small):
@@ -406,44 +429,38 @@
 
 
 def core_sum_kernel(got_ref, keep_ref, keep_group_ref, small_ref, small_near_ref, *refs):
-    *out_refs, own_ref, own_group_ref, small_sum_ref, blocks_ref = refs
-    chips, per, width = keep_ref.shape
-    feats = keep_group_ref.shape[2]
+    *out_refs, small_sum_ref = refs
+    width = keep_ref.shape[2]
     small = small_ref[...] + small_near_ref[...]
     small_sum_ref[...] = small
     small = small_rows(small)
-    chip = lax.axis_index("row") // 2
-    own_ref[...] = keep_ref[chip] + got_ref[chip, :, :width].astype(F32)
-    for q in range(chips):
-        sums = keep_ref[q] + got_ref[q, :, :width].astype(F32)
-        kept = keep_group_ref[q].astype(F32)
-        first, second = in_order("row", kept, got_ref[q, :, width:].astype(F32))
-        block = [stacked(sums), first, second, small]
-        blocks_ref[q] = jnp.concatenate(block, axis=0).astype(BF)
-    size = width // LANES * per
-    own_group_ref[...] = blocks_ref[chip][size : size + 2 * per]
-    for step, out_ref in enumerate(out_refs, 1):
-        out_ref[...] = blocks_ref[partner(chip, step)]
+    for i, out_ref in enumerate(out_refs):
+        sums = keep_ref[i + 1] + got_ref[i, :, :width].astype(F32)
+        kept = keep_group_ref[i + 1].astype(F32)
+        first, second = in_order("row", kept, got_ref[i, :, width:].astype(F32))
+        out_ref[...] = jnp.concatenate([stacked(sums), first, second, small], axis=0).astype(BF)
 
 
 def row_sum_kernel(sizes, *refs):
     rows, cols, width, n_col = sizes
-    own_ref, own_group_ref, small_ref, *refs = refs
+    keep_ref, keep_group_ref, got_own_ref, small_ref, *refs = refs
     got_refs, dm_ref, dm_near_ref, gx_ref, *refs = (refs[:3], *refs[3:])
     *out_refs, gx_sum_ref, slots_ref = refs
     gx_sum_ref[...] = gx_ref[...]
-    per = own_ref.shape[0]
-    feats = own_group_ref.shape[1]
+    per, feats = keep_group_ref.shape[1:]
+    got_own = got_own_ref[...].astype(F32)
+    own = keep_ref[0] + got_own[:, : 4 * width]
     size = 4 * width // LANES * per
 
     def summed(first, part):
         fourth, third, second = [part(ref[...].astype(F32)) for ref in got_refs]
         return (first + second) + (third + fourth)
 
-    sums = summed(stacked(own_ref[...]), lambda value: value[:size])
+    sums = summed(stacked(own), lambda value: value[:size])
     sums = unstacked(sums, per)
     small = summed(small_value(small_rows(small_ref[...])), lambda value: small_value(value[size + 2 * per :]))
-    group = [own_group_ref[...].astype(F32)]
+    own_group = in_order("row", keep_group_ref[0].astype(F32), got_own[:, 4 * width :])
+    group = [jnp.concatenate(own_group, axis=0)]
     group += [ref[...].astype(F32)[size : size + 2 * per] for ref in got_refs[::-1]]
     group = [part[i * per : (i + 1) * per] for i in range(2) for part in group]
     group = jnp.concatenate(group, axis=0)
@@ -641,15 +658,22 @@
     packed = packed and width // LANES < 4 and feats == LANES and depth // n_col == LANES and n_col == 4 and n_row == 8
     if packed:
         sum_shapes = (
-            shape((n_row // 2, per, 4 * width + feats), BF),
+            shape((n_row // 2 - 1, per, 4 * width + feats), BF),
+            shape((per, 4 * width + feats), BF),
             shape((n_row // 2, per, 4 * width), F32),
             shape((n_row // 2, per, feats), BF),
         )
+        sum_scratch = [
+            pltpu.VMEM((n_row // 2, per, 4 * width + feats), BF),
+            pltpu.VMEM((n_row // 2, per, 4 * width), F32),
+            pltpu.VMEM((n_row // 2, per, feats), BF),
+        ]
     else:
         sum_shapes = (
             shape((width, 4 * width), BF),
             shape((groups, 4 * width), BF),
         )
+        sum_scratch = []
     sizes = (rows, cols, width, heads, n_row, n_col)
     tall = ext_rows * wide
     x, y, d_query, d_kv, grad_out, group, scale_part = pl.pallas_call(
@@ -688,18 +712,26 @@
         out_shape=(shape((2 * len(dms) * groups, depth), BF),) + sum_shapes,
         in_specs=vmem(6 + len(dms)),
         out_specs=tuple(vmem(1 + len(sum_shapes))),
+        scratch_shapes=sum_scratch,
         compiler_params=params,
         cost_estimate=pl.CostEstimate(flops=10**9, bytes_accessed=10**6, transcendentals=0),
     )(x, d_query, d_kv, grad_out, group, two_rows, *dms)
+    d_normed, small = pl.pallas_call(
+        functools.partial(gain_kernel, (rows, cols, width, heads)),
+        out_shape=(shape((tall, width), F32), shape((8, LANES), F32)),
+        in_specs=vmem(5),
+        out_specs=tuple(vmem(2)),
+        compiler_params=params,
+        cost_estimate=pl.CostEstimate(flops=3 * 10**8, bytes_accessed=10**6, transcendentals=0),
+    )(x, d_query, d_kv, scale_part, w_qkv)
     gx, *sides = pl.pallas_call(
-        functools.partial(norm_kernel, (rows, cols, width, heads)),
-        out_shape=(shape((ext_rows * cols, width), F32), edge, edge, shape((8, LANES), F32)),
-        in_specs=vmem(7),
-        out_specs=tuple(vmem(4)),
+        functools.partial(norm_kernel, (rows, cols, width)),
+        out_shape=(shape((ext_rows * cols, width), F32), edge, edge),
+        in_specs=vmem(4),
+        out_specs=tuple(vmem(3)),
         compiler_params=params,
-        cost_estimate=pl.CostEstimate(flops=5 * 10**8, bytes_accessed=10**6, transcendentals=0),
-    )(x, d_query, d_kv, scale_part, two_rows, d_y, w_qkv)
-    *sides, small = sides
+        cost_estimate=pl.CostEstimate(flops=2 * 10**8, bytes_accessed=10**6, transcendentals=0),
+    )(x, d_normed, two_rows, d_y)
     sides = swapped(*sides, "col")
     skip_out, merged = pl.pallas_call(
         output_kernel,
@@ -722,15 +754,13 @@
         grad_tokens = add_rows(grad, *swapped(*rims, "row"), rows, cols)
         g_qkv, g_out, g_merge, g_gain, g_scale = plain_sums(width, *sums, small, dm)
     else:
-        send, *kept = sums
+        send, send_own, *kept = sums
         block = shape((4 * width // LANES * per + 2 * per + 8, LANES), BF)
-        *blocks, own, own_group, small = pl.pallas_call(
+        *blocks, small = pl.pallas_call(
             core_sum_kernel,
-            out_shape=(block, block, block)
-            + (shape((per, 4 * width), F32), shape((2 * per, LANES), BF), shape((8, LANES), F32)),
+            out_shape=(block, block, block, shape((8, LANES), F32)),
             in_specs=vmem(5),
-            out_specs=tuple(vmem(6)),
-            scratch_shapes=[pltpu.VMEM((n_row // 2,) + block.shape, BF)],
+            out_specs=tuple(vmem(4)),
             compiler_params=less,
             cost_estimate=pl.CostEstimate(flops=5 * 10**9, bytes_accessed=10**6, transcendentals=0),
         )(swap(send, "row", 1), *kept, small, swap(small, "row", 1))
@@ -739,11 +769,11 @@
         *slots, gx = pl.pallas_call(
             functools.partial(row_sum_kernel, (rows, cols, width, n_col)),
             out_shape=(slot,) * n_col + (shape(gx.shape, F32),),
-            in_specs=vmem(9),
+            in_specs=vmem(10),
             out_specs=tuple(vmem(n_col + 1)),
             scratch_shapes=[pltpu.VMEM((n_col,) + slot.shape, BF)],
             compiler_params=less,
-        )(own, own_group, small, *got, dm_core, swap(dm_core, "row", 1), gx)
+        )(*kept, swap(send_own, "row", 1), small, *got, dm_core, swap(dm_core, "row", 1), gx)
         got = [slots[0]] + [swap(slots[step], "col", step) for step in (3, 2, 1)]
         grad, *rims = side_call(gx, *sides)
         rims = swapped(*rims, "row")

time: 35.1 us -> 35 us (level)
  waiting for transfers between devices: 5.92 us -> 5.17 us
  starting transfers between devices: 21.5 us -> 22 us
    ppermute x15 -> x16, waiting for transfers between devices: 3.97 us -> 3.23 us  [swap(): return lax.ppermute(value, axis, [(i, i ^ step) for i in range(count)])]
    ppermute x15 -> x16, starting transfers between devices: 16.4 us -> 16.9 us  [swap(): return lax.ppermute(value, axis, [(i, i ^ step) for i in range(count)])]
  transfers between devices with their start and end apart: 19 -> 20, of which waited for: 7 -> 7; matrix products, arithmetic and copies ran while one was open for 0% -> 0% of each run, Pallas kernels for 13% -> 14%
where the time goes in v9:
time: 35 us; the launch traced here: 34.8 us
  starting transfers between devices  22 us (63%)
  Pallas kernels  6.15 us (18%)
  waiting for transfers between devices  5.17 us (15%)
  between operations  0.83 us (2%)
  local copies, waits for them, and re-layouts  0.63 us (2%)
    ppermute x16, starting transfers between devices, swap(): return lax.ppermute(value, axis, [(i, i ^ step) for i in range(count)])  16.9 us
    ppermute x4, starting transfers between devices, swapped(): return (swap(near, axis, 1), lax.ppermute(far, ('row', 'col'), pairs))  5.15 us
    ppermute x16, waiting for transfers between devices, swap(): return lax.ppermute(value, axis, [(i, i ^ step) for i in range(count)])  3.23 us
    pallas_call x1, Pallas kernels, on_device(): pl.pallas_call(functools.partial(layer_kernel, sizes), out_shape=(shape((...  1.95 us
    ppermute x4, waiting for transfers between devices, swapped(): return (swap(near, axis, 1), lax.ppermute(far, ('row', 'col'), pairs))  1.94 us
    pallas_call x1, Pallas kernels, on_device(): pl.pallas_call(output_kernel, out_shape=(shape((rows, cols, width), BF),...  0.91 us
    pallas_call x1, Pallas kernels, on_device(): pl.pallas_call(own_kernel, out_shape=(shape((2 * rows * EDGE, width), BF)...  0.79 us
    pallas_call x1, Pallas kernels, on_device(): pl.pallas_call(functools.partial(col_sum_kernel, (rows, cols, width)), ou...  0.75 us
  transfers between devices with their start and end apart: 20, of which 7 were waited for; matrix products, arithmetic and copies ran while one was open for 0% of the time, Pallas kernels for 14%

profile of v9, /device:TPU:0, one launch (start us, length us, event | category | flops | bytes accessed | tf_op | source)
XLA Modules:
  0.0 34.8 jit_solution(17144868617046226093)
XLA Ops:
  0.6 3.1 %collective-permute-start = (bf16[4,32,256]{2,1,0:T(8,128)(2,1)}, bf16[4,32,256]{2,1,0:T(8,128)(2,1)S(1)}, u32[]{:S(2)}, u32[]{:S(2)}) collective-permute-start(bf16[4,32,256]{2,1,0:T(8,128)(2,1)} %tok_ref.3), channel_id=1, source_target_pairs={{0,1},{1,0},{2,3},{3,2},{4,8},{5,9},{6,10},{7,11},{8,4},{9,5},{10,... | collective-permute-start | bytes 196616 | tf_op jit(solution)/shard_map/ppermute | solution.py:590
  3.7 0.0 collective-permute-start.1
  3.8 0.0 copy-start.1
  3.8 0.0 copy-start.2
  3.8 0.0 copy-start.3
  3.8 0.0 copy-start.4
  3.8 0.0 copy-start.5
  3.8 1.6 %collective-permute-start.2 = (bf16[32,512]{1,0:T(8,128)(2,1)}, bf16[32,512]{1,0:T(8,128)(2,1)S(1)}, u32[]{:S(2)}, u32[]{:S(2)}) collective-permute-start(bf16[32,512]{1,0:T(8,128)(2,1)} %bitcast.4), channel_id=1, source_target_pairs={{0,8},{4,12},{8,0},{12,4},{16,24},{20,28},{24,16},{28,20},{1,9},{5... | collective-permute-start | bytes 98312 | tf_op jit(solution)/shard_map/ppermute | solution.py:595
  5.4 0.0 copy-start.6
  5.4 0.0 copy-start.7
  5.4 0.0 copy-done
  5.4 0.0 copy-done.1
  5.4 0.0 copy-done.2
  5.4 0.0 copy-done.3
  5.4 0.0 copy-done.4
  5.5 0.0 copy-done.5
  5.5 0.6 %copy-done.6 = f32[256]{0:T(256)S(1)} copy-done((f32[256]{0:T(256)S(1)}, f32[256]{0:T(256)}, u32[]{:S(2)}) %copy-start.6) | copy-done | bytes 1048
  6.1 0.0 copy-done.7
  6.1 0.8 %shard_map.144 = (bf16[32,256]{1,0:T(8,128)(2,1)S(1)}, f32[8,256]{1,0:T(8,128)S(1)}, f32[128,256]{1,0:T(8,128)S(1)}, f32[128,256]{1,0:T(8,128)S(1)}, f32[128,256...) custom-call(bf16[256,256]{1,0:T(8,128)(2,1)S(1)} %get-tuple-element.56.ones_ref, f32[8,128]{1,0:T(8,128)S(1)} %get-tuple-element.57.parity_ref, ...), custom_call_target="tpu_custom_call" | custom-call | flops 1000000000 | bytes 1000000 | tf_op jit(solution)/shard_map/pallas_call | solution.py:625
  6.9 1.1 %collective-permute-done.2.dm_next_ref = bf16[32,512]{1,0:T(8,128)(2,1)S(1)} collective-permute-done((bf16[32,512]{1,0:T(8,128)(2,1)}, bf16[32,512]{1,0:T(8,128)(2,1)S(1)}, u32[]{:S(2)}, u32[]{:S(2)}) %collective-permute-start.2) | collective-permute-done | bytes 32800 | tf_op jit(solution)/shard_map/ppermute | solution.py:595
  8.0 0.0 collective-permute-done.far_ref.row_far_ref
  8.0 0.0 collective-permute-done.1.near_ref.row_near_ref
  8.0 1.6 %collective-permute-start.3 = (bf16[40,256]{1,0:T(8,128)(2,1)S(1)}, bf16[40,256]{1,0:T(8,128)(2,1)S(1)}, u32[]{:S(2)}, u32[]{:S(2)}) collective-permute-start(bf16[40,256]{1,0:T(8,128)(2,1)S(1)} %get-tuple-element.59), channel_id=1, source_target_pairs={{0,1},{1,0},{2,3},{3,2},{4,5},{5,4},{6,7},{7,6},{8,9},{9,8},{10,11... | collective-permute-start | bytes 61448 | tf_op jit(solution)/shard_map/ppermute | solution.py:595
  9.7 0.0 collective-permute-start.4
  9.7 1.5 %collective-permute-start.5 = (bf16[64,512]{1,0:T(8,128)(2,1)S(1)}, bf16[64,512]{1,0:T(8,128)(2,1)S(1)}, u32[]{:S(2)}, u32[]{:S(2)}) collective-permute-start(bf16[64,512]{1,0:T(8,128)(2,1)S(1)} %get-tuple-element.74.refs_1_), channel_id=1, source_target_pairs={{0,16},{4,20},{8,24},{12,28},{16,0},{20,4},{24,8},{28,12},{1,17},{... | collective-permute-start | bytes 196616 | tf_op jit(solution)/shard_map/ppermute | solution.py:595
  11.2 0.7 %collective-permute-done.3.col_near_ref = bf16[40,256]{1,0:T(8,128)(2,1)S(1)} collective-permute-done((bf16[40,256]{1,0:T(8,128)(2,1)S(1)}, bf16[40,256]{1,0:T(8,128)(2,1)S(1)}, u32[]{:S(2)}, u32[]{:S(2)}) %collective-permute-start.3) | collective-permute-done | bytes 20512 | tf_op jit(solution)/shard_map/ppermute | solution.py:595
  11.9 0.0 collective-permute-done.4.col_far_ref
  11.9 1.9 %shard_map.146 = (f32[480,256]{1,0:T(8,128)S(1)}, bf16[128,256]{1,0:T(8,128)(2,1)S(1)}, bf16[128,256]{1,0:T(8,128)(2,1)S(1)}, bf16[480,512]{1,0:T(8,128)(2,1)S(1...) custom-call(bf16[256,256]{1,0:T(8,128)(2,1)S(1)} %get-tuple-element.56.ones_ref, ...), custom_call_target="tpu_custom_call" | custom-call | flops 4000000000 | bytes 1000000 | tf_op jit(solution)/shard_map/pallas_call | solution.py:679
  13.8 0.3 collective-permute-done.5.refs_0_
  14.2 0.7 %shard_map.148 = (bf16[128,512]{1,0:T(8,128)(2,1)S(1)}, bf16[3,32,1152]{2,1,0:T(8,128)(2,1)S(1)}, bf16[32,1152]{1,0:T(8,128)(2,1)S(1)}, f32[4,32,1024]{2,1,0:T(8,128)S(1)}, bf16[4,32,128]{2,1,0:T(8,128)(2,1)S(1)}) custom-call(f32[480,256]{1,0:T(8,128)S(1)} %get-tuple-element.70.x_ref, bf16[128,256]{1,0:T(8,128)(2,1)S(1)} %get-tuple-element.71.d_query_ref, ...), custom_call_target="tpu_custom_call" | custom-call | flops 1000000000 | bytes 1000000 | tf_op jit(solution)/shard_map/pallas_call | solution.py:710
  14.8 0.1 collective-permute-start.7
  14.9 0.4 %shard_map.149 = (f32[480,256]{1,0:T(8,128)S(1)}, f32[8,128]{1,0:T(8,128)S(1)}) custom-call(f32[480,256]{1,0:T(8,128)S(1)} %get-tuple-element.70.x_ref, bf16[128,256]{1,0:T(8,128)(2,1)S(1)} %get-tuple-element.71.d_query_ref, bf16[480,512]{1,0:T(8,128)(2,1)S(1)} %get-tuple-element.72.d_kv_ref, f32[8,256]{1,0:T(8,128)S(1)} %get-tuple-element.79.scale_part_ref, ...), custom_call_target="tpu_custom_call" | custom-call | flops 300000000 | bytes 1000000 | tf_op jit(solution)/shard_map/pallas_call | solution.py:719
  15.3 0.6 %collective-permute-start.8 = (f32[8,128]{1,0:T(8,128)S(1)}, f32[8,128]{1,0:T(8,128)S(1)}, u32[]{:S(2)}, u32[]{:S(2)}) collective-permute-start(f32[8,128]{1,0:T(8,128)S(1)} %get-tuple-element.80.small_ref), channel_id=1, source_target_pairs={{0,4},{4,0},{8,12},{12,8},{16,20},{20,16},{24,28},{28,24},{1,5},{5... | collective-permute-start | bytes 12296 | tf_op jit(solution)/shard_map/ppermute | solution.py:595
  15.9 0.1 collective-permute-start.6
  15.9 0.4 %collective-permute-start.12 = (bf16[128,512]{1,0:T(8,128)(2,1)S(1)}, bf16[128,512]{1,0:T(8,128)(2,1)S(1)}, u32[]{:S(2)}, u32[]{:S(2)}) collective-permute-start(bf16[128,512]{1,0:T(8,128)(2,1)S(1)} %get-tuple-element.85.refs_7_), channel_id=1, source_target_pairs={{0,4},{4,0},{8,12},{12,8},{16,20},{20,16},{24,28},{28,24},{1,5},{5... | collective-permute-start | bytes 393224 | tf_op jit(solution)/shard_map/ppermute | solution.py:595
  16.4 0.3 collective-permute-done.8.small_near_ref
  16.7 0.0 collective-permute-done.7.got_ref
  16.7 0.1 shard_map.150
  16.7 1.9 %collective-permute-start.9 = (bf16[328,128]{1,0:T(8,128)(2,1)S(1)}, bf16[328,128]{1,0:T(8,128)(2,1)S(1)}, u32[]{:S(2)}, u32[]{:S(2)}) collective-permute-start(bf16[328,128]{1,0:T(8,128)(2,1)S(1)} %get-tuple-element.82), channel_id=1, source_target_pairs={{0,24},{4,28},{8,16},{12,20},{16,8},{20,12},{24,0},{28,4},{1,25},{... | collective-permute-start | bytes 251912 | tf_op jit(solution)/shard_map/ppermute | solution.py:595
  18.6 1.1 %collective-permute-start.10 = (bf16[328,128]{1,0:T(8,128)(2,1)S(1)}, bf16[328,128]{1,0:T(8,128)(2,1)S(1)}, u32[]{:S(2)}, u32[]{:S(2)}) collective-permute-start(bf16[328,128]{1,0:T(8,128)(2,1)S(1)} %get-tuple-element.83), channel_id=1, source_target_pairs={{0,16},{4,20},{8,24},{12,28},{16,0},{20,4},{24,8},{28,12},{1,17},{... | collective-permute-start | bytes 251912 | tf_op jit(solution)/shard_map/ppermute | solution.py:595
  19.8 0.5 %collective-permute-start.11 = (bf16[328,128]{1,0:T(8,128)(2,1)S(1)}, bf16[328,128]{1,0:T(8,128)(2,1)S(1)}, u32[]{:S(2)}, u32[]{:S(2)}) collective-permute-start(bf16[328,128]{1,0:T(8,128)(2,1)S(1)} %get-tuple-element.84), channel_id=1, source_target_pairs={{0,8},{4,12},{8,0},{12,4},{16,24},{20,28},{24,16},{28,20},{1,9},{5... | collective-permute-start | bytes 251912 | tf_op jit(solution)/shard_map/ppermute | solution.py:595
  20.3 0.2 shard_map.151
  20.5 0.0 collective-permute-done.6.refs_2_
  20.6 3.0 %collective-permute-start.16 = (bf16[40,256]{1,0:T(8,128)(2,1)S(1)}, bf16[40,256]{1,0:T(8,128)(2,1)S(1)}, u32[]{:S(2)}, u32[]{:S(2)}) collective-permute-start(bf16[40,256]{1,0:T(8,128)(2,1)S(1)} %get-tuple-element.93), channel_id=1, source_target_pairs={{0,1},{1,0},{2,3},{3,2},{4,5},{5,4},{6,7},{7,6},{8,9},{9,8},{10,11... | collective-permute-start | bytes 61448 | tf_op jit(solution)/shard_map/ppermute | solution.py:595
  23.5 0.0 collective-permute-done.12.refs_8_
  23.5 0.0 collective-permute-start.17
  23.5 0.0 collective-permute-done.9.refs_4_
  23.6 0.7 %collective-permute-done.10.refs_5_ = bf16[328,128]{1,0:T(8,128)(2,1)S(1)} collective-permute-done((bf16[328,128]{1,0:T(8,128)(2,1)S(1)}, bf16[328,128]{1,0:T(8,128)(2,1)S(1)}, u32[]{:S(2)}, u32[]{:S(2)}) %collective-permute-start.10) | collective-permute-done | bytes 84000 | tf_op jit(solution)/shard_map/ppermute | solution.py:595
  24.2 0.1 collective-permute-done.11.refs_6_
  24.3 0.3 shard_map.152
  24.6 3.3 %collective-permute-start.13 = (bf16[200,128]{1,0:T(8,128)(2,1)S(1)}, bf16[200,128]{1,0:T(8,128)(2,1)S(1)}, u32[]{:S(2)}, u32[]{:S(2)}) collective-permute-start(bf16[200,128]{1,0:T(8,128)(2,1)S(1)} %get-tuple-element.89), channel_id=1, source_target_pairs={{0,3},{1,2},{2,1},{3,0},{4,7},{5,6},{6,5},{7,4},{8,11},{9,10},{10,... | collective-permute-start | bytes 153608 | tf_op jit(solution)/shard_map/ppermute | solution.py:595
  28.0 1.1 %collective-permute-start.14 = (bf16[200,128]{1,0:T(8,128)(2,1)S(1)}, bf16[200,128]{1,0:T(8,128)(2,1)S(1)}, u32[]{:S(2)}, u32[]{:S(2)}) collective-permute-start(bf16[200,128]{1,0:T(8,128)(2,1)S(1)} %get-tuple-element.90), channel_id=1, source_target_pairs={{0,2},{1,3},{2,0},{3,1},{4,6},{5,7},{6,4},{7,5},{8,10},{9,11},{10,... | collective-permute-start | bytes 153608 | tf_op jit(solution)/shard_map/ppermute | solution.py:595
  29.1 0.0 collective-permute-start.15
  29.1 0.0 collective-permute-done.16.near_ref
  29.1 0.0 collective-permute-done.17.far_ref
  29.1 2.1 %collective-permute-start.18 = (bf16[96,256]{1,0:T(8,128)(2,1)S(1)}, bf16[96,256]{1,0:T(8,128)(2,1)S(1)}, u32[]{:S(2)}, u32[]{:S(2)}) collective-permute-start(bf16[96,256]{1,0:T(8,128)(2,1)S(1)} %get-tuple-element.96), channel_id=1, source_target_pairs={{0,1},{1,0},{2,3},{3,2},{4,8},{5,9},{6,10},{7,11},{8,4},{9,5},{10,... | collective-permute-start | bytes 147464 | tf_op jit(solution)/shard_map/ppermute | solution.py:590
  31.2 0.0 collective-permute-start.19
  31.2 0.9 %shard_map.147 = (bf16[4,32,256]{2,1,0:T(8,128)(2,1)}, bf16[2,16,512]{2,1,0:T(8,128)(2,1)}) custom-call(bf16[128,256]{1,0:T(8,128)(2,1)S(1)} %get-tuple-element.66.y_ref, bf16[32,1024]{1,0:T(8,128)(2,1)S(1)} %get-tuple-element.67.group_ref, bf16[1024,512]{1,0:T(8,128)(2,1)S(1)} %copy-done.2), custom_call_target="tpu_custom_call" | custom-call | flops 1000000000 | bytes 1000000 | tf_op jit(solution)/shard_map/pallas_call | solution.py:736
  32.1 1.9 %collective-permute-done.18.far_ref = bf16[96,256]{1,0:T(8,128)(2,1)S(1)} collective-permute-done((bf16[96,256]{1,0:T(8,128)(2,1)S(1)}, bf16[96,256]{1,0:T(8,128)(2,1)S(1)}, u32[]{:S(2)}, u32[]{:S(2)}) %collective-permute-start.18) | collective-permute-done | bytes 49184 | tf_op jit(solution)/shard_map/ppermute | solution.py:590
  34.1 0.0 collective-permute-done.19.near_ref
  34.1 0.0 collective-permute-done.13.d_ref
  34.1 0.0 collective-permute-done.14.c_ref
  34.1 0.0 collective-permute-done.15.b_ref
  34.1 0.7 %shard_map.154 = (f32[32,192]{1,0:T(8,128)}, f32[32,64]{1,0:T(8,128)}, f32[128,128]{1,0:T(8,128)}, f32[1,256]{1,0:T(1,128)}, f32[4]{0:T(128)}, /*index=5*/bf16[4,32,256]{2,1,0:T(8,128)(2,1)}) custom-call(bf16[200,128]{1,0:T(8,128)(2,1)S(1)} %get-tuple-element.88.a_ref, bf16[200,128]{1,0:T(8,128)(2,1)S(1)} %collective-permute-done.13.d_ref, ...), custom_call_target="tpu_custom_call" | custom-call | tf_op jit(solution)/shard_map/pallas_call | solution.py:780
  (4 shorter events, 0.1 us)
Async XLA Ops:
  0.6 7.3 %collective-permute-start = (bf16[4,32,256]{2,1,0:T(8,128)(2,1)}, bf16[4,32,256]{2,1,0:T(8,128)(2,1)S(1)}, u32[]{:S(2)}, u32[]{:S(2)}) collective-permute-start(bf16[4,32,256]{2,1,0:T(8,128)(2,1)} %tok_ref.3), channel_id=1, source_target_pairs={{0,1},{1,0},{2,3},{3,2},{4,8},{5,9},{6,10},{7,11},{8,4},{9,5},{10,... | collective-permute-start | bytes 196616 | tf_op jit(solution)/shard_map/ppermute | solution.py:590
  3.7 4.3 %collective-permute-start.1 = (bf16[4,32,256]{2,1,0:T(8,128)(2,1)}, bf16[4,32,256]{2,1,0:T(8,128)(2,1)S(1)}, u32[]{:S(2)}, u32[]{:S(2)}) collective-permute-start(bf16[4,32,256]{2,1,0:T(8,128)(2,1)} %tok_ref.3), channel_id=1, source_target_pairs={{0,4},{4,0},{8,12},{12,8},{16,20},{20,16},{24,28},{28,24},{1,5},{5... | collective-permute-start | bytes 196616 | tf_op jit(solution)/shard_map/ppermute | solution.py:595
  3.8 1.7 %copy-start = (bf16[256,768]{1,0:T(8,128)(2,1)S(1)}, bf16[256,768]{1,0:T(8,128)(2,1)}, u32[]{:S(2)}) copy-start(bf16[256,768]{1,0:T(8,128)(2,1)} %wqkv_ref.5) | copy-start | bytes 1179652
  3.8 1.7 %copy-start.1 = (bf16[2,16,512]{2,1,0:T(8,128)(2,1)S(1)}, bf16[2,16,512]{2,1,0:T(8,128)(2,1)}, u32[]{:S(2)}) copy-start(bf16[2,16,512]{2,1,0:T(8,128)(2,1)} %dm_ref.3) | copy-start | bytes 98308
  3.8 1.7 %copy-start.2 = (bf16[1024,512]{1,0:T(8,128)(2,1)S(1)}, bf16[1024,512]{1,0:T(8,128)(2,1)}, u32[]{:S(2)}) copy-start(bf16[1024,512]{1,0:T(8,128)(2,1)} %wmerge_ref.3) | copy-start | bytes 3145732
  3.8 1.7 %copy-start.3 = (bf16[256,256]{1,0:T(8,128)(2,1)S(1)}, bf16[256,256]{1,0:T(8,128)(2,1)}, u32[]{:S(2)}) copy-start(bf16[256,256]{1,0:T(8,128)(2,1)} %wout_ref.3) | copy-start | bytes 393220
  3.8 1.7 %copy-start.4 = (bf16[4,32,256]{2,1,0:T(8,128)(2,1)S(1)}, bf16[4,32,256]{2,1,0:T(8,128)(2,1)}, u32[]{:S(2)}) copy-start(bf16[4,32,256]{2,1,0:T(8,128)(2,1)} %dskip_ref.1) | copy-start | bytes 196612
  3.8 1.7 %copy-start.5 = (bf16[4,32,256]{2,1,0:T(8,128)(2,1)S(1)}, bf16[4,32,256]{2,1,0:T(8,128)(2,1)}, u32[]{:S(2)}) copy-start(bf16[4,32,256]{2,1,0:T(8,128)(2,1)} %tok_ref.3) | copy-start | bytes 196612
  3.8 4.2 %collective-permute-start.2 = (bf16[32,512]{1,0:T(8,128)(2,1)}, bf16[32,512]{1,0:T(8,128)(2,1)S(1)}, u32[]{:S(2)}, u32[]{:S(2)}) collective-permute-start(bf16[32,512]{1,0:T(8,128)(2,1)} %bitcast.4), channel_id=1, source_target_pairs={{0,8},{4,12},{8,0},{12,4},{16,24},{20,28},{24,16},{28,20},{1,9},{5... | collective-permute-start | bytes 98312 | tf_op jit(solution)/shard_map/ppermute | solution.py:595
  5.4 0.7 %copy-start.6 = (f32[256]{0:T(256)S(1)}, f32[256]{0:T(256)}, u32[]{:S(2)}) copy-start(f32[256]{0:T(256)} %param.9) | copy-start | bytes 3076
  5.4 0.7 %copy-start.7 = (f32[4]{0:T(128)S(1)}, f32[4]{0:T(128)}, u32[]{:S(2)}) copy-start(f32[4]{0:T(128)} %param.11) | copy-start | bytes 52
  8.0 3.8 %collective-permute-start.3 = (bf16[40,256]{1,0:T(8,128)(2,1)S(1)}, bf16[40,256]{1,0:T(8,128)(2,1)S(1)}, u32[]{:S(2)}, u32[]{:S(2)}) collective-permute-start(bf16[40,256]{1,0:T(8,128)(2,1)S(1)} %get-tuple-element.59), channel_id=1, source_target_pairs={{0,1},{1,0},{2,3},{3,2},{4,5},{5,4},{6,7},{7,6},{8,9},{9,8},{10,11... | collective-permute-start | bytes 61448 | tf_op jit(solution)/shard_map/ppermute | solution.py:595
  9.7 2.2 %collective-permute-start.4 = (bf16[40,256]{1,0:T(8,128)(2,1)S(1)}, bf16[40,256]{1,0:T(8,128)(2,1)S(1)}, u32[]{:S(2)}, u32[]{:S(2)}) collective-permute-start(bf16[40,256]{1,0:T(8,128)(2,1)S(1)} %get-tuple-element.60), channel_id=1, source_target_pairs={{0,4},{1,2},{2,1},{3,7},{4,0},{5,6},{6,5},{7,3},{8,12},{9,10},{10,... | collective-permute-start | bytes 61448 | tf_op jit(solution)/shard_map/ppermute | solution.py:590
  9.7 4.5 %collective-permute-start.5 = (bf16[64,512]{1,0:T(8,128)(2,1)S(1)}, bf16[64,512]{1,0:T(8,128)(2,1)S(1)}, u32[]{:S(2)}, u32[]{:S(2)}) collective-permute-start(bf16[64,512]{1,0:T(8,128)(2,1)S(1)} %get-tuple-element.74.refs_1_), channel_id=1, source_target_pairs={{0,16},{4,20},{8,24},{12,28},{16,0},{20,4},{24,8},{28,12},{1,17},{... | collective-permute-start | bytes 196616 | tf_op jit(solution)/shard_map/ppermute | solution.py:595
  14.8 1.9 %collective-permute-start.7 = (bf16[3,32,1152]{2,1,0:T(8,128)(2,1)S(1)}, bf16[3,32,1152]{2,1,0:T(8,128)(2,1)S(1)}, u32[]{:S(2)}, u32[]{:S(2)}) collective-permute-start(bf16[3,32,1152]{2,1,0:T(8,128)(2,1)S(1)} %get-tuple-element.78), channel_id=1, source_target_pairs={{0,4},{4,0},{8,12},{12,8},{16,20},{20,16},{24,28},{28,24},{1,5},{5... | collective-permute-start | bytes 663560 | tf_op jit(solution)/shard_map/ppermute | solution.py:595
  15.3 1.4 %collective-permute-start.8 = (f32[8,128]{1,0:T(8,128)S(1)}, f32[8,128]{1,0:T(8,128)S(1)}, u32[]{:S(2)}, u32[]{:S(2)}) collective-permute-start(f32[8,128]{1,0:T(8,128)S(1)} %get-tuple-element.80.small_ref), channel_id=1, source_target_pairs={{0,4},{4,0},{8,12},{12,8},{16,20},{20,16},{24,28},{28,24},{1,5},{5... | collective-permute-start | bytes 12296 | tf_op jit(solution)/shard_map/ppermute | solution.py:595
  15.9 4.7 %collective-permute-start.6 = (bf16[32,1152]{1,0:T(8,128)(2,1)S(1)}, bf16[32,1152]{1,0:T(8,128)(2,1)S(1)}, u32[]{:S(2)}, u32[]{:S(2)}) collective-permute-start(bf16[32,1152]{1,0:T(8,128)(2,1)S(1)} %get-tuple-element.77), channel_id=1, source_target_pairs={{0,4},{4,0},{8,12},{12,8},{16,20},{20,16},{24,28},{28,24},{1,5},{5... | collective-permute-start | bytes 221192 | tf_op jit(solution)/shard_map/ppermute | solution.py:595
  15.9 7.6 %collective-permute-start.12 = (bf16[128,512]{1,0:T(8,128)(2,1)S(1)}, bf16[128,512]{1,0:T(8,128)(2,1)S(1)}, u32[]{:S(2)}, u32[]{:S(2)}) collective-permute-start(bf16[128,512]{1,0:T(8,128)(2,1)S(1)} %get-tuple-element.85.refs_7_), channel_id=1, source_target_pairs={{0,4},{4,0},{8,12},{12,8},{16,20},{20,16},{24,28},{28,24},{1,5},{5... | collective-permute-start | bytes 393224 | tf_op jit(solution)/shard_map/ppermute | solution.py:595
  16.7 6.8 %collective-permute-start.9 = (bf16[328,128]{1,0:T(8,128)(2,1)S(1)}, bf16[328,128]{1,0:T(8,128)(2,1)S(1)}, u32[]{:S(2)}, u32[]{:S(2)}) collective-permute-start(bf16[328,128]{1,0:T(8,128)(2,1)S(1)} %get-tuple-element.82), channel_id=1, source_target_pairs={{0,24},{4,28},{8,16},{12,20},{16,8},{20,12},{24,0},{28,4},{1,25},{... | collective-permute-start | bytes 251912 | tf_op jit(solution)/shard_map/ppermute | solution.py:595
  18.6 5.6 %collective-permute-start.10 = (bf16[328,128]{1,0:T(8,128)(2,1)S(1)}, bf16[328,128]{1,0:T(8,128)(2,1)S(1)}, u32[]{:S(2)}, u32[]{:S(2)}) collective-permute-start(bf16[328,128]{1,0:T(8,128)(2,1)S(1)} %get-tuple-element.83), channel_id=1, source_target_pairs={{0,16},{4,20},{8,24},{12,28},{16,0},{20,4},{24,8},{28,12},{1,17},{... | collective-permute-start | bytes 251912 | tf_op jit(solution)/shard_map/ppermute | solution.py:595
  19.8 4.5 %collective-permute-start.11 = (bf16[328,128]{1,0:T(8,128)(2,1)S(1)}, bf16[328,128]{1,0:T(8,128)(2,1)S(1)}, u32[]{:S(2)}, u32[]{:S(2)}) collective-permute-start(bf16[328,128]{1,0:T(8,128)(2,1)S(1)} %get-tuple-element.84), channel_id=1, source_target_pairs={{0,8},{4,12},{8,0},{12,4},{16,24},{20,28},{24,16},{28,20},{1,9},{5... | collective-permute-start | bytes 251912 | tf_op jit(solution)/shard_map/ppermute | solution.py:595
  20.6 8.5 %collective-permute-start.16 = (bf16[40,256]{1,0:T(8,128)(2,1)S(1)}, bf16[40,256]{1,0:T(8,128)(2,1)S(1)}, u32[]{:S(2)}, u32[]{:S(2)}) collective-permute-start(bf16[40,256]{1,0:T(8,128)(2,1)S(1)} %get-tuple-element.93), channel_id=1, source_target_pairs={{0,1},{1,0},{2,3},{3,2},{4,5},{5,4},{6,7},{7,6},{8,9},{9,8},{10,11... | collective-permute-start | bytes 61448 | tf_op jit(solution)/shard_map/ppermute | solution.py:595
  23.5 5.6 %collective-permute-start.17 = (bf16[40,256]{1,0:T(8,128)(2,1)S(1)}, bf16[40,256]{1,0:T(8,128)(2,1)S(1)}, u32[]{:S(2)}, u32[]{:S(2)}) collective-permute-start(bf16[40,256]{1,0:T(8,128)(2,1)S(1)} %get-tuple-element.94), channel_id=1, source_target_pairs={{0,4},{1,2},{2,1},{3,7},{4,0},{5,6},{6,5},{7,3},{8,12},{9,10},{10,... | collective-permute-start | bytes 61448 | tf_op jit(solution)/shard_map/ppermute | solution.py:590
  24.6 9.4 %collective-permute-start.13 = (bf16[200,128]{1,0:T(8,128)(2,1)S(1)}, bf16[200,128]{1,0:T(8,128)(2,1)S(1)}, u32[]{:S(2)}, u32[]{:S(2)}) collective-permute-start(bf16[200,128]{1,0:T(8,128)(2,1)S(1)} %get-tuple-element.89), channel_id=1, source_target_pairs={{0,3},{1,2},{2,1},{3,0},{4,7},{5,6},{6,5},{7,4},{8,11},{9,10},{10,... | collective-permute-start | bytes 153608 | tf_op jit(solution)/shard_map/ppermute | solution.py:595
  28.0 6.1 %collective-permute-start.14 = (bf16[200,128]{1,0:T(8,128)(2,1)S(1)}, bf16[200,128]{1,0:T(8,128)(2,1)S(1)}, u32[]{:S(2)}, u32[]{:S(2)}) collective-permute-start(bf16[200,128]{1,0:T(8,128)(2,1)S(1)} %get-tuple-element.90), channel_id=1, source_target_pairs={{0,2},{1,3},{2,0},{3,1},{4,6},{5,7},{6,4},{7,5},{8,10},{9,11},{10,... | collective-permute-start | bytes 153608 | tf_op jit(solution)/shard_map/ppermute | solution.py:595
  29.1 5.0 %collective-permute-start.15 = (bf16[200,128]{1,0:T(8,128)(2,1)S(1)}, bf16[200,128]{1,0:T(8,128)(2,1)S(1)}, u32[]{:S(2)}, u32[]{:S(2)}) collective-permute-start(bf16[200,128]{1,0:T(8,128)(2,1)S(1)} %get-tuple-element.91), channel_id=1, source_target_pairs={{0,1},{1,0},{2,3},{3,2},{4,5},{5,4},{6,7},{7,6},{8,9},{9,8},{10,11... | collective-permute-start | bytes 153608 | tf_op jit(solution)/shard_map/ppermute | solution.py:595
  29.1 4.9 %collective-permute-start.18 = (bf16[96,256]{1,0:T(8,128)(2,1)S(1)}, bf16[96,256]{1,0:T(8,128)(2,1)S(1)}, u32[]{:S(2)}, u32[]{:S(2)}) collective-permute-start(bf16[96,256]{1,0:T(8,128)(2,1)S(1)} %get-tuple-element.96), channel_id=1, source_target_pairs={{0,1},{1,0},{2,3},{3,2},{4,8},{5,9},{6,10},{7,11},{8,4},{9,5},{10,... | collective-permute-start | bytes 147464 | tf_op jit(solution)/shard_map/ppermute | solution.py:590
  31.2 2.8 %collective-permute-start.19 = (bf16[96,256]{1,0:T(8,128)(2,1)S(1)}, bf16[96,256]{1,0:T(8,128)(2,1)S(1)}, u32[]{:S(2)}, u32[]{:S(2)}) collective-permute-start(bf16[96,256]{1,0:T(8,128)(2,1)S(1)} %get-tuple-element.97), channel_id=1, source_target_pairs={{0,4},{4,0},{8,12},{12,8},{16,20},{20,16},{24,28},{28,24},{1,5},{5... | collective-permute-start | bytes 147464 | tf_op jit(solution)/shard_map/ppermute | solution.py:595

commit v10 on v7

--- a/solution.py
+++ b/solution.py
@@ -49,12 +49,13 @@
     parity_ref[...] = jnp.concatenate(parts, axis=0)
 
 
-def edge_kernel(
-    edges_ref, far_ref, near_ref, dm_ref, dm_next_ref, edge_near_ref, edge_far_ref, dm_pair_ref
-):
-    rows, cols, width = near_ref.shape
+def pair_kernel(dm_ref, dm_next_ref, dm_pair_ref):
     size = dm_next_ref.shape[0]
     dm_pair_ref[...] = jnp.concatenate([dm_ref[...].reshape(size, -1), dm_next_ref[...]], axis=0)
+
+
+def edge_kernel(edges_ref, far_ref, near_ref, edge_near_ref, edge_far_ref):
+    rows, cols, width = near_ref.shape
     up, down = by_side("row", near_ref[...].astype(F32), far_ref[...].astype(F32))
     up = up[rows - RADIUS :]
     down = down[:RADIUS]
@@ -625,13 +626,20 @@
         w_out,
         w_merge,
     )
-    edge_near, edge_far, dm_pair = pl.pallas_call(
+    edge_near, edge_far = pl.pallas_call(
         edge_kernel,
-        out_shape=(edge, edge, shape((2 * groups, depth), BF)),
-        in_specs=vmem(5),
-        out_specs=tuple(vmem(3)),
+        out_shape=(edge, edge),
+        in_specs=vmem(3),
+        out_specs=tuple(vmem(2)),
         compiler_params=less,
-    )(edges, row_far, row_near, d_merged, swap(dm, "row", 2))
+    )(edges, row_far, row_near)
+    dm_pair = pl.pallas_call(
+        pair_kernel,
+        out_shape=shape((2 * groups, depth), BF),
+        in_specs=vmem(2),
+        out_specs=vmem(1)[0],
+        compiler_params=less,
+    )(d_merged, swap(dm, "row", 2))
     dms = [swap(dm_pair, "row", 4), dm_pair]
     col_near, col_far = swapped(edge_near, edge_far, "col")
 

time: 35.1 us -> 34.1 us (0.972)
  waiting for transfers between devices: 5.92 us -> 4.73 us
    ppermute x15, waiting for transfers between devices: 3.97 us -> 2.85 us  [swap(): return lax.ppermute(value, axis, [(i, i ^ step) for i in range(count)])]
  transfers between devices with their start and end apart: 19 -> 19, of which waited for: 7 -> 6; matrix products, arithmetic and copies ran while one was open for 0% -> 0% of each run, Pallas kernels for 13% -> 14%
where the time goes in v10:
time: 34.1 us; the launch traced here: 33.9 us
  starting transfers between devices  21.7 us (64%)
  Pallas kernels  6.02 us (18%)
  waiting for transfers between devices  4.73 us (14%)
  between operations  0.84 us (2%)
  local copies, waits for them, and re-layouts  0.63 us (2%)
    ppermute x15, starting transfers between devices, swap(): return lax.ppermute(value, axis, [(i, i ^ step) for i in range(count)])  16.5 us
    ppermute x4, starting transfers between devices, swapped(): return (swap(near, axis, 1), lax.ppermute(far, ('row', 'col'), pairs))  5.17 us
    ppermute x15, waiting for transfers between devices, swap(): return lax.ppermute(value, axis, [(i, i ^ step) for i in range(count)])  2.85 us
    pallas_call x1, Pallas kernels, on_device(): pl.pallas_call(functools.partial(layer_kernel, sizes), out_shape=(shape((...  1.97 us
    ppermute x4, waiting for transfers between devices, swapped(): return (swap(near, axis, 1), lax.ppermute(far, ('row', 'col'), pairs))  1.88 us
    pallas_call x1, Pallas kernels, on_device(): pl.pallas_call(output_kernel, out_shape=(shape((rows, cols, width), BF),...  0.9 us
    pallas_call x1, Pallas kernels, on_device(): pl.pallas_call(own_kernel, out_shape=(shape((2 * rows * EDGE, width), BF)...  0.79 us
    pallas_call x1, Pallas kernels, on_device(): pl.pallas_call(functools.partial(col_sum_kernel, (rows, cols, width)), ou...  0.75 us
  transfers between devices with their start and end apart: 19, of which 6 were waited for; matrix products, arithmetic and copies ran while one was open for 0% of the time, Pallas kernels for 14%

profile of v10, /device:TPU:0, one launch (start us, length us, event | category | flops | bytes accessed | tf_op | source)
XLA Modules:
  0.0 33.9 jit_solution(9521626718177877994)
XLA Ops:
  0.6 3.1 %collective-permute-start = (bf16[4,32,256]{2,1,0:T(8,128)(2,1)}, bf16[4,32,256]{2,1,0:T(8,128)(2,1)S(1)}, u32[]{:S(2)}, u32[]{:S(2)}) collective-permute-start(bf16[4,32,256]{2,1,0:T(8,128)(2,1)} %tok_ref.3), channel_id=1, source_target_pairs={{0,1},{1,0},{2,3},{3,2},{4,8},{5,9},{6,10},{7,11},{8,4},{9,5},{10,... | collective-permute-start | bytes 196616 | tf_op jit(solution)/shard_map/ppermute | solution.py:574
  3.7 0.0 collective-permute-start.1
  3.8 0.0 copy-start
  3.8 0.0 copy-start.1
  3.8 0.0 copy-start.2
  3.8 0.0 copy-start.3
  3.8 0.0 copy-start.4
  3.8 0.0 copy-start.5
  3.8 1.6 %collective-permute-start.4 = (bf16[32,512]{1,0:T(8,128)(2,1)}, bf16[32,512]{1,0:T(8,128)(2,1)S(1)}, u32[]{:S(2)}, u32[]{:S(2)}) collective-permute-start(bf16[32,512]{1,0:T(8,128)(2,1)} %bitcast.4), channel_id=1, source_target_pairs={{0,8},{4,12},{8,0},{12,4},{16,24},{20,28},{24,16},{28,20},{1,9},{5... | collective-permute-start | bytes 98312 | tf_op jit(solution)/shard_map/ppermute | solution.py:579
  5.4 0.0 copy-start.6
  5.4 0.0 copy-start.7
  5.4 0.0 copy-done
  5.4 0.0 copy-done.1
  5.4 0.0 copy-done.2
  5.4 0.0 copy-done.3
  5.4 0.0 copy-done.4
  5.5 0.0 copy-done.5
  5.5 0.6 %copy-done.6 = f32[256]{0:T(256)S(1)} copy-done((f32[256]{0:T(256)S(1)}, f32[256]{0:T(256)}, u32[]{:S(2)}) %copy-start.6) | copy-done | bytes 1048
  6.1 0.0 copy-done.7
  6.1 0.8 %shard_map.144 = (bf16[32,256]{1,0:T(8,128)(2,1)S(1)}, f32[8,256]{1,0:T(8,128)S(1)}, f32[128,256]{1,0:T(8,128)S(1)}, f32[128,256]{1,0:T(8,128)S(1)}, f32[128,256...) custom-call(bf16[256,256]{1,0:T(8,128)(2,1)S(1)} %get-tuple-element.55.ones_ref, f32[8,128]{1,0:T(8,128)S(1)} %get-tuple-element.56.parity_ref, ...), custom_call_target="tpu_custom_call" | custom-call | flops 1000000000 | bytes 1000000 | tf_op jit(solution)/shard_map/pallas_call | solution.py:609
  6.9 0.0 collective-permute-done.far_ref.row_far_ref
  6.9 0.0 collective-permute-done.1.near_ref.row_near_ref
  6.9 1.6 %collective-permute-start.2 = (bf16[40,256]{1,0:T(8,128)(2,1)S(1)}, bf16[40,256]{1,0:T(8,128)(2,1)S(1)}, u32[]{:S(2)}, u32[]{:S(2)}) collective-permute-start(bf16[40,256]{1,0:T(8,128)(2,1)S(1)} %get-tuple-element.58), channel_id=1, source_target_pairs={{0,1},{1,0},{2,3},{3,2},{4,5},{5,4},{6,7},{7,6},{8,9},{9,8},{10,11... | collective-permute-start | bytes 61448 | tf_op jit(solution)/shard_map/ppermute | solution.py:579
  8.6 0.0 collective-permute-start.3
  8.6 0.0 collective-permute-done.4.dm_next_ref
  8.6 1.6 %collective-permute-start.5 = (bf16[64,512]{1,0:T(8,128)(2,1)S(1)}, bf16[64,512]{1,0:T(8,128)(2,1)S(1)}, u32[]{:S(2)}, u32[]{:S(2)}) collective-permute-start(bf16[64,512]{1,0:T(8,128)(2,1)S(1)} %shard_map.148.refs_1_), channel_id=1, source_target_pairs={{0,16},{4,20},{8,24},{12,28},{16,0},{20,4},{24,8},{28,12},{1,17},{... | collective-permute-start | bytes 196616 | tf_op jit(solution)/shard_map/ppermute | solution.py:579
  10.2 0.5 %collective-permute-done.2.col_near_ref = bf16[40,256]{1,0:T(8,128)(2,1)S(1)} collective-permute-done((bf16[40,256]{1,0:T(8,128)(2,1)S(1)}, bf16[40,256]{1,0:T(8,128)(2,1)S(1)}, u32[]{:S(2)}, u32[]{:S(2)}) %collective-permute-start.2) | collective-permute-done | bytes 20512 | tf_op jit(solution)/shard_map/ppermute | solution.py:579
  10.8 0.0 collective-permute-done.3.col_far_ref
  10.8 2.0 %shard_map.146 = (f32[480,256]{1,0:T(8,128)S(1)}, bf16[128,256]{1,0:T(8,128)(2,1)S(1)}, bf16[128,256]{1,0:T(8,128)(2,1)S(1)}, bf16[480,512]{1,0:T(8,128)(2,1)S(1...) custom-call(bf16[256,256]{1,0:T(8,128)(2,1)S(1)} %get-tuple-element.55.ones_ref, ...), custom_call_target="tpu_custom_call" | custom-call | flops 4000000000 | bytes 1000000 | tf_op jit(solution)/shard_map/pallas_call | solution.py:663
  12.7 0.4 %collective-permute-done.5.refs_0_ = bf16[64,512]{1,0:T(8,128)(2,1)S(1)} collective-permute-done((bf16[64,512]{1,0:T(8,128)(2,1)S(1)}, bf16[64,512]{1,0:T(8,128)(2,1)S(1)}, u32[]{:S(2)}, u32[]{:S(2)}) %collective-permute-start.5) | collective-permute-done | bytes 65568 | tf_op jit(solution)/shard_map/ppermute | solution.py:579
  13.1 0.6 %shard_map.149 = (bf16[128,512]{1,0:T(8,128)(2,1)S(1)}, bf16[4,32,1152]{2,1,0:T(8,128)(2,1)S(1)}, f32[4,32,1024]{2,1,0:T(8,128)S(1)}, bf16[4,32,128]{2,1,0:T(8,128)(2,1)S(1)}) custom-call(f32[480,256]{1,0:T(8,128)S(1)} %get-tuple-element.69.x_ref, bf16[128,256]{1,0:T(8,128)(2,1)S(1)} %get-tuple-element.70.d_query_ref, ...), custom_call_target="tpu_custom_call" | custom-call | flops 1000000000 | bytes 1000000 | tf_op jit(solution)/shard_map/pallas_call | solution.py:694
  13.7 0.1 collective-permute-start.6
  13.8 0.5 %shard_map.150 = (f32[320,256]{1,0:T(8,128)S(1)}, bf16[40,256]{1,0:T(8,128)(2,1)S(1)}, bf16[40,256]{1,0:T(8,128)(2,1)S(1)}, f32[8,128]{1,0:T(8,128)S(1)}) custom-call(f32[480,256]{1,0:T(8,128)S(1)} %get-tuple-element.69.x_ref, bf16[128,256]{1,0:T(8,128)(2,1)S(1)} %get-tuple-element.70.d_query_ref, bf16[480,512]{1,0:T(8,128)(2,1)S(1)} %get-tuple-element.71.d_kv_ref, ...), custom_call_target="tpu_custom_call" | custom-call | flops 500000000 | bytes 1000000 | tf_op jit(solution)/shard_map/pallas_call | solution.py:702
  14.4 0.6 %collective-permute-start.7 = (f32[8,128]{1,0:T(8,128)S(1)}, f32[8,128]{1,0:T(8,128)S(1)}, u32[]{:S(2)}, u32[]{:S(2)}) collective-permute-start(f32[8,128]{1,0:T(8,128)S(1)} %get-tuple-element.77.small_ref), channel_id=1, source_target_pairs={{0,4},{4,0},{8,12},{12,8},{16,20},{20,16},{24,28},{28,24},{1,5},{5... | collective-permute-start | bytes 12296 | tf_op jit(solution)/shard_map/ppermute | solution.py:579
  14.9 0.1 collective-permute-start.11
  15.0 0.7 %collective-permute-done.7.small_near_ref = f32[8,128]{1,0:T(8,128)S(1)} collective-permute-done((f32[8,128]{1,0:T(8,128)S(1)}, f32[8,128]{1,0:T(8,128)S(1)}, u32[]{:S(2)}, u32[]{:S(2)}) %collective-permute-start.7) | collective-permute-done | bytes 4128 | tf_op jit(solution)/shard_map/ppermute | solution.py:579
  15.7 0.0 collective-permute-done.6.got_ref
  15.7 0.1 shard_map.151
  15.8 2.4 %collective-permute-start.8 = (bf16[328,128]{1,0:T(8,128)(2,1)S(1)}, bf16[328,128]{1,0:T(8,128)(2,1)S(1)}, u32[]{:S(2)}, u32[]{:S(2)}) collective-permute-start(bf16[328,128]{1,0:T(8,128)(2,1)S(1)} %get-tuple-element.81), channel_id=1, source_target_pairs={{0,24},{4,28},{8,16},{12,20},{16,8},{20,12},{24,0},{28,4},{1,25},{... | collective-permute-start | bytes 251912 | tf_op jit(solution)/shard_map/ppermute | solution.py:579
  18.2 0.7 %collective-permute-start.9 = (bf16[328,128]{1,0:T(8,128)(2,1)S(1)}, bf16[328,128]{1,0:T(8,128)(2,1)S(1)}, u32[]{:S(2)}, u32[]{:S(2)}) collective-permute-start(bf16[328,128]{1,0:T(8,128)(2,1)S(1)} %get-tuple-element.82), channel_id=1, source_target_pairs={{0,16},{4,20},{8,24},{12,28},{16,0},{20,4},{24,8},{28,12},{1,17},{... | collective-permute-start | bytes 251912 | tf_op jit(solution)/shard_map/ppermute | solution.py:579
  18.9 0.5 %collective-permute-start.10 = (bf16[328,128]{1,0:T(8,128)(2,1)S(1)}, bf16[328,128]{1,0:T(8,128)(2,1)S(1)}, u32[]{:S(2)}, u32[]{:S(2)}) collective-permute-start(bf16[328,128]{1,0:T(8,128)(2,1)S(1)} %get-tuple-element.83), channel_id=1, source_target_pairs={{0,8},{4,12},{8,0},{12,4},{16,24},{20,28},{24,16},{28,20},{1,9},{5... | collective-permute-start | bytes 251912 | tf_op jit(solution)/shard_map/ppermute | solution.py:579
  19.4 2.9 %collective-permute-start.15 = (bf16[40,256]{1,0:T(8,128)(2,1)S(1)}, bf16[40,256]{1,0:T(8,128)(2,1)S(1)}, u32[]{:S(2)}, u32[]{:S(2)}) collective-permute-start(bf16[40,256]{1,0:T(8,128)(2,1)S(1)} %get-tuple-element.91), channel_id=1, source_target_pairs={{0,1},{1,0},{2,3},{3,2},{4,5},{5,4},{6,7},{7,6},{8,9},{9,8},{10,11... | collective-permute-start | bytes 61448 | tf_op jit(solution)/shard_map/ppermute | solution.py:579
  22.3 0.0 collective-permute-done.11.refs_7_
  22.3 0.0 collective-permute-start.16
  22.3 0.0 collective-permute-done.8.refs_3_
  22.3 1.0 %collective-permute-done.9.refs_4_ = bf16[328,128]{1,0:T(8,128)(2,1)S(1)} collective-permute-done((bf16[328,128]{1,0:T(8,128)(2,1)S(1)}, bf16[328,128]{1,0:T(8,128)(2,1)S(1)}, u32[]{:S(2)}, u32[]{:S(2)}) %collective-permute-start.9) | collective-permute-done | bytes 84000 | tf_op jit(solution)/shard_map/ppermute | solution.py:579
  23.3 0.1 collective-permute-done.10.refs_5_
  23.5 0.3 shard_map.152
  23.8 3.3 %collective-permute-start.12 = (bf16[200,128]{1,0:T(8,128)(2,1)S(1)}, bf16[200,128]{1,0:T(8,128)(2,1)S(1)}, u32[]{:S(2)}, u32[]{:S(2)}) collective-permute-start(bf16[200,128]{1,0:T(8,128)(2,1)S(1)} %get-tuple-element.87), channel_id=1, source_target_pairs={{0,3},{1,2},{2,1},{3,0},{4,7},{5,6},{6,5},{7,4},{8,11},{9,10},{10,... | collective-permute-start | bytes 153608 | tf_op jit(solution)/shard_map/ppermute | solution.py:579
  27.1 1.2 %collective-permute-start.13 = (bf16[200,128]{1,0:T(8,128)(2,1)S(1)}, bf16[200,128]{1,0:T(8,128)(2,1)S(1)}, u32[]{:S(2)}, u32[]{:S(2)}) collective-permute-start(bf16[200,128]{1,0:T(8,128)(2,1)S(1)} %get-tuple-element.88), channel_id=1, source_target_pairs={{0,2},{1,3},{2,0},{3,1},{4,6},{5,7},{6,4},{7,5},{8,10},{9,11},{10,... | collective-permute-start | bytes 153608 | tf_op jit(solution)/shard_map/ppermute | solution.py:579
  28.2 0.0 collective-permute-start.14
  28.2 0.0 collective-permute-done.15.near_ref
  28.2 0.0 collective-permute-done.16.far_ref
  28.3 2.1 %collective-permute-start.17 = (bf16[96,256]{1,0:T(8,128)(2,1)S(1)}, bf16[96,256]{1,0:T(8,128)(2,1)S(1)}, u32[]{:S(2)}, u32[]{:S(2)}) collective-permute-start(bf16[96,256]{1,0:T(8,128)(2,1)S(1)} %get-tuple-element.94), channel_id=1, source_target_pairs={{0,1},{1,0},{2,3},{3,2},{4,8},{5,9},{6,10},{7,11},{8,4},{9,5},{10,... | collective-permute-start | bytes 147464 | tf_op jit(solution)/shard_map/ppermute | solution.py:574
  30.4 0.0 collective-permute-start.18
  30.4 0.9 %shard_map.147 = (bf16[4,32,256]{2,1,0:T(8,128)(2,1)}, bf16[2,16,512]{2,1,0:T(8,128)(2,1)}) custom-call(bf16[128,256]{1,0:T(8,128)(2,1)S(1)} %get-tuple-element.65.y_ref, bf16[32,1024]{1,0:T(8,128)(2,1)S(1)} %get-tuple-element.66.group_ref, bf16[1024,512]{1,0:T(8,128)(2,1)S(1)} %copy-done.1), custom_call_target="tpu_custom_call" | custom-call | flops 1000000000 | bytes 1000000 | tf_op jit(solution)/shard_map/pallas_call | solution.py:712
  31.3 1.9 %collective-permute-done.17.far_ref = bf16[96,256]{1,0:T(8,128)(2,1)S(1)} collective-permute-done((bf16[96,256]{1,0:T(8,128)(2,1)S(1)}, bf16[96,256]{1,0:T(8,128)(2,1)S(1)}, u32[]{:S(2)}, u32[]{:S(2)}) %collective-permute-start.17) | collective-permute-done | bytes 49184 | tf_op jit(solution)/shard_map/ppermute | solution.py:574
  33.2 0.0 collective-permute-done.18.near_ref
  33.2 0.0 collective-permute-done.12.d_ref
  33.2 0.0 collective-permute-done.13.c_ref
  33.2 0.0 collective-permute-done.14.b_ref
  33.2 0.7 %shard_map.154 = (f32[32,192]{1,0:T(8,128)}, f32[32,64]{1,0:T(8,128)}, f32[128,128]{1,0:T(8,128)}, f32[1,256]{1,0:T(1,128)}, f32[4]{0:T(128)}, /*index=5*/bf16[4,32,256]{2,1,0:T(8,128)(2,1)}) custom-call(bf16[200,128]{1,0:T(8,128)(2,1)S(1)} %get-tuple-element.86.a_ref, bf16[200,128]{1,0:T(8,128)(2,1)S(1)} %collective-permute-done.12.d_ref, ...), custom_call_target="tpu_custom_call" | custom-call | tf_op jit(solution)/shard_map/pallas_call | solution.py:758
  (4 shorter events, 0.1 us)
Async XLA Ops:
  0.6 6.2 %collective-permute-start = (bf16[4,32,256]{2,1,0:T(8,128)(2,1)}, bf16[4,32,256]{2,1,0:T(8,128)(2,1)S(1)}, u32[]{:S(2)}, u32[]{:S(2)}) collective-permute-start(bf16[4,32,256]{2,1,0:T(8,128)(2,1)} %tok_ref.3), channel_id=1, source_target_pairs={{0,1},{1,0},{2,3},{3,2},{4,8},{5,9},{6,10},{7,11},{8,4},{9,5},{10,... | collective-permute-start | bytes 196616 | tf_op jit(solution)/shard_map/ppermute | solution.py:574
  3.7 3.2 %collective-permute-start.1 = (bf16[4,32,256]{2,1,0:T(8,128)(2,1)}, bf16[4,32,256]{2,1,0:T(8,128)(2,1)S(1)}, u32[]{:S(2)}, u32[]{:S(2)}) collective-permute-start(bf16[4,32,256]{2,1,0:T(8,128)(2,1)} %tok_ref.3), channel_id=1, source_target_pairs={{0,4},{4,0},{8,12},{12,8},{16,20},{20,16},{24,28},{28,24},{1,5},{5... | collective-permute-start | bytes 196616 | tf_op jit(solution)/shard_map/ppermute | solution.py:579
  3.8 1.7 %copy-start = (bf16[2,16,512]{2,1,0:T(8,128)(2,1)S(1)}, bf16[2,16,512]{2,1,0:T(8,128)(2,1)}, u32[]{:S(2)}) copy-start(bf16[2,16,512]{2,1,0:T(8,128)(2,1)} %dm_ref.3) | copy-start | bytes 98308
  3.8 1.7 %copy-start.1 = (bf16[1024,512]{1,0:T(8,128)(2,1)S(1)}, bf16[1024,512]{1,0:T(8,128)(2,1)}, u32[]{:S(2)}) copy-start(bf16[1024,512]{1,0:T(8,128)(2,1)} %wmerge_ref.3) | copy-start | bytes 3145732
  3.8 1.7 %copy-start.2 = (bf16[256,768]{1,0:T(8,128)(2,1)S(1)}, bf16[256,768]{1,0:T(8,128)(2,1)}, u32[]{:S(2)}) copy-start(bf16[256,768]{1,0:T(8,128)(2,1)} %wqkv_ref.5) | copy-start | bytes 1179652
  3.8 1.7 %copy-start.3 = (bf16[256,256]{1,0:T(8,128)(2,1)S(1)}, bf16[256,256]{1,0:T(8,128)(2,1)}, u32[]{:S(2)}) copy-start(bf16[256,256]{1,0:T(8,128)(2,1)} %wout_ref.3) | copy-start | bytes 393220
  3.8 1.7 %copy-start.4 = (bf16[4,32,256]{2,1,0:T(8,128)(2,1)S(1)}, bf16[4,32,256]{2,1,0:T(8,128)(2,1)}, u32[]{:S(2)}) copy-start(bf16[4,32,256]{2,1,0:T(8,128)(2,1)} %dskip_ref.1) | copy-start | bytes 196612
  3.8 1.7 %copy-start.5 = (bf16[4,32,256]{2,1,0:T(8,128)(2,1)S(1)}, bf16[4,32,256]{2,1,0:T(8,128)(2,1)}, u32[]{:S(2)}) copy-start(bf16[4,32,256]{2,1,0:T(8,128)(2,1)} %tok_ref.3) | copy-start | bytes 196612
  3.8 4.8 %collective-permute-start.4 = (bf16[32,512]{1,0:T(8,128)(2,1)}, bf16[32,512]{1,0:T(8,128)(2,1)S(1)}, u32[]{:S(2)}, u32[]{:S(2)}) collective-permute-start(bf16[32,512]{1,0:T(8,128)(2,1)} %bitcast.4), channel_id=1, source_target_pairs={{0,8},{4,12},{8,0},{12,4},{16,24},{20,28},{24,16},{28,20},{1,9},{5... | collective-permute-start | bytes 98312 | tf_op jit(solution)/shard_map/ppermute | solution.py:579
  5.4 0.7 %copy-start.6 = (f32[256]{0:T(256)S(1)}, f32[256]{0:T(256)}, u32[]{:S(2)}) copy-start(f32[256]{0:T(256)} %param.9) | copy-start | bytes 3076
  5.4 0.7 %copy-start.7 = (f32[4]{0:T(128)S(1)}, f32[4]{0:T(128)}, u32[]{:S(2)}) copy-start(f32[4]{0:T(128)} %param.11) | copy-start | bytes 52
  6.9 3.8 %collective-permute-start.2 = (bf16[40,256]{1,0:T(8,128)(2,1)S(1)}, bf16[40,256]{1,0:T(8,128)(2,1)S(1)}, u32[]{:S(2)}, u32[]{:S(2)}) collective-permute-start(bf16[40,256]{1,0:T(8,128)(2,1)S(1)} %get-tuple-element.58), channel_id=1, source_target_pairs={{0,1},{1,0},{2,3},{3,2},{4,5},{5,4},{6,7},{7,6},{8,9},{9,8},{10,11... | collective-permute-start | bytes 61448 | tf_op jit(solution)/shard_map/ppermute | solution.py:579
  8.6 2.2 %collective-permute-start.3 = (bf16[40,256]{1,0:T(8,128)(2,1)S(1)}, bf16[40,256]{1,0:T(8,128)(2,1)S(1)}, u32[]{:S(2)}, u32[]{:S(2)}) collective-permute-start(bf16[40,256]{1,0:T(8,128)(2,1)S(1)} %get-tuple-element.59), channel_id=1, source_target_pairs={{0,4},{1,2},{2,1},{3,7},{4,0},{5,6},{6,5},{7,3},{8,12},{9,10},{10,... | collective-permute-start | bytes 61448 | tf_op jit(solution)/shard_map/ppermute | solution.py:574
  8.6 4.6 %collective-permute-start.5 = (bf16[64,512]{1,0:T(8,128)(2,1)S(1)}, bf16[64,512]{1,0:T(8,128)(2,1)S(1)}, u32[]{:S(2)}, u32[]{:S(2)}) collective-permute-start(bf16[64,512]{1,0:T(8,128)(2,1)S(1)} %shard_map.148.refs_1_), channel_id=1, source_target_pairs={{0,16},{4,20},{8,24},{12,28},{16,0},{20,4},{24,8},{28,12},{1,17},{... | collective-permute-start | bytes 196616 | tf_op jit(solution)/shard_map/ppermute | solution.py:579
  13.7 2.0 %collective-permute-start.6 = (bf16[4,32,1152]{2,1,0:T(8,128)(2,1)S(1)}, bf16[4,32,1152]{2,1,0:T(8,128)(2,1)S(1)}, u32[]{:S(2)}, u32[]{:S(2)}) collective-permute-start(bf16[4,32,1152]{2,1,0:T(8,128)(2,1)S(1)} %get-tuple-element.73), channel_id=1, source_target_pairs={{0,4},{4,0},{8,12},{12,8},{16,20},{20,16},{24,28},{28,24},{1,5},{5... | collective-permute-start | bytes 884744 | tf_op jit(solution)/shard_map/ppermute | solution.py:579
  14.4 1.4 %collective-permute-start.7 = (f32[8,128]{1,0:T(8,128)S(1)}, f32[8,128]{1,0:T(8,128)S(1)}, u32[]{:S(2)}, u32[]{:S(2)}) collective-permute-start(f32[8,128]{1,0:T(8,128)S(1)} %get-tuple-element.77.small_ref), channel_id=1, source_target_pairs={{0,4},{4,0},{8,12},{12,8},{16,20},{20,16},{24,28},{28,24},{1,5},{5... | collective-permute-start | bytes 12296 | tf_op jit(solution)/shard_map/ppermute | solution.py:579
  14.9 7.4 %collective-permute-start.11 = (bf16[128,512]{1,0:T(8,128)(2,1)S(1)}, bf16[128,512]{1,0:T(8,128)(2,1)S(1)}, u32[]{:S(2)}, u32[]{:S(2)}) collective-permute-start(bf16[128,512]{1,0:T(8,128)(2,1)S(1)} %get-tuple-element.84.refs_6_), channel_id=1, source_target_pairs={{0,4},{4,0},{8,12},{12,8},{16,20},{20,16},{24,28},{28,24},{1,5},{5... | collective-permute-start | bytes 393224 | tf_op jit(solution)/shard_map/ppermute | solution.py:579
  15.8 6.5 %collective-permute-start.8 = (bf16[328,128]{1,0:T(8,128)(2,1)S(1)}, bf16[328,128]{1,0:T(8,128)(2,1)S(1)}, u32[]{:S(2)}, u32[]{:S(2)}) collective-permute-start(bf16[328,128]{1,0:T(8,128)(2,1)S(1)} %get-tuple-element.81), channel_id=1, source_target_pairs={{0,24},{4,28},{8,16},{12,20},{16,8},{20,12},{24,0},{28,4},{1,25},{... | collective-permute-start | bytes 251912 | tf_op jit(solution)/shard_map/ppermute | solution.py:579
  18.2 5.1 %collective-permute-start.9 = (bf16[328,128]{1,0:T(8,128)(2,1)S(1)}, bf16[328,128]{1,0:T(8,128)(2,1)S(1)}, u32[]{:S(2)}, u32[]{:S(2)}) collective-permute-start(bf16[328,128]{1,0:T(8,128)(2,1)S(1)} %get-tuple-element.82), channel_id=1, source_target_pairs={{0,16},{4,20},{8,24},{12,28},{16,0},{20,4},{24,8},{28,12},{1,17},{... | collective-permute-start | bytes 251912 | tf_op jit(solution)/shard_map/ppermute | solution.py:579
  18.9 4.6 %collective-permute-start.10 = (bf16[328,128]{1,0:T(8,128)(2,1)S(1)}, bf16[328,128]{1,0:T(8,128)(2,1)S(1)}, u32[]{:S(2)}, u32[]{:S(2)}) collective-permute-start(bf16[328,128]{1,0:T(8,128)(2,1)S(1)} %get-tuple-element.83), channel_id=1, source_target_pairs={{0,8},{4,12},{8,0},{12,4},{16,24},{20,28},{24,16},{28,20},{1,9},{5... | collective-permute-start | bytes 251912 | tf_op jit(solution)/shard_map/ppermute | solution.py:579
  19.4 8.9 %collective-permute-start.15 = (bf16[40,256]{1,0:T(8,128)(2,1)S(1)}, bf16[40,256]{1,0:T(8,128)(2,1)S(1)}, u32[]{:S(2)}, u32[]{:S(2)}) collective-permute-start(bf16[40,256]{1,0:T(8,128)(2,1)S(1)} %get-tuple-element.91), channel_id=1, source_target_pairs={{0,1},{1,0},{2,3},{3,2},{4,5},{5,4},{6,7},{7,6},{8,9},{9,8},{10,11... | collective-permute-start | bytes 61448 | tf_op jit(solution)/shard_map/ppermute | solution.py:579
  22.3 5.9 %collective-permute-start.16 = (bf16[40,256]{1,0:T(8,128)(2,1)S(1)}, bf16[40,256]{1,0:T(8,128)(2,1)S(1)}, u32[]{:S(2)}, u32[]{:S(2)}) collective-permute-start(bf16[40,256]{1,0:T(8,128)(2,1)S(1)} %get-tuple-element.92), channel_id=1, source_target_pairs={{0,4},{1,2},{2,1},{3,7},{4,0},{5,6},{6,5},{7,3},{8,12},{9,10},{10,... | collective-permute-start | bytes 61448 | tf_op jit(solution)/shard_map/ppermute | solution.py:574
  23.8 9.4 %collective-permute-start.12 = (bf16[200,128]{1,0:T(8,128)(2,1)S(1)}, bf16[200,128]{1,0:T(8,128)(2,1)S(1)}, u32[]{:S(2)}, u32[]{:S(2)}) collective-permute-start(bf16[200,128]{1,0:T(8,128)(2,1)S(1)} %get-tuple-element.87), channel_id=1, source_target_pairs={{0,3},{1,2},{2,1},{3,0},{4,7},{5,6},{6,5},{7,4},{8,11},{9,10},{10,... | collective-permute-start | bytes 153608 | tf_op jit(solution)/shard_map/ppermute | solution.py:579
  27.1 6.1 %collective-permute-start.13 = (bf16[200,128]{1,0:T(8,128)(2,1)S(1)}, bf16[200,128]{1,0:T(8,128)(2,1)S(1)}, u32[]{:S(2)}, u32[]{:S(2)}) collective-permute-start(bf16[200,128]{1,0:T(8,128)(2,1)S(1)} %get-tuple-element.88), channel_id=1, source_target_pairs={{0,2},{1,3},{2,0},{3,1},{4,6},{5,7},{6,4},{7,5},{8,10},{9,11},{10,... | collective-permute-start | bytes 153608 | tf_op jit(solution)/shard_map/ppermute | solution.py:579
  28.2 4.9 %collective-permute-start.14 = (bf16[200,128]{1,0:T(8,128)(2,1)S(1)}, bf16[200,128]{1,0:T(8,128)(2,1)S(1)}, u32[]{:S(2)}, u32[]{:S(2)}) collective-permute-start(bf16[200,128]{1,0:T(8,128)(2,1)S(1)} %get-tuple-element.89), channel_id=1, source_target_pairs={{0,1},{1,0},{2,3},{3,2},{4,5},{5,4},{6,7},{7,6},{8,9},{9,8},{10,11... | collective-permute-start | bytes 153608 | tf_op jit(solution)/shard_map/ppermute | solution.py:579
  28.3 4.9 %collective-permute-start.17 = (bf16[96,256]{1,0:T(8,128)(2,1)S(1)}, bf16[96,256]{1,0:T(8,128)(2,1)S(1)}, u32[]{:S(2)}, u32[]{:S(2)}) collective-permute-start(bf16[96,256]{1,0:T(8,128)(2,1)S(1)} %get-tuple-element.94), channel_id=1, source_target_pairs={{0,1},{1,0},{2,3},{3,2},{4,8},{5,9},{6,10},{7,11},{8,4},{9,5},{10,... | collective-permute-start | bytes 147464 | tf_op jit(solution)/shard_map/ppermute | solution.py:574
  30.4 2.8 %collective-permute-start.18 = (bf16[96,256]{1,0:T(8,128)(2,1)S(1)}, bf16[96,256]{1,0:T(8,128)(2,1)S(1)}, u32[]{:S(2)}, u32[]{:S(2)}) collective-permute-start(bf16[96,256]{1,0:T(8,128)(2,1)S(1)} %get-tuple-element.95), channel_id=1, source_target_pairs={{0,4},{4,0},{8,12},{12,8},{16,20},{20,16},{24,28},{28,24},{1,5},{5... | collective-permute-start | bytes 147464 | tf_op jit(solution)/shard_map/ppermute | solution.py:579

commit v11 on v10

--- a/solution.py
+++ b/solution.py
@@ -85,19 +85,12 @@
     parity_ref,
     scale_ref,
     tok_ref,
-    dm_ref,
-    dskip_ref,
     gain_ref,
     wqkv_ref,
-    wout_ref,
-    wmerge_ref,
     edges_ref,
     rows_ref,
     q_norm_ref,
     q_unit_ref,
-    dy_ref,
-    d_attn_ref,
-    dscr,
 ):
     rows, cols, width = tok_ref.shape
     tokens = rows * cols
@@ -121,6 +114,11 @@
     q_norm = lax.rsqrt(head_sum(query * query, ones_ref) + EPS)
     q_norm_ref[...] = q_norm
     q_unit_ref[...] = query * q_norm
+
+
+def cotangent_kernel(dm_ref, dskip_ref, wout_ref, wmerge_ref, dy_ref, d_attn_ref, dscr):
+    rows, cols, width = dskip_ref.shape
+    tokens = rows * cols
     group_wide = cols // 2
     d_in = mm_t(dm_ref[...].reshape(-1, dm_ref.shape[2]), wmerge_ref[...])
     for i in range(rows // 2):
@@ -606,26 +604,23 @@
     dm = d_merged.reshape(groups, depth)
     tile = shape((rows * cols, width), F32)
     half = shape((rows * cols, width), BF)
-    edges, two_rows, q_norm, q_unit, d_y, d_attn = pl.pallas_call(
+    edges, two_rows, q_norm, q_unit = pl.pallas_call(
         own_kernel,
-        out_shape=(shape((2 * rows * EDGE, width), BF), shape((8, width), F32), tile, tile, tile, half),
-        in_specs=vmem(10),
-        out_specs=tuple(vmem(6)),
+        out_shape=(shape((2 * rows * EDGE, width), BF), shape((8, width), F32), tile, tile),
+        in_specs=vmem(6),
+        out_specs=tuple(vmem(4)),
+        compiler_params=params,
+        cost_estimate=pl.CostEstimate(flops=5 * 10**8, bytes_accessed=10**6, transcendentals=0),
+    )(ones, parity, head_scale.reshape(1, heads), tokens, gain.reshape(1, width), w_qkv)
+    d_y, d_attn = pl.pallas_call(
+        cotangent_kernel,
+        out_shape=(tile, half),
+        in_specs=vmem(4),
+        out_specs=tuple(vmem(2)),
         scratch_shapes=[pltpu.VMEM((width // LANES, rows, cols, LANES), F32)],
         compiler_params=params,
-        cost_estimate=pl.CostEstimate(flops=10**9, bytes_accessed=10**6, transcendentals=0),
-    )(
-        ones,
-        parity,
-        head_scale.reshape(1, heads),
-        tokens,
-        d_merged,
-        d_skip,
-        gain.reshape(1, width),
-        w_qkv,
-        w_out,
-        w_merge,
-    )
+        cost_estimate=pl.CostEstimate(flops=5 * 10**8, bytes_accessed=10**6, transcendentals=0),
+    )(d_merged, d_skip, w_out, w_merge)
     edge_near, edge_far = pl.pallas_call(
         edge_kernel,
         out_shape=(edge, edge),

time: 34.1 us -> 34.5 us (1.012)
    pallas_call x0 -> x1, Pallas kernels: none -> 0.62 us  [on_device(): pl.pallas_call(cotangent_kernel, out_shape=(tile, half), in_specs=vmem(4)...]
    pallas_call x1, Pallas kernels: 0.79 us -> 0.39 us  [on_device(): pl.pallas_call(own_kernel, out_shape=(shape((2 * rows * EDGE, width), BF)...]
  transfers between devices with their start and end apart: 19 -> 19, of which waited for: 6 -> 5; matrix products, arithmetic and copies ran while one was open for 0% -> 0% of each run, Pallas kernels for 14% -> 14%
where the time goes in v11:
time: 34.5 us; the launch traced here: 34.4 us
  starting transfers between devices  22 us (64%)
  Pallas kernels  6.24 us (18%)
  waiting for transfers between devices  4.62 us (13%)
  between operations  0.84 us (2%)
  local copies, waits for them, and re-layouts  0.64 us (2%)
    ppermute x15, starting transfers between devices, swap(): return lax.ppermute(value, axis, [(i, i ^ step) for i in range(count)])  16.9 us
    ppermute x4, starting transfers between devices, swapped(): return (swap(near, axis, 1), lax.ppermute(far, ('row', 'col'), pairs))  5.17 us
    ppermute x15, waiting for transfers between devices, swap(): return lax.ppermute(value, axis, [(i, i ^ step) for i in range(count)])  2.95 us
    pallas_call x1, Pallas kernels, on_device(): pl.pallas_call(functools.partial(layer_kernel, sizes), out_shape=(shape((...  1.96 us
    ppermute x4, waiting for transfers between devices, swapped(): return (swap(near, axis, 1), lax.ppermute(far, ('row', 'col'), pairs))  1.67 us
    pallas_call x1, Pallas kernels, on_device(): pl.pallas_call(output_kernel, out_shape=(shape((rows, cols, width), BF),...  0.91 us
    pallas_call x1, Pallas kernels, on_device(): pl.pallas_call(functools.partial(col_sum_kernel, (rows, cols, width)), ou...  0.75 us
  transfers between devices with their start and end apart: 19, of which 5 were waited for; matrix products, arithmetic and copies ran while one was open for 0% of the time, Pallas kernels for 14%

profile of v11, /device:TPU:0, one launch (start us, length us, event | category | flops | bytes accessed | tf_op | source)
XLA Modules:
  0.0 34.4 jit_solution(3228633125625826218)
XLA Ops:
  0.6 3.1 %collective-permute-start = (bf16[4,32,256]{2,1,0:T(8,128)(2,1)}, bf16[4,32,256]{2,1,0:T(8,128)(2,1)S(1)}, u32[]{:S(2)}, u32[]{:S(2)}) collective-permute-start(bf16[4,32,256]{2,1,0:T(8,128)(2,1)} %tok_ref.3), channel_id=1, source_target_pairs={{0,1},{1,0},{2,3},{3,2},{4,8},{5,9},{6,10},{7,11},{8,4},{9,5},{10,... | collective-permute-start | bytes 196616 | tf_op jit(solution)/shard_map/ppermute | solution.py:572
  3.7 0.0 collective-permute-start.1
  3.8 0.0 copy-start.2
  3.8 0.0 copy-start.5
  3.8 1.5 %collective-permute-start.4 = (bf16[32,512]{1,0:T(8,128)(2,1)}, bf16[32,512]{1,0:T(8,128)(2,1)S(1)}, u32[]{:S(2)}, u32[]{:S(2)}) collective-permute-start(bf16[32,512]{1,0:T(8,128)(2,1)} %bitcast.4), channel_id=1, source_target_pairs={{0,8},{4,12},{8,0},{12,4},{16,24},{20,28},{24,16},{28,20},{1,9},{5... | collective-permute-start | bytes 98312 | tf_op jit(solution)/shard_map/ppermute | solution.py:577
  5.2 0.0 copy-start.6
  5.3 0.0 copy-start.7
  5.3 0.0 copy-start.1
  5.3 0.0 copy-done.2
  5.3 0.0 copy-done.5
  5.3 0.6 %copy-done.6 = f32[256]{0:T(256)S(1)} copy-done((f32[256]{0:T(256)S(1)}, f32[256]{0:T(256)}, u32[]{:S(2)}) %copy-start.6) | copy-done | bytes 1048
  5.9 0.0 copy-done.7
  5.9 0.0 copy-start.3
  5.9 0.4 %shard_map.144 = (bf16[32,256]{1,0:T(8,128)(2,1)S(1)}, f32[8,256]{1,0:T(8,128)S(1)}, f32[128,256]{1,0:T(8,128)S(1)}, f32[128,256]{1,0:T(8,128)S(1)}) custom-call(bf16[256,256]{1,0:T(8,128)(2,1)S(1)} %get-tuple-element.55.ones_ref, f32[8,128]{1,0:T(8,128)S(1)} %get-tuple-element.56.parity_ref, f32[1,4]{1,0:T(1,128)S(1)} %bitcast.6, ...), custom_call_target="tpu_custom_call" | custom-call | flops 500000000 | bytes 1000000 | tf_op jit(solution)/shard_map/pallas_call | solution.py:607
  6.3 0.0 collective-permute-done.far_ref.row_far_ref
  6.3 0.0 collective-permute-done.1.near_ref.row_near_ref
  6.4 0.0 copy-start
  6.4 0.0 copy-start.4
  6.4 1.9 %collective-permute-start.2 = (bf16[40,256]{1,0:T(8,128)(2,1)S(1)}, bf16[40,256]{1,0:T(8,128)(2,1)S(1)}, u32[]{:S(2)}, u32[]{:S(2)}) collective-permute-start(bf16[40,256]{1,0:T(8,128)(2,1)S(1)} %get-tuple-element.58), channel_id=1, source_target_pairs={{0,1},{1,0},{2,3},{3,2},{4,5},{5,4},{6,7},{7,6},{8,9},{9,8},{10,11... | collective-permute-start | bytes 61448 | tf_op jit(solution)/shard_map/ppermute | solution.py:577
  8.3 0.0 collective-permute-start.3
  8.3 0.0 copy-done.1
  8.3 0.0 copy-done.3
  8.3 0.0 copy-done
  8.3 0.0 copy-done.4
  8.3 0.6 %shard_map.146 = (f32[128,256]{1,0:T(8,128)S(1)}, bf16[128,256]{1,0:T(8,128)(2,1)S(1)}) custom-call(bf16[2,16,512]{2,1,0:T(8,128)(2,1)S(1)} %copy-done, bf16[4,32,256]{2,1,0:T(8,128)(2,1)S(1)} %copy-done.4, bf16[256,256]{1,0:T(8,128)(2,1)S(1)} %copy-done.3, bf16[1024,512]{1,0:T(8,128)(2,1)S(1)} %copy-done.1), custom_call_target="tpu_custom_call" | custom-call | flops 500000000 | bytes 1000000 | tf_op jit(solution)/shard_map/pallas_call | solution.py:615
  9.0 0.0 collective-permute-done.4.dm_next_ref
  9.0 1.9 %collective-permute-start.5 = (bf16[64,512]{1,0:T(8,128)(2,1)S(1)}, bf16[64,512]{1,0:T(8,128)(2,1)S(1)}, u32[]{:S(2)}, u32[]{:S(2)}) collective-permute-start(bf16[64,512]{1,0:T(8,128)(2,1)S(1)} %shard_map.149.refs_1_), channel_id=1, source_target_pairs={{0,16},{4,20},{8,24},{12,28},{16,0},{20,4},{24,8},{28,12},{1,17},{... | collective-permute-start | bytes 196616 | tf_op jit(solution)/shard_map/ppermute | solution.py:577
  10.9 0.0 collective-permute-done.2.col_near_ref
  10.9 0.0 collective-permute-done.3.col_far_ref
  10.9 2.0 %shard_map.147 = (f32[480,256]{1,0:T(8,128)S(1)}, bf16[128,256]{1,0:T(8,128)(2,1)S(1)}, bf16[128,256]{1,0:T(8,128)(2,1)S(1)}, bf16[480,512]{1,0:T(8,128)(2,1)S(1...) custom-call(bf16[256,256]{1,0:T(8,128)(2,1)S(1)} %get-tuple-element.55.ones_ref, ...), custom_call_target="tpu_custom_call" | custom-call | flops 4000000000 | bytes 1000000 | tf_op jit(solution)/shard_map/pallas_call | solution.py:658
  12.9 0.8 %collective-permute-done.5.refs_0_ = bf16[64,512]{1,0:T(8,128)(2,1)S(1)} collective-permute-done((bf16[64,512]{1,0:T(8,128)(2,1)S(1)}, bf16[64,512]{1,0:T(8,128)(2,1)S(1)}, u32[]{:S(2)}, u32[]{:S(2)}) %collective-permute-start.5) | collective-permute-done | bytes 65568 | tf_op jit(solution)/shard_map/ppermute | solution.py:577
  13.6 0.6 %shard_map.150 = (bf16[128,512]{1,0:T(8,128)(2,1)S(1)}, bf16[4,32,1152]{2,1,0:T(8,128)(2,1)S(1)}, f32[4,32,1024]{2,1,0:T(8,128)S(1)}, bf16[4,32,128]{2,1,0:T(8,128)(2,1)S(1)}) custom-call(f32[480,256]{1,0:T(8,128)S(1)} %get-tuple-element.69.x_ref, bf16[128,256]{1,0:T(8,128)(2,1)S(1)} %get-tuple-element.70.d_query_ref, ...), custom_call_target="tpu_custom_call" | custom-call | flops 1000000000 | bytes 1000000 | tf_op jit(solution)/shard_map/pallas_call | solution.py:689
  14.2 0.1 collective-permute-start.6
  14.3 0.5 %shard_map.151 = (f32[320,256]{1,0:T(8,128)S(1)}, bf16[40,256]{1,0:T(8,128)(2,1)S(1)}, bf16[40,256]{1,0:T(8,128)(2,1)S(1)}, f32[8,128]{1,0:T(8,128)S(1)}) custom-call(f32[480,256]{1,0:T(8,128)S(1)} %get-tuple-element.69.x_ref, bf16[128,256]{1,0:T(8,128)(2,1)S(1)} %get-tuple-element.70.d_query_ref, bf16[480,512]{1,0:T(8,128)(2,1)S(1)} %get-tuple-element.71.d_kv_ref, ...), custom_call_target="tpu_custom_call" | custom-call | flops 500000000 | bytes 1000000 | tf_op jit(solution)/shard_map/pallas_call | solution.py:697
  14.8 0.6 %collective-permute-start.7 = (f32[8,128]{1,0:T(8,128)S(1)}, f32[8,128]{1,0:T(8,128)S(1)}, u32[]{:S(2)}, u32[]{:S(2)}) collective-permute-start(f32[8,128]{1,0:T(8,128)S(1)} %get-tuple-element.77.small_ref), channel_id=1, source_target_pairs={{0,4},{4,0},{8,12},{12,8},{16,20},{20,16},{24,28},{28,24},{1,5},{5... | collective-permute-start | bytes 12296 | tf_op jit(solution)/shard_map/ppermute | solution.py:577
  15.4 0.1 collective-permute-start.11
  15.5 0.7 %collective-permute-done.7.small_near_ref = f32[8,128]{1,0:T(8,128)S(1)} collective-permute-done((f32[8,128]{1,0:T(8,128)S(1)}, f32[8,128]{1,0:T(8,128)S(1)}, u32[]{:S(2)}, u32[]{:S(2)}) %collective-permute-start.7) | collective-permute-done | bytes 4128 | tf_op jit(solution)/shard_map/ppermute | solution.py:577
  16.2 0.0 collective-permute-done.6.got_ref
  16.2 0.1 shard_map.152
  16.3 2.5 %collective-permute-start.8 = (bf16[328,128]{1,0:T(8,128)(2,1)S(1)}, bf16[328,128]{1,0:T(8,128)(2,1)S(1)}, u32[]{:S(2)}, u32[]{:S(2)}) collective-permute-start(bf16[328,128]{1,0:T(8,128)(2,1)S(1)} %get-tuple-element.81), channel_id=1, source_target_pairs={{0,24},{4,28},{8,16},{12,20},{16,8},{20,12},{24,0},{28,4},{1,25},{... | collective-permute-start | bytes 251912 | tf_op jit(solution)/shard_map/ppermute | solution.py:577
  18.9 0.7 %collective-permute-start.9 = (bf16[328,128]{1,0:T(8,128)(2,1)S(1)}, bf16[328,128]{1,0:T(8,128)(2,1)S(1)}, u32[]{:S(2)}, u32[]{:S(2)}) collective-permute-start(bf16[328,128]{1,0:T(8,128)(2,1)S(1)} %get-tuple-element.82), channel_id=1, source_target_pairs={{0,16},{4,20},{8,24},{12,28},{16,0},{20,4},{24,8},{28,12},{1,17},{... | collective-permute-start | bytes 251912 | tf_op jit(solution)/shard_map/ppermute | solution.py:577
  19.5 0.3 collective-permute-start.10
  19.9 2.8 %collective-permute-start.15 = (bf16[40,256]{1,0:T(8,128)(2,1)S(1)}, bf16[40,256]{1,0:T(8,128)(2,1)S(1)}, u32[]{:S(2)}, u32[]{:S(2)}) collective-permute-start(bf16[40,256]{1,0:T(8,128)(2,1)S(1)} %get-tuple-element.91), channel_id=1, source_target_pairs={{0,1},{1,0},{2,3},{3,2},{4,5},{5,4},{6,7},{7,6},{8,9},{9,8},{10,11... | collective-permute-start | bytes 61448 | tf_op jit(solution)/shard_map/ppermute | solution.py:577
  22.7 0.0 collective-permute-done.11.refs_7_
  22.7 0.0 collective-permute-start.16
  22.7 0.0 collective-permute-done.8.refs_3_
  22.7 1.1 %collective-permute-done.9.refs_4_ = bf16[328,128]{1,0:T(8,128)(2,1)S(1)} collective-permute-done((bf16[328,128]{1,0:T(8,128)(2,1)S(1)}, bf16[328,128]{1,0:T(8,128)(2,1)S(1)}, u32[]{:S(2)}, u32[]{:S(2)}) %collective-permute-start.9) | collective-permute-done | bytes 84000 | tf_op jit(solution)/shard_map/ppermute | solution.py:577
  23.8 0.3 collective-permute-done.10.refs_5_
  24.1 0.3 shard_map.153
  24.4 2.7 %collective-permute-start.12 = (bf16[200,128]{1,0:T(8,128)(2,1)S(1)}, bf16[200,128]{1,0:T(8,128)(2,1)S(1)}, u32[]{:S(2)}, u32[]{:S(2)}) collective-permute-start(bf16[200,128]{1,0:T(8,128)(2,1)S(1)} %get-tuple-element.87), channel_id=1, source_target_pairs={{0,3},{1,2},{2,1},{3,0},{4,7},{5,6},{6,5},{7,4},{8,11},{9,10},{10,... | collective-permute-start | bytes 153608 | tf_op jit(solution)/shard_map/ppermute | solution.py:577
  27.2 1.7 %collective-permute-start.13 = (bf16[200,128]{1,0:T(8,128)(2,1)S(1)}, bf16[200,128]{1,0:T(8,128)(2,1)S(1)}, u32[]{:S(2)}, u32[]{:S(2)}) collective-permute-start(bf16[200,128]{1,0:T(8,128)(2,1)S(1)} %get-tuple-element.88), channel_id=1, source_target_pairs={{0,2},{1,3},{2,0},{3,1},{4,6},{5,7},{6,4},{7,5},{8,10},{9,11},{10,... | collective-permute-start | bytes 153608 | tf_op jit(solution)/shard_map/ppermute | solution.py:577
  28.9 0.0 collective-permute-start.14
  28.9 0.0 collective-permute-done.15.near_ref
  28.9 0.0 collective-permute-done.16.far_ref
  29.0 2.1 %collective-permute-start.17 = (bf16[96,256]{1,0:T(8,128)(2,1)S(1)}, bf16[96,256]{1,0:T(8,128)(2,1)S(1)}, u32[]{:S(2)}, u32[]{:S(2)}) collective-permute-start(bf16[96,256]{1,0:T(8,128)(2,1)S(1)} %get-tuple-element.94), channel_id=1, source_target_pairs={{0,1},{1,0},{2,3},{3,2},{4,8},{5,9},{6,10},{7,11},{8,4},{9,5},{10,... | collective-permute-start | bytes 147464 | tf_op jit(solution)/shard_map/ppermute | solution.py:572
  31.0 0.0 collective-permute-start.18
  31.0 0.9 %shard_map.148 = (bf16[4,32,256]{2,1,0:T(8,128)(2,1)}, bf16[2,16,512]{2,1,0:T(8,128)(2,1)}) custom-call(bf16[128,256]{1,0:T(8,128)(2,1)S(1)} %get-tuple-element.65.y_ref, bf16[32,1024]{1,0:T(8,128)(2,1)S(1)} %get-tuple-element.66.group_ref, bf16[1024,512]{1,0:T(8,128)(2,1)S(1)} %copy-done.1), custom_call_target="tpu_custom_call" | custom-call | flops 1000000000 | bytes 1000000 | tf_op jit(solution)/shard_map/pallas_call | solution.py:707
  32.0 1.7 %collective-permute-done.17.far_ref = bf16[96,256]{1,0:T(8,128)(2,1)S(1)} collective-permute-done((bf16[96,256]{1,0:T(8,128)(2,1)S(1)}, bf16[96,256]{1,0:T(8,128)(2,1)S(1)}, u32[]{:S(2)}, u32[]{:S(2)}) %collective-permute-start.17) | collective-permute-done | bytes 49184 | tf_op jit(solution)/shard_map/ppermute | solution.py:572
  33.6 0.0 collective-permute-done.18.near_ref
  33.6 0.0 collective-permute-done.12.d_ref
  33.6 0.0 collective-permute-done.13.c_ref
  33.6 0.0 collective-permute-done.14.b_ref
  33.6 0.7 %shard_map.155 = (f32[32,192]{1,0:T(8,128)}, f32[32,64]{1,0:T(8,128)}, f32[128,128]{1,0:T(8,128)}, f32[1,256]{1,0:T(1,128)}, f32[4]{0:T(128)}, /*index=5*/bf16[4,32,256]{2,1,0:T(8,128)(2,1)}) custom-call(bf16[200,128]{1,0:T(8,128)(2,1)S(1)} %get-tuple-element.86.a_ref, bf16[200,128]{1,0:T(8,128)(2,1)S(1)} %collective-permute-done.12.d_ref, ...), custom_call_target="tpu_custom_call" | custom-call | tf_op jit(solution)/shard_map/pallas_call | solution.py:753
  (4 shorter events, 0.1 us)
Async XLA Ops:
  0.6 5.7 %collective-permute-start = (bf16[4,32,256]{2,1,0:T(8,128)(2,1)}, bf16[4,32,256]{2,1,0:T(8,128)(2,1)S(1)}, u32[]{:S(2)}, u32[]{:S(2)}) collective-permute-start(bf16[4,32,256]{2,1,0:T(8,128)(2,1)} %tok_ref.3), channel_id=1, source_target_pairs={{0,1},{1,0},{2,3},{3,2},{4,8},{5,9},{6,10},{7,11},{8,4},{9,5},{10,... | collective-permute-start | bytes 196616 | tf_op jit(solution)/shard_map/ppermute | solution.py:572
  3.7 2.6 %collective-permute-start.1 = (bf16[4,32,256]{2,1,0:T(8,128)(2,1)}, bf16[4,32,256]{2,1,0:T(8,128)(2,1)S(1)}, u32[]{:S(2)}, u32[]{:S(2)}) collective-permute-start(bf16[4,32,256]{2,1,0:T(8,128)(2,1)} %tok_ref.3), channel_id=1, source_target_pairs={{0,4},{4,0},{8,12},{12,8},{16,20},{20,16},{24,28},{28,24},{1,5},{5... | collective-permute-start | bytes 196616 | tf_op jit(solution)/shard_map/ppermute | solution.py:577
  3.8 1.6 %copy-start.2 = (bf16[256,768]{1,0:T(8,128)(2,1)S(1)}, bf16[256,768]{1,0:T(8,128)(2,1)}, u32[]{:S(2)}) copy-start(bf16[256,768]{1,0:T(8,128)(2,1)} %wqkv_ref.5) | copy-start | bytes 1179652
  3.8 1.6 %copy-start.5 = (bf16[4,32,256]{2,1,0:T(8,128)(2,1)S(1)}, bf16[4,32,256]{2,1,0:T(8,128)(2,1)}, u32[]{:S(2)}) copy-start(bf16[4,32,256]{2,1,0:T(8,128)(2,1)} %tok_ref.3) | copy-start | bytes 196612
  3.8 5.2 %collective-permute-start.4 = (bf16[32,512]{1,0:T(8,128)(2,1)}, bf16[32,512]{1,0:T(8,128)(2,1)S(1)}, u32[]{:S(2)}, u32[]{:S(2)}) collective-permute-start(bf16[32,512]{1,0:T(8,128)(2,1)} %bitcast.4), channel_id=1, source_target_pairs={{0,8},{4,12},{8,0},{12,4},{16,24},{20,28},{24,16},{28,20},{1,9},{5... | collective-permute-start | bytes 98312 | tf_op jit(solution)/shard_map/ppermute | solution.py:577
  5.2 0.7 %copy-start.6 = (f32[256]{0:T(256)S(1)}, f32[256]{0:T(256)}, u32[]{:S(2)}) copy-start(f32[256]{0:T(256)} %param.9) | copy-start | bytes 3076
  5.3 0.7 %copy-start.7 = (f32[4]{0:T(128)S(1)}, f32[4]{0:T(128)}, u32[]{:S(2)}) copy-start(f32[4]{0:T(128)} %param.11) | copy-start | bytes 52
  5.3 3.0 %copy-start.1 = (bf16[1024,512]{1,0:T(8,128)(2,1)S(1)}, bf16[1024,512]{1,0:T(8,128)(2,1)}, u32[]{:S(2)}) copy-start(bf16[1024,512]{1,0:T(8,128)(2,1)} %wmerge_ref.3) | copy-start | bytes 3145732
  5.9 2.4 %copy-start.3 = (bf16[256,256]{1,0:T(8,128)(2,1)S(1)}, bf16[256,256]{1,0:T(8,128)(2,1)}, u32[]{:S(2)}) copy-start(bf16[256,256]{1,0:T(8,128)(2,1)} %wout_ref.3) | copy-start | bytes 393220
  6.4 2.0 %copy-start = (bf16[2,16,512]{2,1,0:T(8,128)(2,1)S(1)}, bf16[2,16,512]{2,1,0:T(8,128)(2,1)}, u32[]{:S(2)}) copy-start(bf16[2,16,512]{2,1,0:T(8,128)(2,1)} %dm_ref.3) | copy-start | bytes 98308
  6.4 2.0 %copy-start.4 = (bf16[4,32,256]{2,1,0:T(8,128)(2,1)S(1)}, bf16[4,32,256]{2,1,0:T(8,128)(2,1)}, u32[]{:S(2)}) copy-start(bf16[4,32,256]{2,1,0:T(8,128)(2,1)} %dskip_ref.1) | copy-start | bytes 196612
  6.4 4.5 %collective-permute-start.2 = (bf16[40,256]{1,0:T(8,128)(2,1)S(1)}, bf16[40,256]{1,0:T(8,128)(2,1)S(1)}, u32[]{:S(2)}, u32[]{:S(2)}) collective-permute-start(bf16[40,256]{1,0:T(8,128)(2,1)S(1)} %get-tuple-element.58), channel_id=1, source_target_pairs={{0,1},{1,0},{2,3},{3,2},{4,5},{5,4},{6,7},{7,6},{8,9},{9,8},{10,11... | collective-permute-start | bytes 61448 | tf_op jit(solution)/shard_map/ppermute | solution.py:577
  8.3 2.6 %collective-permute-start.3 = (bf16[40,256]{1,0:T(8,128)(2,1)S(1)}, bf16[40,256]{1,0:T(8,128)(2,1)S(1)}, u32[]{:S(2)}, u32[]{:S(2)}) collective-permute-start(bf16[40,256]{1,0:T(8,128)(2,1)S(1)} %get-tuple-element.59), channel_id=1, source_target_pairs={{0,4},{1,2},{2,1},{3,7},{4,0},{5,6},{6,5},{7,3},{8,12},{9,10},{10,... | collective-permute-start | bytes 61448 | tf_op jit(solution)/shard_map/ppermute | solution.py:572
  9.0 4.7 %collective-permute-start.5 = (bf16[64,512]{1,0:T(8,128)(2,1)S(1)}, bf16[64,512]{1,0:T(8,128)(2,1)S(1)}, u32[]{:S(2)}, u32[]{:S(2)}) collective-permute-start(bf16[64,512]{1,0:T(8,128)(2,1)S(1)} %shard_map.149.refs_1_), channel_id=1, source_target_pairs={{0,16},{4,20},{8,24},{12,28},{16,0},{20,4},{24,8},{28,12},{1,17},{... | collective-permute-start | bytes 196616 | tf_op jit(solution)/shard_map/ppermute | solution.py:577
  14.2 2.0 %collective-permute-start.6 = (bf16[4,32,1152]{2,1,0:T(8,128)(2,1)S(1)}, bf16[4,32,1152]{2,1,0:T(8,128)(2,1)S(1)}, u32[]{:S(2)}, u32[]{:S(2)}) collective-permute-start(bf16[4,32,1152]{2,1,0:T(8,128)(2,1)S(1)} %get-tuple-element.73), channel_id=1, source_target_pairs={{0,4},{4,0},{8,12},{12,8},{16,20},{20,16},{24,28},{28,24},{1,5},{5... | collective-permute-start | bytes 884744 | tf_op jit(solution)/shard_map/ppermute | solution.py:577
  14.8 1.4 %collective-permute-start.7 = (f32[8,128]{1,0:T(8,128)S(1)}, f32[8,128]{1,0:T(8,128)S(1)}, u32[]{:S(2)}, u32[]{:S(2)}) collective-permute-start(f32[8,128]{1,0:T(8,128)S(1)} %get-tuple-element.77.small_ref), channel_id=1, source_target_pairs={{0,4},{4,0},{8,12},{12,8},{16,20},{20,16},{24,28},{28,24},{1,5},{5... | collective-permute-start | bytes 12296 | tf_op jit(solution)/shard_map/ppermute | solution.py:577
  15.4 7.3 %collective-permute-start.11 = (bf16[128,512]{1,0:T(8,128)(2,1)S(1)}, bf16[128,512]{1,0:T(8,128)(2,1)S(1)}, u32[]{:S(2)}, u32[]{:S(2)}) collective-permute-start(bf16[128,512]{1,0:T(8,128)(2,1)S(1)} %get-tuple-element.84.refs_6_), channel_id=1, source_target_pairs={{0,4},{4,0},{8,12},{12,8},{16,20},{20,16},{24,28},{28,24},{1,5},{5... | collective-permute-start | bytes 393224 | tf_op jit(solution)/shard_map/ppermute | solution.py:577
  16.3 6.4 %collective-permute-start.8 = (bf16[328,128]{1,0:T(8,128)(2,1)S(1)}, bf16[328,128]{1,0:T(8,128)(2,1)S(1)}, u32[]{:S(2)}, u32[]{:S(2)}) collective-permute-start(bf16[328,128]{1,0:T(8,128)(2,1)S(1)} %get-tuple-element.81), channel_id=1, source_target_pairs={{0,24},{4,28},{8,16},{12,20},{16,8},{20,12},{24,0},{28,4},{1,25},{... | collective-permute-start | bytes 251912 | tf_op jit(solution)/shard_map/ppermute | solution.py:577
  18.9 5.0 %collective-permute-start.9 = (bf16[328,128]{1,0:T(8,128)(2,1)S(1)}, bf16[328,128]{1,0:T(8,128)(2,1)S(1)}, u32[]{:S(2)}, u32[]{:S(2)}) collective-permute-start(bf16[328,128]{1,0:T(8,128)(2,1)S(1)} %get-tuple-element.82), channel_id=1, source_target_pairs={{0,16},{4,20},{8,24},{12,28},{16,0},{20,4},{24,8},{28,12},{1,17},{... | collective-permute-start | bytes 251912 | tf_op jit(solution)/shard_map/ppermute | solution.py:577
  19.5 4.6 %collective-permute-start.10 = (bf16[328,128]{1,0:T(8,128)(2,1)S(1)}, bf16[328,128]{1,0:T(8,128)(2,1)S(1)}, u32[]{:S(2)}, u32[]{:S(2)}) collective-permute-start(bf16[328,128]{1,0:T(8,128)(2,1)S(1)} %get-tuple-element.83), channel_id=1, source_target_pairs={{0,8},{4,12},{8,0},{12,4},{16,24},{20,28},{24,16},{28,20},{1,9},{5... | collective-permute-start | bytes 251912 | tf_op jit(solution)/shard_map/ppermute | solution.py:577
  19.9 9.0 %collective-permute-start.15 = (bf16[40,256]{1,0:T(8,128)(2,1)S(1)}, bf16[40,256]{1,0:T(8,128)(2,1)S(1)}, u32[]{:S(2)}, u32[]{:S(2)}) collective-permute-start(bf16[40,256]{1,0:T(8,128)(2,1)S(1)} %get-tuple-element.91), channel_id=1, source_target_pairs={{0,1},{1,0},{2,3},{3,2},{4,5},{5,4},{6,7},{7,6},{8,9},{9,8},{10,11... | collective-permute-start | bytes 61448 | tf_op jit(solution)/shard_map/ppermute | solution.py:577
  22.7 6.2 %collective-permute-start.16 = (bf16[40,256]{1,0:T(8,128)(2,1)S(1)}, bf16[40,256]{1,0:T(8,128)(2,1)S(1)}, u32[]{:S(2)}, u32[]{:S(2)}) collective-permute-start(bf16[40,256]{1,0:T(8,128)(2,1)S(1)} %get-tuple-element.92), channel_id=1, source_target_pairs={{0,4},{1,2},{2,1},{3,7},{4,0},{5,6},{6,5},{7,3},{8,12},{9,10},{10,... | collective-permute-start | bytes 61448 | tf_op jit(solution)/shard_map/ppermute | solution.py:572
  24.4 9.2 %collective-permute-start.12 = (bf16[200,128]{1,0:T(8,128)(2,1)S(1)}, bf16[200,128]{1,0:T(8,128)(2,1)S(1)}, u32[]{:S(2)}, u32[]{:S(2)}) collective-permute-start(bf16[200,128]{1,0:T(8,128)(2,1)S(1)} %get-tuple-element.87), channel_id=1, source_target_pairs={{0,3},{1,2},{2,1},{3,0},{4,7},{5,6},{6,5},{7,4},{8,11},{9,10},{10,... | collective-permute-start | bytes 153608 | tf_op jit(solution)/shard_map/ppermute | solution.py:577
  27.2 6.5 %collective-permute-start.13 = (bf16[200,128]{1,0:T(8,128)(2,1)S(1)}, bf16[200,128]{1,0:T(8,128)(2,1)S(1)}, u32[]{:S(2)}, u32[]{:S(2)}) collective-permute-start(bf16[200,128]{1,0:T(8,128)(2,1)S(1)} %get-tuple-element.88), channel_id=1, source_target_pairs={{0,2},{1,3},{2,0},{3,1},{4,6},{5,7},{6,4},{7,5},{8,10},{9,11},{10,... | collective-permute-start | bytes 153608 | tf_op jit(solution)/shard_map/ppermute | solution.py:577
  28.9 4.7 %collective-permute-start.14 = (bf16[200,128]{1,0:T(8,128)(2,1)S(1)}, bf16[200,128]{1,0:T(8,128)(2,1)S(1)}, u32[]{:S(2)}, u32[]{:S(2)}) collective-permute-start(bf16[200,128]{1,0:T(8,128)(2,1)S(1)} %get-tuple-element.89), channel_id=1, source_target_pairs={{0,1},{1,0},{2,3},{3,2},{4,5},{5,4},{6,7},{7,6},{8,9},{9,8},{10,11... | collective-permute-start | bytes 153608 | tf_op jit(solution)/shard_map/ppermute | solution.py:577
  29.0 4.7 %collective-permute-start.17 = (bf16[96,256]{1,0:T(8,128)(2,1)S(1)}, bf16[96,256]{1,0:T(8,128)(2,1)S(1)}, u32[]{:S(2)}, u32[]{:S(2)}) collective-permute-start(bf16[96,256]{1,0:T(8,128)(2,1)S(1)} %get-tuple-element.94), channel_id=1, source_target_pairs={{0,1},{1,0},{2,3},{3,2},{4,8},{5,9},{6,10},{7,11},{8,4},{9,5},{10,... | collective-permute-start | bytes 147464 | tf_op jit(solution)/shard_map/ppermute | solution.py:572
  31.0 2.6 %collective-permute-start.18 = (bf16[96,256]{1,0:T(8,128)(2,1)S(1)}, bf16[96,256]{1,0:T(8,128)(2,1)S(1)}, u32[]{:S(2)}, u32[]{:S(2)}) collective-permute-start(bf16[96,256]{1,0:T(8,128)(2,1)S(1)} %get-tuple-element.95), channel_id=1, source_target_pairs={{0,4},{4,0},{8,12},{12,8},{16,20},{20,16},{24,28},{28,24},{1,5},{5... | collective-permute-start | bytes 147464 | tf_op jit(solution)/shard_map/ppermute | solution.py:577

commit v12 on v10

--- a/solution.py
+++ b/solution.py
@@ -430,9 +430,8 @@
 def row_sum_kernel(sizes, *refs):
     rows, cols, width, n_col = sizes
     own_ref, own_group_ref, small_ref, *refs = refs
-    got_refs, dm_ref, dm_near_ref, gx_ref, *refs = (refs[:3], *refs[3:])
-    *out_refs, gx_sum_ref, slots_ref = refs
-    gx_sum_ref[...] = gx_ref[...]
+    got_refs, dm_ref, dm_near_ref, *refs = (refs[:3], *refs[3:])
+    *out_refs, slots_ref = refs
     per = own_ref.shape[0]
     feats = own_group_ref.shape[1]
     size = 4 * width // LANES * per
@@ -744,14 +743,14 @@
         )(swap(send, "row", 1), *kept, small, swap(small, "row", 1))
         got = [swap(blocks[step - 1], "row", 2 * step) for step in (3, 2, 1)]
         slot = shape((4 * width // n_col // LANES * per + feats + 8, LANES), BF)
-        *slots, gx = pl.pallas_call(
+        slots = pl.pallas_call(
             functools.partial(row_sum_kernel, (rows, cols, width, n_col)),
-            out_shape=(slot,) * n_col + (shape(gx.shape, F32),),
-            in_specs=vmem(9),
-            out_specs=tuple(vmem(n_col + 1)),
+            out_shape=(slot,) * n_col,
+            in_specs=vmem(8),
+            out_specs=tuple(vmem(n_col)),
             scratch_shapes=[pltpu.VMEM((n_col,) + slot.shape, BF)],
             compiler_params=less,
-        )(own, own_group, small, *got, dm_core, swap(dm_core, "row", 1), gx)
+        )(own, own_group, small, *got, dm_core, swap(dm_core, "row", 1))
         got = [slots[0]] + [swap(slots[step], "col", step) for step in (3, 2, 1)]
         grad, *rims = side_call(gx, *sides)
         rims = swapped(*rims, "row")

time: 34.1 us -> 39.5 us (1.16)
  waiting for transfers between devices: 4.73 us -> 7.54 us
  starting transfers between devices: 21.7 us -> 24.3 us
    ppermute x15, waiting for transfers between devices: 2.85 us -> 6.35 us  [swap(): return lax.ppermute(value, axis, [(i, i ^ step) for i in range(count)])]
    ppermute x4, starting transfers between devices: 5.17 us -> 7.77 us  [swapped(): return (swap(near, axis, 1), lax.ppermute(far, ('row', 'col'), pairs))]
    ppermute x4, waiting for transfers between devices: 1.88 us -> 1.19 us  [swapped(): return (swap(near, axis, 1), lax.ppermute(far, ('row', 'col'), pairs))]
  transfers between devices with their start and end apart: 19 -> 19, of which waited for: 6 -> 7; matrix products, arithmetic and copies ran while one was open for 0% -> 0% of each run, Pallas kernels for 14% -> 12%
where the time goes in v12:
time: 39.5 us; the launch traced here: 39.3 us
  starting transfers between devices  24.3 us (62%)
  waiting for transfers between devices  7.54 us (19%)
  Pallas kernels  6.02 us (15%)
  between operations  0.84 us (2%)
  local copies, waits for them, and re-layouts  0.63 us (2%)
    ppermute x15, starting transfers between devices, swap(): return lax.ppermute(value, axis, [(i, i ^ step) for i in range(count)])  16.5 us
    ppermute x4, starting transfers between devices, swapped(): return (swap(near, axis, 1), lax.ppermute(far, ('row', 'col'), pairs))  7.77 us
    ppermute x15, waiting for transfers between devices, swap(): return lax.ppermute(value, axis, [(i, i ^ step) for i in range(count)])  6.35 us
    pallas_call x1, Pallas kernels, on_device(): pl.pallas_call(functools.partial(layer_kernel, sizes), out_shape=(shape((...  1.97 us
    ppermute x4, waiting for transfers between devices, swapped(): return (swap(near, axis, 1), lax.ppermute(far, ('row', 'col'), pairs))  1.19 us
    pallas_call x1, Pallas kernels, on_device(): pl.pallas_call(output_kernel, out_shape=(shape((rows, cols, width), BF),...  0.9 us
    pallas_call x1, Pallas kernels, on_device(): pl.pallas_call(own_kernel, out_shape=(shape((2 * rows * EDGE, width), BF)...  0.79 us
  transfers between devices with their start and end apart: 19, of which 7 were waited for; matrix products, arithmetic and copies ran while one was open for 0% of the time, Pallas kernels for 12%

profile of v12, /device:TPU:0, one launch (start us, length us, event | category | flops | bytes accessed | tf_op | source)
XLA Modules:
  0.0 39.3 jit_solution(6267215448190052015)
XLA Ops:
  0.6 3.1 %collective-permute-start = (bf16[4,32,256]{2,1,0:T(8,128)(2,1)}, bf16[4,32,256]{2,1,0:T(8,128)(2,1)S(1)}, u32[]{:S(2)}, u32[]{:S(2)}) collective-permute-start(bf16[4,32,256]{2,1,0:T(8,128)(2,1)} %tok_ref.3), channel_id=1, source_target_pairs={{0,1},{1,0},{2,3},{3,2},{4,8},{5,9},{6,10},{7,11},{8,4},{9,5},{10,... | collective-permute-start | bytes 196616 | tf_op jit(solution)/shard_map/ppermute | solution.py:573
  3.7 0.0 collective-permute-start.1
  3.8 0.0 copy-start
  3.8 0.0 copy-start.1
  3.8 0.0 copy-start.2
  3.8 0.0 copy-start.3
  3.8 0.0 copy-start.4
  3.8 0.0 copy-start.5
  3.8 1.6 %collective-permute-start.4 = (bf16[32,512]{1,0:T(8,128)(2,1)}, bf16[32,512]{1,0:T(8,128)(2,1)S(1)}, u32[]{:S(2)}, u32[]{:S(2)}) collective-permute-start(bf16[32,512]{1,0:T(8,128)(2,1)} %bitcast.4), channel_id=1, source_target_pairs={{0,8},{4,12},{8,0},{12,4},{16,24},{20,28},{24,16},{28,20},{1,9},{5... | collective-permute-start | bytes 98312 | tf_op jit(solution)/shard_map/ppermute | solution.py:578
  5.4 0.0 copy-start.6
  5.4 0.0 copy-start.7
  5.4 0.0 copy-done
  5.4 0.0 copy-done.1
  5.4 0.0 copy-done.2
  5.4 0.0 copy-done.3
  5.4 0.0 copy-done.4
  5.5 0.0 copy-done.5
  5.5 0.6 %copy-done.6 = f32[256]{0:T(256)S(1)} copy-done((f32[256]{0:T(256)S(1)}, f32[256]{0:T(256)}, u32[]{:S(2)}) %copy-start.6) | copy-done | bytes 1048
  6.1 0.0 copy-done.7
  6.1 0.8 %shard_map.144 = (bf16[32,256]{1,0:T(8,128)(2,1)S(1)}, f32[8,256]{1,0:T(8,128)S(1)}, f32[128,256]{1,0:T(8,128)S(1)}, f32[128,256]{1,0:T(8,128)S(1)}, f32[128,256...) custom-call(bf16[256,256]{1,0:T(8,128)(2,1)S(1)} %get-tuple-element.54.ones_ref, f32[8,128]{1,0:T(8,128)S(1)} %get-tuple-element.55.parity_ref, ...), custom_call_target="tpu_custom_call" | custom-call | flops 1000000000 | bytes 1000000 | tf_op jit(solution)/shard_map/pallas_call | solution.py:608
  6.9 0.0 collective-permute-done.far_ref.row_far_ref
  6.9 0.0 collective-permute-done.1.near_ref.row_near_ref
  6.9 1.6 %collective-permute-start.2 = (bf16[40,256]{1,0:T(8,128)(2,1)S(1)}, bf16[40,256]{1,0:T(8,128)(2,1)S(1)}, u32[]{:S(2)}, u32[]{:S(2)}) collective-permute-start(bf16[40,256]{1,0:T(8,128)(2,1)S(1)} %get-tuple-element.57), channel_id=1, source_target_pairs={{0,1},{1,0},{2,3},{3,2},{4,5},{5,4},{6,7},{7,6},{8,9},{9,8},{10,11... | collective-permute-start | bytes 61448 | tf_op jit(solution)/shard_map/ppermute | solution.py:578
  8.6 0.0 collective-permute-start.3
  8.6 0.0 collective-permute-done.4.dm_next_ref
  8.6 1.6 %collective-permute-start.5 = (bf16[64,512]{1,0:T(8,128)(2,1)S(1)}, bf16[64,512]{1,0:T(8,128)(2,1)S(1)}, u32[]{:S(2)}, u32[]{:S(2)}) collective-permute-start(bf16[64,512]{1,0:T(8,128)(2,1)S(1)} %shard_map.148.refs_1_), channel_id=1, source_target_pairs={{0,16},{4,20},{8,24},{12,28},{16,0},{20,4},{24,8},{28,12},{1,17},{... | collective-permute-start | bytes 196616 | tf_op jit(solution)/shard_map/ppermute | solution.py:578
  10.2 0.5 %collective-permute-done.2.col_near_ref = bf16[40,256]{1,0:T(8,128)(2,1)S(1)} collective-permute-done((bf16[40,256]{1,0:T(8,128)(2,1)S(1)}, bf16[40,256]{1,0:T(8,128)(2,1)S(1)}, u32[]{:S(2)}, u32[]{:S(2)}) %collective-permute-start.2) | collective-permute-done | bytes 20512 | tf_op jit(solution)/shard_map/ppermute | solution.py:578
  10.8 0.0 collective-permute-done.3.col_far_ref
  10.8 2.0 %shard_map.146 = (f32[480,256]{1,0:T(8,128)S(1)}, bf16[128,256]{1,0:T(8,128)(2,1)S(1)}, bf16[128,256]{1,0:T(8,128)(2,1)S(1)}, bf16[480,512]{1,0:T(8,128)(2,1)S(1...) custom-call(bf16[256,256]{1,0:T(8,128)(2,1)S(1)} %get-tuple-element.54.ones_ref, ...), custom_call_target="tpu_custom_call" | custom-call | flops 4000000000 | bytes 1000000 | tf_op jit(solution)/shard_map/pallas_call | solution.py:662
  12.7 0.4 %collective-permute-done.5.refs_0_ = bf16[64,512]{1,0:T(8,128)(2,1)S(1)} collective-permute-done((bf16[64,512]{1,0:T(8,128)(2,1)S(1)}, bf16[64,512]{1,0:T(8,128)(2,1)S(1)}, u32[]{:S(2)}, u32[]{:S(2)}) %collective-permute-start.5) | collective-permute-done | bytes 65568 | tf_op jit(solution)/shard_map/ppermute | solution.py:578
  13.1 0.6 %shard_map.149 = (bf16[128,512]{1,0:T(8,128)(2,1)S(1)}, bf16[4,32,1152]{2,1,0:T(8,128)(2,1)S(1)}, f32[4,32,1024]{2,1,0:T(8,128)S(1)}, bf16[4,32,128]{2,1,0:T(8,128)(2,1)S(1)}) custom-call(f32[480,256]{1,0:T(8,128)S(1)} %get-tuple-element.68.x_ref, bf16[128,256]{1,0:T(8,128)(2,1)S(1)} %get-tuple-element.69.d_query_ref, ...), custom_call_target="tpu_custom_call" | custom-call | flops 1000000000 | bytes 1000000 | tf_op jit(solution)/shard_map/pallas_call | solution.py:693
  13.7 0.1 collective-permute-start.6
  13.8 0.5 %shard_map.150 = (f32[320,256]{1,0:T(8,128)S(1)}, bf16[40,256]{1,0:T(8,128)(2,1)S(1)}, bf16[40,256]{1,0:T(8,128)(2,1)S(1)}, f32[8,128]{1,0:T(8,128)S(1)}) custom-call(f32[480,256]{1,0:T(8,128)S(1)} %get-tuple-element.68.x_ref, bf16[128,256]{1,0:T(8,128)(2,1)S(1)} %get-tuple-element.69.d_query_ref, bf16[480,512]{1,0:T(8,128)(2,1)S(1)} %get-tuple-element.70.d_kv_ref, ...), custom_call_target="tpu_custom_call" | custom-call | flops 500000000 | bytes 1000000 | tf_op jit(solution)/shard_map/pallas_call | solution.py:701
  14.4 0.6 %collective-permute-start.7 = (f32[8,128]{1,0:T(8,128)S(1)}, f32[8,128]{1,0:T(8,128)S(1)}, u32[]{:S(2)}, u32[]{:S(2)}) collective-permute-start(f32[8,128]{1,0:T(8,128)S(1)} %get-tuple-element.76.small_ref), channel_id=1, source_target_pairs={{0,4},{4,0},{8,12},{12,8},{16,20},{20,16},{24,28},{28,24},{1,5},{5... | collective-permute-start | bytes 12296 | tf_op jit(solution)/shard_map/ppermute | solution.py:578
  14.9 0.1 collective-permute-start.11
  15.0 0.7 %collective-permute-done.7.small_near_ref = f32[8,128]{1,0:T(8,128)S(1)} collective-permute-done((f32[8,128]{1,0:T(8,128)S(1)}, f32[8,128]{1,0:T(8,128)S(1)}, u32[]{:S(2)}, u32[]{:S(2)}) %collective-permute-start.7) | collective-permute-done | bytes 4128 | tf_op jit(solution)/shard_map/ppermute | solution.py:578
  15.7 0.0 collective-permute-done.6.got_ref
  15.7 0.1 shard_map.151
  15.8 2.4 %collective-permute-start.8 = (bf16[328,128]{1,0:T(8,128)(2,1)S(1)}, bf16[328,128]{1,0:T(8,128)(2,1)S(1)}, u32[]{:S(2)}, u32[]{:S(2)}) collective-permute-start(bf16[328,128]{1,0:T(8,128)(2,1)S(1)} %get-tuple-element.80), channel_id=1, source_target_pairs={{0,24},{4,28},{8,16},{12,20},{16,8},{20,12},{24,0},{28,4},{1,25},{... | collective-permute-start | bytes 251912 | tf_op jit(solution)/shard_map/ppermute | solution.py:578
  18.2 0.7 %collective-permute-start.9 = (bf16[328,128]{1,0:T(8,128)(2,1)S(1)}, bf16[328,128]{1,0:T(8,128)(2,1)S(1)}, u32[]{:S(2)}, u32[]{:S(2)}) collective-permute-start(bf16[328,128]{1,0:T(8,128)(2,1)S(1)} %get-tuple-element.81), channel_id=1, source_target_pairs={{0,16},{4,20},{8,24},{12,28},{16,0},{20,4},{24,8},{28,12},{1,17},{... | collective-permute-start | bytes 251912 | tf_op jit(solution)/shard_map/ppermute | solution.py:578
  18.9 0.5 %collective-permute-start.10 = (bf16[328,128]{1,0:T(8,128)(2,1)S(1)}, bf16[328,128]{1,0:T(8,128)(2,1)S(1)}, u32[]{:S(2)}, u32[]{:S(2)}) collective-permute-start(bf16[328,128]{1,0:T(8,128)(2,1)S(1)} %get-tuple-element.82), channel_id=1, source_target_pairs={{0,8},{4,12},{8,0},{12,4},{16,24},{20,28},{24,16},{28,20},{1,9},{5... | collective-permute-start | bytes 251912 | tf_op jit(solution)/shard_map/ppermute | solution.py:578
  19.4 2.9 %collective-permute-start.15 = (bf16[40,256]{1,0:T(8,128)(2,1)S(1)}, bf16[40,256]{1,0:T(8,128)(2,1)S(1)}, u32[]{:S(2)}, u32[]{:S(2)}) collective-permute-start(bf16[40,256]{1,0:T(8,128)(2,1)S(1)} %get-tuple-element.89), channel_id=1, source_target_pairs={{0,1},{1,0},{2,3},{3,2},{4,5},{5,4},{6,7},{7,6},{8,9},{9,8},{10,11... | collective-permute-start | bytes 61448 | tf_op jit(solution)/shard_map/ppermute | solution.py:578
  22.3 1.8 %collective-permute-done.15.near_ref = bf16[40,256]{1,0:T(8,128)(2,1)S(1)} collective-permute-done((bf16[40,256]{1,0:T(8,128)(2,1)S(1)}, bf16[40,256]{1,0:T(8,128)(2,1)S(1)}, u32[]{:S(2)}, u32[]{:S(2)}) %collective-permute-start.15) | collective-permute-done | bytes 20512 | tf_op jit(solution)/shard_map/ppermute | solution.py:578
  24.1 0.0 collective-permute-start.16
  24.1 1.2 %collective-permute-done.16.far_ref = bf16[40,256]{1,0:T(8,128)(2,1)S(1)} collective-permute-done((bf16[40,256]{1,0:T(8,128)(2,1)S(1)}, bf16[40,256]{1,0:T(8,128)(2,1)S(1)}, u32[]{:S(2)}, u32[]{:S(2)}) %collective-permute-start.16) | collective-permute-done | bytes 20512 | tf_op jit(solution)/shard_map/ppermute | solution.py:573
  25.3 4.7 %collective-permute-start.17 = (bf16[96,256]{1,0:T(8,128)(2,1)S(1)}, bf16[96,256]{1,0:T(8,128)(2,1)S(1)}, u32[]{:S(2)}, u32[]{:S(2)}) collective-permute-start(bf16[96,256]{1,0:T(8,128)(2,1)S(1)} %get-tuple-element.92), channel_id=1, source_target_pairs={{0,1},{1,0},{2,3},{3,2},{4,8},{5,9},{6,10},{7,11},{8,4},{9,5},{10,... | collective-permute-start | bytes 147464 | tf_op jit(solution)/shard_map/ppermute | solution.py:573
  30.0 0.0 collective-permute-done.11.refs_7_
  30.0 0.0 collective-permute-start.18
  30.0 0.0 collective-permute-done.8.refs_3_
  30.0 0.0 collective-permute-done.9.refs_4_
  30.0 0.0 collective-permute-done.10.refs_5_
  30.0 0.3 shard_map.152
  30.3 2.4 %collective-permute-start.12 = (bf16[200,128]{1,0:T(8,128)(2,1)S(1)}, bf16[200,128]{1,0:T(8,128)(2,1)S(1)}, u32[]{:S(2)}, u32[]{:S(2)}) collective-permute-start(bf16[200,128]{1,0:T(8,128)(2,1)S(1)} %get-tuple-element.85), channel_id=1, source_target_pairs={{0,3},{1,2},{2,1},{3,0},{4,7},{5,6},{6,5},{7,4},{8,11},{9,10},{10,... | collective-permute-start | bytes 153608 | tf_op jit(solution)/shard_map/ppermute | solution.py:578
  32.7 0.5 %collective-permute-start.13 = (bf16[200,128]{1,0:T(8,128)(2,1)S(1)}, bf16[200,128]{1,0:T(8,128)(2,1)S(1)}, u32[]{:S(2)}, u32[]{:S(2)}) collective-permute-start(bf16[200,128]{1,0:T(8,128)(2,1)S(1)} %get-tuple-element.86), channel_id=1, source_target_pairs={{0,2},{1,3},{2,0},{3,1},{4,6},{5,7},{6,4},{7,5},{8,10},{9,11},{10,... | collective-permute-start | bytes 153608 | tf_op jit(solution)/shard_map/ppermute | solution.py:578
  33.2 1.6 %collective-permute-start.14 = (bf16[200,128]{1,0:T(8,128)(2,1)S(1)}, bf16[200,128]{1,0:T(8,128)(2,1)S(1)}, u32[]{:S(2)}, u32[]{:S(2)}) collective-permute-start(bf16[200,128]{1,0:T(8,128)(2,1)S(1)} %get-tuple-element.87), channel_id=1, source_target_pairs={{0,1},{1,0},{2,3},{3,2},{4,5},{5,4},{6,7},{7,6},{8,9},{9,8},{10,11... | collective-permute-start | bytes 153608 | tf_op jit(solution)/shard_map/ppermute | solution.py:578
  34.8 0.9 %shard_map.147 = (bf16[4,32,256]{2,1,0:T(8,128)(2,1)}, bf16[2,16,512]{2,1,0:T(8,128)(2,1)}) custom-call(bf16[128,256]{1,0:T(8,128)(2,1)S(1)} %get-tuple-element.64.y_ref, bf16[32,1024]{1,0:T(8,128)(2,1)S(1)} %get-tuple-element.65.group_ref, bf16[1024,512]{1,0:T(8,128)(2,1)S(1)} %copy-done.1), custom_call_target="tpu_custom_call" | custom-call | flops 1000000000 | bytes 1000000 | tf_op jit(solution)/shard_map/pallas_call | solution.py:711
  35.7 0.0 collective-permute-done.17.far_ref
  35.7 0.0 collective-permute-done.18.near_ref
  35.7 1.1 %collective-permute-done.12.d_ref = bf16[200,128]{1,0:T(8,128)(2,1)S(1)} collective-permute-done((bf16[200,128]{1,0:T(8,128)(2,1)S(1)}, bf16[200,128]{1,0:T(8,128)(2,1)S(1)}, u32[]{:S(2)}, u32[]{:S(2)}) %collective-permute-start.12) | collective-permute-done | bytes 51232 | tf_op jit(solution)/shard_map/ppermute | solution.py:578
  36.8 1.8 %collective-permute-done.13.c_ref = bf16[200,128]{1,0:T(8,128)(2,1)S(1)} collective-permute-done((bf16[200,128]{1,0:T(8,128)(2,1)S(1)}, bf16[200,128]{1,0:T(8,128)(2,1)S(1)}, u32[]{:S(2)}, u32[]{:S(2)}) %collective-permute-start.13) | collective-permute-done | bytes 51232 | tf_op jit(solution)/shard_map/ppermute | solution.py:578
  38.6 0.0 collective-permute-done.14.b_ref
  38.6 0.7 %shard_map.154 = (f32[32,192]{1,0:T(8,128)}, f32[32,64]{1,0:T(8,128)}, f32[128,128]{1,0:T(8,128)}, f32[1,256]{1,0:T(1,128)}, f32[4]{0:T(128)}, /*index=5*/bf16[4,32,256]{2,1,0:T(8,128)(2,1)}) custom-call(bf16[200,128]{1,0:T(8,128)(2,1)S(1)} %get-tuple-element.84.a_ref, bf16[200,128]{1,0:T(8,128)(2,1)S(1)} %collective-permute-done.12.d_ref, ...), custom_call_target="tpu_custom_call" | custom-call | tf_op jit(solution)/shard_map/pallas_call | solution.py:757
  (4 shorter events, 0.1 us)
Async XLA Ops:
  0.6 6.2 %collective-permute-start = (bf16[4,32,256]{2,1,0:T(8,128)(2,1)}, bf16[4,32,256]{2,1,0:T(8,128)(2,1)S(1)}, u32[]{:S(2)}, u32[]{:S(2)}) collective-permute-start(bf16[4,32,256]{2,1,0:T(8,128)(2,1)} %tok_ref.3), channel_id=1, source_target_pairs={{0,1},{1,0},{2,3},{3,2},{4,8},{5,9},{6,10},{7,11},{8,4},{9,5},{10,... | collective-permute-start | bytes 196616 | tf_op jit(solution)/shard_map/ppermute | solution.py:573
  3.7 3.2 %collective-permute-start.1 = (bf16[4,32,256]{2,1,0:T(8,128)(2,1)}, bf16[4,32,256]{2,1,0:T(8,128)(2,1)S(1)}, u32[]{:S(2)}, u32[]{:S(2)}) collective-permute-start(bf16[4,32,256]{2,1,0:T(8,128)(2,1)} %tok_ref.3), channel_id=1, source_target_pairs={{0,4},{4,0},{8,12},{12,8},{16,20},{20,16},{24,28},{28,24},{1,5},{5... | collective-permute-start | bytes 196616 | tf_op jit(solution)/shard_map/ppermute | solution.py:578
  3.8 1.7 %copy-start = (bf16[2,16,512]{2,1,0:T(8,128)(2,1)S(1)}, bf16[2,16,512]{2,1,0:T(8,128)(2,1)}, u32[]{:S(2)}) copy-start(bf16[2,16,512]{2,1,0:T(8,128)(2,1)} %dm_ref.3) | copy-start | bytes 98308
  3.8 1.7 %copy-start.1 = (bf16[1024,512]{1,0:T(8,128)(2,1)S(1)}, bf16[1024,512]{1,0:T(8,128)(2,1)}, u32[]{:S(2)}) copy-start(bf16[1024,512]{1,0:T(8,128)(2,1)} %wmerge_ref.3) | copy-start | bytes 3145732
  3.8 1.7 %copy-start.2 = (bf16[256,768]{1,0:T(8,128)(2,1)S(1)}, bf16[256,768]{1,0:T(8,128)(2,1)}, u32[]{:S(2)}) copy-start(bf16[256,768]{1,0:T(8,128)(2,1)} %wqkv_ref.5) | copy-start | bytes 1179652
  3.8 1.7 %copy-start.3 = (bf16[256,256]{1,0:T(8,128)(2,1)S(1)}, bf16[256,256]{1,0:T(8,128)(2,1)}, u32[]{:S(2)}) copy-start(bf16[256,256]{1,0:T(8,128)(2,1)} %wout_ref.3) | copy-start | bytes 393220
  3.8 1.7 %copy-start.4 = (bf16[4,32,256]{2,1,0:T(8,128)(2,1)S(1)}, bf16[4,32,256]{2,1,0:T(8,128)(2,1)}, u32[]{:S(2)}) copy-start(bf16[4,32,256]{2,1,0:T(8,128)(2,1)} %dskip_ref.1) | copy-start | bytes 196612
  3.8 1.7 %copy-start.5 = (bf16[4,32,256]{2,1,0:T(8,128)(2,1)S(1)}, bf16[4,32,256]{2,1,0:T(8,128)(2,1)}, u32[]{:S(2)}) copy-start(bf16[4,32,256]{2,1,0:T(8,128)(2,1)} %tok_ref.3) | copy-start | bytes 196612
  3.8 4.8 %collective-permute-start.4 = (bf16[32,512]{1,0:T(8,128)(2,1)}, bf16[32,512]{1,0:T(8,128)(2,1)S(1)}, u32[]{:S(2)}, u32[]{:S(2)}) collective-permute-start(bf16[32,512]{1,0:T(8,128)(2,1)} %bitcast.4), channel_id=1, source_target_pairs={{0,8},{4,12},{8,0},{12,4},{16,24},{20,28},{24,16},{28,20},{1,9},{5... | collective-permute-start | bytes 98312 | tf_op jit(solution)/shard_map/ppermute | solution.py:578
  5.4 0.7 %copy-start.6 = (f32[256]{0:T(256)S(1)}, f32[256]{0:T(256)}, u32[]{:S(2)}) copy-start(f32[256]{0:T(256)} %param.9) | copy-start | bytes 3076
  5.4 0.7 %copy-start.7 = (f32[4]{0:T(128)S(1)}, f32[4]{0:T(128)}, u32[]{:S(2)}) copy-start(f32[4]{0:T(128)} %param.11) | copy-start | bytes 52
  6.9 3.8 %collective-permute-start.2 = (bf16[40,256]{1,0:T(8,128)(2,1)S(1)}, bf16[40,256]{1,0:T(8,128)(2,1)S(1)}, u32[]{:S(2)}, u32[]{:S(2)}) collective-permute-start(bf16[40,256]{1,0:T(8,128)(2,1)S(1)} %get-tuple-element.57), channel_id=1, source_target_pairs={{0,1},{1,0},{2,3},{3,2},{4,5},{5,4},{6,7},{7,6},{8,9},{9,8},{10,11... | collective-permute-start | bytes 61448 | tf_op jit(solution)/shard_map/ppermute | solution.py:578
  8.6 2.2 %collective-permute-start.3 = (bf16[40,256]{1,0:T(8,128)(2,1)S(1)}, bf16[40,256]{1,0:T(8,128)(2,1)S(1)}, u32[]{:S(2)}, u32[]{:S(2)}) collective-permute-start(bf16[40,256]{1,0:T(8,128)(2,1)S(1)} %get-tuple-element.58), channel_id=1, source_target_pairs={{0,4},{1,2},{2,1},{3,7},{4,0},{5,6},{6,5},{7,3},{8,12},{9,10},{10,... | collective-permute-start | bytes 61448 | tf_op jit(solution)/shard_map/ppermute | solution.py:573
  8.6 4.6 %collective-permute-start.5 = (bf16[64,512]{1,0:T(8,128)(2,1)S(1)}, bf16[64,512]{1,0:T(8,128)(2,1)S(1)}, u32[]{:S(2)}, u32[]{:S(2)}) collective-permute-start(bf16[64,512]{1,0:T(8,128)(2,1)S(1)} %shard_map.148.refs_1_), channel_id=1, source_target_pairs={{0,16},{4,20},{8,24},{12,28},{16,0},{20,4},{24,8},{28,12},{1,17},{... | collective-permute-start | bytes 196616 | tf_op jit(solution)/shard_map/ppermute | solution.py:578
  13.7 2.0 %collective-permute-start.6 = (bf16[4,32,1152]{2,1,0:T(8,128)(2,1)S(1)}, bf16[4,32,1152]{2,1,0:T(8,128)(2,1)S(1)}, u32[]{:S(2)}, u32[]{:S(2)}) collective-permute-start(bf16[4,32,1152]{2,1,0:T(8,128)(2,1)S(1)} %get-tuple-element.72), channel_id=1, source_target_pairs={{0,4},{4,0},{8,12},{12,8},{16,20},{20,16},{24,28},{28,24},{1,5},{5... | collective-permute-start | bytes 884744 | tf_op jit(solution)/shard_map/ppermute | solution.py:578
  14.4 1.4 %collective-permute-start.7 = (f32[8,128]{1,0:T(8,128)S(1)}, f32[8,128]{1,0:T(8,128)S(1)}, u32[]{:S(2)}, u32[]{:S(2)}) collective-permute-start(f32[8,128]{1,0:T(8,128)S(1)} %get-tuple-element.76.small_ref), channel_id=1, source_target_pairs={{0,4},{4,0},{8,12},{12,8},{16,20},{20,16},{24,28},{28,24},{1,5},{5... | collective-permute-start | bytes 12296 | tf_op jit(solution)/shard_map/ppermute | solution.py:578
  14.9 15.1 %collective-permute-start.11 = (bf16[128,512]{1,0:T(8,128)(2,1)S(1)}, bf16[128,512]{1,0:T(8,128)(2,1)S(1)}, u32[]{:S(2)}, u32[]{:S(2)}) collective-permute-start(bf16[128,512]{1,0:T(8,128)(2,1)S(1)} %get-tuple-element.83.refs_6_), channel_id=1, source_target_pairs={{0,4},{4,0},{8,12},{12,8},{16,20},{20,16},{24,28},{28,24},{1,5},{5... | collective-permute-start | bytes 393224 | tf_op jit(solution)/shard_map/ppermute | solution.py:578
  15.8 14.2 %collective-permute-start.8 = (bf16[328,128]{1,0:T(8,128)(2,1)S(1)}, bf16[328,128]{1,0:T(8,128)(2,1)S(1)}, u32[]{:S(2)}, u32[]{:S(2)}) collective-permute-start(bf16[328,128]{1,0:T(8,128)(2,1)S(1)} %get-tuple-element.80), channel_id=1, source_target_pairs={{0,24},{4,28},{8,16},{12,20},{16,8},{20,12},{24,0},{28,4},{1,25},{... | collective-permute-start | bytes 251912 | tf_op jit(solution)/shard_map/ppermute | solution.py:578
  18.2 11.8 %collective-permute-start.9 = (bf16[328,128]{1,0:T(8,128)(2,1)S(1)}, bf16[328,128]{1,0:T(8,128)(2,1)S(1)}, u32[]{:S(2)}, u32[]{:S(2)}) collective-permute-start(bf16[328,128]{1,0:T(8,128)(2,1)S(1)} %get-tuple-element.81), channel_id=1, source_target_pairs={{0,16},{4,20},{8,24},{12,28},{16,0},{20,4},{24,8},{28,12},{1,17},{... | collective-permute-start | bytes 251912 | tf_op jit(solution)/shard_map/ppermute | solution.py:578
  18.9 11.1 %collective-permute-start.10 = (bf16[328,128]{1,0:T(8,128)(2,1)S(1)}, bf16[328,128]{1,0:T(8,128)(2,1)S(1)}, u32[]{:S(2)}, u32[]{:S(2)}) collective-permute-start(bf16[328,128]{1,0:T(8,128)(2,1)S(1)} %get-tuple-element.82), channel_id=1, source_target_pairs={{0,8},{4,12},{8,0},{12,4},{16,24},{20,28},{24,16},{28,20},{1,9},{5... | collective-permute-start | bytes 251912 | tf_op jit(solution)/shard_map/ppermute | solution.py:578
  19.4 4.7 %collective-permute-start.15 = (bf16[40,256]{1,0:T(8,128)(2,1)S(1)}, bf16[40,256]{1,0:T(8,128)(2,1)S(1)}, u32[]{:S(2)}, u32[]{:S(2)}) collective-permute-start(bf16[40,256]{1,0:T(8,128)(2,1)S(1)} %get-tuple-element.89), channel_id=1, source_target_pairs={{0,1},{1,0},{2,3},{3,2},{4,5},{5,4},{6,7},{7,6},{8,9},{9,8},{10,11... | collective-permute-start | bytes 61448 | tf_op jit(solution)/shard_map/ppermute | solution.py:578
  24.1 1.2 %collective-permute-start.16 = (bf16[40,256]{1,0:T(8,128)(2,1)S(1)}, bf16[40,256]{1,0:T(8,128)(2,1)S(1)}, u32[]{:S(2)}, u32[]{:S(2)}) collective-permute-start(bf16[40,256]{1,0:T(8,128)(2,1)S(1)} %get-tuple-element.90), channel_id=1, source_target_pairs={{0,4},{1,2},{2,1},{3,7},{4,0},{5,6},{6,5},{7,3},{8,12},{9,10},{10,... | collective-permute-start | bytes 61448 | tf_op jit(solution)/shard_map/ppermute | solution.py:573
  25.3 10.4 %collective-permute-start.17 = (bf16[96,256]{1,0:T(8,128)(2,1)S(1)}, bf16[96,256]{1,0:T(8,128)(2,1)S(1)}, u32[]{:S(2)}, u32[]{:S(2)}) collective-permute-start(bf16[96,256]{1,0:T(8,128)(2,1)S(1)} %get-tuple-element.92), channel_id=1, source_target_pairs={{0,1},{1,0},{2,3},{3,2},{4,8},{5,9},{6,10},{7,11},{8,4},{9,5},{10,... | collective-permute-start | bytes 147464 | tf_op jit(solution)/shard_map/ppermute | solution.py:573
  30.0 5.7 %collective-permute-start.18 = (bf16[96,256]{1,0:T(8,128)(2,1)S(1)}, bf16[96,256]{1,0:T(8,128)(2,1)S(1)}, u32[]{:S(2)}, u32[]{:S(2)}) collective-permute-start(bf16[96,256]{1,0:T(8,128)(2,1)S(1)} %get-tuple-element.93), channel_id=1, source_target_pairs={{0,4},{4,0},{8,12},{12,8},{16,20},{20,16},{24,28},{28,24},{1,5},{5... | collective-permute-start | bytes 147464 | tf_op jit(solution)/shard_map/ppermute | solution.py:578
  30.3 6.5 %collective-permute-start.12 = (bf16[200,128]{1,0:T(8,128)(2,1)S(1)}, bf16[200,128]{1,0:T(8,128)(2,1)S(1)}, u32[]{:S(2)}, u32[]{:S(2)}) collective-permute-start(bf16[200,128]{1,0:T(8,128)(2,1)S(1)} %get-tuple-element.85), channel_id=1, source_target_pairs={{0,3},{1,2},{2,1},{3,0},{4,7},{5,6},{6,5},{7,4},{8,11},{9,10},{10,... | collective-permute-start | bytes 153608 | tf_op jit(solution)/shard_map/ppermute | solution.py:578
  32.7 5.9 %collective-permute-start.13 = (bf16[200,128]{1,0:T(8,128)(2,1)S(1)}, bf16[200,128]{1,0:T(8,128)(2,1)S(1)}, u32[]{:S(2)}, u32[]{:S(2)}) collective-permute-start(bf16[200,128]{1,0:T(8,128)(2,1)S(1)} %get-tuple-element.86), channel_id=1, source_target_pairs={{0,2},{1,3},{2,0},{3,1},{4,6},{5,7},{6,4},{7,5},{8,10},{9,11},{10,... | collective-permute-start | bytes 153608 | tf_op jit(solution)/shard_map/ppermute | solution.py:578
  33.2 5.4 %collective-permute-start.14 = (bf16[200,128]{1,0:T(8,128)(2,1)S(1)}, bf16[200,128]{1,0:T(8,128)(2,1)S(1)}, u32[]{:S(2)}, u32[]{:S(2)}) collective-permute-start(bf16[200,128]{1,0:T(8,128)(2,1)S(1)} %get-tuple-element.87), channel_id=1, source_target_pairs={{0,1},{1,0},{2,3},{3,2},{4,5},{5,4},{6,7},{7,6},{8,9},{9,8},{10,11... | collective-permute-start | bytes 153608 | tf_op jit(solution)/shard_map/ppermute | solution.py:578

commit v13 on v9

--- a/solution.py
+++ b/solution.py
@@ -49,12 +49,13 @@
     parity_ref[...] = jnp.concatenate(parts, axis=0)
 
 
-def edge_kernel(
-    edges_ref, far_ref, near_ref, dm_ref, dm_next_ref, edge_near_ref, edge_far_ref, dm_pair_ref
-):
-    rows, cols, width = near_ref.shape
+def pair_kernel(dm_ref, dm_next_ref, dm_pair_ref):
     size = dm_next_ref.shape[0]
     dm_pair_ref[...] = jnp.concatenate([dm_ref[...].reshape(size, -1), dm_next_ref[...]], axis=0)
+
+
+def edge_kernel(edges_ref, far_ref, near_ref, edge_near_ref, edge_far_ref):
+    rows, cols, width = near_ref.shape
     up, down = by_side("row", near_ref[...].astype(F32), far_ref[...].astype(F32))
     up = up[rows - RADIUS :]
     down = down[:RADIUS]
@@ -642,13 +643,20 @@
         w_out,
         w_merge,
     )
-    edge_near, edge_far, dm_pair = pl.pallas_call(
+    edge_near, edge_far = pl.pallas_call(
         edge_kernel,
-        out_shape=(edge, edge, shape((2 * groups, depth), BF)),
-        in_specs=vmem(5),
-        out_specs=tuple(vmem(3)),
+        out_shape=(edge, edge),
+        in_specs=vmem(3),
+        out_specs=tuple(vmem(2)),
         compiler_params=less,
-    )(edges, row_far, row_near, d_merged, swap(dm, "row", 2))
+    )(edges, row_far, row_near)
+    dm_pair = pl.pallas_call(
+        pair_kernel,
+        out_shape=shape((2 * groups, depth), BF),
+        in_specs=vmem(2),
+        out_specs=vmem(1)[0],
+        compiler_params=less,
+    )(d_merged, swap(dm, "row", 2))
     dms = [swap(dm_pair, "row", 4), dm_pair]
     col_near, col_far = swapped(edge_near, edge_far, "col")
 

time: 35 us -> 34 us (0.971)
  waiting for transfers between devices: 5.17 us -> 3.97 us
    ppermute x16, waiting for transfers between devices: 3.23 us -> 2.12 us  [swap(): return lax.ppermute(value, axis, [(i, i ^ step) for i in range(count)])]
  transfers between devices with their start and end apart: 20 -> 20, of which waited for: 7 -> 6; matrix products, arithmetic and copies ran while one was open for 0% -> 0% of each run, Pallas kernels for 14% -> 14%
where the time goes in v13:
time: 34 us; the launch traced here: 33.8 us
  starting transfers between devices  22.2 us (65%)
  Pallas kernels  6.17 us (18%)
  waiting for transfers between devices  3.97 us (12%)
  between operations  0.85 us (2%)
  local copies, waits for them, and re-layouts  0.63 us (2%)
    ppermute x16, starting transfers between devices, swap(): return lax.ppermute(value, axis, [(i, i ^ step) for i in range(count)])  17 us
    ppermute x4, starting transfers between devices, swapped(): return (swap(near, axis, 1), lax.ppermute(far, ('row', 'col'), pairs))  5.17 us
    ppermute x16, waiting for transfers between devices, swap(): return lax.ppermute(value, axis, [(i, i ^ step) for i in range(count)])  2.12 us
    pallas_call x1, Pallas kernels, on_device(): pl.pallas_call(functools.partial(layer_kernel, sizes), out_shape=(shape((...  1.95 us
    ppermute x4, waiting for transfers between devices, swapped(): return (swap(near, axis, 1), lax.ppermute(far, ('row', 'col'), pairs))  1.85 us
    pallas_call x1, Pallas kernels, on_device(): pl.pallas_call(output_kernel, out_shape=(shape((rows, cols, width), BF),...  0.91 us
    pallas_call x1, Pallas kernels, on_device(): pl.pallas_call(own_kernel, out_shape=(shape((2 * rows * EDGE, width), BF)...  0.79 us
    pallas_call x1, Pallas kernels, on_device(): pl.pallas_call(functools.partial(col_sum_kernel, (rows, cols, width)), ou...  0.75 us
  transfers between devices with their start and end apart: 20, of which 6 were waited for; matrix products, arithmetic and copies ran while one was open for 0% of the time, Pallas kernels for 14%

profile of v13, /device:TPU:0, one launch (start us, length us, event | category | flops | bytes accessed | tf_op | source)
XLA Modules:
  0.0 33.8 jit_solution(3968114150341271255)
XLA Ops:
  0.6 3.1 %collective-permute-start = (bf16[4,32,256]{2,1,0:T(8,128)(2,1)}, bf16[4,32,256]{2,1,0:T(8,128)(2,1)S(1)}, u32[]{:S(2)}, u32[]{:S(2)}) collective-permute-start(bf16[4,32,256]{2,1,0:T(8,128)(2,1)} %tok_ref.3), channel_id=1, source_target_pairs={{0,1},{1,0},{2,3},{3,2},{4,8},{5,9},{6,10},{7,11},{8,4},{9,5},{10,... | collective-permute-start | bytes 196616 | tf_op jit(solution)/shard_map/ppermute | solution.py:591
  3.7 0.0 collective-permute-start.1
  3.8 0.0 copy-start
  3.8 0.0 copy-start.1
  3.8 0.0 copy-start.2
  3.8 0.0 copy-start.4
  3.8 0.0 copy-start.5
  3.8 1.6 %collective-permute-start.4 = (bf16[32,512]{1,0:T(8,128)(2,1)}, bf16[32,512]{1,0:T(8,128)(2,1)S(1)}, u32[]{:S(2)}, u32[]{:S(2)}) collective-permute-start(bf16[32,512]{1,0:T(8,128)(2,1)} %bitcast.4), channel_id=1, source_target_pairs={{0,8},{4,12},{8,0},{12,4},{16,24},{20,28},{24,16},{28,20},{1,9},{5... | collective-permute-start | bytes 98312 | tf_op jit(solution)/shard_map/ppermute | solution.py:596
  5.4 0.0 copy-start.6
  5.4 0.0 copy-start.7
  5.4 0.0 copy-done
  5.4 0.0 copy-done.1
  5.4 0.0 copy-done.2
  5.4 0.0 copy-done.3
  5.4 0.0 copy-done.4
  5.5 0.0 copy-done.5
  5.5 0.6 %copy-done.6 = f32[256]{0:T(256)S(1)} copy-done((f32[256]{0:T(256)S(1)}, f32[256]{0:T(256)}, u32[]{:S(2)}) %copy-start.6) | copy-done | bytes 1048
  6.1 0.0 copy-done.7
  6.1 0.8 %shard_map.144 = (bf16[32,256]{1,0:T(8,128)(2,1)S(1)}, f32[8,256]{1,0:T(8,128)S(1)}, f32[128,256]{1,0:T(8,128)S(1)}, f32[128,256]{1,0:T(8,128)S(1)}, f32[128,256...) custom-call(bf16[256,256]{1,0:T(8,128)(2,1)S(1)} %get-tuple-element.55.ones_ref, f32[8,128]{1,0:T(8,128)S(1)} %get-tuple-element.56.parity_ref, ...), custom_call_target="tpu_custom_call" | custom-call | flops 1000000000 | bytes 1000000 | tf_op jit(solution)/shard_map/pallas_call | solution.py:626
  6.9 0.0 collective-permute-done.far_ref.row_far_ref
  6.9 0.0 collective-permute-done.1.near_ref.row_near_ref
  6.9 1.6 %collective-permute-start.2 = (bf16[40,256]{1,0:T(8,128)(2,1)S(1)}, bf16[40,256]{1,0:T(8,128)(2,1)S(1)}, u32[]{:S(2)}, u32[]{:S(2)}) collective-permute-start(bf16[40,256]{1,0:T(8,128)(2,1)S(1)} %get-tuple-element.58), channel_id=1, source_target_pairs={{0,1},{1,0},{2,3},{3,2},{4,5},{5,4},{6,7},{7,6},{8,9},{9,8},{10,11... | collective-permute-start | bytes 61448 | tf_op jit(solution)/shard_map/ppermute | solution.py:596
  8.6 0.0 collective-permute-start.3
  8.6 0.0 collective-permute-done.4.dm_next_ref
  8.6 1.6 %collective-permute-start.5 = (bf16[64,512]{1,0:T(8,128)(2,1)S(1)}, bf16[64,512]{1,0:T(8,128)(2,1)S(1)}, u32[]{:S(2)}, u32[]{:S(2)}) collective-permute-start(bf16[64,512]{1,0:T(8,128)(2,1)S(1)} %shard_map.148.refs_1_), channel_id=1, source_target_pairs={{0,16},{4,20},{8,24},{12,28},{16,0},{20,4},{24,8},{28,12},{1,17},{... | collective-permute-start | bytes 196616 | tf_op jit(solution)/shard_map/ppermute | solution.py:596
  10.2 0.5 %collective-permute-done.2.col_near_ref = bf16[40,256]{1,0:T(8,128)(2,1)S(1)} collective-permute-done((bf16[40,256]{1,0:T(8,128)(2,1)S(1)}, bf16[40,256]{1,0:T(8,128)(2,1)S(1)}, u32[]{:S(2)}, u32[]{:S(2)}) %collective-permute-start.2) | collective-permute-done | bytes 20512 | tf_op jit(solution)/shard_map/ppermute | solution.py:596
  10.8 0.0 collective-permute-done.3.col_far_ref
  10.8 2.0 %shard_map.146 = (f32[480,256]{1,0:T(8,128)S(1)}, bf16[128,256]{1,0:T(8,128)(2,1)S(1)}, bf16[128,256]{1,0:T(8,128)(2,1)S(1)}, bf16[480,512]{1,0:T(8,128)(2,1)S(1...) custom-call(bf16[256,256]{1,0:T(8,128)(2,1)S(1)} %get-tuple-element.55.ones_ref, ...), custom_call_target="tpu_custom_call" | custom-call | flops 4000000000 | bytes 1000000 | tf_op jit(solution)/shard_map/pallas_call | solution.py:687
  12.7 0.4 %collective-permute-done.5.refs_0_ = bf16[64,512]{1,0:T(8,128)(2,1)S(1)} collective-permute-done((bf16[64,512]{1,0:T(8,128)(2,1)S(1)}, bf16[64,512]{1,0:T(8,128)(2,1)S(1)}, u32[]{:S(2)}, u32[]{:S(2)}) %collective-permute-start.5) | collective-permute-done | bytes 65568 | tf_op jit(solution)/shard_map/ppermute | solution.py:596
  13.1 0.7 %shard_map.149 = (bf16[128,512]{1,0:T(8,128)(2,1)S(1)}, bf16[3,32,1152]{2,1,0:T(8,128)(2,1)S(1)}, bf16[32,1152]{1,0:T(8,128)(2,1)S(1)}, f32[4,32,1024]{2,1,0:T(8,128)S(1)}, bf16[4,32,128]{2,1,0:T(8,128)(2,1)S(1)}) custom-call(f32[480,256]{1,0:T(8,128)S(1)} %get-tuple-element.69.x_ref, bf16[128,256]{1,0:T(8,128)(2,1)S(1)} %get-tuple-element.70.d_query_ref, ...), custom_call_target="tpu_custom_call" | custom-call | flops 1000000000 | bytes 1000000 | tf_op jit(solution)/shard_map/pallas_call | solution.py:718
  13.8 0.1 collective-permute-start.7
  13.9 0.4 %shard_map.150 = (f32[480,256]{1,0:T(8,128)S(1)}, f32[8,128]{1,0:T(8,128)S(1)}) custom-call(f32[480,256]{1,0:T(8,128)S(1)} %get-tuple-element.69.x_ref, bf16[128,256]{1,0:T(8,128)(2,1)S(1)} %get-tuple-element.70.d_query_ref, bf16[480,512]{1,0:T(8,128)(2,1)S(1)} %get-tuple-element.71.d_kv_ref, f32[8,256]{1,0:T(8,128)S(1)} %get-tuple-element.77.scale_part_ref, ...), custom_call_target="tpu_custom_call" | custom-call | flops 300000000 | bytes 1000000 | tf_op jit(solution)/shard_map/pallas_call | solution.py:727
  14.3 0.6 %collective-permute-start.8 = (f32[8,128]{1,0:T(8,128)S(1)}, f32[8,128]{1,0:T(8,128)S(1)}, u32[]{:S(2)}, u32[]{:S(2)}) collective-permute-start(f32[8,128]{1,0:T(8,128)S(1)} %get-tuple-element.78.small_ref), channel_id=1, source_target_pairs={{0,4},{4,0},{8,12},{12,8},{16,20},{20,16},{24,28},{28,24},{1,5},{5... | collective-permute-start | bytes 12296 | tf_op jit(solution)/shard_map/ppermute | solution.py:596
  14.8 0.1 collective-permute-start.6
  14.9 0.4 %collective-permute-start.12 = (bf16[128,512]{1,0:T(8,128)(2,1)S(1)}, bf16[128,512]{1,0:T(8,128)(2,1)S(1)}, u32[]{:S(2)}, u32[]{:S(2)}) collective-permute-start(bf16[128,512]{1,0:T(8,128)(2,1)S(1)} %get-tuple-element.83.refs_7_), channel_id=1, source_target_pairs={{0,4},{4,0},{8,12},{12,8},{16,20},{20,16},{24,28},{28,24},{1,5},{5... | collective-permute-start | bytes 393224 | tf_op jit(solution)/shard_map/ppermute | solution.py:596
  15.4 0.3 collective-permute-done.8.small_near_ref
  15.7 0.0 collective-permute-done.7.got_ref
  15.7 0.1 shard_map.151
  15.7 2.4 %collective-permute-start.9 = (bf16[328,128]{1,0:T(8,128)(2,1)S(1)}, bf16[328,128]{1,0:T(8,128)(2,1)S(1)}, u32[]{:S(2)}, u32[]{:S(2)}) collective-permute-start(bf16[328,128]{1,0:T(8,128)(2,1)S(1)} %get-tuple-element.80), channel_id=1, source_target_pairs={{0,24},{4,28},{8,16},{12,20},{16,8},{20,12},{24,0},{28,4},{1,25},{... | collective-permute-start | bytes 251912 | tf_op jit(solution)/shard_map/ppermute | solution.py:596
  18.1 0.7 %collective-permute-start.10 = (bf16[328,128]{1,0:T(8,128)(2,1)S(1)}, bf16[328,128]{1,0:T(8,128)(2,1)S(1)}, u32[]{:S(2)}, u32[]{:S(2)}) collective-permute-start(bf16[328,128]{1,0:T(8,128)(2,1)S(1)} %get-tuple-element.81), channel_id=1, source_target_pairs={{0,16},{4,20},{8,24},{12,28},{16,0},{20,4},{24,8},{28,12},{1,17},{... | collective-permute-start | bytes 251912 | tf_op jit(solution)/shard_map/ppermute | solution.py:596
  18.8 0.5 %collective-permute-start.11 = (bf16[328,128]{1,0:T(8,128)(2,1)S(1)}, bf16[328,128]{1,0:T(8,128)(2,1)S(1)}, u32[]{:S(2)}, u32[]{:S(2)}) collective-permute-start(bf16[328,128]{1,0:T(8,128)(2,1)S(1)} %get-tuple-element.82), channel_id=1, source_target_pairs={{0,8},{4,12},{8,0},{12,4},{16,24},{20,28},{24,16},{28,20},{1,9},{5... | collective-permute-start | bytes 251912 | tf_op jit(solution)/shard_map/ppermute | solution.py:596
  19.3 0.2 shard_map.152
  19.5 0.0 collective-permute-done.6.refs_2_
  19.5 3.0 %collective-permute-start.16 = (bf16[40,256]{1,0:T(8,128)(2,1)S(1)}, bf16[40,256]{1,0:T(8,128)(2,1)S(1)}, u32[]{:S(2)}, u32[]{:S(2)}) collective-permute-start(bf16[40,256]{1,0:T(8,128)(2,1)S(1)} %get-tuple-element.91), channel_id=1, source_target_pairs={{0,1},{1,0},{2,3},{3,2},{4,5},{5,4},{6,7},{7,6},{8,9},{9,8},{10,11... | collective-permute-start | bytes 61448 | tf_op jit(solution)/shard_map/ppermute | solution.py:596
  22.5 0.0 collective-permute-done.12.refs_8_
  22.5 0.0 collective-permute-start.17
  22.5 0.0 collective-permute-done.9.refs_4_
  22.5 0.7 %collective-permute-done.10.refs_5_ = bf16[328,128]{1,0:T(8,128)(2,1)S(1)} collective-permute-done((bf16[328,128]{1,0:T(8,128)(2,1)S(1)}, bf16[328,128]{1,0:T(8,128)(2,1)S(1)}, u32[]{:S(2)}, u32[]{:S(2)}) %collective-permute-start.10) | collective-permute-done | bytes 84000 | tf_op jit(solution)/shard_map/ppermute | solution.py:596
  23.2 0.1 collective-permute-done.11.refs_6_
  23.4 0.3 shard_map.153
  23.7 3.3 %collective-permute-start.13 = (bf16[200,128]{1,0:T(8,128)(2,1)S(1)}, bf16[200,128]{1,0:T(8,128)(2,1)S(1)}, u32[]{:S(2)}, u32[]{:S(2)}) collective-permute-start(bf16[200,128]{1,0:T(8,128)(2,1)S(1)} %get-tuple-element.87), channel_id=1, source_target_pairs={{0,3},{1,2},{2,1},{3,0},{4,7},{5,6},{6,5},{7,4},{8,11},{9,10},{10,... | collective-permute-start | bytes 153608 | tf_op jit(solution)/shard_map/ppermute | solution.py:596
  27.0 1.2 %collective-permute-start.14 = (bf16[200,128]{1,0:T(8,128)(2,1)S(1)}, bf16[200,128]{1,0:T(8,128)(2,1)S(1)}, u32[]{:S(2)}, u32[]{:S(2)}) collective-permute-start(bf16[200,128]{1,0:T(8,128)(2,1)S(1)} %get-tuple-element.88), channel_id=1, source_target_pairs={{0,2},{1,3},{2,0},{3,1},{4,6},{5,7},{6,4},{7,5},{8,10},{9,11},{10,... | collective-permute-start | bytes 153608 | tf_op jit(solution)/shard_map/ppermute | solution.py:596
  28.2 0.0 collective-permute-start.15
  28.2 0.0 collective-permute-done.16.near_ref
  28.2 0.0 collective-permute-done.17.far_ref
  28.2 2.1 %collective-permute-start.18 = (bf16[96,256]{1,0:T(8,128)(2,1)S(1)}, bf16[96,256]{1,0:T(8,128)(2,1)S(1)}, u32[]{:S(2)}, u32[]{:S(2)}) collective-permute-start(bf16[96,256]{1,0:T(8,128)(2,1)S(1)} %get-tuple-element.94), channel_id=1, source_target_pairs={{0,1},{1,0},{2,3},{3,2},{4,8},{5,9},{6,10},{7,11},{8,4},{9,5},{10,... | collective-permute-start | bytes 147464 | tf_op jit(solution)/shard_map/ppermute | solution.py:591
  30.3 0.0 collective-permute-start.19
  30.3 0.9 %shard_map.147 = (bf16[4,32,256]{2,1,0:T(8,128)(2,1)}, bf16[2,16,512]{2,1,0:T(8,128)(2,1)}) custom-call(bf16[128,256]{1,0:T(8,128)(2,1)S(1)} %get-tuple-element.65.y_ref, bf16[32,1024]{1,0:T(8,128)(2,1)S(1)} %get-tuple-element.66.group_ref, bf16[1024,512]{1,0:T(8,128)(2,1)S(1)} %copy-done.2), custom_call_target="tpu_custom_call" | custom-call | flops 1000000000 | bytes 1000000 | tf_op jit(solution)/shard_map/pallas_call | solution.py:744
  31.2 1.8 %collective-permute-done.18.far_ref = bf16[96,256]{1,0:T(8,128)(2,1)S(1)} collective-permute-done((bf16[96,256]{1,0:T(8,128)(2,1)S(1)}, bf16[96,256]{1,0:T(8,128)(2,1)S(1)}, u32[]{:S(2)}, u32[]{:S(2)}) %collective-permute-start.18) | collective-permute-done | bytes 49184 | tf_op jit(solution)/shard_map/ppermute | solution.py:591
  33.1 0.0 collective-permute-done.19.near_ref
  33.1 0.0 collective-permute-done.13.d_ref
  33.1 0.0 collective-permute-done.14.c_ref
  33.1 0.0 collective-permute-done.15.b_ref
  33.1 0.7 %shard_map.155 = (f32[32,192]{1,0:T(8,128)}, f32[32,64]{1,0:T(8,128)}, f32[128,128]{1,0:T(8,128)}, f32[1,256]{1,0:T(1,128)}, f32[4]{0:T(128)}, /*index=5*/bf16[4,32,256]{2,1,0:T(8,128)(2,1)}) custom-call(bf16[200,128]{1,0:T(8,128)(2,1)S(1)} %get-tuple-element.86.a_ref, bf16[200,128]{1,0:T(8,128)(2,1)S(1)} %collective-permute-done.13.d_ref, ...), custom_call_target="tpu_custom_call" | custom-call | tf_op jit(solution)/shard_map/pallas_call | solution.py:788
  (5 shorter events, 0.1 us)
Async XLA Ops:
  0.6 6.2 %collective-permute-start = (bf16[4,32,256]{2,1,0:T(8,128)(2,1)}, bf16[4,32,256]{2,1,0:T(8,128)(2,1)S(1)}, u32[]{:S(2)}, u32[]{:S(2)}) collective-permute-start(bf16[4,32,256]{2,1,0:T(8,128)(2,1)} %tok_ref.3), channel_id=1, source_target_pairs={{0,1},{1,0},{2,3},{3,2},{4,8},{5,9},{6,10},{7,11},{8,4},{9,5},{10,... | collective-permute-start | bytes 196616 | tf_op jit(solution)/shard_map/ppermute | solution.py:591
  3.7 3.2 %collective-permute-start.1 = (bf16[4,32,256]{2,1,0:T(8,128)(2,1)}, bf16[4,32,256]{2,1,0:T(8,128)(2,1)S(1)}, u32[]{:S(2)}, u32[]{:S(2)}) collective-permute-start(bf16[4,32,256]{2,1,0:T(8,128)(2,1)} %tok_ref.3), channel_id=1, source_target_pairs={{0,4},{4,0},{8,12},{12,8},{16,20},{20,16},{24,28},{28,24},{1,5},{5... | collective-permute-start | bytes 196616 | tf_op jit(solution)/shard_map/ppermute | solution.py:596
  3.8 1.7 %copy-start = (bf16[256,768]{1,0:T(8,128)(2,1)S(1)}, bf16[256,768]{1,0:T(8,128)(2,1)}, u32[]{:S(2)}) copy-start(bf16[256,768]{1,0:T(8,128)(2,1)} %wqkv_ref.5) | copy-start | bytes 1179652
  3.8 1.7 %copy-start.1 = (bf16[2,16,512]{2,1,0:T(8,128)(2,1)S(1)}, bf16[2,16,512]{2,1,0:T(8,128)(2,1)}, u32[]{:S(2)}) copy-start(bf16[2,16,512]{2,1,0:T(8,128)(2,1)} %dm_ref.3) | copy-start | bytes 98308
  3.8 1.7 %copy-start.2 = (bf16[1024,512]{1,0:T(8,128)(2,1)S(1)}, bf16[1024,512]{1,0:T(8,128)(2,1)}, u32[]{:S(2)}) copy-start(bf16[1024,512]{1,0:T(8,128)(2,1)} %wmerge_ref.3) | copy-start | bytes 3145732
  3.8 1.7 %copy-start.3 = (bf16[256,256]{1,0:T(8,128)(2,1)S(1)}, bf16[256,256]{1,0:T(8,128)(2,1)}, u32[]{:S(2)}) copy-start(bf16[256,256]{1,0:T(8,128)(2,1)} %wout_ref.3) | copy-start | bytes 393220
  3.8 1.7 %copy-start.4 = (bf16[4,32,256]{2,1,0:T(8,128)(2,1)S(1)}, bf16[4,32,256]{2,1,0:T(8,128)(2,1)}, u32[]{:S(2)}) copy-start(bf16[4,32,256]{2,1,0:T(8,128)(2,1)} %dskip_ref.1) | copy-start | bytes 196612
  3.8 1.7 %copy-start.5 = (bf16[4,32,256]{2,1,0:T(8,128)(2,1)S(1)}, bf16[4,32,256]{2,1,0:T(8,128)(2,1)}, u32[]{:S(2)}) copy-start(bf16[4,32,256]{2,1,0:T(8,128)(2,1)} %tok_ref.3) | copy-start | bytes 196612
  3.8 4.8 %collective-permute-start.4 = (bf16[32,512]{1,0:T(8,128)(2,1)}, bf16[32,512]{1,0:T(8,128)(2,1)S(1)}, u32[]{:S(2)}, u32[]{:S(2)}) collective-permute-start(bf16[32,512]{1,0:T(8,128)(2,1)} %bitcast.4), channel_id=1, source_target_pairs={{0,8},{4,12},{8,0},{12,4},{16,24},{20,28},{24,16},{28,20},{1,9},{5... | collective-permute-start | bytes 98312 | tf_op jit(solution)/shard_map/ppermute | solution.py:596
  5.4 0.7 %copy-start.6 = (f32[256]{0:T(256)S(1)}, f32[256]{0:T(256)}, u32[]{:S(2)}) copy-start(f32[256]{0:T(256)} %param.9) | copy-start | bytes 3076
  5.4 0.7 %copy-start.7 = (f32[4]{0:T(128)S(1)}, f32[4]{0:T(128)}, u32[]{:S(2)}) copy-start(f32[4]{0:T(128)} %param.11) | copy-start | bytes 52
  6.9 3.8 %collective-permute-start.2 = (bf16[40,256]{1,0:T(8,128)(2,1)S(1)}, bf16[40,256]{1,0:T(8,128)(2,1)S(1)}, u32[]{:S(2)}, u32[]{:S(2)}) collective-permute-start(bf16[40,256]{1,0:T(8,128)(2,1)S(1)} %get-tuple-element.58), channel_id=1, source_target_pairs={{0,1},{1,0},{2,3},{3,2},{4,5},{5,4},{6,7},{7,6},{8,9},{9,8},{10,11... | collective-permute-start | bytes 61448 | tf_op jit(solution)/shard_map/ppermute | solution.py:596
  8.6 2.2 %collective-permute-start.3 = (bf16[40,256]{1,0:T(8,128)(2,1)S(1)}, bf16[40,256]{1,0:T(8,128)(2,1)S(1)}, u32[]{:S(2)}, u32[]{:S(2)}) collective-permute-start(bf16[40,256]{1,0:T(8,128)(2,1)S(1)} %get-tuple-element.59), channel_id=1, source_target_pairs={{0,4},{1,2},{2,1},{3,7},{4,0},{5,6},{6,5},{7,3},{8,12},{9,10},{10,... | collective-permute-start | bytes 61448 | tf_op jit(solution)/shard_map/ppermute | solution.py:591
  8.6 4.6 %collective-permute-start.5 = (bf16[64,512]{1,0:T(8,128)(2,1)S(1)}, bf16[64,512]{1,0:T(8,128)(2,1)S(1)}, u32[]{:S(2)}, u32[]{:S(2)}) collective-permute-start(bf16[64,512]{1,0:T(8,128)(2,1)S(1)} %shard_map.148.refs_1_), channel_id=1, source_target_pairs={{0,16},{4,20},{8,24},{12,28},{16,0},{20,4},{24,8},{28,12},{1,17},{... | collective-permute-start | bytes 196616 | tf_op jit(solution)/shard_map/ppermute | solution.py:596
  13.8 1.9 %collective-permute-start.7 = (bf16[3,32,1152]{2,1,0:T(8,128)(2,1)S(1)}, bf16[3,32,1152]{2,1,0:T(8,128)(2,1)S(1)}, u32[]{:S(2)}, u32[]{:S(2)}) collective-permute-start(bf16[3,32,1152]{2,1,0:T(8,128)(2,1)S(1)} %get-tuple-element.76), channel_id=1, source_target_pairs={{0,4},{4,0},{8,12},{12,8},{16,20},{20,16},{24,28},{28,24},{1,5},{5... | collective-permute-start | bytes 663560 | tf_op jit(solution)/shard_map/ppermute | solution.py:596
  14.3 1.4 %collective-permute-start.8 = (f32[8,128]{1,0:T(8,128)S(1)}, f32[8,128]{1,0:T(8,128)S(1)}, u32[]{:S(2)}, u32[]{:S(2)}) collective-permute-start(f32[8,128]{1,0:T(8,128)S(1)} %get-tuple-element.78.small_ref), channel_id=1, source_target_pairs={{0,4},{4,0},{8,12},{12,8},{16,20},{20,16},{24,28},{28,24},{1,5},{5... | collective-permute-start | bytes 12296 | tf_op jit(solution)/shard_map/ppermute | solution.py:596
  14.8 4.7 %collective-permute-start.6 = (bf16[32,1152]{1,0:T(8,128)(2,1)S(1)}, bf16[32,1152]{1,0:T(8,128)(2,1)S(1)}, u32[]{:S(2)}, u32[]{:S(2)}) collective-permute-start(bf16[32,1152]{1,0:T(8,128)(2,1)S(1)} %get-tuple-element.75), channel_id=1, source_target_pairs={{0,4},{4,0},{8,12},{12,8},{16,20},{20,16},{24,28},{28,24},{1,5},{5... | collective-permute-start | bytes 221192 | tf_op jit(solution)/shard_map/ppermute | solution.py:596
  14.9 7.6 %collective-permute-start.12 = (bf16[128,512]{1,0:T(8,128)(2,1)S(1)}, bf16[128,512]{1,0:T(8,128)(2,1)S(1)}, u32[]{:S(2)}, u32[]{:S(2)}) collective-permute-start(bf16[128,512]{1,0:T(8,128)(2,1)S(1)} %get-tuple-element.83.refs_7_), channel_id=1, source_target_pairs={{0,4},{4,0},{8,12},{12,8},{16,20},{20,16},{24,28},{28,24},{1,5},{5... | collective-permute-start | bytes 393224 | tf_op jit(solution)/shard_map/ppermute | solution.py:596
  15.7 6.8 %collective-permute-start.9 = (bf16[328,128]{1,0:T(8,128)(2,1)S(1)}, bf16[328,128]{1,0:T(8,128)(2,1)S(1)}, u32[]{:S(2)}, u32[]{:S(2)}) collective-permute-start(bf16[328,128]{1,0:T(8,128)(2,1)S(1)} %get-tuple-element.80), channel_id=1, source_target_pairs={{0,24},{4,28},{8,16},{12,20},{16,8},{20,12},{24,0},{28,4},{1,25},{... | collective-permute-start | bytes 251912 | tf_op jit(solution)/shard_map/ppermute | solution.py:596
  18.1 5.1 %collective-permute-start.10 = (bf16[328,128]{1,0:T(8,128)(2,1)S(1)}, bf16[328,128]{1,0:T(8,128)(2,1)S(1)}, u32[]{:S(2)}, u32[]{:S(2)}) collective-permute-start(bf16[328,128]{1,0:T(8,128)(2,1)S(1)} %get-tuple-element.81), channel_id=1, source_target_pairs={{0,16},{4,20},{8,24},{12,28},{16,0},{20,4},{24,8},{28,12},{1,17},{... | collective-permute-start | bytes 251912 | tf_op jit(solution)/shard_map/ppermute | solution.py:596
  18.8 4.6 %collective-permute-start.11 = (bf16[328,128]{1,0:T(8,128)(2,1)S(1)}, bf16[328,128]{1,0:T(8,128)(2,1)S(1)}, u32[]{:S(2)}, u32[]{:S(2)}) collective-permute-start(bf16[328,128]{1,0:T(8,128)(2,1)S(1)} %get-tuple-element.82), channel_id=1, source_target_pairs={{0,8},{4,12},{8,0},{12,4},{16,24},{20,28},{24,16},{28,20},{1,9},{5... | collective-permute-start | bytes 251912 | tf_op jit(solution)/shard_map/ppermute | solution.py:596
  19.5 8.6 %collective-permute-start.16 = (bf16[40,256]{1,0:T(8,128)(2,1)S(1)}, bf16[40,256]{1,0:T(8,128)(2,1)S(1)}, u32[]{:S(2)}, u32[]{:S(2)}) collective-permute-start(bf16[40,256]{1,0:T(8,128)(2,1)S(1)} %get-tuple-element.91), channel_id=1, source_target_pairs={{0,1},{1,0},{2,3},{3,2},{4,5},{5,4},{6,7},{7,6},{8,9},{9,8},{10,11... | collective-permute-start | bytes 61448 | tf_op jit(solution)/shard_map/ppermute | solution.py:596
  22.5 5.7 %collective-permute-start.17 = (bf16[40,256]{1,0:T(8,128)(2,1)S(1)}, bf16[40,256]{1,0:T(8,128)(2,1)S(1)}, u32[]{:S(2)}, u32[]{:S(2)}) collective-permute-start(bf16[40,256]{1,0:T(8,128)(2,1)S(1)} %get-tuple-element.92), channel_id=1, source_target_pairs={{0,4},{1,2},{2,1},{3,7},{4,0},{5,6},{6,5},{7,3},{8,12},{9,10},{10,... | collective-permute-start | bytes 61448 | tf_op jit(solution)/shard_map/ppermute | solution.py:591
  23.7 9.4 %collective-permute-start.13 = (bf16[200,128]{1,0:T(8,128)(2,1)S(1)}, bf16[200,128]{1,0:T(8,128)(2,1)S(1)}, u32[]{:S(2)}, u32[]{:S(2)}) collective-permute-start(bf16[200,128]{1,0:T(8,128)(2,1)S(1)} %get-tuple-element.87), channel_id=1, source_target_pairs={{0,3},{1,2},{2,1},{3,0},{4,7},{5,6},{6,5},{7,4},{8,11},{9,10},{10,... | collective-permute-start | bytes 153608 | tf_op jit(solution)/shard_map/ppermute | solution.py:596
  27.0 6.1 %collective-permute-start.14 = (bf16[200,128]{1,0:T(8,128)(2,1)S(1)}, bf16[200,128]{1,0:T(8,128)(2,1)S(1)}, u32[]{:S(2)}, u32[]{:S(2)}) collective-permute-start(bf16[200,128]{1,0:T(8,128)(2,1)S(1)} %get-tuple-element.88), channel_id=1, source_target_pairs={{0,2},{1,3},{2,0},{3,1},{4,6},{5,7},{6,4},{7,5},{8,10},{9,11},{10,... | collective-permute-start | bytes 153608 | tf_op jit(solution)/shard_map/ppermute | solution.py:596
  28.2 4.9 %collective-permute-start.15 = (bf16[200,128]{1,0:T(8,128)(2,1)S(1)}, bf16[200,128]{1,0:T(8,128)(2,1)S(1)}, u32[]{:S(2)}, u32[]{:S(2)}) collective-permute-start(bf16[200,128]{1,0:T(8,128)(2,1)S(1)} %get-tuple-element.89), channel_id=1, source_target_pairs={{0,1},{1,0},{2,3},{3,2},{4,5},{5,4},{6,7},{7,6},{8,9},{9,8},{10,11... | collective-permute-start | bytes 153608 | tf_op jit(solution)/shard_map/ppermute | solution.py:596
  28.2 4.8 %collective-permute-start.18 = (bf16[96,256]{1,0:T(8,128)(2,1)S(1)}, bf16[96,256]{1,0:T(8,128)(2,1)S(1)}, u32[]{:S(2)}, u32[]{:S(2)}) collective-permute-start(bf16[96,256]{1,0:T(8,128)(2,1)S(1)} %get-tuple-element.94), channel_id=1, source_target_pairs={{0,1},{1,0},{2,3},{3,2},{4,8},{5,9},{6,10},{7,11},{8,4},{9,5},{10,... | collective-permute-start | bytes 147464 | tf_op jit(solution)/shard_map/ppermute | solution.py:591
  30.3 2.8 %collective-permute-start.19 = (bf16[96,256]{1,0:T(8,128)(2,1)S(1)}, bf16[96,256]{1,0:T(8,128)(2,1)S(1)}, u32[]{:S(2)}, u32[]{:S(2)}) collective-permute-start(bf16[96,256]{1,0:T(8,128)(2,1)S(1)} %get-tuple-element.95), channel_id=1, source_target_pairs={{0,4},{4,0},{8,12},{12,8},{16,20},{20,16},{24,28},{28,24},{1,5},{5... | collective-permute-start | bytes 147464 | tf_op jit(solution)/shard_map/ppermute | solution.py:596
